TPU v7x, 32 devices: a whole 2x2x4 slice. The times are simulated.
32 devices in a mesh: groups: 2 (over y), depth: 4 (over z), probe: 2 (over x), lat: 2 (over core).
Axes of the slice: x: 2, y: 2, z: 4, core: 2. Of those that a mesh axis runs over, the one named last changes fastest.
Arguments:
- specimen: float32 [2, 16, 768, 768], P(None, ('groups', 'depth'), 'lat'), parts along dimension 1, may hold values from -1 to 1, as said below
- illumination: float32 [2, 128, 128], replicated, may hold values from -5 to 5
- positions: int32 [1024, 2], P('groups'), parts along dimension 0, may hold values from 0 to 640
- scan_index: int32 [32, 4], P('groups', ('probe', 'lat')), parts along dimension 0, may hold values from 0 to 511
- frames: float32 [32, 4, 128, 128], P('groups', ('probe', 'lat')), parts along dimension 0, may hold values from 0 to 2
Outputs:
- specimen_grad: float32 [2, 16, 768, 768], P(None, ('groups', 'depth'), ('probe', 'lat')), parts along dimension 1
There are 2 independent parts, one for each index of `groups`. A program takes and returns all parts, laid end to end along the dimension named above; an argument that names none is the same for every part. Nothing has to cross between parts.
Inputs may be any that keep to these rules, and one draw needn't show every extreme that they name: `specimen`: every pixel's complex transmission has a magnitude of 0.99 to 1.
All inputs are finite; a program needn't handle non-finite values.
Results may differ from a plain program's by a relative error of at most 0.00055.
Values sent between devices are 32-bit elements; how exact they have to be, the bound alone decides.
No kernel may reach another device: no remote copies, remote signals or barrier semaphores. Data moves between devices by JAX's collectives and lax.ppermute only.
A program may use at most 128 MiB of HBM per device.

v0:
```python
import functools
import math

import jax
import jax.numpy as jnp
import ml_dtypes
import numpy as np
from jax import lax
from jax.experimental import pallas as pl
from jax.experimental.pallas import tpu as pltpu
from jax.sharding import PartitionSpec as P

FRESNEL = 8.0
SCOPED = 8 << 20
CROSSING = 3
F32 = jnp.float32
BF16 = jnp.bfloat16
HBM = pl.BlockSpec(memory_space=pl.ANY)
VMEM = pl.BlockSpec(memory_space=pltpu.VMEM)
SMEM = pl.BlockSpec(memory_space=pltpu.SMEM)


def in_hbm(x):
    return pltpu.with_memory_space_constraint(x, pltpu.HBM)


def in_vmem(x):
    return pltpu.with_memory_space_constraint(x, pltpu.VMEM)


def real_blocks(matrix):
    real, imag = matrix.real, matrix.imag
    left = np.block([[real, -imag], [imag, real]])
    right = np.block([[real, imag], [-imag, real]])
    return np.stack([left, right])


@functools.lru_cache(maxsize=None)
def make_tables(pixels):
    index = np.arange(pixels)
    freq = np.where(index < pixels // 2, index, index - pixels) / pixels
    spread = index[:, None] - index[None, :]
    phase = 2.0 * math.pi * freq * spread[:, :, None] - math.pi * FRESNEL * freq * freq
    propagator = np.mean(np.exp(1j * phase), axis=-1)
    turns = index[:, None] * index[None, :] % pixels
    fourier = np.exp(-2j * math.pi * turns / pixels) / math.sqrt(pixels)
    blocks = np.stack([real_blocks(propagator), real_blocks(fourier)]).astype(np.float32)
    high = blocks.astype(ml_dtypes.bfloat16)
    low = (blocks - high.astype(np.float32)).astype(ml_dtypes.bfloat16)
    return np.stack([high, low], axis=2)


def halves(x):
    high = x.astype(BF16)
    return high, (x - high.astype(F32)).astype(BF16)


def dot(a, b):
    return jnp.dot(a, b, preferred_element_type=F32)


def transform(left, right, fields):
    size = fields[0][0].shape[0]
    stacked = jnp.concatenate(
        [
            jnp.concatenate([real for real, _ in fields], axis=1),
            jnp.concatenate([imag for _, imag in fields], axis=1),
        ],
        axis=0,
    )
    high, low = halves(stacked)
    mid = dot(left[0], high) + (dot(left[1], high) + dot(left[0], low))
    rows = jnp.concatenate(
        [
            jnp.concatenate(
                [mid[:size, i * size : (i + 1) * size], mid[size:, i * size : (i + 1) * size]], axis=1
            )
            for i in range(len(fields))
        ],
        axis=0,
    )
    high, low = halves(rows)
    out = dot(high, right[0]) + (dot(high, right[1]) + dot(low, right[0]))
    return [
        (out[i * size : (i + 1) * size, :size], out[i * size : (i + 1) * size, size:])
        for i in range(len(fields))
    ]


def times(a, b):
    return a[0] * b[0] - a[1] * b[1], a[0] * b[1] + a[1] * b[0]


def times_conj(a, b):
    return a[0] * b[0] + a[1] * b[1], a[1] * b[0] - a[0] * b[1]


class Layout:
    def __init__(self, probes, count, layers, pixels, rows, height, width, only_sums=False):
        self.probes, self.count, self.layers, self.pixels = probes, count, layers, pixels
        self.groups = probes // count
        self.tall = pixels + 8
        self.rows, self.height, self.width = rows, height, width
        self.blocks = width // pixels
        self.deep = rows + 2 * self.tall
        self.column_bits = (width - 1).bit_length()
        self.name_bits = (4 * probes - 1).bit_length()
        self.stack = probes * layers * 2 * pixels
        self.seen_from = self.stack
        self.grads_from = 2 * self.stack
        self.frames_from = 3 * self.stack
        self.total_from = 0 if only_sums else self.frames_from + probes * pixels
        self.shape = (self.total_from + 2 * layers * self.blocks * self.deep, pixels)

    def stacked(self, group, i, layer, part):
        probe = group * self.count + i
        return ((probe * self.layers + layer) * 2 + part) * self.pixels

    def tile(self, start):
        return pl.ds(pl.multiple_of(start, 8), self.pixels)

    def patch(self, group, i, layer, part):
        return self.tile(self.stacked(group, i, layer, part))

    def seen(self, group, i, layer, part):
        return self.tile(self.seen_from + self.stacked(group, i, layer, part))

    def grad(self, group, i, layer, part):
        return self.tile(self.grads_from + self.stacked(group, i, layer, part))

    def grads_of(self, begin, end):
        each = self.stack // self.groups
        return self.grads_from + begin * each, self.grads_from + end * each

    def frame(self, group, i):
        return self.tile(self.frames_from + (group * self.count + i) * self.pixels)

    def total(self, part, layer, block, row):
        block = (part * self.layers + layer) * self.blocks + block
        return self.total_from + block * self.deep + row

    def pack(self, row, column, name):
        return (((row << self.column_bits) + column) << self.name_bits) + name

    def row(self, key):
        return key >> (self.column_bits + self.name_bits)

    def window(self, info, probe, partner=False):
        lane = lax.broadcasted_iota(jnp.int32, info.shape, 1)
        key = jnp.sum(jnp.where(lane == probe + partner * self.probes, info[...], 0))
        row = self.row(key)
        column = (key >> self.name_bits) & ((1 << self.column_bits) - 1)
        row0 = jnp.minimum(row // 8 * 8, self.height - self.tall)
        block = jnp.minimum(column // self.pixels, self.blocks - 2)
        return row0, row - row0, block, column - block * self.pixels


def call(lay, body, state, before, outs, scratch=(), flag=False, flops=1000, moved=1000, name=None):
    spaces = {"hbm": (HBM, in_hbm), "vmem": (VMEM, in_vmem), "smem": (SMEM, lambda x: x)}
    specs = [spaces[kind][0] for kind, _ in before]
    operands = [spaces[kind][1](x) for kind, x in before]
    at = len(before)
    aliases = {}
    if state is not None:
        specs.append(VMEM)
        operands.append(in_vmem(state))
        aliases = {at: 0}

    def kernel(*refs):
        body(*refs[:at], *refs[at + len(aliases) :])

    return pl.pallas_call(
        kernel,
        in_specs=specs,
        out_specs=[VMEM] * (1 + len(outs)) + [SMEM] * flag,
        out_shape=[pltpu.VMEM(shape, F32) for shape in (lay.shape, *outs)]
        + [jax.ShapeDtypeStruct((1,), jnp.int32)] * flag,
        scratch_shapes=list(scratch),
        input_output_aliases=aliases,
        compiler_params=pltpu.CompilerParams(vmem_limit_bytes=SCOPED),
        cost_estimate=pl.CostEstimate(flops=flops, bytes_accessed=moved, transcendentals=0),
        name=name,
    )(*operands)


def clear_total(lay, state):
    start = lay.total_from

    def body(state):
        state[pl.ds(start, lay.shape[0] - start), :] = jnp.zeros((lay.shape[0] - start, lay.pixels), F32)

    return call(lay, body, state, [], [], name="clear_total")[0]


def place_frames(lay, sections, info, everyone, pools, state):
    def body(info, everyone, *refs):
        *pools, state, late, sems = refs
        nearest = 2 * lay.probes
        reach = jnp.bool_(False)
        for ref in (info, everyone):
            reach |= lay.row(ref[0, nearest]) + lay.pixels > lay.rows
            reach |= lay.row(ref[0, nearest + 1]) < lay.rows
        late[0] = reach.astype(jnp.int32)
        lat, side = lax.axis_index("lat"), lax.axis_index("probe")
        section = lax.axis_index("depth")
        for act in ("start", "wait"):
            for probe in range(lay.probes):
                name = info[0, probe] & ((1 << lay.name_bits) - 1)
                owner = name // lay.probes
                slot = name % lay.probes
                if len(pools) > 1:
                    slot += ((owner // 2) ^ side) * lay.probes + ((owner % 2) ^ lat) * 2 * lay.probes
                first = 0
                for pool in pools:
                    size = pool.shape[0] // lay.pixels

                    @pl.when((section == sections - 1) & (slot >= first) & (slot < first + size))
                    def _(pool=pool, first=first, probe=probe, slot=slot):
                        copy = pltpu.make_async_copy(
                            pool.at[lay.tile((slot - first) * lay.pixels), :],
                            state.at[lay.frame(0, probe), :],
                            sems.at[probe],
                        )
                        getattr(copy, act)()

                    first += size

    pools = [("hbm", pool.reshape((-1, lay.pixels))) for pool in pools]
    return call(
        lay,
        body,
        state,
        [("smem", info), ("smem", everyone), *pools],
        [],
        flag=True,
        scratch=[pltpu.SemaphoreType.DMA((lay.probes,))],
        name="place_frames",
    )


def cut_patches(lay, info, own, other, state, begin, end):
    half = own.shape[2]
    tall, pixels = lay.tall, lay.pixels

    def one(probe, info, own, other, state, window):
        row0, down, block, shift = lay.window(info, probe)
        own_top = lax.axis_index("lat") == 0
        near_at = pl.ds(pl.multiple_of(block * pixels, pixels), pixels)
        far_at = pl.ds(pl.multiple_of((block + 1) * pixels, pixels), pixels)
        for source, is_top in ((own, own_top), (other, jnp.logical_not(own_top))):
            start = jnp.clip(row0 - jnp.where(is_top, 0, half), 0, half - tall)
            to = pl.ds(pl.multiple_of(jnp.where(is_top, 0, tall), 8), tall)
            rows = pl.ds(pl.multiple_of(start, 8), tall)

            @pl.when(jnp.where(is_top, row0 < half, row0 + tall > half))
            def _(source=source, rows=rows, to=to):
                for part in range(2):
                    for layer in range(lay.layers):
                        window[part, layer, to, 0:pixels] = source[part, layer, rows, near_at]
                        window[part, layer, to, pixels : 2 * pixels] = source[part, layer, rows, far_at]

        offset = jnp.where(row0 < half, jnp.maximum(row0 - (half - tall), 0), tall)
        rows = pl.ds(pl.multiple_of(offset, 8), tall)
        turn = (pixels - shift) % pixels
        lane = lax.broadcasted_iota(jnp.int32, (tall, pixels), 1)
        for part in range(2):
            for layer in range(lay.layers):
                near = pltpu.roll(window[part, layer, rows, 0:pixels], turn, 1)
                far = pltpu.roll(window[part, layer, rows, pixels : 2 * pixels], turn, 1)
                patch = jnp.where(lane < pixels - shift, near, far)
                patch = pltpu.roll(patch, (tall - down) % tall, 0)[:pixels]
                state[lay.patch(0, probe, layer, part), :] = patch

    def body(info, *refs):
        lax.fori_loop(begin, end, lambda probe, _: one(probe, info, *refs) or 0, 0)

    return call(
        lay,
        body,
        state,
        [("vmem", info), ("vmem", own), ("vmem", other)],
        [],
        scratch=[pltpu.VMEM((2, lay.layers, 2 * tall, 2 * pixels), F32)],
        name="cut_patches",
    )[0]


def section_cost(lay):
    size = lay.count * lay.pixels**2
    return dict(flops=lay.layers * 2 * 3 * 8 * size * lay.pixels, moved=(lay.layers * 2 + 4) * 8 * size)


def pair(ref, at):
    return ref[at(0), :], ref[at(1), :]


def run_forward(lay, tick, sections, tables, state, arrived, start_wave):
    def body(tables, *refs):
        arrived_ref = refs[0] if arrived is not None else None
        start_ref = refs[-3] if start_wave is not None else None
        state, leave = refs[-2:]
        section = lax.axis_index("depth")
        group = tick - section
        final = (section == sections - 1).astype(jnp.int32)

        @pl.when((group >= 0) & (group < lay.groups))
        def _():
            wave = []
            for i in range(lay.count):
                if arrived is None:
                    wave.append((start_ref[0], start_ref[1]))
                elif start_wave is None:
                    wave.append((arrived_ref[i, 0], arrived_ref[i, 1]))
                else:
                    wave.append(
                        tuple(jnp.where(section == 0, start_ref[p], arrived_ref[i, p]) for p in range(2))
                    )
            for layer in range(lay.layers):
                chi = []
                for i in range(lay.count):
                    for part in range(2):
                        state[lay.seen(group, i, layer, part), :] = wave[i][part]
                    chi.append(times(pair(state, functools.partial(lay.patch, group, i, layer)), wave[i]))
                at = final if layer == lay.layers - 1 else 0
                wave = transform((tables[at, 0, 0], tables[at, 0, 1]), (tables[at, 1, 0], tables[at, 1, 1]), chi)
            for i in range(lay.count):
                real, imag = wave[i]
                misfit = real * real + imag * imag - state[lay.frame(group, i), :]
                factor = jnp.where(final == 1, misfit, 1.0)
                leave[i, 0] = real * factor
                leave[i, 1] = imag * factor

    waves = [("vmem", x) for x in (arrived, start_wave) if x is not None]
    return call(
        lay,
        body,
        state,
        [("vmem", tables), *waves],
        [(lay.count, 2, lay.pixels, lay.pixels)],
        name="forward_section",
        **section_cost(lay),
    )


def run_backward(lay, tick, sections, tables, state, arrived, own):
    def body(tables, *refs):
        arrived_ref = refs[0] if arrived is not None else None
        own_ref = refs[-3] if own is not None else None
        state, leave = refs[-2:]
        section = lax.axis_index("depth")
        group = tick - (2 * (sections - 1) - section)
        final = (section == sections - 1).astype(jnp.int32)

        @pl.when((group >= 0) & (group < lay.groups))
        def _():
            wave = []
            for i in range(lay.count):
                if arrived is None:
                    wave.append((own_ref[i, 0], own_ref[i, 1]))
                elif own is None:
                    wave.append((arrived_ref[i, 0], arrived_ref[i, 1]))
                else:
                    wave.append(
                        tuple(jnp.where(final == 1, own_ref[i, p], arrived_ref[i, p]) for p in range(2))
                    )
            for layer in reversed(range(lay.layers)):
                at = final if layer == lay.layers - 1 else 0
                chi = transform((tables[at, 1, 0], tables[at, 1, 1]), (tables[at, 0, 0], tables[at, 0, 1]), wave)
                wave = []
                for i in range(lay.count):
                    real, imag = times_conj(chi[i], pair(state, functools.partial(lay.seen, group, i, layer)))
                    state[lay.grad(group, i, layer, 0), :] = real
                    state[lay.grad(group, i, layer, 1), :] = imag
                    wave.append(times_conj(chi[i], pair(state, functools.partial(lay.patch, group, i, layer))))
            for i in range(lay.count):
                leave[i, 0] = wave[i][0]
                leave[i, 1] = wave[i][1]

    waves = [("vmem", x) for x in (arrived, own) if x is not None]
    return call(
        lay,
        body,
        state,
        [("vmem", tables), *waves],
        [(lay.count, 2, lay.pixels, lay.pixels)],
        name="backward_section",
        **section_cost(lay),
    )


def deposit(lay, tick, sections, info, received, state):
    pixels, tall = lay.pixels, lay.tall

    def body(info, *refs):
        state = refs[-1]
        lane = lax.broadcasted_iota(jnp.int32, (tall, pixels), 1)
        blank = jnp.zeros((8, pixels), F32)
        base = lax.axis_index("probe") * lay.rows if lay.rows < lay.height else 0

        def add(probe, partner, active, load):
            row0, down, block, shift = lay.window(info, probe, partner)
            start = row0 - base + tall

            @pl.when(active & (start > 0) & (start < lay.rows + tall))
            def _():
                for layer in range(lay.layers):
                    for part in range(2):
                        padded = jnp.concatenate([load(layer, part), blank], axis=0)
                        turned = pltpu.roll(pltpu.roll(padded, down, 0), shift % pixels, 1)
                        near = pl.ds(pl.multiple_of(lay.total(part, layer, block, start), 8), tall)
                        far = pl.ds(pl.multiple_of(lay.total(part, layer, block + 1, start), 8), tall)
                        state[near, :] += jnp.where(lane >= shift, turned, 0.0)
                        state[far, :] += jnp.where(lane >= shift, 0.0, turned)

        if tick is not None:
            group = tick - (2 * (sections - 1) - lax.axis_index("depth"))
            active = (group >= 0) & (group < lay.groups)
            group = jnp.clip(group, 0, lay.groups - 1)
            for i in range(lay.count):
                add(
                    group * lay.count + i,
                    False,
                    active,
                    lambda layer, part, i=i: state[lay.grad(group, i, layer, part), :],
                )
        for ref, (first, grads) in zip(refs, received):

            def one(i, _, ref=ref, first=first):
                add(
                    first * lay.count + i,
                    True,
                    True,
                    lambda layer, part: ref[lay.patch(0, i, layer, part), :],
                )
                return 0

            lax.fori_loop(0, grads.shape[0] // (lay.layers * 2 * pixels), one, 0)

    return call(
        lay,
        body,
        state,
        [("vmem", info)] + [("vmem", grads) for _, grads in received],
        [],
        name="deposit_patches",
    )[0]


def split_rows(lay, state, owners, taken=(0, 8)):
    rows = lay.rows // (2 * owners)
    pieces = 4 * owners * lay.layers * lay.blocks

    def body(state, keep, send, rest, sems):
        lat = lax.axis_index("lat")
        copies = [pltpu.make_async_copy(state.at[pl.ds(taken[0], taken[1] - taken[0]), :], rest, sems.at[pieces])]
        for owner in range(owners):
            for kind, target in ((lat, keep), (1 - lat, send)):
                for part in range(2):
                    for layer in range(lay.layers):
                        for block in range(lay.blocks):
                            start = lay.total(part, layer, block, lay.tall + (2 * owner + kind) * rows)
                            copies.append(
                                pltpu.make_async_copy(
                                    state.at[pl.ds(pl.multiple_of(start, 8), rows), :],
                                    target.at[part, layer, owner, :, pl.ds(block * lay.pixels, lay.pixels)],
                                    sems.at[len(copies) - 1],
                                )
                            )
        for copy in copies:
            copy.start()
        for copy in copies:
            copy.wait()

    half = (2, lay.layers, owners, rows, lay.width)
    return pl.pallas_call(
        body,
        in_specs=[VMEM],
        out_specs=[VMEM, VMEM, HBM],
        out_shape=[
            pltpu.VMEM(half, F32),
            pltpu.VMEM(half, F32),
            pltpu.HBM((taken[1] - taken[0], lay.pixels), F32),
        ],
        scratch_shapes=[pltpu.SemaphoreType.DMA((pieces + 1,))],
        compiler_params=pltpu.CompilerParams(vmem_limit_bytes=SCOPED),
        name="split_rows",
    )(in_vmem(state))


def add_up(a, b):
    each = pl.BlockSpec((1, 1, *a.shape[2:]), lambda i, j: (i, j, 0, 0, 0))

    def body(a, b, out):
        out[...] = a[...] + b[...]

    return pl.pallas_call(
        body,
        grid=a.shape[:2],
        in_specs=[each, each],
        out_specs=each,
        out_shape=pltpu.HBM(a.shape, F32),
        compiler_params=pltpu.CompilerParams(vmem_limit_bytes=SCOPED),
        name="add_up",
    )(a, b)


def swap(shard, axis):
    return lax.ppermute(shard, axis, [(0, 1), (1, 0)])


def sort_probes(lay, early, positions, indices, specimen):
    n = lay.probes
    total = 4 * n

    def body(positions, *refs):
        *scans, specimen, info, brought, sem = refs
        copy = pltpu.make_async_copy(specimen, brought, sem)
        copy.start()
        lat, side = lax.axis_index("lat"), lax.axis_index("probe")
        lane = lax.broadcasted_iota(jnp.int32, (1, 128), 1)
        at = lax.broadcasted_iota(jnp.int32, (total, 128), 0)
        across = jnp.full((1, 128), jnp.iinfo(jnp.int32).max, jnp.int32)
        down = jnp.zeros((total, 128), jnp.int32)
        for which, scan in enumerate(scans):
            owner = (side ^ (which % 2)) * 2 + (lat ^ (which // 2))
            for i in range(n):
                place = scan[i]
                key = lay.pack(positions[0, place], positions[1, place], owner * n + i)
                across = jnp.where(lane == which * n + i, key, across)
                down = jnp.where(at == which * n + i, key, down)
        rank = jnp.sum((across < down).astype(jnp.int32), axis=1, keepdims=True)
        partner = lane // n
        order = 2 * (lane % n) + lat
        wanted = jnp.where((side ^ partner) == 0, 2 * n - 1 - order, 2 * n + order)
        reach = 2 * early * lay.count
        wanted = jnp.where(lane == 2 * n, 2 * n - 1 - reach, wanted)
        wanted = jnp.where(lane == 2 * n + 1, 2 * n + reach, wanted)
        wanted = jnp.where(lane > 2 * n + 1, -1, wanted)
        info[...] = jnp.sum(jnp.where(rank == wanted, down, 0), axis=0, keepdims=True)
        copy.wait()

    return pl.pallas_call(
        body,
        in_specs=[SMEM] * 5 + [HBM],
        out_specs=[VMEM, VMEM],
        out_shape=[pltpu.VMEM((1, 128), jnp.int32), pltpu.VMEM(specimen.shape, F32)],
        scratch_shapes=[pltpu.SemaphoreType.DMA(())],
        compiler_params=pltpu.CompilerParams(vmem_limit_bytes=SCOPED),
        name="sort_probes",
    )(positions.T, *indices, in_hbm(specimen))


def local(specimen, illumination, positions, scan_index, frames):
    pixels = illumination.shape[-1]
    _, layers, half, width = specimen.shape
    height = 2 * half
    tables = jnp.asarray(make_tables(pixels))
    sections = lax.axis_size("depth")
    owners = lax.axis_size("probe")
    paired = owners == 2 and lax.axis_size("groups") <= 2
    probes = scan_index.size
    count = 2 if probes % 4 == 0 else 1
    lay = Layout(probes, count, layers, pixels, half if paired else height, height, width)
    early = lay.groups // 2

    everyone = mine = None
    if paired:
        scan = scan_index.reshape(-1)
        beside = swap(scan, "lat")
        half_rows, beside = lax.optimization_barrier((specimen, beside))
        other = swap(half_rows, "lat")
        indices = [scan, swap(scan, "probe"), beside, swap(beside, "probe")]
        measured, *indices[1:] = lax.optimization_barrier((frames, *indices[1:]))
        end = sections - 1
        ends = [(2 * end, 2 * end + 1), (2 * end + 1, 2 * end)]
        mine = lax.ppermute(measured, ("depth", "probe"), ends)
        info, specimen = sort_probes(lay, early, positions, indices, specimen)
        everyone = swap(info, "groups") if lax.axis_size("groups") == 2 else info
    else:
        other = swap(specimen, "lat")
        corners = positions[scan_index.reshape(-1)]
        info = lay.pack(corners[:, 0], corners[:, 1], jnp.arange(probes, dtype=jnp.int32))
        info = everyone = jnp.pad(info, (0, 3 * probes))[None]
    state = cut_patches(lay, info, specimen, other, None, 0, count)
    def busy(tick, source, by):
        delay = source if by > 0 else 2 * (sections - 1) - source
        return 0 <= tick - delay < lay.groups

    def pass_on(wave, tick, by):
        pairs = [
            (source, source + by)
            for source in range(sections)
            if 0 <= source + by < sections and busy(tick, source, by)
        ]
        return lax.ppermute(wave, "depth", pairs) if pairs else None

    def grads_of(state, begin, end):
        begin, end = lay.grads_of(begin, end)
        return lax.slice_in_dim(state, begin, end)

    fill = sections - 1
    parts = [(0, early // 2), (early // 2, early)] if paired else []
    crossing = {}
    down = up = None
    middle = min(1 + -(-lay.groups // 2), lay.groups) * count
    cuts = {0: (count, middle), min(fill - 1, lay.groups // 2): (middle, probes)}
    for tick in range(lay.groups + 2 * fill):
        own = None
        if paired and tick == fill - 1:
            down, mine, everyone = lax.optimization_barrier((down, mine, everyone))
            crossed = [lax.ppermute(x, ("depth", "lat"), ends) for x in (frames, mine)]
        if tick < lay.groups + fill:
            start_wave = illumination if tick < lay.groups else None
            state, own = run_forward(lay, tick, sections, tables, state, down, start_wave)
            down = pass_on(own, tick, 1)
            if tick in cuts:
                state = cut_patches(lay, info, specimen, other, state, *cuts[tick])
            if tick == 0:
                state = clear_total(lay, state)
            if tick == fill - 1:
                pools = [frames, mine, *crossed] if paired else [frames]
                state, late = place_frames(lay, sections, info, everyone, pools, state)
        if tick >= fill:
            state, rising = run_backward(lay, tick, sections, tables, state, up, own)
            up = pass_on(rising, tick, -1)
            received = crossing.pop(tick, [])
            for begin, end in parts:
                if tick == end - 1 + 2 * fill:
                    due = min(tick + CROSSING, lay.groups + 2 * fill - 1)
                    crossing.setdefault(due, []).append((begin, swap(grads_of(state, begin, end), "probe")))
            state = deposit(lay, tick, sections, info, received, state)
    if not paired:
        keep, send, _ = split_rows(lay, state, owners)
        return lax.psum_scatter(keep + swap(send, "lat"), "probe", scatter_dimension=2, tiled=False)

    keep, send, late_grads = split_rows(lay, state, 1, lay.grads_of(early, lay.groups))

    def as_they_are(keep, received, grads):
        return add_up(keep, received)

    def with_partners(keep, received, grads):
        sums = Layout(probes, count, layers, pixels, half, height, width, only_sums=True)
        state = clear_total(sums, None)
        state = deposit(sums, None, sections, info, [(early, swap(grads, "probe"))], state)
        more, send, _ = split_rows(sums, state, 1)
        return add_up(keep + more, received + swap(send, "lat"))

    result = lax.cond(late[0] > 0, with_partners, as_they_are, keep, swap(send, "lat"), late_grads)
    return result[:, :, 0]


def solution(mesh):
    return jax.shard_map(
        local,
        mesh=mesh,
        in_specs=(
            P(None, ("groups", "depth"), "lat", None),
            P(),
            P("groups", None),
            P("groups", ("probe", "lat")),
            P("groups", ("probe", "lat"), None, None),
        ),
        out_specs=P(None, ("groups", "depth"), ("probe", "lat"), None),
        check_vma=False,
    )
```

profile of v0, /device:TPU:0, one launch (start us, length us, event | category | flops | bytes accessed | tf_op | source)
XLA Modules:
  0.0 162.8 jit_solution(1691563463847964855)
XLA Ops:
  1.7 2.7 %collective-permute-start.2 = (s32[16]{0:T(128)}, s32[16]{0:T(128)S(1)}, u32[]{:S(2)}, u32[]{:S(2)}) collective-permute-start(s32[16]{0:T(128)} %bitcast.11), channel_id=1, source_target_pairs={{0,2},{2,0},{1,3},{3,1},{4,6},{6,4},{5,7},{7,5},{8,10},{10,8},{9,1... | collective-permute-start | bytes 200 | tf_op jit(solution)/shard_map/ppermute | solution.py:508
  4.4 1.6 collective-permute-done.2.refs_1_
  6.1 1.9 %collective-permute-done.4.refs_3_ = s32[16]{0:T(128)S(1)} collective-permute-done((s32[16]{0:T(128)S(1)}, s32[16]{0:T(128)S(1)}, u32[]{:S(2)}, u32[]{:S(2)}) %collective-permute-start.4) | collective-permute-done | bytes 96 | tf_op jit(solution)/shard_map/ppermute | solution.py:508
  10.0 3.2 %sort_probes.1 = (s32[1,128]{1,0:T(1,128)S(1)}, f32[2,2,384,768]{3,2,1,0:T(8,128)S(1)}) custom-call(s32[2,512]{1,0:T(2,128)S(1)} %bitcast.9, s32[16]{0:T(128)S(1)} %bitcast.12, s32[16]{0:T(128)S(1)} %collective-permute-done.2.refs_1_, s32[16]{0:T(128)S(1)} %collective-permute-done.3.refs_2_, s32[16]{0:T(128)S(1)} %collective-permute-done.4.refs_3_, ...), custom_call_target="tpu_custom_call" | custom-call | tf_op jit(solution)/shard_map/sort_probes/pallas_call | solution.py:542
  14.2 1.3 forward_section.11
  15.5 2.2 %collective-permute-start.6 = (f32[2,2,128,128]{3,2,1,0:T(8,128)S(1)}, f32[2,2,128,128]{3,2,1,0:T(8,128)S(1)}, u32[]{:S(2)}, u32[]{:S(2)}) collective-permute-start(f32[2,2,128,128]{3,2,1,0:T(8,128)S(1)} %get-tuple-element.95), channel_id=1, source_target_pairs={{0,4},{1,5},{2,6},{3,7},{16,20},{17,21},{18,22},{19,23}} | collective-permute-start | bytes 786440 | tf_op jit(solution)/shard_map/ppermute | solution.py:595
  17.7 3.5 %cut_patches.4.refs_0_ = f32[42368,128]{1,0:T(8,128)S(1)} custom-call(s32[1,128]{1,0:T(1,128)S(1)} %get-tuple-element.92.refs_0_, f32[2,2,384,768]{3,2,1,0:T(8,128)S(1)} %get-tuple-element.93.refs_1_, f32[2,2,384,768]{3,2,1,0:T(8,128)S(1)} %collective-permute-done.5.refs_2_, f32[42368,128]{1,0:T(8,128)S(1)} %get-tuple-element.96.refs_3_), custom_call_target="tpu_custom_call", output_to_operand_aliasing={{}: (3, {})} | custom-call | flops 1000 | bytes 1000 | tf_op jit(solution)/shard_map/cut_patches/pallas_call | solution.py:172
  22.3 1.3 forward_section.12
  23.6 4.4 %collective-permute-start.7 = (f32[2,2,128,128]{3,2,1,0:T(8,128)S(1)}, f32[2,2,128,128]{3,2,1,0:T(8,128)S(1)}, u32[]{:S(2)}, u32[]{:S(2)}) collective-permute-start(f32[2,2,128,128]{3,2,1,0:T(8,128)S(1)} %get-tuple-element.97), channel_id=1, source_target_pairs={{0,4},{4,8},{1,5},{5,9},{2,6},{6,10},{3,7},{7,11},{16,20},{20,24},... | collective-permute-start | bytes 786440 | tf_op jit(solution)/shard_map/ppermute | solution.py:595
  28.1 1.6 collective-permute-start.9
  30.4 1.3 collective-permute-done.9.refs_1_
  32.6 1.3 forward_section.13
  34.0 4.4 %collective-permute-start.12 = (f32[2,2,128,128]{3,2,1,0:T(8,128)S(1)}, f32[2,2,128,128]{3,2,1,0:T(8,128)S(1)}, u32[]{:S(2)}, u32[]{:S(2)}) collective-permute-start(f32[2,2,128,128]{3,2,1,0:T(8,128)S(1)} %get-tuple-element.105), channel_id=1, source_target_pairs={{0,4},{4,8},{8,12},{1,5},{5,9},{9,13},{2,6},{6,10},{10,14},{3,7},{... | collective-permute-start | bytes 786440 | tf_op jit(solution)/shard_map/ppermute | solution.py:595
  38.4 2.5 %cut_patches.5.refs_6_ = f32[42368,128]{1,0:T(8,128)S(1)} custom-call(s32[1,128]{1,0:T(1,128)S(1)} %get-tuple-element.92.refs_0_, f32[2,2,384,768]{3,2,1,0:T(8,128)S(1)} %get-tuple-element.93.refs_1_, f32[2,2,384,768]{3,2,1,0:T(8,128)S(1)} %collective-permute-done.5.refs_2_, f32[42368,128]{1,0:T(8,128)S(1)} %get-tuple-element.103.refs_3_), custom_call_target="tpu_custom_call", output_to_operand_aliasing={{}: (3, {})} | custom-call | flops 1000 | bytes 1000 | tf_op jit(solution)/shard_map/cut_patches/pallas_call | solution.py:172
  42.3 2.0 %place_frames.1 = (f32[42368,128]{1,0:T(8,128)S(1)}, s32[1]{0:T(128)}) custom-call(s32[1,128]{1,0:T(1,128)S(1)} %get-tuple-element.92.refs_0_, s32[1,128]{1,0:T(1,128)S(1)} %collective-permute-done.9.refs_1_, f32[2048,128]{1,0:T(8,128)} %bitcast.15, f32[2048,128]{1,0:T(8,128)} %bitcast.16, f32[2048,128]{1,0:T(8,128)} %bitcast.17, ...), custom_call_target="tpu_custom_call", output_to_operand_aliasing={{0}: (6, {})} | custom-call | flops 1000 | bytes 1000 | tf_op jit(solution)/shard_map/place_frames/pallas_call | solution.py:172
  44.3 1.3 forward_section.14
  45.6 2.4 %collective-permute-start.14 = (f32[2,2,128,128]{3,2,1,0:T(8,128)S(1)}, f32[2,2,128,128]{3,2,1,0:T(8,128)S(1)}, u32[]{:S(2)}, u32[]{:S(2)}) collective-permute-start(f32[2,2,128,128]{3,2,1,0:T(8,128)S(1)} %get-tuple-element.107.refs_1_), channel_id=1, source_target_pairs={{0,4},{4,8},{8,12},{1,5},{5,9},{9,13},{2,6},{6,10},{10,14},{3,7},{... | collective-permute-start | bytes 786440 | tf_op jit(solution)/shard_map/ppermute | solution.py:595
  49.0 2.9 %collective-permute-done.14.refs_1_ = f32[2,2,128,128]{3,2,1,0:T(8,128)S(1)} collective-permute-done((f32[2,2,128,128]{3,2,1,0:T(8,128)S(1)}, f32[2,2,128,128]{3,2,1,0:T(8,128)S(1)}, u32[]{:S(2)}, u32[]{:S(2)}) %collective-permute-start.14) | collective-permute-done | bytes 262176 | tf_op jit(solution)/shard_map/ppermute | solution.py:595
  51.9 1.3 forward_section.15
  53.2 7.7 %collective-permute-start.16 = (f32[2,2,128,128]{3,2,1,0:T(8,128)S(1)}, f32[2,2,128,128]{3,2,1,0:T(8,128)S(1)}, u32[]{:S(2)}, u32[]{:S(2)}) collective-permute-start(f32[2,2,128,128]{3,2,1,0:T(8,128)S(1)} %get-tuple-element.111.refs_2_), channel_id=1, source_target_pairs={{0,4},{4,8},{8,12},{1,5},{5,9},{9,13},{2,6},{6,10},{10,14},{3,7},{... | collective-permute-start | bytes 786440 | tf_op jit(solution)/shard_map/ppermute | solution.py:595
  61.9 3.7 %collective-permute-done.16.refs_1_ = f32[2,2,128,128]{3,2,1,0:T(8,128)S(1)} collective-permute-done((f32[2,2,128,128]{3,2,1,0:T(8,128)S(1)}, f32[2,2,128,128]{3,2,1,0:T(8,128)S(1)}, u32[]{:S(2)}, u32[]{:S(2)}) %collective-permute-start.16) | collective-permute-done | bytes 262176 | tf_op jit(solution)/shard_map/ppermute | solution.py:595
  65.6 1.3 forward_section.16
  67.0 4.4 %collective-permute-start.18 = (f32[2,2,128,128]{3,2,1,0:T(8,128)S(1)}, f32[2,2,128,128]{3,2,1,0:T(8,128)S(1)}, u32[]{:S(2)}, u32[]{:S(2)}) collective-permute-start(f32[2,2,128,128]{3,2,1,0:T(8,128)S(1)} %get-tuple-element.115.refs_2_), channel_id=1, source_target_pairs={{0,4},{4,8},{8,12},{1,5},{5,9},{9,13},{2,6},{6,10},{10,14},{3,7},{... | collective-permute-start | bytes 786440 | tf_op jit(solution)/shard_map/ppermute | solution.py:595
  71.4 1.3 collective-permute-start.17
  73.2 2.0 %collective-permute-done.18.refs_1_ = f32[2,2,128,128]{3,2,1,0:T(8,128)S(1)} collective-permute-done((f32[2,2,128,128]{3,2,1,0:T(8,128)S(1)}, f32[2,2,128,128]{3,2,1,0:T(8,128)S(1)}, u32[]{:S(2)}, u32[]{:S(2)}) %collective-permute-start.18) | collective-permute-done | bytes 262176 | tf_op jit(solution)/shard_map/ppermute | solution.py:595
  75.2 1.3 forward_section.17
  76.6 5.1 %collective-permute-start.20 = (f32[2,2,128,128]{3,2,1,0:T(8,128)S(1)}, f32[2,2,128,128]{3,2,1,0:T(8,128)S(1)}, u32[]{:S(2)}, u32[]{:S(2)}) collective-permute-start(f32[2,2,128,128]{3,2,1,0:T(8,128)S(1)} %get-tuple-element.119.refs_2_), channel_id=1, source_target_pairs={{0,4},{4,8},{8,12},{1,5},{5,9},{9,13},{2,6},{6,10},{10,14},{3,7},{... | collective-permute-start | bytes 786440 | tf_op jit(solution)/shard_map/ppermute | solution.py:595
  81.7 1.3 backward_section.14
  83.0 1.3 collective-permute-start.19
  85.5 1.3 forward_section.18
  86.9 4.5 %collective-permute-start.22 = (f32[2,2,128,128]{3,2,1,0:T(8,128)S(1)}, f32[2,2,128,128]{3,2,1,0:T(8,128)S(1)}, u32[]{:S(2)}, u32[]{:S(2)}) collective-permute-start(f32[2,2,128,128]{3,2,1,0:T(8,128)S(1)} %get-tuple-element.123.refs_2_), channel_id=1, source_target_pairs={{0,4},{4,8},{8,12},{1,5},{5,9},{9,13},{2,6},{6,10},{10,14},{3,7},{... | collective-permute-start | bytes 786440 | tf_op jit(solution)/shard_map/ppermute | solution.py:595
  91.4 1.3 backward_section.15
  96.5 4.5 %collective-permute-done.21.refs_1_ = f32[2,2,128,128]{3,2,1,0:T(8,128)S(1)} collective-permute-done((f32[2,2,128,128]{3,2,1,0:T(8,128)S(1)}, f32[2,2,128,128]{3,2,1,0:T(8,128)S(1)}, u32[]{:S(2)}, u32[]{:S(2)}) %collective-permute-start.21) | collective-permute-done | bytes 262176 | tf_op jit(solution)/shard_map/ppermute | solution.py:595
  105.3 5.9 %collective-permute-done.23.refs_1_ = f32[2,2,128,128]{3,2,1,0:T(8,128)S(1)} collective-permute-done((f32[2,2,128,128]{3,2,1,0:T(8,128)S(1)}, f32[2,2,128,128]{3,2,1,0:T(8,128)S(1)}, u32[]{:S(2)}, u32[]{:S(2)}) %collective-permute-start.23) | collective-permute-done | bytes 262176 | tf_op jit(solution)/shard_map/ppermute | solution.py:595
  112.5 1.3 collective-permute-start.25
  113.9 1.6 collective-permute-start.31
  116.6 4.2 %collective-permute-done.25.refs_1_ = f32[2,2,128,128]{3,2,1,0:T(8,128)S(1)} collective-permute-done((f32[2,2,128,128]{3,2,1,0:T(8,128)S(1)}, f32[2,2,128,128]{3,2,1,0:T(8,128)S(1)}, u32[]{:S(2)}, u32[]{:S(2)}) %collective-permute-start.25) | collective-permute-done | bytes 262176 | tf_op jit(solution)/shard_map/ppermute | solution.py:595
  122.1 1.3 collective-permute-start.27
  123.4 1.8 %deposit_patches.20.refs_2_ = f32[42368,128]{1,0:T(8,128)S(1)} custom-call(s32[1,128]{1,0:T(1,128)S(1)} %get-tuple-element.92.refs_0_, f32[2048,128]{1,0:T(8,128)S(1)} %collective-permute-done.28.refs_1_, f32[42368,128]{1,0:T(8,128)S(1)} %get-tuple-element.138.refs_2_), custom_call_target="tpu_custom_call", output_to_operand_aliasing={{}: (2, {})} | custom-call | flops 1000 | bytes 1000 | tf_op jit(solution)/shard_map/deposit_patches/pallas_call | solution.py:172
  125.2 5.4 %collective-permute-done.27.refs_1_ = f32[2,2,128,128]{3,2,1,0:T(8,128)S(1)} collective-permute-done((f32[2,2,128,128]{3,2,1,0:T(8,128)S(1)}, f32[2,2,128,128]{3,2,1,0:T(8,128)S(1)}, u32[]{:S(2)}, u32[]{:S(2)}) %collective-permute-start.27) | collective-permute-done | bytes 262176 | tf_op jit(solution)/shard_map/ppermute | solution.py:595
  134.3 7.4 %collective-permute-done.29.refs_1_ = f32[2,2,128,128]{3,2,1,0:T(8,128)S(1)} collective-permute-done((f32[2,2,128,128]{3,2,1,0:T(8,128)S(1)}, f32[2,2,128,128]{3,2,1,0:T(8,128)S(1)}, u32[]{:S(2)}, u32[]{:S(2)}) %collective-permute-start.29) | collective-permute-done | bytes 262176 | tf_op jit(solution)/shard_map/ppermute | solution.py:595
  144.3 1.7 %deposit_patches.22.refs_2_ = f32[42368,128]{1,0:T(8,128)S(1)} custom-call(s32[1,128]{1,0:T(1,128)S(1)} %get-tuple-element.92.refs_0_, f32[2048,128]{1,0:T(8,128)S(1)} %collective-permute-done.31.refs_1_, f32[42368,128]{1,0:T(8,128)S(1)} %get-tuple-element.142.refs_2_), custom_call_target="tpu_custom_call", output_to_operand_aliasing={{}: (2, {})} | custom-call | flops 1000 | bytes 1000 | tf_op jit(solution)/shard_map/deposit_patches/pallas_call | solution.py:172
  146.0 5.3 %collective-permute-done.30.refs_1_ = f32[2,2,128,128]{3,2,1,0:T(8,128)S(1)} collective-permute-done((f32[2,2,128,128]{3,2,1,0:T(8,128)S(1)}, f32[2,2,128,128]{3,2,1,0:T(8,128)S(1)}, u32[]{:S(2)}, u32[]{:S(2)}) %collective-permute-start.30) | collective-permute-done | bytes 262176 | tf_op jit(solution)/shard_map/ppermute | solution.py:595
  151.3 2.0 %backward_section.21 = (f32[42368,128]{1,0:T(8,128)S(1)}, f32[2,2,128,128]{3,2,1,0:T(8,128)}) custom-call(bf16[2,2,2,256,256]{4,3,2,1,0:T(8,128)(2,1)S(1)} %copy-done, f32[2,2,128,128]{3,2,1,0:T(8,128)S(1)} %collective-permute-done.30.refs_1_, f32[42368,128]{1,0:T(8,128)S(1)} %deposit_patches.22.refs_2_), custom_call_target="tpu_custom_call", output_to_operand_aliasing={{0}: (2, {})} | custom-call | flops 402653184 | bytes 2097152 | tf_op jit(solution)/shard_map/backward_section/pallas_call | solution.py:172
  154.4 1.9 %split_rows.3 = (f32[2,2,1,192,768]{4,3,2,1,0:T(8,128)S(1)}, f32[2,2,1,192,768]{4,3,2,1,0:T(8,128)S(1)}, f32[4096,128]{1,0:T(8,128)}) custom-call(f32[42368,128]{1,0:T(8,128)S(1)} %deposit_patches.23.state), custom_call_target="tpu_custom_call" | custom-call | tf_op jit(solution)/shard_map/split_rows/pallas_call | solution.py:475
  157.0 3.8 %collective-permute-done.32 = f32[2,2,1,192,768]{4,3,2,1,0:T(8,128)S(1)} collective-permute-done((f32[2,2,1,192,768]{4,3,2,1,0:T(8,128)S(1)}, f32[2,2,1,192,768]{4,3,2,1,0:T(8,128)S(1)}, u32[]{:S(2)}, u32[]{:S(2)}) %collective-permute-start.32) | collective-permute-done | bytes 2359328 | tf_op jit(solution)/shard_map/ppermute | solution.py:508
  160.8 1.9 %conditional.1 = (f32[2,2,192,768]{3,2,1,0:T(8,128)}) conditional(s32[]{:T(128)} %bitcast.8, (f32[2,2,1,192,768]{4,3,2,1,0:T(8,128)S(1)}, f32[2,2,1,192,768]{4,3,2,1,0:T(8,128)S(1)}) %tuple.19, (f32[4096,128]{1,0:T(8,128)}, s32[1,128]{1,0:T(1,128)S(1)}, f32[2,2,1,192,768]{4,3,2,1,0:T(8,128)S(1)}, f32[2,2,1,192,768]{4,3,2,1,0:T(8,128)S(1)}) %tuple.20), branch_computations={%region_0.0_spmd, %region_1.0_spmd} | conditional | flops 1181648 | bytes 31983656 | solution.py:648
  160.8 1.9 %add_up.2 = f32[2,2,1,192,768]{4,3,2,1,0:T(8,128)} custom-call(f32[2,2,1,192,768]{4,3,2,1,0:T(8,128)S(1)} %get-tuple-element.21.a, f32[2,2,1,192,768]{4,3,2,1,0:T(8,128)S(1)} %get-tuple-element.22.b), custom_call_target="tpu_custom_call" | custom-call | tf_op jit(solution)/shard_map/cond/branch_0_fun/add_up/pallas_call | solution.py:496
  (74 shorter events, 31.7 us)
Async XLA Ops:
  0.0 14.2 %copy-start = (bf16[2,2,2,256,256]{4,3,2,1,0:T(8,128)(2,1)S(1)}, bf16[2,2,2,256,256]{4,3,2,1,0:T(8,128)(2,1)}, u32[]{:S(2)}) copy-start(bf16[2,2,2,256,256]{4,3,2,1,0:T(8,128)(2,1)} %constant.5.clone.refs_0_) | copy-start | bytes 3145732
  0.0 14.2 %copy-start.1 = (f32[2,128,128]{2,1,0:T(8,128)S(1)}, f32[2,128,128]{2,1,0:T(8,128)}, u32[]{:S(2)}) copy-start(f32[2,128,128]{2,1,0:T(8,128)} %refs_2_.13) | copy-start | bytes 393220
  0.0 1.4 collective-permute-start.3
  1.4 11.9 %collective-permute-start.5 = (f32[2,2,384,768]{3,2,1,0:T(8,128)}, f32[2,2,384,768]{3,2,1,0:T(8,128)S(1)}, u32[]{:S(2)}, u32[]{:S(2)}) collective-permute-start(f32[2,2,384,768]{3,2,1,0:T(8,128)} %refs_4_.1), channel_id=1, source_target_pairs={{0,1},{1,0},{2,3},{3,2},{4,5},{5,4},{6,7},{7,6},{8,9},{9,8},{10,11... | collective-permute-start | bytes 14155784 | tf_op jit(solution)/shard_map/ppermute | solution.py:508
  1.7 4.3 %collective-permute-start.2 = (s32[16]{0:T(128)}, s32[16]{0:T(128)S(1)}, u32[]{:S(2)}, u32[]{:S(2)}) collective-permute-start(s32[16]{0:T(128)} %bitcast.11), channel_id=1, source_target_pairs={{0,2},{2,0},{1,3},{3,1},{4,6},{6,4},{5,7},{7,5},{8,10},{10,8},{9,1... | collective-permute-start | bytes 200 | tf_op jit(solution)/shard_map/ppermute | solution.py:508
  4.4 3.5 %collective-permute-start.4 = (s32[16]{0:T(128)S(1)}, s32[16]{0:T(128)S(1)}, u32[]{:S(2)}, u32[]{:S(2)}) collective-permute-start(s32[16]{0:T(128)S(1)} %collective-permute-done.3.refs_2_), channel_id=1, source_target_pairs={{0,2},{2,0},{1,3},{3,1},{4,6},{6,4},{5,7},{7,5},{8,10},{10,8},{9,1... | collective-permute-start | bytes 200 | tf_op jit(solution)/shard_map/ppermute | solution.py:508
  7.9 23.7 %collective-permute-start.8 = (f32[16,1,128,128]{3,2,1,0:T(8,128)}, f32[16,1,128,128]{3,2,1,0:T(8,128)S(1)}, u32[]{:S(2)}, u32[]{:S(2)}) collective-permute-start(f32[16,1,128,128]{3,2,1,0:T(8,128)} %param.12), channel_id=1, source_target_pairs={{12,14},{14,12},{13,15},{15,13},{28,30},{30,28},{29,31},{31,29}} | collective-permute-start | bytes 3145736 | tf_op jit(solution)/shard_map/ppermute | solution.py:576
  8.7 0.7 copy-start.2
  9.4 0.7 copy-start.3
  15.5 6.8 %collective-permute-start.6 = (f32[2,2,128,128]{3,2,1,0:T(8,128)S(1)}, f32[2,2,128,128]{3,2,1,0:T(8,128)S(1)}, u32[]{:S(2)}, u32[]{:S(2)}) collective-permute-start(f32[2,2,128,128]{3,2,1,0:T(8,128)S(1)} %get-tuple-element.95), channel_id=1, source_target_pairs={{0,4},{1,5},{2,6},{3,7},{16,20},{17,21},{18,22},{19,23}} | collective-permute-start | bytes 786440 | tf_op jit(solution)/shard_map/ppermute | solution.py:595
  21.8 7.9 %copy-start.4 = (f32[16,1,128,128]{3,2,1,0:T(8,128)S(1)}, f32[16,1,128,128]{3,2,1,0:T(8,128)}, u32[]{:S(2)}) copy-start(f32[16,1,128,128]{3,2,1,0:T(8,128)} %param.12) | copy-start | bytes 3145732
  23.6 8.3 %collective-permute-start.7 = (f32[2,2,128,128]{3,2,1,0:T(8,128)S(1)}, f32[2,2,128,128]{3,2,1,0:T(8,128)S(1)}, u32[]{:S(2)}, u32[]{:S(2)}) collective-permute-start(f32[2,2,128,128]{3,2,1,0:T(8,128)S(1)} %get-tuple-element.97), channel_id=1, source_target_pairs={{0,4},{4,8},{1,5},{5,9},{2,6},{6,10},{3,7},{7,11},{16,20},{20,24},... | collective-permute-start | bytes 786440 | tf_op jit(solution)/shard_map/ppermute | solution.py:595
  28.1 3.6 %collective-permute-start.9 = (s32[1,128]{1,0:T(1,128)S(1)}, s32[1,128]{1,0:T(1,128)S(1)}, u32[]{:S(2)}, u32[]{:S(2)}) collective-permute-start(s32[1,128]{1,0:T(1,128)S(1)} %get-tuple-element.92.refs_0_), channel_id=1, source_target_pairs={{0,16},{16,0},{1,17},{17,1},{2,18},{18,2},{3,19},{19,3},{4,20},{20... | collective-permute-start | bytes 1544 | tf_op jit(solution)/shard_map/ppermute | solution.py:508
  29.6 11.3 %collective-permute-start.10 = (f32[16,1,128,128]{3,2,1,0:T(8,128)S(1)}, f32[16,1,128,128]{3,2,1,0:T(8,128)S(1)}, u32[]{:S(2)}, u32[]{:S(2)}) collective-permute-start(f32[16,1,128,128]{3,2,1,0:T(8,128)S(1)} %copy-done.4), channel_id=1, source_target_pairs={{12,13},{13,12},{14,15},{15,14},{28,29},{29,28},{30,31},{31,30}} | collective-permute-start | bytes 3145736 | tf_op jit(solution)/shard_map/ppermute | solution.py:611
  31.7 9.2 %copy-start.5 = (f32[16,1,128,128]{3,2,1,0:T(8,128)}, f32[16,1,128,128]{3,2,1,0:T(8,128)S(1)}, u32[]{:S(2)}) copy-start(f32[16,1,128,128]{3,2,1,0:T(8,128)S(1)} %collective-permute-done.8) | copy-start | bytes 3145732
  31.9 9.0 %collective-permute-start.11 = (f32[16,1,128,128]{3,2,1,0:T(8,128)S(1)}, f32[16,1,128,128]{3,2,1,0:T(8,128)S(1)}, u32[]{:S(2)}, u32[]{:S(2)}) collective-permute-start(f32[16,1,128,128]{3,2,1,0:T(8,128)S(1)} %collective-permute-done.8), channel_id=1, source_target_pairs={{12,13},{13,12},{14,15},{15,14},{28,29},{29,28},{30,31},{31,30}} | collective-permute-start | bytes 3145736 | tf_op jit(solution)/shard_map/ppermute | solution.py:611
  34.0 10.3 %collective-permute-start.12 = (f32[2,2,128,128]{3,2,1,0:T(8,128)S(1)}, f32[2,2,128,128]{3,2,1,0:T(8,128)S(1)}, u32[]{:S(2)}, u32[]{:S(2)}) collective-permute-start(f32[2,2,128,128]{3,2,1,0:T(8,128)S(1)} %get-tuple-element.105), channel_id=1, source_target_pairs={{0,4},{4,8},{8,12},{1,5},{5,9},{9,13},{2,6},{6,10},{10,14},{3,7},{... | collective-permute-start | bytes 786440 | tf_op jit(solution)/shard_map/ppermute | solution.py:595
  40.9 1.0 copy-start.6
  40.9 1.3 copy-start.7
  45.6 6.2 %collective-permute-start.14 = (f32[2,2,128,128]{3,2,1,0:T(8,128)S(1)}, f32[2,2,128,128]{3,2,1,0:T(8,128)S(1)}, u32[]{:S(2)}, u32[]{:S(2)}) collective-permute-start(f32[2,2,128,128]{3,2,1,0:T(8,128)S(1)} %get-tuple-element.107.refs_1_), channel_id=1, source_target_pairs={{0,4},{4,8},{8,12},{1,5},{5,9},{9,13},{2,6},{6,10},{10,14},{3,7},{... | collective-permute-start | bytes 786440 | tf_op jit(solution)/shard_map/ppermute | solution.py:595
  48.0 12.9 %collective-permute-start.13 = (f32[2,2,128,128]{3,2,1,0:T(8,128)S(1)}, f32[2,2,128,128]{3,2,1,0:T(8,128)S(1)}, u32[]{:S(2)}, u32[]{:S(2)}) collective-permute-start(f32[2,2,128,128]{3,2,1,0:T(8,128)S(1)} %get-tuple-element.109), channel_id=1, source_target_pairs={{12,8},{13,9},{14,10},{15,11},{28,24},{29,25},{30,26},{31,27}} | collective-permute-start | bytes 786440 | tf_op jit(solution)/shard_map/ppermute | solution.py:595
  53.2 12.4 %collective-permute-start.16 = (f32[2,2,128,128]{3,2,1,0:T(8,128)S(1)}, f32[2,2,128,128]{3,2,1,0:T(8,128)S(1)}, u32[]{:S(2)}, u32[]{:S(2)}) collective-permute-start(f32[2,2,128,128]{3,2,1,0:T(8,128)S(1)} %get-tuple-element.111.refs_2_), channel_id=1, source_target_pairs={{0,4},{4,8},{8,12},{1,5},{5,9},{9,13},{2,6},{6,10},{10,14},{3,7},{... | collective-permute-start | bytes 786440 | tf_op jit(solution)/shard_map/ppermute | solution.py:595
  60.9 10.4 %collective-permute-start.15 = (f32[2,2,128,128]{3,2,1,0:T(8,128)S(1)}, f32[2,2,128,128]{3,2,1,0:T(8,128)S(1)}, u32[]{:S(2)}, u32[]{:S(2)}) collective-permute-start(f32[2,2,128,128]{3,2,1,0:T(8,128)S(1)} %get-tuple-element.113), channel_id=1, source_target_pairs={{8,4},{12,8},{9,5},{13,9},{10,6},{14,10},{11,7},{15,11},{24,20},{2... | collective-permute-start | bytes 786440 | tf_op jit(solution)/shard_map/ppermute | solution.py:595
  67.0 8.3 %collective-permute-start.18 = (f32[2,2,128,128]{3,2,1,0:T(8,128)S(1)}, f32[2,2,128,128]{3,2,1,0:T(8,128)S(1)}, u32[]{:S(2)}, u32[]{:S(2)}) collective-permute-start(f32[2,2,128,128]{3,2,1,0:T(8,128)S(1)} %get-tuple-element.115.refs_2_), channel_id=1, source_target_pairs={{0,4},{4,8},{8,12},{1,5},{5,9},{9,13},{2,6},{6,10},{10,14},{3,7},{... | collective-permute-start | bytes 786440 | tf_op jit(solution)/shard_map/ppermute | solution.py:595
  71.4 10.3 %collective-permute-start.17 = (f32[2,2,128,128]{3,2,1,0:T(8,128)S(1)}, f32[2,2,128,128]{3,2,1,0:T(8,128)S(1)}, u32[]{:S(2)}, u32[]{:S(2)}) collective-permute-start(f32[2,2,128,128]{3,2,1,0:T(8,128)S(1)} %get-tuple-element.117), channel_id=1, source_target_pairs={{4,0},{8,4},{12,8},{5,1},{9,5},{13,9},{6,2},{10,6},{14,10},{7,3},{... | collective-permute-start | bytes 786440 | tf_op jit(solution)/shard_map/ppermute | solution.py:595
  76.6 9.0 %collective-permute-start.20 = (f32[2,2,128,128]{3,2,1,0:T(8,128)S(1)}, f32[2,2,128,128]{3,2,1,0:T(8,128)S(1)}, u32[]{:S(2)}, u32[]{:S(2)}) collective-permute-start(f32[2,2,128,128]{3,2,1,0:T(8,128)S(1)} %get-tuple-element.119.refs_2_), channel_id=1, source_target_pairs={{0,4},{4,8},{8,12},{1,5},{5,9},{9,13},{2,6},{6,10},{10,14},{3,7},{... | collective-permute-start | bytes 786440 | tf_op jit(solution)/shard_map/ppermute | solution.py:595
  83.0 8.3 %collective-permute-start.19 = (f32[2,2,128,128]{3,2,1,0:T(8,128)S(1)}, f32[2,2,128,128]{3,2,1,0:T(8,128)S(1)}, u32[]{:S(2)}, u32[]{:S(2)}) collective-permute-start(f32[2,2,128,128]{3,2,1,0:T(8,128)S(1)} %get-tuple-element.121), channel_id=1, source_target_pairs={{4,0},{8,4},{12,8},{5,1},{9,5},{13,9},{6,2},{10,6},{14,10},{7,3},{... | collective-permute-start | bytes 786440 | tf_op jit(solution)/shard_map/ppermute | solution.py:595
  86.9 8.8 %collective-permute-start.22 = (f32[2,2,128,128]{3,2,1,0:T(8,128)S(1)}, f32[2,2,128,128]{3,2,1,0:T(8,128)S(1)}, u32[]{:S(2)}, u32[]{:S(2)}) collective-permute-start(f32[2,2,128,128]{3,2,1,0:T(8,128)S(1)} %get-tuple-element.123.refs_2_), channel_id=1, source_target_pairs={{0,4},{4,8},{8,12},{1,5},{5,9},{9,13},{2,6},{6,10},{10,14},{3,7},{... | collective-permute-start | bytes 786440 | tf_op jit(solution)/shard_map/ppermute | solution.py:595
  92.7 8.3 %collective-permute-start.21 = (f32[2,2,128,128]{3,2,1,0:T(8,128)S(1)}, f32[2,2,128,128]{3,2,1,0:T(8,128)S(1)}, u32[]{:S(2)}, u32[]{:S(2)}) collective-permute-start(f32[2,2,128,128]{3,2,1,0:T(8,128)S(1)} %get-tuple-element.125), channel_id=1, source_target_pairs={{4,0},{8,4},{12,8},{5,1},{9,5},{13,9},{6,2},{10,6},{14,10},{7,3},{... | collective-permute-start | bytes 786440 | tf_op jit(solution)/shard_map/ppermute | solution.py:595
  94.1 29.4 %collective-permute-start.28 = (f32[2048,128]{1,0:T(8,128)S(1)}, f32[2048,128]{1,0:T(8,128)S(1)}, u32[]{:S(2)}, u32[]{:S(2)}) collective-permute-start(f32[2048,128]{1,0:T(8,128)S(1)} %slice.6), channel_id=1, source_target_pairs={{0,2},{2,0},{1,3},{3,1},{4,6},{6,4},{5,7},{7,5},{8,10},{10,8},{9,1... | collective-permute-start | bytes 3145736 | tf_op jit(solution)/shard_map/ppermute | solution.py:508
  95.8 8.9 %collective-permute-start.24 = (f32[2,2,128,128]{3,2,1,0:T(8,128)S(1)}, f32[2,2,128,128]{3,2,1,0:T(8,128)S(1)}, u32[]{:S(2)}, u32[]{:S(2)}) collective-permute-start(f32[2,2,128,128]{3,2,1,0:T(8,128)S(1)} %get-tuple-element.127.refs_2_), channel_id=1, source_target_pairs={{4,8},{8,12},{5,9},{9,13},{6,10},{10,14},{7,11},{11,15},{20,24},{2... | collective-permute-start | bytes 786440 | tf_op jit(solution)/shard_map/ppermute | solution.py:595
  102.2 9.0 %collective-permute-start.23 = (f32[2,2,128,128]{3,2,1,0:T(8,128)S(1)}, f32[2,2,128,128]{3,2,1,0:T(8,128)S(1)}, u32[]{:S(2)}, u32[]{:S(2)}) collective-permute-start(f32[2,2,128,128]{3,2,1,0:T(8,128)S(1)} %get-tuple-element.129), channel_id=1, source_target_pairs={{4,0},{8,4},{12,8},{5,1},{9,5},{13,9},{6,2},{10,6},{14,10},{7,3},{... | collective-permute-start | bytes 786440 | tf_op jit(solution)/shard_map/ppermute | solution.py:595
  104.7 11.9 %collective-permute-start.26 = (f32[2,2,128,128]{3,2,1,0:T(8,128)S(1)}, f32[2,2,128,128]{3,2,1,0:T(8,128)S(1)}, u32[]{:S(2)}, u32[]{:S(2)}) collective-permute-start(f32[2,2,128,128]{3,2,1,0:T(8,128)S(1)} %get-tuple-element.131.refs_2_), channel_id=1, source_target_pairs={{8,12},{9,13},{10,14},{11,15},{24,28},{25,29},{26,30},{27,31}} | collective-permute-start | bytes 786440 | tf_op jit(solution)/shard_map/ppermute | solution.py:595
  112.5 8.3 %collective-permute-start.25 = (f32[2,2,128,128]{3,2,1,0:T(8,128)S(1)}, f32[2,2,128,128]{3,2,1,0:T(8,128)S(1)}, u32[]{:S(2)}, u32[]{:S(2)}) collective-permute-start(f32[2,2,128,128]{3,2,1,0:T(8,128)S(1)} %get-tuple-element.133), channel_id=1, source_target_pairs={{4,0},{8,4},{12,8},{5,1},{9,5},{13,9},{6,2},{10,6},{14,10},{7,3},{... | collective-permute-start | bytes 786440 | tf_op jit(solution)/shard_map/ppermute | solution.py:595
  113.9 30.4 %collective-permute-start.31 = (f32[2048,128]{1,0:T(8,128)S(1)}, f32[2048,128]{1,0:T(8,128)S(1)}, u32[]{:S(2)}, u32[]{:S(2)}) collective-permute-start(f32[2048,128]{1,0:T(8,128)S(1)} %slice.7), channel_id=1, source_target_pairs={{0,2},{2,0},{1,3},{3,1},{4,6},{6,4},{5,7},{7,5},{8,10},{10,8},{9,1... | collective-permute-start | bytes 3145736 | tf_op jit(solution)/shard_map/ppermute | solution.py:508
  122.1 8.5 %collective-permute-start.27 = (f32[2,2,128,128]{3,2,1,0:T(8,128)S(1)}, f32[2,2,128,128]{3,2,1,0:T(8,128)S(1)}, u32[]{:S(2)}, u32[]{:S(2)}) collective-permute-start(f32[2,2,128,128]{3,2,1,0:T(8,128)S(1)} %get-tuple-element.137), channel_id=1, source_target_pairs={{4,0},{8,4},{12,8},{5,1},{9,5},{13,9},{6,2},{10,6},{14,10},{7,3},{... | collective-permute-start | bytes 786440 | tf_op jit(solution)/shard_map/ppermute | solution.py:595
  131.9 9.8 %collective-permute-start.29 = (f32[2,2,128,128]{3,2,1,0:T(8,128)S(1)}, f32[2,2,128,128]{3,2,1,0:T(8,128)S(1)}, u32[]{:S(2)}, u32[]{:S(2)}) collective-permute-start(f32[2,2,128,128]{3,2,1,0:T(8,128)S(1)} %get-tuple-element.139), channel_id=1, source_target_pairs={{4,0},{8,4},{5,1},{9,5},{6,2},{10,6},{7,3},{11,7},{20,16},{24,20},... | collective-permute-start | bytes 786440 | tf_op jit(solution)/shard_map/ppermute | solution.py:595
  143.0 8.3 %collective-permute-start.30 = (f32[2,2,128,128]{3,2,1,0:T(8,128)S(1)}, f32[2,2,128,128]{3,2,1,0:T(8,128)S(1)}, u32[]{:S(2)}, u32[]{:S(2)}) collective-permute-start(f32[2,2,128,128]{3,2,1,0:T(8,128)S(1)} %get-tuple-element.141), channel_id=1, source_target_pairs={{4,0},{5,1},{6,2},{7,3},{20,16},{21,17},{22,18},{23,19}} | collective-permute-start | bytes 786440 | tf_op jit(solution)/shard_map/ppermute | solution.py:595
  156.2 4.6 %collective-permute-start.32 = (f32[2,2,1,192,768]{4,3,2,1,0:T(8,128)S(1)}, f32[2,2,1,192,768]{4,3,2,1,0:T(8,128)S(1)}, u32[]{:S(2)}, u32[]{:S(2)}) collective-permute-start(f32[2,2,1,192,768]{4,3,2,1,0:T(8,128)S(1)} %get-tuple-element.145), channel_id=1, source_target_pairs={{0,1},{1,0},{2,3},{3,2},{4,5},{5,4},{6,7},{7,6},{8,9},{9,8},{10,11... | collective-permute-start | bytes 7077896 | tf_op jit(solution)/shard_map/ppermute | solution.py:508
where the time goes:
time: 163 us
  starting transfers between devices  57.6 us (35%)
  waiting for transfers between devices  51.9 us (32%)
  Pallas kernels  49.2 us (30%)
  local copies, waits for them, and re-layouts  2.81 us (2%)
    ppermute x20, starting transfers between devices, pass_on(): return lax.ppermute(wave, 'depth', pairs) if pairs else None  48.1 us
    ppermute x20, waiting for transfers between devices, pass_on(): return lax.ppermute(wave, 'depth', pairs) if pairs else None  42.3 us
    pallas_call x38, Pallas kernels, call(): pl.pallas_call(kernel, in_specs=specs, out_specs=[VMEM] * (1 + len(outs))...  42.1 us
    ppermute x8, waiting for transfers between devices, swap(): return lax.ppermute(shard, axis, [(0, 1), (1, 0)])  9.61 us
    ppermute x8, starting transfers between devices, swap(): return lax.ppermute(shard, axis, [(0, 1), (1, 0)])  7.29 us
  transfers between devices with their start and end apart: 31, of which 17 were waited for; matrix products, arithmetic and copies ran while one was open for 0% of the time, Pallas kernels for 25%

commit v1 on v0

--- a/solution.py
+++ b/solution.py
@@ -145,9 +145,9 @@
     def row(self, key):
         return key >> (self.column_bits + self.name_bits)
 
-    def window(self, info, probe, partner=False):
+    def window(self, info, probe, whose=0):
         lane = lax.broadcasted_iota(jnp.int32, info.shape, 1)
-        key = jnp.sum(jnp.where(lane == probe + partner * self.probes, info[...], 0))
+        key = jnp.sum(jnp.where(lane == probe + whose * self.probes, info[...], 0))
         row = self.row(key)
         column = (key >> self.name_bits) & ((1 << self.column_bits) - 1)
         row0 = jnp.minimum(row // 8 * 8, self.height - self.tall)
@@ -172,9 +172,9 @@
     return pl.pallas_call(
         kernel,
         in_specs=specs,
-        out_specs=[VMEM] * (1 + len(outs)) + [SMEM] * flag,
+        out_specs=[VMEM] * (1 + len(outs) + flag),
         out_shape=[pltpu.VMEM(shape, F32) for shape in (lay.shape, *outs)]
-        + [jax.ShapeDtypeStruct((1,), jnp.int32)] * flag,
+        + [pltpu.VMEM((1, 128), jnp.int32)] * flag,
         scratch_shapes=list(scratch),
         input_output_aliases=aliases,
         compiler_params=pltpu.CompilerParams(vmem_limit_bytes=SCOPED),
@@ -195,37 +195,40 @@
 def place_frames(lay, sections, info, everyone, pools, state):
     def body(info, everyone, *refs):
         *pools, state, late, sems = refs
-        nearest = 2 * lay.probes
+        nearest = 3 * lay.probes
         reach = jnp.bool_(False)
         for ref in (info, everyone):
             reach |= lay.row(ref[0, nearest]) + lay.pixels > lay.rows
             reach |= lay.row(ref[0, nearest + 1]) < lay.rows
-        late[0] = reach.astype(jnp.int32)
+        late[...] = jnp.full(late.shape, reach.astype(jnp.int32), jnp.int32)
         lat, side = lax.axis_index("lat"), lax.axis_index("probe")
-        section = lax.axis_index("depth")
-        for act in ("start", "wait"):
-            for probe in range(lay.probes):
-                name = info[0, probe] & ((1 << lay.name_bits) - 1)
-                owner = name // lay.probes
-                slot = name % lay.probes
-                if len(pools) > 1:
-                    slot += ((owner // 2) ^ side) * lay.probes + ((owner % 2) ^ lat) * 2 * lay.probes
-                first = 0
-                for pool in pools:
-                    size = pool.shape[0] // lay.pixels
-
-                    @pl.when((section == sections - 1) & (slot >= first) & (slot < first + size))
-                    def _(pool=pool, first=first, probe=probe, slot=slot):
-                        copy = pltpu.make_async_copy(
-                            pool.at[lay.tile((slot - first) * lay.pixels), :],
-                            state.at[lay.frame(0, probe), :],
-                            sems.at[probe],
-                        )
-                        getattr(copy, act)()
-
-                    first += size
-
-    pools = [("hbm", pool.reshape((-1, lay.pixels))) for pool in pools]
+
+        @pl.when(lax.axis_index("depth") == sections - 1)
+        def _():
+            for act in ("start", "wait"):
+                for probe in range(lay.probes):
+                    name = info[0, probe] & ((1 << lay.name_bits) - 1)
+                    owner = name // lay.probes
+                    slot = name % lay.probes
+                    if len(pools) > 1:
+                        slot += ((owner // 2) ^ side) * lay.probes + ((owner % 2) ^ lat) * 2 * lay.probes
+                    first = 0
+                    for pool in pools:
+                        size = pool.shape[0] // lay.pixels
+
+                        @pl.when((slot >= first) & (slot < first + size))
+                        def _(pool=pool, first=first, probe=probe, slot=slot):
+                            copy = pltpu.make_async_copy(
+                                pool.at[lay.tile((slot - first) * lay.pixels), :],
+                                state.at[lay.frame(0, probe), :],
+                                sems.at[probe],
+                            )
+                            getattr(copy, act)()
+
+                        first += size
+
+    pools = [pool.reshape((-1, lay.pixels)) for pool in pools]
+    pools = [("hbm", pools[0]), *(("vmem", pool) for pool in pools[1:])]
     return call(
         lay,
         body,
@@ -272,7 +275,9 @@
                 state[lay.patch(0, probe, layer, part), :] = patch
 
     def body(info, *refs):
-        lax.fori_loop(begin, end, lambda probe, _: one(probe, info, *refs) or 0, 0)
+        section = lax.axis_index("depth")
+        bounds = [x(section) if callable(x) else x for x in (begin, end)]
+        lax.fori_loop(*bounds, lambda probe, _: one(probe, info, *refs) or 0, 0)
 
     return call(
         lay,
@@ -342,11 +347,11 @@
     )
 
 
-def run_backward(lay, tick, sections, tables, state, arrived, own):
+def run_backward(lay, tick, sections, tables, state, arrived, own, copied=False):
     def body(tables, *refs):
         arrived_ref = refs[0] if arrived is not None else None
-        own_ref = refs[-3] if own is not None else None
-        state, leave = refs[-2:]
+        own_ref = refs[1 if arrived is not None else 0] if own is not None else None
+        state, leave = refs[-3:-1] if copied else refs[-2:]
         section = lax.axis_index("depth")
         group = tick - (2 * (sections - 1) - section)
         final = (section == sections - 1).astype(jnp.int32)
@@ -371,6 +376,9 @@
                     real, imag = times_conj(chi[i], pair(state, functools.partial(lay.seen, group, i, layer)))
                     state[lay.grad(group, i, layer, 0), :] = real
                     state[lay.grad(group, i, layer, 1), :] = imag
+                    if copied:
+                        refs[-1][lay.patch(0, i, layer, 0), :] = real
+                        refs[-1][lay.patch(0, i, layer, 1), :] = imag
                     wave.append(times_conj(chi[i], pair(state, functools.partial(lay.patch, group, i, layer))))
             for i in range(lay.count):
                 leave[i, 0] = wave[i][0]
@@ -382,7 +390,7 @@
         body,
         state,
         [("vmem", tables), *waves],
-        [(lay.count, 2, lay.pixels, lay.pixels)],
+        [(lay.count, 2, lay.pixels, lay.pixels)] + [(lay.stack // lay.groups, lay.pixels)] * copied,
         name="backward_section",
         **section_cost(lay),
     )
@@ -397,8 +405,8 @@
         blank = jnp.zeros((8, pixels), F32)
         base = lax.axis_index("probe") * lay.rows if lay.rows < lay.height else 0
 
-        def add(probe, partner, active, load):
-            row0, down, block, shift = lay.window(info, probe, partner)
+        def add(probe, whose, active, load):
+            row0, down, block, shift = lay.window(info, probe, whose)
             start = row0 - base + tall
 
             @pl.when(active & (start > 0) & (start < lay.rows + tall))
@@ -419,17 +427,17 @@
             for i in range(lay.count):
                 add(
                     group * lay.count + i,
-                    False,
+                    0,
                     active,
                     lambda layer, part, i=i: state[lay.grad(group, i, layer, part), :],
                 )
-        for ref, (first, grads) in zip(refs, received):
-
-            def one(i, _, ref=ref, first=first):
+        for ref, (first, whose, grads) in zip(refs, received):
+
+            def one(i, _, ref=ref, first=first, whose=whose):
                 add(
                     first * lay.count + i,
-                    True,
-                    True,
+                    whose,
+                    (lax.axis_index("depth") == 0) | (whose != 2),
                     lambda layer, part: ref[lay.patch(0, i, layer, part), :],
                 )
                 return 0
@@ -440,82 +448,88 @@
         lay,
         body,
         state,
-        [("vmem", info)] + [("vmem", grads) for _, grads in received],
+        [("vmem", info)] + [("vmem", grads) for *_, grads in received],
         [],
         name="deposit_patches",
     )[0]
 
 
-def split_rows(lay, state, owners, taken=(0, 8)):
+def take_rows(lay, state, owners, others):
     rows = lay.rows // (2 * owners)
-    pieces = 4 * owners * lay.layers * lay.blocks
-
-    def body(state, keep, send, rest, sems):
-        lat = lax.axis_index("lat")
-        copies = [pltpu.make_async_copy(state.at[pl.ds(taken[0], taken[1] - taken[0]), :], rest, sems.at[pieces])]
-        for owner in range(owners):
-            for kind, target in ((lat, keep), (1 - lat, send)):
-                for part in range(2):
-                    for layer in range(lay.layers):
-                        for block in range(lay.blocks):
-                            start = lay.total(part, layer, block, lay.tall + (2 * owner + kind) * rows)
-                            copies.append(
-                                pltpu.make_async_copy(
-                                    state.at[pl.ds(pl.multiple_of(start, 8), rows), :],
-                                    target.at[part, layer, owner, :, pl.ds(block * lay.pixels, lay.pixels)],
-                                    sems.at[len(copies) - 1],
-                                )
-                            )
-        for copy in copies:
-            copy.start()
-        for copy in copies:
-            copy.wait()
-
-    half = (2, lay.layers, owners, rows, lay.width)
+    pieces = [(p, l, o, b) for p in range(2) for l in range(lay.layers) for o in range(owners) for b in range(lay.blocks)]
+
+    def body(state, out, sems):
+        core = lax.axis_index("lat")
+        core = 1 - core if others else core
+        for act in ("start", "wait"):
+            for i, (part, layer, owner, block) in enumerate(pieces):
+                start = lay.total(part, layer, block, lay.tall + (2 * owner + core) * rows)
+                copy = pltpu.make_async_copy(
+                    state.at[pl.ds(pl.multiple_of(start, 8), rows), :],
+                    out.at[part, layer, owner, block],
+                    sems.at[i],
+                )
+                getattr(copy, act)()
+
     return pl.pallas_call(
         body,
         in_specs=[VMEM],
-        out_specs=[VMEM, VMEM, HBM],
-        out_shape=[
-            pltpu.VMEM(half, F32),
-            pltpu.VMEM(half, F32),
-            pltpu.HBM((taken[1] - taken[0], lay.pixels), F32),
-        ],
-        scratch_shapes=[pltpu.SemaphoreType.DMA((pieces + 1,))],
+        out_specs=VMEM,
+        out_shape=pltpu.VMEM((2, lay.layers, owners, lay.blocks, rows, lay.pixels), F32),
+        scratch_shapes=[pltpu.SemaphoreType.DMA((len(pieces),))],
         compiler_params=pltpu.CompilerParams(vmem_limit_bytes=SCOPED),
-        name="split_rows",
+        cost_estimate=pl.CostEstimate(flops=1000, bytes_accessed=1000, transcendentals=0),
+        name="take_rows",
     )(in_vmem(state))
 
 
-def add_up(a, b):
-    each = pl.BlockSpec((1, 1, *a.shape[2:]), lambda i, j: (i, j, 0, 0, 0))
-
-    def body(a, b, out):
-        out[...] = a[...] + b[...]
-
+def room(shape):
     return pl.pallas_call(
-        body,
-        grid=a.shape[:2],
-        in_specs=[each, each],
-        out_specs=each,
-        out_shape=pltpu.HBM(a.shape, F32),
+        lambda out: None,
+        out_specs=VMEM,
+        out_shape=pltpu.VMEM(shape, F32),
         compiler_params=pltpu.CompilerParams(vmem_limit_bytes=SCOPED),
-        name="add_up",
-    )(a, b)
+        name="room",
+    )()
+
+
+def finish(lay, state, received, more, late):
+    rows = lay.rows // 2
+
+    def body(late, state, received, more, out):
+        part, layer = pl.program_id(0), pl.program_id(1)
+        is_late = jnp.max(late[...]) > 0
+        for block in range(lay.blocks):
+            start = lay.total(part, layer, block, lay.tall + lax.axis_index("lat") * rows)
+            columns = pl.ds(block * lay.pixels, lay.pixels)
+            here = state[pl.ds(pl.multiple_of(start, 8), rows), :] + received[part, layer, 0, block]
+            out[0, 0, :, columns] = here
+
+            @pl.when(is_late)
+            def _(block=block, columns=columns, here=here):
+                out[0, 0, :, columns] = here + more[part, layer, 0, block]
+
+    return pl.pallas_call(
+        body,
+        grid=(2, lay.layers),
+        in_specs=[VMEM] * 4,
+        out_specs=pl.BlockSpec((1, 1, rows, lay.width), lambda i, j: (i, j, 0, 0)),
+        out_shape=pltpu.HBM((2, lay.layers, rows, lay.width), F32),
+        compiler_params=pltpu.CompilerParams(vmem_limit_bytes=SCOPED),
+        name="finish",
+    )(*map(in_vmem, (late, state, received, more)))
 
 
 def swap(shard, axis):
     return lax.ppermute(shard, axis, [(0, 1), (1, 0)])
 
 
-def sort_probes(lay, early, positions, indices, specimen):
+def sort_probes(lay, early, positions, indices):
     n = lay.probes
     total = 4 * n
 
     def body(positions, *refs):
-        *scans, specimen, info, brought, sem = refs
-        copy = pltpu.make_async_copy(specimen, brought, sem)
-        copy.start()
+        *scans, info = refs
         lat, side = lax.axis_index("lat"), lax.axis_index("probe")
         lane = lax.broadcasted_iota(jnp.int32, (1, 128), 1)
         at = lax.broadcasted_iota(jnp.int32, (total, 128), 0)
@@ -529,25 +543,41 @@
                 across = jnp.where(lane == which * n + i, key, across)
                 down = jnp.where(at == which * n + i, key, down)
         rank = jnp.sum((across < down).astype(jnp.int32), axis=1, keepdims=True)
-        partner = lane // n
-        order = 2 * (lane % n) + lat
-        wanted = jnp.where((side ^ partner) == 0, 2 * n - 1 - order, 2 * n + order)
+        whose = lane // n
+        order = 2 * (lane % n) + jnp.where(whose == 2, 1 - lat, lat)
+        wanted = jnp.where(jnp.where(whose == 1, 1 - side, side) == 0, 2 * n - 1 - order, 2 * n + order)
         reach = 2 * early * lay.count
-        wanted = jnp.where(lane == 2 * n, 2 * n - 1 - reach, wanted)
-        wanted = jnp.where(lane == 2 * n + 1, 2 * n + reach, wanted)
-        wanted = jnp.where(lane > 2 * n + 1, -1, wanted)
+        wanted = jnp.where(lane == 3 * n, 2 * n - 1 - reach, wanted)
+        wanted = jnp.where(lane == 3 * n + 1, 2 * n + reach, wanted)
+        wanted = jnp.where(lane > 3 * n + 1, -1, wanted)
         info[...] = jnp.sum(jnp.where(rank == wanted, down, 0), axis=0, keepdims=True)
+
+    return pl.pallas_call(
+        body,
+        in_specs=[SMEM] * 5,
+        out_specs=VMEM,
+        out_shape=pltpu.VMEM((1, 128), jnp.int32),
+        compiler_params=pltpu.CompilerParams(vmem_limit_bytes=SCOPED),
+        name="sort_probes",
+    )(positions.T, *indices)
+
+
+def bring(x):
+    def body(x, out, sem):
+        copy = pltpu.make_async_copy(x, out, sem)
+        copy.start()
         copy.wait()
 
     return pl.pallas_call(
         body,
-        in_specs=[SMEM] * 5 + [HBM],
-        out_specs=[VMEM, VMEM],
-        out_shape=[pltpu.VMEM((1, 128), jnp.int32), pltpu.VMEM(specimen.shape, F32)],
+        in_specs=[HBM],
+        out_specs=VMEM,
+        out_shape=pltpu.VMEM(x.shape, x.dtype),
         scratch_shapes=[pltpu.SemaphoreType.DMA(())],
         compiler_params=pltpu.CompilerParams(vmem_limit_bytes=SCOPED),
-        name="sort_probes",
-    )(positions.T, *indices, in_hbm(specimen))
+        cost_estimate=pl.CostEstimate(flops=0, bytes_accessed=2 * x.size * 4, transcendentals=0),
+        name="bring",
+    )(in_hbm(x))
 
 
 def local(specimen, illumination, positions, scan_index, frames):
@@ -574,7 +604,8 @@
         end = sections - 1
         ends = [(2 * end, 2 * end + 1), (2 * end + 1, 2 * end)]
         mine = lax.ppermute(measured, ("depth", "probe"), ends)
-        info, specimen = sort_probes(lay, early, positions, indices, specimen)
+        specimen = bring(specimen)
+        info = sort_probes(lay, early, positions, indices)
         everyone = swap(info, "groups") if lax.axis_size("groups") == 2 else info
     else:
         other = swap(specimen, "lat")
@@ -603,7 +634,10 @@
     crossing = {}
     down = up = None
     middle = min(1 + -(-lay.groups // 2), lay.groups) * count
-    cuts = {0: (count, middle), min(fill - 1, lay.groups // 2): (middle, probes)}
+    part = lambda section: jnp.where(section < 2, middle, probes)
+    cuts = {0: (count, part), min(fill, lay.groups // 2): (part, probes)}
+    last_tick = lay.groups + 2 * fill - 1
+    sent = None
     for tick in range(lay.groups + 2 * fill):
         own = None
         if paired and tick == fill - 1:
@@ -621,32 +655,37 @@
                 pools = [frames, mine, *crossed] if paired else [frames]
                 state, late = place_frames(lay, sections, info, everyone, pools, state)
         if tick >= fill:
-            state, rising = run_backward(lay, tick, sections, tables, state, up, own)
+            copied = paired and tick == last_tick
+            state, rising, *rest = run_backward(lay, tick, sections, tables, state, up, own, copied)
             up = pass_on(rising, tick, -1)
             received = crossing.pop(tick, [])
             for begin, end in parts:
                 if tick == end - 1 + 2 * fill:
-                    due = min(tick + CROSSING, lay.groups + 2 * fill - 1)
-                    crossing.setdefault(due, []).append((begin, swap(grads_of(state, begin, end), "probe")))
+                    due = min(tick + CROSSING, last_tick - 1)
+                    crossing.setdefault(due, []).append((begin, 1, swap(grads_of(state, begin, end), "probe")))
             state = deposit(lay, tick, sections, info, received, state)
+            if paired and tick == last_tick - 1:
+                state, up = lax.optimization_barrier((state, up))
+                sent = swap(take_rows(lay, state, 1, True), "lat")
+    if paired:
+        last = swap(rest[0], "lat")
+        state = deposit(lay, None, sections, info, [(lay.groups - 1, 2, last)], state)
     if not paired:
-        keep, send, _ = split_rows(lay, state, owners)
-        return lax.psum_scatter(keep + swap(send, "lat"), "probe", scatter_dimension=2, tiled=False)
-
-    keep, send, late_grads = split_rows(lay, state, 1, lay.grads_of(early, lay.groups))
-
-    def as_they_are(keep, received, grads):
-        return add_up(keep, received)
-
-    def with_partners(keep, received, grads):
+        whole = take_rows(lay, state, owners, False) + swap(take_rows(lay, state, owners, True), "lat")
+        whole = jnp.moveaxis(whole, 3, 4).reshape((2, layers, owners, -1, width))
+        return lax.psum_scatter(whole, "probe", scatter_dimension=2, tiled=False)
+
+    def nothing_more(grads):
+        return room(sent.shape)
+
+    def from_partners(grads):
         sums = Layout(probes, count, layers, pixels, half, height, width, only_sums=True)
-        state = clear_total(sums, None)
-        state = deposit(sums, None, sections, info, [(early, swap(grads, "probe"))], state)
-        more, send, _ = split_rows(sums, state, 1)
-        return add_up(keep + more, received + swap(send, "lat"))
-
-    result = lax.cond(late[0] > 0, with_partners, as_they_are, keep, swap(send, "lat"), late_grads)
-    return result[:, :, 0]
+        sums_state = clear_total(sums, None)
+        sums_state = deposit(sums, None, sections, info, [(early, 1, swap(grads, "probe"))], sums_state)
+        return take_rows(sums, sums_state, 1, False) + swap(take_rows(sums, sums_state, 1, True), "lat")
+
+    more = lax.cond(late[0, 0] > 0, from_partners, nothing_more, grads_of(state, early, lay.groups))
+    return finish(lay, state, sent, more, late)
 
 
 def solution(mesh):

time: 163 us -> 181 us (1.11)
  local copies, waits for them, and re-layouts: 2.81 us -> 15.9 us
  Pallas kernels: 49.2 us -> 51.7 us
  starting transfers between devices: 57.6 us -> 60 us
    unnamed x16 -> x14, local copies, waits for them, and re-layouts: 2.67 us -> 15.7 us
    ppermute x20, waiting for transfers between devices: 42.3 us -> 45 us  [pass_on(): return lax.ppermute(wave, 'depth', pairs) if pairs else None]
    pallas_call x41 -> x44, Pallas kernels: 49.2 us -> 51.7 us  [the longest x39 39.6 us: call(): pl.pallas_call(kernel, in_specs=specs, out_specs=[VMEM] * (1 + len(outs)...]
    ppermute x8 -> x9, waiting for transfers between devices: 9.61 us -> 7.31 us  [swap(): return lax.ppermute(shard, axis, [(0, 1), (1, 0)])]
    ppermute x8 -> x9, starting transfers between devices: 7.29 us -> 8.19 us  [swap(): return lax.ppermute(shard, axis, [(0, 1), (1, 0)])]
  transfers between devices with their start and end apart: 31 -> 32, of which waited for: 17 -> 20; matrix products, arithmetic and copies ran while one was open for 0% -> 0% of each run, Pallas kernels for 25% -> 23%
where the time goes in v1:
time: 181 us
  starting transfers between devices  60 us (33%)
  waiting for transfers between devices  52.3 us (29%)
  Pallas kernels  51.7 us (29%)
  local copies, waits for them, and re-layouts  15.9 us (9%)
    ppermute x20, starting transfers between devices, pass_on(): return lax.ppermute(wave, 'depth', pairs) if pairs else None  49.6 us
    ppermute x20, waiting for transfers between devices, pass_on(): return lax.ppermute(wave, 'depth', pairs) if pairs else None  45 us
    pallas_call x39, Pallas kernels, call(): pl.pallas_call(kernel, in_specs=specs, out_specs=[VMEM] * (1 + len(outs)...  39.6 us
    unnamed x14, local copies, waits for them, and re-layouts  15.7 us
    ppermute x9, starting transfers between devices, swap(): return lax.ppermute(shard, axis, [(0, 1), (1, 0)])  8.19 us
    ppermute x9, waiting for transfers between devices, swap(): return lax.ppermute(shard, axis, [(0, 1), (1, 0)])  7.31 us
    pallas_call x1, Pallas kernels, take_rows(): pl.pallas_call(body, in_specs=[VMEM], out_specs=VMEM, out_shape=pltpu.VME...  4.67 us
    pallas_call x1, Pallas kernels, finish(): pl.pallas_call(body, grid=(2, lay.layers), in_specs=[VMEM] * 4, out_specs...  4.09 us
  transfers between devices with their start and end apart: 32, of which 20 were waited for; matrix products, arithmetic and copies ran while one was open for 0% of the time, Pallas kernels for 23%

profile of v1, /device:TPU:0, one launch (start us, length us, event | category | flops | bytes accessed | tf_op | source)
XLA Modules:
  0.0 180.5 jit_solution(7400296177353114096)
XLA Ops:
  1.7 2.7 %collective-permute-start.2 = (s32[16]{0:T(128)}, s32[16]{0:T(128)S(1)}, u32[]{:S(2)}, u32[]{:S(2)}) collective-permute-start(s32[16]{0:T(128)} %bitcast.13), channel_id=1, source_target_pairs={{0,2},{2,0},{1,3},{3,1},{4,6},{6,4},{5,7},{7,5},{8,10},{10,8},{9,1... | collective-permute-start | bytes 200 | tf_op jit(solution)/shard_map/ppermute | solution.py:524
  4.4 1.6 collective-permute-done.2.refs_1_
  6.1 1.9 %collective-permute-done.4.refs_3_ = s32[16]{0:T(128)S(1)} collective-permute-done((s32[16]{0:T(128)S(1)}, s32[16]{0:T(128)S(1)}, u32[]{:S(2)}, u32[]{:S(2)}) %collective-permute-start.4) | collective-permute-done | bytes 96 | tf_op jit(solution)/shard_map/ppermute | solution.py:524
  8.7 2.3 %bring.1.refs_1_ = f32[2,2,384,768]{3,2,1,0:T(8,128)S(1)} custom-call(f32[2,2,384,768]{3,2,1,0:T(8,128)} %x.1), custom_call_target="tpu_custom_call" | custom-call | bytes 9437184 | tf_op jit(solution)/shard_map/bring/pallas_call | solution.py:571
  14.2 1.3 forward_section.11
  15.6 2.2 %collective-permute-start.6 = (f32[2,2,128,128]{3,2,1,0:T(8,128)S(1)}, f32[2,2,128,128]{3,2,1,0:T(8,128)S(1)}, u32[]{:S(2)}, u32[]{:S(2)}) collective-permute-start(f32[2,2,128,128]{3,2,1,0:T(8,128)S(1)} %get-tuple-element.77), channel_id=1, source_target_pairs={{0,4},{1,5},{2,6},{3,7},{16,20},{17,21},{18,22},{19,23}} | collective-permute-start | bytes 786440 | tf_op jit(solution)/shard_map/ppermute | solution.py:626
  17.8 3.5 %cut_patches.4.refs_0_ = f32[42368,128]{1,0:T(8,128)S(1)} custom-call(s32[1,128]{1,0:T(1,128)S(1)} %sort_probes.1.refs_0_, f32[2,2,384,768]{3,2,1,0:T(8,128)S(1)} %bring.1.refs_1_, f32[2,2,384,768]{3,2,1,0:T(8,128)S(1)} %collective-permute-done.5.refs_2_, f32[42368,128]{1,0:T(8,128)S(1)} %get-tuple-element.78.refs_3_), custom_call_target="tpu_custom_call", output_to_operand_aliasing={{}: (3, {})} | custom-call | flops 1000 | bytes 1000 | tf_op jit(solution)/shard_map/cut_patches/pallas_call | solution.py:172
  22.3 1.3 forward_section.12
  23.7 4.4 %collective-permute-start.7 = (f32[2,2,128,128]{3,2,1,0:T(8,128)S(1)}, f32[2,2,128,128]{3,2,1,0:T(8,128)S(1)}, u32[]{:S(2)}, u32[]{:S(2)}) collective-permute-start(f32[2,2,128,128]{3,2,1,0:T(8,128)S(1)} %get-tuple-element.79), channel_id=1, source_target_pairs={{0,4},{4,8},{1,5},{5,9},{2,6},{6,10},{3,7},{7,11},{16,20},{20,24},... | collective-permute-start | bytes 786440 | tf_op jit(solution)/shard_map/ppermute | solution.py:626
  28.1 1.7 collective-permute-start.9
  32.7 1.3 forward_section.13
  34.0 4.4 %collective-permute-start.12 = (f32[2,2,128,128]{3,2,1,0:T(8,128)S(1)}, f32[2,2,128,128]{3,2,1,0:T(8,128)S(1)}, u32[]{:S(2)}, u32[]{:S(2)}) collective-permute-start(f32[2,2,128,128]{3,2,1,0:T(8,128)S(1)} %get-tuple-element.87), channel_id=1, source_target_pairs={{0,4},{4,8},{8,12},{1,5},{5,9},{9,13},{2,6},{6,10},{10,14},{3,7},{... | collective-permute-start | bytes 786440 | tf_op jit(solution)/shard_map/ppermute | solution.py:626
  39.2 3.1 %collective-permute-done.12.refs_1_ = f32[2,2,128,128]{3,2,1,0:T(8,128)S(1)} collective-permute-done((f32[2,2,128,128]{3,2,1,0:T(8,128)S(1)}, f32[2,2,128,128]{3,2,1,0:T(8,128)S(1)}, u32[]{:S(2)}, u32[]{:S(2)}) %collective-permute-start.12) | collective-permute-done | bytes 262176 | tf_op jit(solution)/shard_map/ppermute | solution.py:626
  42.3 1.3 forward_section.14
  43.6 4.4 %collective-permute-start.14 = (f32[2,2,128,128]{3,2,1,0:T(8,128)S(1)}, f32[2,2,128,128]{3,2,1,0:T(8,128)S(1)}, u32[]{:S(2)}, u32[]{:S(2)}) collective-permute-start(f32[2,2,128,128]{3,2,1,0:T(8,128)S(1)} %get-tuple-element.89.refs_1_), channel_id=1, source_target_pairs={{0,4},{4,8},{8,12},{1,5},{5,9},{9,13},{2,6},{6,10},{10,14},{3,7},{... | collective-permute-start | bytes 786440 | tf_op jit(solution)/shard_map/ppermute | solution.py:626
  48.1 2.5 %cut_patches.5.refs_2_ = f32[42368,128]{1,0:T(8,128)S(1)} custom-call(s32[1,128]{1,0:T(1,128)S(1)} %sort_probes.1.refs_0_, f32[2,2,384,768]{3,2,1,0:T(8,128)S(1)} %bring.1.refs_1_, f32[2,2,384,768]{3,2,1,0:T(8,128)S(1)} %collective-permute-done.5.refs_2_, f32[42368,128]{1,0:T(8,128)S(1)} %get-tuple-element.90.refs_3_), custom_call_target="tpu_custom_call", output_to_operand_aliasing={{}: (3, {})} | custom-call | flops 1000 | bytes 1000 | tf_op jit(solution)/shard_map/cut_patches/pallas_call | solution.py:172
  51.9 1.3 forward_section.15
  53.3 7.5 %collective-permute-start.16 = (f32[2,2,128,128]{3,2,1,0:T(8,128)S(1)}, f32[2,2,128,128]{3,2,1,0:T(8,128)S(1)}, u32[]{:S(2)}, u32[]{:S(2)}) collective-permute-start(f32[2,2,128,128]{3,2,1,0:T(8,128)S(1)} %get-tuple-element.93.refs_2_), channel_id=1, source_target_pairs={{0,4},{4,8},{8,12},{1,5},{5,9},{9,13},{2,6},{6,10},{10,14},{3,7},{... | collective-permute-start | bytes 786440 | tf_op jit(solution)/shard_map/ppermute | solution.py:626
  61.8 3.5 %collective-permute-done.16.refs_1_ = f32[2,2,128,128]{3,2,1,0:T(8,128)S(1)} collective-permute-done((f32[2,2,128,128]{3,2,1,0:T(8,128)S(1)}, f32[2,2,128,128]{3,2,1,0:T(8,128)S(1)}, u32[]{:S(2)}, u32[]{:S(2)}) %collective-permute-start.16) | collective-permute-done | bytes 262176 | tf_op jit(solution)/shard_map/ppermute | solution.py:626
  65.3 1.3 forward_section.16
  66.6 4.4 %collective-permute-start.18 = (f32[2,2,128,128]{3,2,1,0:T(8,128)S(1)}, f32[2,2,128,128]{3,2,1,0:T(8,128)S(1)}, u32[]{:S(2)}, u32[]{:S(2)}) collective-permute-start(f32[2,2,128,128]{3,2,1,0:T(8,128)S(1)} %get-tuple-element.97.refs_2_), channel_id=1, source_target_pairs={{0,4},{4,8},{8,12},{1,5},{5,9},{9,13},{2,6},{6,10},{10,14},{3,7},{... | collective-permute-start | bytes 786440 | tf_op jit(solution)/shard_map/ppermute | solution.py:626
  71.1 1.5 collective-permute-start.17
  72.8 2.0 %collective-permute-done.18.refs_1_ = f32[2,2,128,128]{3,2,1,0:T(8,128)S(1)} collective-permute-done((f32[2,2,128,128]{3,2,1,0:T(8,128)S(1)}, f32[2,2,128,128]{3,2,1,0:T(8,128)S(1)}, u32[]{:S(2)}, u32[]{:S(2)}) %collective-permute-start.18) | collective-permute-done | bytes 262176 | tf_op jit(solution)/shard_map/ppermute | solution.py:626
  74.9 1.3 forward_section.17
  76.2 4.7 %collective-permute-start.20 = (f32[2,2,128,128]{3,2,1,0:T(8,128)S(1)}, f32[2,2,128,128]{3,2,1,0:T(8,128)S(1)}, u32[]{:S(2)}, u32[]{:S(2)}) collective-permute-start(f32[2,2,128,128]{3,2,1,0:T(8,128)S(1)} %get-tuple-element.101.refs_2_), channel_id=1, source_target_pairs={{0,4},{4,8},{8,12},{1,5},{5,9},{9,13},{2,6},{6,10},{10,14},{3,7},{... | collective-permute-start | bytes 786440 | tf_op jit(solution)/shard_map/ppermute | solution.py:626
  81.5 1.3 backward_section.14
  84.8 1.3 forward_section.18
  86.2 4.4 %collective-permute-start.22 = (f32[2,2,128,128]{3,2,1,0:T(8,128)S(1)}, f32[2,2,128,128]{3,2,1,0:T(8,128)S(1)}, u32[]{:S(2)}, u32[]{:S(2)}) collective-permute-start(f32[2,2,128,128]{3,2,1,0:T(8,128)S(1)} %get-tuple-element.105.refs_2_), channel_id=1, source_target_pairs={{0,4},{4,8},{8,12},{1,5},{5,9},{9,13},{2,6},{6,10},{10,14},{3,7},{... | collective-permute-start | bytes 786440 | tf_op jit(solution)/shard_map/ppermute | solution.py:626
  91.1 1.3 backward_section.15
  95.7 5.3 %collective-permute-done.21.refs_1_ = f32[2,2,128,128]{3,2,1,0:T(8,128)S(1)} collective-permute-done((f32[2,2,128,128]{3,2,1,0:T(8,128)S(1)}, f32[2,2,128,128]{3,2,1,0:T(8,128)S(1)}, u32[]{:S(2)}, u32[]{:S(2)}) %collective-permute-start.21) | collective-permute-done | bytes 262176 | tf_op jit(solution)/shard_map/ppermute | solution.py:626
  101.0 1.3 backward_section.16
  105.4 5.9 %collective-permute-done.23.refs_1_ = f32[2,2,128,128]{3,2,1,0:T(8,128)S(1)} collective-permute-done((f32[2,2,128,128]{3,2,1,0:T(8,128)S(1)}, f32[2,2,128,128]{3,2,1,0:T(8,128)S(1)}, u32[]{:S(2)}, u32[]{:S(2)}) %collective-permute-start.23) | collective-permute-done | bytes 262176 | tf_op jit(solution)/shard_map/ppermute | solution.py:626
  111.3 1.3 backward_section.17
  114.0 1.6 collective-permute-start.25
  116.7 4.2 %collective-permute-done.26.refs_1_ = f32[2,2,128,128]{3,2,1,0:T(8,128)S(1)} collective-permute-done((f32[2,2,128,128]{3,2,1,0:T(8,128)S(1)}, f32[2,2,128,128]{3,2,1,0:T(8,128)S(1)}, u32[]{:S(2)}, u32[]{:S(2)}) %collective-permute-start.26) | collective-permute-done | bytes 262176 | tf_op jit(solution)/shard_map/ppermute | solution.py:626
  120.9 1.3 backward_section.18
  123.5 1.7 deposit_patches.21.refs_2_
  125.2 5.6 %collective-permute-done.28.refs_1_ = f32[2,2,128,128]{3,2,1,0:T(8,128)S(1)} collective-permute-done((f32[2,2,128,128]{3,2,1,0:T(8,128)S(1)}, f32[2,2,128,128]{3,2,1,0:T(8,128)S(1)}, u32[]{:S(2)}, u32[]{:S(2)}) %collective-permute-start.28) | collective-permute-done | bytes 262176 | tf_op jit(solution)/shard_map/ppermute | solution.py:626
  134.4 7.4 %collective-permute-done.30.refs_1_ = f32[2,2,128,128]{3,2,1,0:T(8,128)S(1)} collective-permute-done((f32[2,2,128,128]{3,2,1,0:T(8,128)S(1)}, f32[2,2,128,128]{3,2,1,0:T(8,128)S(1)}, u32[]{:S(2)}, u32[]{:S(2)}) %collective-permute-start.30) | collective-permute-done | bytes 262176 | tf_op jit(solution)/shard_map/ppermute | solution.py:626
  141.9 1.3 backward_section.20
  144.5 1.7 deposit_patches.23.refs_2_.state
  146.1 5.3 %collective-permute-done.31.refs_1_ = f32[2,2,128,128]{3,2,1,0:T(8,128)S(1)} collective-permute-done((f32[2,2,128,128]{3,2,1,0:T(8,128)S(1)}, f32[2,2,128,128]{3,2,1,0:T(8,128)S(1)}, u32[]{:S(2)}, u32[]{:S(2)}) %collective-permute-start.31) | collective-permute-done | bytes 262176 | tf_op jit(solution)/shard_map/ppermute | solution.py:626
  151.4 4.7 %take_rows.5 = f32[2,2,1,6,192,128]{5,4,3,2,1,0:T(8,128)} custom-call(f32[42368,128]{1,0:T(8,128)S(1)} %deposit_patches.23.refs_2_.state), custom_call_target="tpu_custom_call" | custom-call | flops 1000 | bytes 1000 | tf_op jit(solution)/shard_map/take_rows/pallas_call | solution.py:474
  156.2 2.0 %backward_section.21 = (f32[42368,128]{1,0:T(8,128)S(1)}, f32[2,2,128,128]{3,2,1,0:T(8,128)}, f32[1024,128]{1,0:T(8,128)S(1)}) custom-call(bf16[2,2,2,256,256]{4,3,2,1,0:T(8,128)(2,1)S(1)} %copy-done.2, f32[2,2,128,128]{3,2,1,0:T(8,128)S(1)} %collective-permute-done.31.refs_1_, ...), custom_call_target="tpu_custom_call", output_to_operand_aliasing={{0}: (2, {})} | custom-call | flops 402653184 | bytes 2097152 | tf_op jit(solution)/shard_map/backward_section/pallas_call | solution.py:172
  159.8 1.6 collective-permute-done.32.refs_1_
  162.1 7.2 %copy-done = f32[42368,128]{1,0:T(8,128)} copy-done((f32[42368,128]{1,0:T(8,128)}, f32[42368,128]{1,0:T(8,128)S(1)}, u32[]{:S(2)}) %copy-start) | copy-done | bytes 21692440
  169.3 7.2 %copy-done.1 = f32[42368,128]{1,0:T(8,128)S(1)} copy-done((f32[42368,128]{1,0:T(8,128)S(1)}, f32[42368,128]{1,0:T(8,128)}, u32[]{:S(2)}) %copy-start.1) | copy-done | bytes 21692440
  176.5 4.1 %finish.1 = f32[2,2,192,768]{3,2,1,0:T(8,128)} custom-call(s32[1,128]{1,0:T(1,128)S(1)} %get-tuple-element.86.late, f32[42368,128]{1,0:T(8,128)S(1)} %copy-done.1, f32[2,2,1,6,192,128]{5,4,3,2,1,0:T(8,128)} %collective-permute-done.33.received, f32[2,2,1,6,192,128]{5,4,3,2,1,0:T(8,128)S(1)} %get-tuple-element.129.more), custom_call_target="tpu_custom_call" | custom-call | tf_op jit(solution)/shard_map/finish/pallas_call | solution.py:512
  (77 shorter events, 33.3 us)
Async XLA Ops:
  0.0 14.2 %copy-start.2 = (bf16[2,2,2,256,256]{4,3,2,1,0:T(8,128)(2,1)S(1)}, bf16[2,2,2,256,256]{4,3,2,1,0:T(8,128)(2,1)}, u32[]{:S(2)}) copy-start(bf16[2,2,2,256,256]{4,3,2,1,0:T(8,128)(2,1)} %constant.5.clone.refs_0_) | copy-start | bytes 3145732
  0.0 14.2 %copy-start.3 = (f32[2,128,128]{2,1,0:T(8,128)S(1)}, f32[2,128,128]{2,1,0:T(8,128)}, u32[]{:S(2)}) copy-start(f32[2,128,128]{2,1,0:T(8,128)} %refs_2_.13) | copy-start | bytes 393220
  0.0 1.4 collective-permute-start.3
  1.4 12.0 %collective-permute-start.5 = (f32[2,2,384,768]{3,2,1,0:T(8,128)}, f32[2,2,384,768]{3,2,1,0:T(8,128)S(1)}, u32[]{:S(2)}, u32[]{:S(2)}) collective-permute-start(f32[2,2,384,768]{3,2,1,0:T(8,128)} %x.1), channel_id=1, source_target_pairs={{0,1},{1,0},{2,3},{3,2},{4,5},{5,4},{6,7},{7,6},{8,9},{9,8},{10,11... | collective-permute-start | bytes 14155784 | tf_op jit(solution)/shard_map/ppermute | solution.py:524
  1.7 4.3 %collective-permute-start.2 = (s32[16]{0:T(128)}, s32[16]{0:T(128)S(1)}, u32[]{:S(2)}, u32[]{:S(2)}) collective-permute-start(s32[16]{0:T(128)} %bitcast.13), channel_id=1, source_target_pairs={{0,2},{2,0},{1,3},{3,1},{4,6},{6,4},{5,7},{7,5},{8,10},{10,8},{9,1... | collective-permute-start | bytes 200 | tf_op jit(solution)/shard_map/ppermute | solution.py:524
  4.4 3.5 %collective-permute-start.4 = (s32[16]{0:T(128)S(1)}, s32[16]{0:T(128)S(1)}, u32[]{:S(2)}, u32[]{:S(2)}) collective-permute-start(s32[16]{0:T(128)S(1)} %collective-permute-done.3.refs_2_), channel_id=1, source_target_pairs={{0,2},{2,0},{1,3},{3,1},{4,6},{6,4},{5,7},{7,5},{8,10},{10,8},{9,1... | collective-permute-start | bytes 200 | tf_op jit(solution)/shard_map/ppermute | solution.py:524
  7.9 23.8 %collective-permute-start.8 = (f32[16,1,128,128]{3,2,1,0:T(8,128)}, f32[16,1,128,128]{3,2,1,0:T(8,128)S(1)}, u32[]{:S(2)}, u32[]{:S(2)}) collective-permute-start(f32[16,1,128,128]{3,2,1,0:T(8,128)} %param.12), channel_id=1, source_target_pairs={{12,14},{14,12},{13,15},{15,13},{28,30},{30,28},{29,31},{31,29}} | collective-permute-start | bytes 3145736 | tf_op jit(solution)/shard_map/ppermute | solution.py:606
  11.0 0.7 copy-start.4
  11.7 0.7 copy-start.5
  15.6 6.8 %collective-permute-start.6 = (f32[2,2,128,128]{3,2,1,0:T(8,128)S(1)}, f32[2,2,128,128]{3,2,1,0:T(8,128)S(1)}, u32[]{:S(2)}, u32[]{:S(2)}) collective-permute-start(f32[2,2,128,128]{3,2,1,0:T(8,128)S(1)} %get-tuple-element.77), channel_id=1, source_target_pairs={{0,4},{1,5},{2,6},{3,7},{16,20},{17,21},{18,22},{19,23}} | collective-permute-start | bytes 786440 | tf_op jit(solution)/shard_map/ppermute | solution.py:626
  21.8 8.0 %copy-start.6 = (f32[16,1,128,128]{3,2,1,0:T(8,128)S(1)}, f32[16,1,128,128]{3,2,1,0:T(8,128)}, u32[]{:S(2)}) copy-start(f32[16,1,128,128]{3,2,1,0:T(8,128)} %param.12) | copy-start | bytes 3145732
  23.7 8.3 %collective-permute-start.7 = (f32[2,2,128,128]{3,2,1,0:T(8,128)S(1)}, f32[2,2,128,128]{3,2,1,0:T(8,128)S(1)}, u32[]{:S(2)}, u32[]{:S(2)}) collective-permute-start(f32[2,2,128,128]{3,2,1,0:T(8,128)S(1)} %get-tuple-element.79), channel_id=1, source_target_pairs={{0,4},{4,8},{1,5},{5,9},{2,6},{6,10},{3,7},{7,11},{16,20},{20,24},... | collective-permute-start | bytes 786440 | tf_op jit(solution)/shard_map/ppermute | solution.py:626
  28.1 3.6 %collective-permute-start.9 = (s32[1,128]{1,0:T(1,128)S(1)}, s32[1,128]{1,0:T(1,128)S(1)}, u32[]{:S(2)}, u32[]{:S(2)}) collective-permute-start(s32[1,128]{1,0:T(1,128)S(1)} %sort_probes.1.refs_0_), channel_id=1, source_target_pairs={{0,16},{16,0},{1,17},{17,1},{2,18},{18,2},{3,19},{19,3},{4,20},{20... | collective-permute-start | bytes 1544 | tf_op jit(solution)/shard_map/ppermute | solution.py:524
  29.8 8.7 %collective-permute-start.10 = (f32[16,1,128,128]{3,2,1,0:T(8,128)S(1)}, f32[16,1,128,128]{3,2,1,0:T(8,128)S(1)}, u32[]{:S(2)}, u32[]{:S(2)}) collective-permute-start(f32[16,1,128,128]{3,2,1,0:T(8,128)S(1)} %copy-done.6), channel_id=1, source_target_pairs={{12,13},{13,12},{14,15},{15,14},{28,29},{29,28},{30,31},{31,30}} | collective-permute-start | bytes 3145736 | tf_op jit(solution)/shard_map/ppermute | solution.py:645
  32.0 6.5 %collective-permute-start.11 = (f32[16,1,128,128]{3,2,1,0:T(8,128)S(1)}, f32[16,1,128,128]{3,2,1,0:T(8,128)S(1)}, u32[]{:S(2)}, u32[]{:S(2)}) collective-permute-start(f32[16,1,128,128]{3,2,1,0:T(8,128)S(1)} %collective-permute-done.8), channel_id=1, source_target_pairs={{12,13},{13,12},{14,15},{15,14},{28,29},{29,28},{30,31},{31,30}} | collective-permute-start | bytes 3145736 | tf_op jit(solution)/shard_map/ppermute | solution.py:645
  34.0 8.3 %collective-permute-start.12 = (f32[2,2,128,128]{3,2,1,0:T(8,128)S(1)}, f32[2,2,128,128]{3,2,1,0:T(8,128)S(1)}, u32[]{:S(2)}, u32[]{:S(2)}) collective-permute-start(f32[2,2,128,128]{3,2,1,0:T(8,128)S(1)} %get-tuple-element.87), channel_id=1, source_target_pairs={{0,4},{4,8},{8,12},{1,5},{5,9},{9,13},{2,6},{6,10},{10,14},{3,7},{... | collective-permute-start | bytes 786440 | tf_op jit(solution)/shard_map/ppermute | solution.py:626
  43.6 8.3 %collective-permute-start.14 = (f32[2,2,128,128]{3,2,1,0:T(8,128)S(1)}, f32[2,2,128,128]{3,2,1,0:T(8,128)S(1)}, u32[]{:S(2)}, u32[]{:S(2)}) collective-permute-start(f32[2,2,128,128]{3,2,1,0:T(8,128)S(1)} %get-tuple-element.89.refs_1_), channel_id=1, source_target_pairs={{0,4},{4,8},{8,12},{1,5},{5,9},{9,13},{2,6},{6,10},{10,14},{3,7},{... | collective-permute-start | bytes 786440 | tf_op jit(solution)/shard_map/ppermute | solution.py:626
  50.6 10.1 %collective-permute-start.13 = (f32[2,2,128,128]{3,2,1,0:T(8,128)S(1)}, f32[2,2,128,128]{3,2,1,0:T(8,128)S(1)}, u32[]{:S(2)}, u32[]{:S(2)}) collective-permute-start(f32[2,2,128,128]{3,2,1,0:T(8,128)S(1)} %get-tuple-element.91), channel_id=1, source_target_pairs={{12,8},{13,9},{14,10},{15,11},{28,24},{29,25},{30,26},{31,27}} | collective-permute-start | bytes 786440 | tf_op jit(solution)/shard_map/ppermute | solution.py:626
  53.3 12.0 %collective-permute-start.16 = (f32[2,2,128,128]{3,2,1,0:T(8,128)S(1)}, f32[2,2,128,128]{3,2,1,0:T(8,128)S(1)}, u32[]{:S(2)}, u32[]{:S(2)}) collective-permute-start(f32[2,2,128,128]{3,2,1,0:T(8,128)S(1)} %get-tuple-element.93.refs_2_), channel_id=1, source_target_pairs={{0,4},{4,8},{8,12},{1,5},{5,9},{9,13},{2,6},{6,10},{10,14},{3,7},{... | collective-permute-start | bytes 786440 | tf_op jit(solution)/shard_map/ppermute | solution.py:626
  60.8 10.2 %collective-permute-start.15 = (f32[2,2,128,128]{3,2,1,0:T(8,128)S(1)}, f32[2,2,128,128]{3,2,1,0:T(8,128)S(1)}, u32[]{:S(2)}, u32[]{:S(2)}) collective-permute-start(f32[2,2,128,128]{3,2,1,0:T(8,128)S(1)} %get-tuple-element.95), channel_id=1, source_target_pairs={{8,4},{12,8},{9,5},{13,9},{10,6},{14,10},{11,7},{15,11},{24,20},{2... | collective-permute-start | bytes 786440 | tf_op jit(solution)/shard_map/ppermute | solution.py:626
  66.6 8.3 %collective-permute-start.18 = (f32[2,2,128,128]{3,2,1,0:T(8,128)S(1)}, f32[2,2,128,128]{3,2,1,0:T(8,128)S(1)}, u32[]{:S(2)}, u32[]{:S(2)}) collective-permute-start(f32[2,2,128,128]{3,2,1,0:T(8,128)S(1)} %get-tuple-element.97.refs_2_), channel_id=1, source_target_pairs={{0,4},{4,8},{8,12},{1,5},{5,9},{9,13},{2,6},{6,10},{10,14},{3,7},{... | collective-permute-start | bytes 786440 | tf_op jit(solution)/shard_map/ppermute | solution.py:626
  71.1 10.5 %collective-permute-start.17 = (f32[2,2,128,128]{3,2,1,0:T(8,128)S(1)}, f32[2,2,128,128]{3,2,1,0:T(8,128)S(1)}, u32[]{:S(2)}, u32[]{:S(2)}) collective-permute-start(f32[2,2,128,128]{3,2,1,0:T(8,128)S(1)} %get-tuple-element.99), channel_id=1, source_target_pairs={{4,0},{8,4},{12,8},{5,1},{9,5},{13,9},{6,2},{10,6},{14,10},{7,3},{... | collective-permute-start | bytes 786440 | tf_op jit(solution)/shard_map/ppermute | solution.py:626
  76.2 8.6 %collective-permute-start.20 = (f32[2,2,128,128]{3,2,1,0:T(8,128)S(1)}, f32[2,2,128,128]{3,2,1,0:T(8,128)S(1)}, u32[]{:S(2)}, u32[]{:S(2)}) collective-permute-start(f32[2,2,128,128]{3,2,1,0:T(8,128)S(1)} %get-tuple-element.101.refs_2_), channel_id=1, source_target_pairs={{0,4},{4,8},{8,12},{1,5},{5,9},{9,13},{2,6},{6,10},{10,14},{3,7},{... | collective-permute-start | bytes 786440 | tf_op jit(solution)/shard_map/ppermute | solution.py:626
  82.8 8.3 %collective-permute-start.19 = (f32[2,2,128,128]{3,2,1,0:T(8,128)S(1)}, f32[2,2,128,128]{3,2,1,0:T(8,128)S(1)}, u32[]{:S(2)}, u32[]{:S(2)}) collective-permute-start(f32[2,2,128,128]{3,2,1,0:T(8,128)S(1)} %get-tuple-element.103), channel_id=1, source_target_pairs={{4,0},{8,4},{12,8},{5,1},{9,5},{13,9},{6,2},{10,6},{14,10},{7,3},{... | collective-permute-start | bytes 786440 | tf_op jit(solution)/shard_map/ppermute | solution.py:626
  86.2 8.9 %collective-permute-start.22 = (f32[2,2,128,128]{3,2,1,0:T(8,128)S(1)}, f32[2,2,128,128]{3,2,1,0:T(8,128)S(1)}, u32[]{:S(2)}, u32[]{:S(2)}) collective-permute-start(f32[2,2,128,128]{3,2,1,0:T(8,128)S(1)} %get-tuple-element.105.refs_2_), channel_id=1, source_target_pairs={{0,4},{4,8},{8,12},{1,5},{5,9},{9,13},{2,6},{6,10},{10,14},{3,7},{... | collective-permute-start | bytes 786440 | tf_op jit(solution)/shard_map/ppermute | solution.py:626
  92.4 8.6 %collective-permute-start.21 = (f32[2,2,128,128]{3,2,1,0:T(8,128)S(1)}, f32[2,2,128,128]{3,2,1,0:T(8,128)S(1)}, u32[]{:S(2)}, u32[]{:S(2)}) collective-permute-start(f32[2,2,128,128]{3,2,1,0:T(8,128)S(1)} %get-tuple-element.107), channel_id=1, source_target_pairs={{4,0},{8,4},{12,8},{5,1},{9,5},{13,9},{6,2},{10,6},{14,10},{7,3},{... | collective-permute-start | bytes 786440 | tf_op jit(solution)/shard_map/ppermute | solution.py:626
  93.8 29.7 %collective-permute-start.29 = (f32[2048,128]{1,0:T(8,128)S(1)}, f32[2048,128]{1,0:T(8,128)S(1)}, u32[]{:S(2)}, u32[]{:S(2)}) collective-permute-start(f32[2048,128]{1,0:T(8,128)S(1)} %slice.14), channel_id=1, source_target_pairs={{0,2},{2,0},{1,3},{3,1},{4,6},{6,4},{5,7},{7,5},{8,10},{10,8},{9,1... | collective-permute-start | bytes 3145736 | tf_op jit(solution)/shard_map/ppermute | solution.py:524
  95.1 9.7 %collective-permute-start.24 = (f32[2,2,128,128]{3,2,1,0:T(8,128)S(1)}, f32[2,2,128,128]{3,2,1,0:T(8,128)S(1)}, u32[]{:S(2)}, u32[]{:S(2)}) collective-permute-start(f32[2,2,128,128]{3,2,1,0:T(8,128)S(1)} %get-tuple-element.109.refs_2_), channel_id=1, source_target_pairs={{4,8},{8,12},{5,9},{9,13},{6,10},{10,14},{7,11},{11,15},{20,24},{2... | collective-permute-start | bytes 786440 | tf_op jit(solution)/shard_map/ppermute | solution.py:626
  102.3 9.0 %collective-permute-start.23 = (f32[2,2,128,128]{3,2,1,0:T(8,128)S(1)}, f32[2,2,128,128]{3,2,1,0:T(8,128)S(1)}, u32[]{:S(2)}, u32[]{:S(2)}) collective-permute-start(f32[2,2,128,128]{3,2,1,0:T(8,128)S(1)} %get-tuple-element.111), channel_id=1, source_target_pairs={{4,0},{8,4},{12,8},{5,1},{9,5},{13,9},{6,2},{10,6},{14,10},{7,3},{... | collective-permute-start | bytes 786440 | tf_op jit(solution)/shard_map/ppermute | solution.py:626
  104.7 11.9 %collective-permute-start.27 = (f32[2,2,128,128]{3,2,1,0:T(8,128)S(1)}, f32[2,2,128,128]{3,2,1,0:T(8,128)S(1)}, u32[]{:S(2)}, u32[]{:S(2)}) collective-permute-start(f32[2,2,128,128]{3,2,1,0:T(8,128)S(1)} %get-tuple-element.113.refs_2_), channel_id=1, source_target_pairs={{8,12},{9,13},{10,14},{11,15},{24,28},{25,29},{26,30},{27,31}} | collective-permute-start | bytes 786440 | tf_op jit(solution)/shard_map/ppermute | solution.py:626
  112.6 8.3 %collective-permute-start.26 = (f32[2,2,128,128]{3,2,1,0:T(8,128)S(1)}, f32[2,2,128,128]{3,2,1,0:T(8,128)S(1)}, u32[]{:S(2)}, u32[]{:S(2)}) collective-permute-start(f32[2,2,128,128]{3,2,1,0:T(8,128)S(1)} %get-tuple-element.116), channel_id=1, source_target_pairs={{4,0},{8,4},{12,8},{5,1},{9,5},{13,9},{6,2},{10,6},{14,10},{7,3},{... | collective-permute-start | bytes 786440 | tf_op jit(solution)/shard_map/ppermute | solution.py:626
  114.0 30.4 %collective-permute-start.25 = (f32[2048,128]{1,0:T(8,128)S(1)}, f32[2048,128]{1,0:T(8,128)S(1)}, u32[]{:S(2)}, u32[]{:S(2)}) collective-permute-start(f32[2048,128]{1,0:T(8,128)S(1)} %slice.13), channel_id=1, source_target_pairs={{0,2},{2,0},{1,3},{3,1},{4,6},{6,4},{5,7},{7,5},{8,10},{10,8},{9,1... | collective-permute-start | bytes 3145736 | tf_op jit(solution)/shard_map/ppermute | solution.py:524
  122.2 8.5 %collective-permute-start.28 = (f32[2,2,128,128]{3,2,1,0:T(8,128)S(1)}, f32[2,2,128,128]{3,2,1,0:T(8,128)S(1)}, u32[]{:S(2)}, u32[]{:S(2)}) collective-permute-start(f32[2,2,128,128]{3,2,1,0:T(8,128)S(1)} %get-tuple-element.119), channel_id=1, source_target_pairs={{4,0},{8,4},{12,8},{5,1},{9,5},{13,9},{6,2},{10,6},{14,10},{7,3},{... | collective-permute-start | bytes 786440 | tf_op jit(solution)/shard_map/ppermute | solution.py:626
  132.0 9.8 %collective-permute-start.30 = (f32[2,2,128,128]{3,2,1,0:T(8,128)S(1)}, f32[2,2,128,128]{3,2,1,0:T(8,128)S(1)}, u32[]{:S(2)}, u32[]{:S(2)}) collective-permute-start(f32[2,2,128,128]{3,2,1,0:T(8,128)S(1)} %get-tuple-element.121), channel_id=1, source_target_pairs={{4,0},{8,4},{5,1},{9,5},{6,2},{10,6},{7,3},{11,7},{20,16},{24,20},... | collective-permute-start | bytes 786440 | tf_op jit(solution)/shard_map/ppermute | solution.py:626
  143.2 8.3 %collective-permute-start.31 = (f32[2,2,128,128]{3,2,1,0:T(8,128)S(1)}, f32[2,2,128,128]{3,2,1,0:T(8,128)S(1)}, u32[]{:S(2)}, u32[]{:S(2)}) collective-permute-start(f32[2,2,128,128]{3,2,1,0:T(8,128)S(1)} %get-tuple-element.124), channel_id=1, source_target_pairs={{4,0},{5,1},{6,2},{7,3},{20,16},{21,17},{22,18},{23,19}} | collective-permute-start | bytes 786440 | tf_op jit(solution)/shard_map/ppermute | solution.py:626
  156.1 13.2 %collective-permute-start.33 = (f32[2,2,1,6,192,128]{5,4,3,2,1,0:T(8,128)}, f32[2,2,1,6,192,128]{5,4,3,2,1,0:T(8,128)}, u32[]{:S(2)}, u32[]{:S(2)}) collective-permute-start(f32[2,2,1,6,192,128]{5,4,3,2,1,0:T(8,128)} %take_rows.5), channel_id=1, source_target_pairs={{0,1},{1,0},{2,3},{3,2},{4,5},{5,4},{6,7},{7,6},{8,9},{9,8},{10,11... | collective-permute-start | bytes 7077896 | tf_op jit(solution)/shard_map/ppermute | solution.py:524
  158.2 3.2 %collective-permute-start.32 = (f32[1024,128]{1,0:T(8,128)S(1)}, f32[1024,128]{1,0:T(8,128)S(1)}, u32[]{:S(2)}, u32[]{:S(2)}) collective-permute-start(f32[1024,128]{1,0:T(8,128)S(1)} %get-tuple-element.127), channel_id=1, source_target_pairs={{0,1},{1,0},{2,3},{3,2},{4,5},{5,4},{6,7},{7,6},{8,9},{9,8},{10,11... | collective-permute-start | bytes 1572872 | tf_op jit(solution)/shard_map/ppermute | solution.py:524
  162.1 7.2 %copy-start = (f32[42368,128]{1,0:T(8,128)}, f32[42368,128]{1,0:T(8,128)S(1)}, u32[]{:S(2)}) copy-start(f32[42368,128]{1,0:T(8,128)S(1)} %deposit_patches.25.state) | copy-start | bytes 65077252
  169.3 7.2 %copy-start.1 = (f32[42368,128]{1,0:T(8,128)S(1)}, f32[42368,128]{1,0:T(8,128)}, u32[]{:S(2)}) copy-start(f32[42368,128]{1,0:T(8,128)} %copy-done) | copy-start | bytes 65077252

commit v2 on v1

--- a/solution.py
+++ b/solution.py
@@ -61,30 +61,15 @@
 
 def transform(left, right, fields):
     size = fields[0][0].shape[0]
-    stacked = jnp.concatenate(
-        [
-            jnp.concatenate([real for real, _ in fields], axis=1),
-            jnp.concatenate([imag for _, imag in fields], axis=1),
-        ],
-        axis=0,
-    )
-    high, low = halves(stacked)
-    mid = dot(left[0], high) + (dot(left[1], high) + dot(left[0], low))
-    rows = jnp.concatenate(
-        [
-            jnp.concatenate(
-                [mid[:size, i * size : (i + 1) * size], mid[size:, i * size : (i + 1) * size]], axis=1
-            )
-            for i in range(len(fields))
-        ],
-        axis=0,
-    )
-    high, low = halves(rows)
-    out = dot(high, right[0]) + (dot(high, right[1]) + dot(low, right[0]))
-    return [
-        (out[i * size : (i + 1) * size, :size], out[i * size : (i + 1) * size, size:])
-        for i in range(len(fields))
-    ]
+    mids = []
+    for high, low in [halves(jnp.concatenate(field, axis=0)) for field in fields]:
+        both = dot(left[0], jnp.concatenate([high, low], axis=1))
+        mids.append(both[:, :size] + (both[:, size:] + dot(left[1], high)))
+    outs = []
+    for high, low in [halves(jnp.concatenate([mid[:size], mid[size:]], axis=1)) for mid in mids]:
+        both = dot(jnp.concatenate([high, low], axis=0), right[0])
+        outs.append(both[:size] + (both[size:] + dot(high, right[1])))
+    return [(out[:, :size], out[:, size:]) for out in outs]
 
 
 def times(a, b):
@@ -241,11 +226,11 @@
     )
 
 
-def cut_patches(lay, info, own, other, state, begin, end):
+def cut_patches(lay, info, own, other, state, begin, end, from_hbm=False):
     half = own.shape[2]
     tall, pixels = lay.tall, lay.pixels
 
-    def one(probe, info, own, other, state, window):
+    def one(probe, info, own, other, state, window, sem):
         row0, down, block, shift = lay.window(info, probe)
         own_top = lax.axis_index("lat") == 0
         near_at = pl.ds(pl.multiple_of(block * pixels, pixels), pixels)
@@ -257,6 +242,12 @@
 
             @pl.when(jnp.where(is_top, row0 < half, row0 + tall > half))
             def _(source=source, rows=rows, to=to):
+                if source is own and from_hbm:
+                    both = pl.ds(pl.multiple_of(block * pixels, pixels), 2 * pixels)
+                    copy = pltpu.make_async_copy(source.at[:, :, rows, both], window.at[:, :, to, :], sem)
+                    copy.start()
+                    copy.wait()
+                    return
                 for part in range(2):
                     for layer in range(lay.layers):
                         window[part, layer, to, 0:pixels] = source[part, layer, rows, near_at]
@@ -283,9 +274,9 @@
         lay,
         body,
         state,
-        [("vmem", info), ("vmem", own), ("vmem", other)],
+        [("vmem", info), ("hbm" if from_hbm else "vmem", own), ("vmem", other)],
         [],
-        scratch=[pltpu.VMEM((2, lay.layers, 2 * tall, 2 * pixels), F32)],
+        scratch=[pltpu.VMEM((2, lay.layers, 2 * tall, 2 * pixels), F32), pltpu.SemaphoreType.DMA(())],
         name="cut_patches",
     )[0]
 
@@ -456,68 +447,63 @@
 
 def take_rows(lay, state, owners, others):
     rows = lay.rows // (2 * owners)
-    pieces = [(p, l, o, b) for p in range(2) for l in range(lay.layers) for o in range(owners) for b in range(lay.blocks)]
-
-    def body(state, out, sems):
+
+    def body(state, out):
         core = lax.axis_index("lat")
         core = 1 - core if others else core
-        for act in ("start", "wait"):
-            for i, (part, layer, owner, block) in enumerate(pieces):
-                start = lay.total(part, layer, block, lay.tall + (2 * owner + core) * rows)
-                copy = pltpu.make_async_copy(
-                    state.at[pl.ds(pl.multiple_of(start, 8), rows), :],
-                    out.at[part, layer, owner, block],
-                    sems.at[i],
-                )
-                getattr(copy, act)()
+        for part in range(2):
+            for layer in range(lay.layers):
+                for owner in range(owners):
+                    for block in range(lay.blocks):
+                        start = lay.total(part, layer, block, lay.tall + (2 * owner + core) * rows)
+                        out[part, layer, owner, block] = state[pl.ds(pl.multiple_of(start, 8), rows), :]
 
     return pl.pallas_call(
         body,
         in_specs=[VMEM],
         out_specs=VMEM,
         out_shape=pltpu.VMEM((2, lay.layers, owners, lay.blocks, rows, lay.pixels), F32),
-        scratch_shapes=[pltpu.SemaphoreType.DMA((len(pieces),))],
         compiler_params=pltpu.CompilerParams(vmem_limit_bytes=SCOPED),
         cost_estimate=pl.CostEstimate(flops=1000, bytes_accessed=1000, transcendentals=0),
         name="take_rows",
     )(in_vmem(state))
 
 
-def room(shape):
+def put_aside(state, begin, end):
+    def body(state, out, sem):
+        copy = pltpu.make_async_copy(state.at[pl.ds(begin, end - begin), :], out, sem)
+        copy.start()
+        copy.wait()
+
     return pl.pallas_call(
-        lambda out: None,
-        out_specs=VMEM,
-        out_shape=pltpu.VMEM(shape, F32),
+        body,
+        in_specs=[VMEM],
+        out_specs=HBM,
+        out_shape=pltpu.HBM((end - begin, state.shape[1]), F32),
+        scratch_shapes=[pltpu.SemaphoreType.DMA(())],
         compiler_params=pltpu.CompilerParams(vmem_limit_bytes=SCOPED),
-        name="room",
-    )()
-
-
-def finish(lay, state, received, more, late):
-    rows = lay.rows // 2
-
-    def body(late, state, received, more, out):
-        part, layer = pl.program_id(0), pl.program_id(1)
-        is_late = jnp.max(late[...]) > 0
-        for block in range(lay.blocks):
-            start = lay.total(part, layer, block, lay.tall + lax.axis_index("lat") * rows)
-            columns = pl.ds(block * lay.pixels, lay.pixels)
-            here = state[pl.ds(pl.multiple_of(start, 8), rows), :] + received[part, layer, 0, block]
-            out[0, 0, :, columns] = here
-
-            @pl.when(is_late)
-            def _(block=block, columns=columns, here=here):
-                out[0, 0, :, columns] = here + more[part, layer, 0, block]
+        cost_estimate=pl.CostEstimate(flops=1000, bytes_accessed=1000, transcendentals=0),
+        name="put_aside",
+    )(in_vmem(state))
+
+
+def add_up(kept, received):
+    _, layers, _, blocks, rows, pixels = kept.shape
+    each = pl.BlockSpec((1, 1, 1, blocks, rows, pixels), lambda i, j: (i, j, 0, 0, 0, 0))
+
+    def body(kept, received, out):
+        for block in range(blocks):
+            out[0, 0, :, pl.ds(block * pixels, pixels)] = kept[0, 0, 0, block] + received[0, 0, 0, block]
 
     return pl.pallas_call(
         body,
-        grid=(2, lay.layers),
-        in_specs=[VMEM] * 4,
-        out_specs=pl.BlockSpec((1, 1, rows, lay.width), lambda i, j: (i, j, 0, 0)),
-        out_shape=pltpu.HBM((2, lay.layers, rows, lay.width), F32),
+        grid=(2, layers),
+        in_specs=[each, each],
+        out_specs=pl.BlockSpec((1, 1, rows, blocks * pixels), lambda i, j: (i, j, 0, 0)),
+        out_shape=pltpu.HBM((2, layers, rows, blocks * pixels), F32),
         compiler_params=pltpu.CompilerParams(vmem_limit_bytes=SCOPED),
-        name="finish",
-    )(*map(in_vmem, (late, state, received, more)))
+        name="add_up",
+    )(kept, received)
 
 
 def swap(shard, axis):
@@ -528,8 +514,11 @@
     n = lay.probes
     total = 4 * n
 
-    def body(positions, *refs):
-        *scans, info = refs
+    def body(listed, *refs):
+        *scans, info, positions, sem = refs
+        copy = pltpu.make_async_copy(listed, positions, sem)
+        copy.start()
+        copy.wait()
         lat, side = lax.axis_index("lat"), lax.axis_index("probe")
         lane = lax.broadcasted_iota(jnp.int32, (1, 128), 1)
         at = lax.broadcasted_iota(jnp.int32, (total, 128), 0)
@@ -554,12 +543,13 @@
 
     return pl.pallas_call(
         body,
-        in_specs=[SMEM] * 5,
+        in_specs=[HBM] + [SMEM] * 4,
         out_specs=VMEM,
         out_shape=pltpu.VMEM((1, 128), jnp.int32),
+        scratch_shapes=[pltpu.SMEM(positions.T.shape, jnp.int32), pltpu.SemaphoreType.DMA(())],
         compiler_params=pltpu.CompilerParams(vmem_limit_bytes=SCOPED),
         name="sort_probes",
-    )(positions.T, *indices)
+    )(in_hbm(positions.T), *indices)
 
 
 def bring(x):
@@ -575,7 +565,7 @@
         out_shape=pltpu.VMEM(x.shape, x.dtype),
         scratch_shapes=[pltpu.SemaphoreType.DMA(())],
         compiler_params=pltpu.CompilerParams(vmem_limit_bytes=SCOPED),
-        cost_estimate=pl.CostEstimate(flops=0, bytes_accessed=2 * x.size * 4, transcendentals=0),
+        cost_estimate=pl.CostEstimate(flops=1000, bytes_accessed=1000, transcendentals=0),
         name="bring",
     )(in_hbm(x))
 
@@ -604,7 +594,6 @@
         end = sections - 1
         ends = [(2 * end, 2 * end + 1), (2 * end + 1, 2 * end)]
         mine = lax.ppermute(measured, ("depth", "probe"), ends)
-        specimen = bring(specimen)
         info = sort_probes(lay, early, positions, indices)
         everyone = swap(info, "groups") if lax.axis_size("groups") == 2 else info
     else:
@@ -612,7 +601,7 @@
         corners = positions[scan_index.reshape(-1)]
         info = lay.pack(corners[:, 0], corners[:, 1], jnp.arange(probes, dtype=jnp.int32))
         info = everyone = jnp.pad(info, (0, 3 * probes))[None]
-    state = cut_patches(lay, info, specimen, other, None, 0, count)
+    state = cut_patches(lay, info, specimen, other, None, 0, count, from_hbm=True)
     def busy(tick, source, by):
         delay = source if by > 0 else 2 * (sections - 1) - source
         return 0 <= tick - delay < lay.groups
@@ -633,9 +622,11 @@
     parts = [(0, early // 2), (early // 2, early)] if paired else []
     crossing = {}
     down = up = None
-    middle = min(1 + -(-lay.groups // 2), lay.groups) * count
-    part = lambda section: jnp.where(section < 2, middle, probes)
-    cuts = {0: (count, part), min(fill, lay.groups // 2): (part, probes)}
+    def upto(group):
+        early_sections = min(group, lay.groups) * count
+        return lambda section: jnp.where(section < 2, early_sections, probes)
+
+    cuts = {0: (count, upto(3)), 2: (upto(3), upto(5)), 3: (upto(5), probes)}
     last_tick = lay.groups + 2 * fill - 1
     sent = None
     for tick in range(lay.groups + 2 * fill):
@@ -646,9 +637,12 @@
         if tick < lay.groups + fill:
             start_wave = illumination if tick < lay.groups else None
             state, own = run_forward(lay, tick, sections, tables, state, down, start_wave)
+            if tick == 0:
+                own, specimen = lax.optimization_barrier((own, specimen))
+                brought = bring(specimen)
             down = pass_on(own, tick, 1)
             if tick in cuts:
-                state = cut_patches(lay, info, specimen, other, state, *cuts[tick])
+                state = cut_patches(lay, info, brought, other, state, *cuts[tick])
             if tick == 0:
                 state = clear_total(lay, state)
             if tick == fill - 1:
@@ -665,8 +659,10 @@
                     crossing.setdefault(due, []).append((begin, 1, swap(grads_of(state, begin, end), "probe")))
             state = deposit(lay, tick, sections, info, received, state)
             if paired and tick == last_tick - 1:
-                state, up = lax.optimization_barrier((state, up))
-                sent = swap(take_rows(lay, state, 1, True), "lat")
+                aside = put_aside(state, *lay.grads_of(early, lay.groups))
+                going = take_rows(lay, state, 1, True)
+                going, aside, up = lax.optimization_barrier((going, aside, up))
+                sent = swap(going, "lat")
     if paired:
         last = swap(rest[0], "lat")
         state = deposit(lay, None, sections, info, [(lay.groups - 1, 2, last)], state)
@@ -675,17 +671,22 @@
         whole = jnp.moveaxis(whole, 3, 4).reshape((2, layers, owners, -1, width))
         return lax.psum_scatter(whole, "probe", scatter_dimension=2, tiled=False)
 
-    def nothing_more(grads):
-        return room(sent.shape)
-
-    def from_partners(grads):
+    def as_they_are(kept, received, grads, last):
+        return add_up(kept, received)
+
+    def with_partners(kept, received, grads, last):
+        each = grads.shape[0] // (lay.groups - early)
+        last = jnp.where(section == 0, last, grads[-each:])
+        grads = swap(jnp.concatenate([grads[:-each], last]), "probe")
         sums = Layout(probes, count, layers, pixels, half, height, width, only_sums=True)
-        sums_state = clear_total(sums, None)
-        sums_state = deposit(sums, None, sections, info, [(early, 1, swap(grads, "probe"))], sums_state)
-        return take_rows(sums, sums_state, 1, False) + swap(take_rows(sums, sums_state, 1, True), "lat")
-
-    more = lax.cond(late[0, 0] > 0, from_partners, nothing_more, grads_of(state, early, lay.groups))
-    return finish(lay, state, sent, more, late)
+        state = clear_total(sums, None)
+        state = deposit(sums, None, sections, info, [(early, 1, grads)], state)
+        kept = kept + take_rows(sums, state, 1, False)
+        return add_up(kept, received + swap(take_rows(sums, state, 1, True), "lat"))
+
+    section = lax.axis_index("depth")
+    kept = take_rows(lay, state, 1, False)
+    return lax.cond(late[0, 0] > 0, with_partners, as_they_are, kept, sent, aside, rest[0])
 
 
 def solution(mesh):

time: 181 us -> 188 us (1.039)
  local copies, waits for them, and re-layouts: 15.9 us -> 29.6 us
  waiting for transfers between devices: 52.3 us -> 49.2 us
  Pallas kernels: 51.7 us -> 48.8 us
    unnamed x14 -> x16, local copies, waits for them, and re-layouts: 15.7 us -> 29.5 us
    pallas_call x1 -> x2, Pallas kernels: 4.67 us -> 1.72 us  [take_rows(): pl.pallas_call(body, in_specs=[VMEM], out_specs=VMEM, out_shape=pltpu.VME...]
    pallas_call x3, Pallas kernels: 5.09 us -> 7 us  [the longest x1 3.94 us: add_up(): pl.pallas_call(body, grid=(2, layers), in_specs=[each, each], out_specs=p...]
    pallas_call x39 -> x40, Pallas kernels: 39.6 us -> 37.8 us  [call(): pl.pallas_call(kernel, in_specs=specs, out_specs=[VMEM] * (1 + len(outs)...]
  transfers between devices with their start and end apart: 32 -> 32, of which waited for: 20 -> 19; matrix products, arithmetic and copies ran while one was open for 0% -> 0% of each run, Pallas kernels for 23% -> 23%
where the time goes in v2:
time: 188 us; the launch traced here: 187 us
  starting transfers between devices  59 us (31%)
  waiting for transfers between devices  49.2 us (26%)
  Pallas kernels  48.8 us (26%)
  local copies, waits for them, and re-layouts  29.6 us (16%)
    ppermute x20, starting transfers between devices, pass_on(): return lax.ppermute(wave, 'depth', pairs) if pairs else None  49.1 us
    ppermute x20, waiting for transfers between devices, pass_on(): return lax.ppermute(wave, 'depth', pairs) if pairs else None  43.4 us
    pallas_call x40, Pallas kernels, call(): pl.pallas_call(kernel, in_specs=specs, out_specs=[VMEM] * (1 + len(outs)...  37.8 us
    unnamed x16, local copies, waits for them, and re-layouts  29.5 us
    ppermute x9, starting transfers between devices, swap(): return lax.ppermute(shard, axis, [(0, 1), (1, 0)])  7.74 us
    ppermute x9, waiting for transfers between devices, swap(): return lax.ppermute(shard, axis, [(0, 1), (1, 0)])  5.77 us
    pallas_call x1, Pallas kernels, add_up(): pl.pallas_call(body, grid=(2, layers), in_specs=[each, each], out_specs=p...  3.94 us
  transfers between devices with their start and end apart: 32, of which 19 were waited for; matrix products, arithmetic and copies ran while one was open for 0% of the time, Pallas kernels for 23%

profile of v2, /device:TPU:0, one launch (start us, length us, event | category | flops | bytes accessed | tf_op | source)
XLA Modules:
  0.0 187.4 jit_solution(5395965595305699654)
XLA Ops:
  1.7 2.7 %collective-permute-start.2 = (s32[16]{0:T(128)}, s32[16]{0:T(128)S(1)}, u32[]{:S(2)}, u32[]{:S(2)}) collective-permute-start(s32[16]{0:T(128)} %bitcast.12), channel_id=1, source_target_pairs={{0,2},{2,0},{1,3},{3,1},{4,6},{6,4},{5,7},{7,5},{8,10},{10,8},{9,1... | collective-permute-start | bytes 200 | tf_op jit(solution)/shard_map/ppermute | solution.py:510
  4.4 1.6 collective-permute-done.2.refs_1_
  6.1 1.9 %collective-permute-done.4.refs_3_ = s32[16]{0:T(128)S(1)} collective-permute-done((s32[16]{0:T(128)S(1)}, s32[16]{0:T(128)S(1)}, u32[]{:S(2)}, u32[]{:S(2)}) %collective-permute-start.4) | collective-permute-done | bytes 96 | tf_op jit(solution)/shard_map/ppermute | solution.py:510
  9.3 1.7 sort_probes.1.refs_0_
  11.0 2.9 %cut_patches.4.refs_2_ = f32[42368,128]{1,0:T(8,128)S(1)} custom-call(s32[1,128]{1,0:T(1,128)S(1)} %sort_probes.1.refs_0_, f32[2,2,384,768]{3,2,1,0:T(8,128)} %x, f32[2,2,384,768]{3,2,1,0:T(8,128)S(1)} %collective-permute-done.5.refs_2_), custom_call_target="tpu_custom_call" | custom-call | flops 1000 | bytes 1000 | tf_op jit(solution)/shard_map/cut_patches/pallas_call | solution.py:157
  14.9 2.6 %collective-permute-start.6 = (f32[2,2,128,128]{3,2,1,0:T(8,128)S(1)}, f32[2,2,128,128]{3,2,1,0:T(8,128)S(1)}, u32[]{:S(2)}, u32[]{:S(2)}) collective-permute-start(f32[2,2,128,128]{3,2,1,0:T(8,128)S(1)} %get-tuple-element.98), channel_id=1, source_target_pairs={{0,4},{1,5},{2,6},{3,7},{16,20},{17,21},{18,22},{19,23}} | collective-permute-start | bytes 786440 | tf_op jit(solution)/shard_map/ppermute | solution.py:615
  17.5 2.3 %bring.1.refs_1_ = f32[2,2,384,768]{3,2,1,0:T(8,128)S(1)} custom-call(f32[2,2,384,768]{3,2,1,0:T(8,128)} %x), custom_call_target="tpu_custom_call" | custom-call | flops 1000 | bytes 1000 | tf_op jit(solution)/shard_map/bring/pallas_call | solution.py:561
  19.9 1.8 cut_patches.5.refs_0_
  24.2 4.4 %collective-permute-start.7 = (f32[2,2,128,128]{3,2,1,0:T(8,128)S(1)}, f32[2,2,128,128]{3,2,1,0:T(8,128)S(1)}, u32[]{:S(2)}, u32[]{:S(2)}) collective-permute-start(f32[2,2,128,128]{3,2,1,0:T(8,128)S(1)} %get-tuple-element.101), channel_id=1, source_target_pairs={{0,4},{4,8},{1,5},{5,9},{2,6},{6,10},{3,7},{7,11},{16,20},{20,24},... | collective-permute-start | bytes 786440 | tf_op jit(solution)/shard_map/ppermute | solution.py:615
  28.6 1.6 collective-permute-start.9
  30.9 1.3 collective-permute-done.9.refs_1_
  35.1 4.4 %collective-permute-start.12 = (f32[2,2,128,128]{3,2,1,0:T(8,128)S(1)}, f32[2,2,128,128]{3,2,1,0:T(8,128)S(1)}, u32[]{:S(2)}, u32[]{:S(2)}) collective-permute-start(f32[2,2,128,128]{3,2,1,0:T(8,128)S(1)} %get-tuple-element.109), channel_id=1, source_target_pairs={{0,4},{4,8},{8,12},{1,5},{5,9},{9,13},{2,6},{6,10},{10,14},{3,7},{... | collective-permute-start | bytes 786440 | tf_op jit(solution)/shard_map/ppermute | solution.py:615
  39.5 1.7 cut_patches.6.refs_6_
  42.0 1.5 collective-permute-done.12.refs_1_
  44.4 4.4 %collective-permute-start.14 = (f32[2,2,128,128]{3,2,1,0:T(8,128)S(1)}, f32[2,2,128,128]{3,2,1,0:T(8,128)S(1)}, u32[]{:S(2)}, u32[]{:S(2)}) collective-permute-start(f32[2,2,128,128]{3,2,1,0:T(8,128)S(1)} %get-tuple-element.111.refs_1_), channel_id=1, source_target_pairs={{0,4},{4,8},{8,12},{1,5},{5,9},{9,13},{2,6},{6,10},{10,14},{3,7},{... | collective-permute-start | bytes 786440 | tf_op jit(solution)/shard_map/ppermute | solution.py:615
  48.8 2.5 %cut_patches.7.refs_2_ = f32[42368,128]{1,0:T(8,128)S(1)} custom-call(s32[1,128]{1,0:T(1,128)S(1)} %sort_probes.1.refs_0_, f32[2,2,384,768]{3,2,1,0:T(8,128)S(1)} %bring.1.refs_1_, f32[2,2,384,768]{3,2,1,0:T(8,128)S(1)} %collective-permute-done.5.refs_2_, f32[42368,128]{1,0:T(8,128)S(1)} %get-tuple-element.112.refs_3_), custom_call_target="tpu_custom_call", output_to_operand_aliasing={{}: (3, {})} | custom-call | flops 1000 | bytes 1000 | tf_op jit(solution)/shard_map/cut_patches/pallas_call | solution.py:157
  53.6 6.3 %collective-permute-start.16 = (f32[2,2,128,128]{3,2,1,0:T(8,128)S(1)}, f32[2,2,128,128]{3,2,1,0:T(8,128)S(1)}, u32[]{:S(2)}, u32[]{:S(2)}) collective-permute-start(f32[2,2,128,128]{3,2,1,0:T(8,128)S(1)} %get-tuple-element.115.refs_2_), channel_id=1, source_target_pairs={{0,4},{4,8},{8,12},{1,5},{5,9},{9,13},{2,6},{6,10},{10,14},{3,7},{... | collective-permute-start | bytes 786440 | tf_op jit(solution)/shard_map/ppermute | solution.py:615
  60.9 3.5 %collective-permute-done.16.refs_1_ = f32[2,2,128,128]{3,2,1,0:T(8,128)S(1)} collective-permute-done((f32[2,2,128,128]{3,2,1,0:T(8,128)S(1)}, f32[2,2,128,128]{3,2,1,0:T(8,128)S(1)}, u32[]{:S(2)}, u32[]{:S(2)}) %collective-permute-start.16) | collective-permute-done | bytes 262176 | tf_op jit(solution)/shard_map/ppermute | solution.py:615
  65.4 4.4 %collective-permute-start.18 = (f32[2,2,128,128]{3,2,1,0:T(8,128)S(1)}, f32[2,2,128,128]{3,2,1,0:T(8,128)S(1)}, u32[]{:S(2)}, u32[]{:S(2)}) collective-permute-start(f32[2,2,128,128]{3,2,1,0:T(8,128)S(1)} %get-tuple-element.119.refs_2_), channel_id=1, source_target_pairs={{0,4},{4,8},{8,12},{1,5},{5,9},{9,13},{2,6},{6,10},{10,14},{3,7},{... | collective-permute-start | bytes 786440 | tf_op jit(solution)/shard_map/ppermute | solution.py:615
  70.0 1.3 collective-permute-start.17
  71.6 2.0 %collective-permute-done.18.refs_1_ = f32[2,2,128,128]{3,2,1,0:T(8,128)S(1)} collective-permute-done((f32[2,2,128,128]{3,2,1,0:T(8,128)S(1)}, f32[2,2,128,128]{3,2,1,0:T(8,128)S(1)}, u32[]{:S(2)}, u32[]{:S(2)}) %collective-permute-start.18) | collective-permute-done | bytes 262176 | tf_op jit(solution)/shard_map/ppermute | solution.py:615
  74.6 5.0 %collective-permute-start.20 = (f32[2,2,128,128]{3,2,1,0:T(8,128)S(1)}, f32[2,2,128,128]{3,2,1,0:T(8,128)S(1)}, u32[]{:S(2)}, u32[]{:S(2)}) collective-permute-start(f32[2,2,128,128]{3,2,1,0:T(8,128)S(1)} %get-tuple-element.123.refs_2_), channel_id=1, source_target_pairs={{0,4},{4,8},{8,12},{1,5},{5,9},{9,13},{2,6},{6,10},{10,14},{3,7},{... | collective-permute-start | bytes 786440 | tf_op jit(solution)/shard_map/ppermute | solution.py:615
  80.8 1.3 collective-permute-start.19
  84.3 4.6 %collective-permute-start.22 = (f32[2,2,128,128]{3,2,1,0:T(8,128)S(1)}, f32[2,2,128,128]{3,2,1,0:T(8,128)S(1)}, u32[]{:S(2)}, u32[]{:S(2)}) collective-permute-start(f32[2,2,128,128]{3,2,1,0:T(8,128)S(1)} %get-tuple-element.127.refs_2_), channel_id=1, source_target_pairs={{0,4},{4,8},{8,12},{1,5},{5,9},{9,13},{2,6},{6,10},{10,14},{3,7},{... | collective-permute-start | bytes 786440 | tf_op jit(solution)/shard_map/ppermute | solution.py:615
  90.2 1.3 collective-permute-start.21
  93.9 4.5 %collective-permute-done.21.refs_1_ = f32[2,2,128,128]{3,2,1,0:T(8,128)S(1)} collective-permute-done((f32[2,2,128,128]{3,2,1,0:T(8,128)S(1)}, f32[2,2,128,128]{3,2,1,0:T(8,128)S(1)}, u32[]{:S(2)}, u32[]{:S(2)}) %collective-permute-start.21) | collective-permute-done | bytes 262176 | tf_op jit(solution)/shard_map/ppermute | solution.py:615
  99.4 1.3 collective-permute-start.23
  102.5 5.5 %collective-permute-done.23.refs_1_ = f32[2,2,128,128]{3,2,1,0:T(8,128)S(1)} collective-permute-done((f32[2,2,128,128]{3,2,1,0:T(8,128)S(1)}, f32[2,2,128,128]{3,2,1,0:T(8,128)S(1)}, u32[]{:S(2)}, u32[]{:S(2)}) %collective-permute-start.23) | collective-permute-done | bytes 262176 | tf_op jit(solution)/shard_map/ppermute | solution.py:615
  108.9 1.3 collective-permute-start.26
  110.2 1.6 collective-permute-start.25
  112.9 4.9 %collective-permute-done.26.refs_1_ = f32[2,2,128,128]{3,2,1,0:T(8,128)S(1)} collective-permute-done((f32[2,2,128,128]{3,2,1,0:T(8,128)S(1)}, f32[2,2,128,128]{3,2,1,0:T(8,128)S(1)}, u32[]{:S(2)}, u32[]{:S(2)}) %collective-permute-start.26) | collective-permute-done | bytes 262176 | tf_op jit(solution)/shard_map/ppermute | solution.py:615
  118.7 1.3 collective-permute-start.28
  120.0 2.3 %deposit_patches.21.refs_2_ = f32[42368,128]{1,0:T(8,128)S(1)} custom-call(s32[1,128]{1,0:T(1,128)S(1)} %sort_probes.1.refs_0_, f32[2048,128]{1,0:T(8,128)S(1)} %collective-permute-done.29.refs_1_, f32[42368,128]{1,0:T(8,128)S(1)} %get-tuple-element.142.refs_2_), custom_call_target="tpu_custom_call", output_to_operand_aliasing={{}: (2, {})} | custom-call | flops 1000 | bytes 1000 | tf_op jit(solution)/shard_map/deposit_patches/pallas_call | solution.py:157
  122.3 6.6 %collective-permute-done.28.refs_1_ = f32[2,2,128,128]{3,2,1,0:T(8,128)S(1)} collective-permute-done((f32[2,2,128,128]{3,2,1,0:T(8,128)S(1)}, f32[2,2,128,128]{3,2,1,0:T(8,128)S(1)}, u32[]{:S(2)}, u32[]{:S(2)}) %collective-permute-start.28) | collective-permute-done | bytes 262176 | tf_op jit(solution)/shard_map/ppermute | solution.py:615
  129.8 1.3 collective-permute-start.30
  132.2 9.2 %collective-permute-done.30.refs_1_ = f32[2,2,128,128]{3,2,1,0:T(8,128)S(1)} collective-permute-done((f32[2,2,128,128]{3,2,1,0:T(8,128)S(1)}, f32[2,2,128,128]{3,2,1,0:T(8,128)S(1)}, u32[]{:S(2)}, u32[]{:S(2)}) %collective-permute-start.30) | collective-permute-done | bytes 262176 | tf_op jit(solution)/shard_map/ppermute | solution.py:615
  142.4 1.3 collective-permute-start.31
  143.7 1.8 deposit_patches.23.state.refs_2_
  145.5 1.6 take_rows.6
  147.1 1.4 put_aside.1
  148.5 2.2 %collective-permute-done.31.refs_1_ = f32[2,2,128,128]{3,2,1,0:T(8,128)S(1)} collective-permute-done((f32[2,2,128,128]{3,2,1,0:T(8,128)S(1)}, f32[2,2,128,128]{3,2,1,0:T(8,128)S(1)}, u32[]{:S(2)}, u32[]{:S(2)}) %collective-permute-start.31) | collective-permute-done | bytes 262176 | tf_op jit(solution)/shard_map/ppermute | solution.py:615
  150.6 1.6 backward_section.21
  152.2 7.2 %copy-done = f32[42368,128]{1,0:T(8,128)} copy-done((f32[42368,128]{1,0:T(8,128)}, f32[42368,128]{1,0:T(8,128)S(1)}, u32[]{:S(2)}) %copy-start) | copy-done | bytes 21692440
  160.0 7.2 %copy-done.1 = f32[42368,128]{1,0:T(8,128)S(1)} copy-done((f32[42368,128]{1,0:T(8,128)S(1)}, f32[42368,128]{1,0:T(8,128)}, u32[]{:S(2)}) %copy-start.1) | copy-done | bytes 21692440
  168.9 7.2 %copy-done.2 = f32[42368,128]{1,0:T(8,128)} copy-done((f32[42368,128]{1,0:T(8,128)}, f32[42368,128]{1,0:T(8,128)S(1)}, u32[]{:S(2)}) %copy-start.2) | copy-done | bytes 21692440
  176.1 7.2 %copy-done.3 = f32[42368,128]{1,0:T(8,128)S(1)} copy-done((f32[42368,128]{1,0:T(8,128)S(1)}, f32[42368,128]{1,0:T(8,128)}, u32[]{:S(2)}) %copy-start.3) | copy-done | bytes 21692440
  183.5 4.0 %conditional.1 = (f32[2,2,192,768]{3,2,1,0:T(8,128)}) conditional(s32[]{:T(128)} %bitcast.6, (f32[2,2,1,6,192,128]{5,4,3,2,1,0:T(8,128)S(1)}, f32[2,2,1,6,192,128]{5,4,3,2,1,0:T(8,128)}) %tuple.21, (f32[4096,128]{1,0:T(8,128)}, s32[]{:T(128)}, f32[1024,128]{1,0:T(8,128)S(1)}, s32[1,128]{1,0:T(1,128)S(1)}, f32[2,2,1,6,192,128]{5,4,3,2,1,0:T(8,128)S(1)}, ...), branch_computations={%region_0.0_spmd, %region_1.2_spmd} | conditional | flops 1839009 | bytes 40898560 | solution.py:689
  183.5 3.9 %add_up.2 = f32[2,2,192,768]{3,2,1,0:T(8,128)} custom-call(f32[2,2,1,6,192,128]{5,4,3,2,1,0:T(8,128)S(1)} %get-tuple-element.24.kept, f32[2,2,1,6,192,128]{5,4,3,2,1,0:T(8,128)} %get-tuple-element.25.received), custom_call_target="tpu_custom_call" | custom-call | tf_op jit(solution)/shard_map/cond/branch_0_fun/add_up/pallas_call | solution.py:498
  (81 shorter events, 35.3 us)
Async XLA Ops:
  0.0 14.0 %copy-start.4 = (bf16[2,2,2,256,256]{4,3,2,1,0:T(8,128)(2,1)S(1)}, bf16[2,2,2,256,256]{4,3,2,1,0:T(8,128)(2,1)}, u32[]{:S(2)}) copy-start(bf16[2,2,2,256,256]{4,3,2,1,0:T(8,128)(2,1)} %constant.12.clone.refs_0_) | copy-start | bytes 3145732
  0.0 14.0 %copy-start.5 = (f32[2,128,128]{2,1,0:T(8,128)S(1)}, f32[2,128,128]{2,1,0:T(8,128)}, u32[]{:S(2)}) copy-start(f32[2,128,128]{2,1,0:T(8,128)} %refs_2_.13) | copy-start | bytes 393220
  0.0 1.4 collective-permute-start.3
  1.4 9.6 %collective-permute-start.5 = (f32[2,2,384,768]{3,2,1,0:T(8,128)}, f32[2,2,384,768]{3,2,1,0:T(8,128)S(1)}, u32[]{:S(2)}, u32[]{:S(2)}) collective-permute-start(f32[2,2,384,768]{3,2,1,0:T(8,128)} %x), channel_id=1, source_target_pairs={{0,1},{1,0},{2,3},{3,2},{4,5},{5,4},{6,7},{7,6},{8,9},{9,8},{10,11... | collective-permute-start | bytes 14155784 | tf_op jit(solution)/shard_map/ppermute | solution.py:510
  1.7 4.3 %collective-permute-start.2 = (s32[16]{0:T(128)}, s32[16]{0:T(128)S(1)}, u32[]{:S(2)}, u32[]{:S(2)}) collective-permute-start(s32[16]{0:T(128)} %bitcast.12), channel_id=1, source_target_pairs={{0,2},{2,0},{1,3},{3,1},{4,6},{6,4},{5,7},{7,5},{8,10},{10,8},{9,1... | collective-permute-start | bytes 200 | tf_op jit(solution)/shard_map/ppermute | solution.py:510
  4.4 3.5 %collective-permute-start.4 = (s32[16]{0:T(128)S(1)}, s32[16]{0:T(128)S(1)}, u32[]{:S(2)}, u32[]{:S(2)}) collective-permute-start(s32[16]{0:T(128)S(1)} %collective-permute-done.3.refs_2_), channel_id=1, source_target_pairs={{0,2},{2,0},{1,3},{3,1},{4,6},{6,4},{5,7},{7,5},{8,10},{10,8},{9,1... | collective-permute-start | bytes 200 | tf_op jit(solution)/shard_map/ppermute | solution.py:510
  7.9 24.2 %collective-permute-start.8 = (f32[16,1,128,128]{3,2,1,0:T(8,128)}, f32[16,1,128,128]{3,2,1,0:T(8,128)S(1)}, u32[]{:S(2)}, u32[]{:S(2)}) collective-permute-start(f32[16,1,128,128]{3,2,1,0:T(8,128)} %param.12), channel_id=1, source_target_pairs={{12,14},{14,12},{13,15},{15,13},{28,30},{30,28},{29,31},{31,29}} | collective-permute-start | bytes 3145736 | tf_op jit(solution)/shard_map/ppermute | solution.py:596
  8.7 0.7 copy-start.6
  14.9 8.3 %collective-permute-start.6 = (f32[2,2,128,128]{3,2,1,0:T(8,128)S(1)}, f32[2,2,128,128]{3,2,1,0:T(8,128)S(1)}, u32[]{:S(2)}, u32[]{:S(2)}) collective-permute-start(f32[2,2,128,128]{3,2,1,0:T(8,128)S(1)} %get-tuple-element.98), channel_id=1, source_target_pairs={{0,4},{1,5},{2,6},{3,7},{16,20},{17,21},{18,22},{19,23}} | collective-permute-start | bytes 786440 | tf_op jit(solution)/shard_map/ppermute | solution.py:615
  22.2 8.0 %copy-start.7 = (f32[16,1,128,128]{3,2,1,0:T(8,128)S(1)}, f32[16,1,128,128]{3,2,1,0:T(8,128)}, u32[]{:S(2)}) copy-start(f32[16,1,128,128]{3,2,1,0:T(8,128)} %param.12) | copy-start | bytes 3145732
  24.2 9.3 %collective-permute-start.7 = (f32[2,2,128,128]{3,2,1,0:T(8,128)S(1)}, f32[2,2,128,128]{3,2,1,0:T(8,128)S(1)}, u32[]{:S(2)}, u32[]{:S(2)}) collective-permute-start(f32[2,2,128,128]{3,2,1,0:T(8,128)S(1)} %get-tuple-element.101), channel_id=1, source_target_pairs={{0,4},{4,8},{1,5},{5,9},{2,6},{6,10},{3,7},{7,11},{16,20},{20,24},... | collective-permute-start | bytes 786440 | tf_op jit(solution)/shard_map/ppermute | solution.py:615
  28.6 3.6 %collective-permute-start.9 = (s32[1,128]{1,0:T(1,128)S(1)}, s32[1,128]{1,0:T(1,128)S(1)}, u32[]{:S(2)}, u32[]{:S(2)}) collective-permute-start(s32[1,128]{1,0:T(1,128)S(1)} %sort_probes.1.refs_0_), channel_id=1, source_target_pairs={{0,16},{16,0},{1,17},{17,1},{2,18},{18,2},{3,19},{19,3},{4,20},{20... | collective-permute-start | bytes 1544 | tf_op jit(solution)/shard_map/ppermute | solution.py:510
  30.2 11.1 %collective-permute-start.10 = (f32[16,1,128,128]{3,2,1,0:T(8,128)S(1)}, f32[16,1,128,128]{3,2,1,0:T(8,128)S(1)}, u32[]{:S(2)}, u32[]{:S(2)}) collective-permute-start(f32[16,1,128,128]{3,2,1,0:T(8,128)S(1)} %copy-done.7), channel_id=1, source_target_pairs={{12,13},{13,12},{14,15},{15,14},{28,29},{29,28},{30,31},{31,30}} | collective-permute-start | bytes 3145736 | tf_op jit(solution)/shard_map/ppermute | solution.py:636
  33.4 7.8 %collective-permute-start.11 = (f32[16,1,128,128]{3,2,1,0:T(8,128)S(1)}, f32[16,1,128,128]{3,2,1,0:T(8,128)S(1)}, u32[]{:S(2)}, u32[]{:S(2)}) collective-permute-start(f32[16,1,128,128]{3,2,1,0:T(8,128)S(1)} %collective-permute-done.8), channel_id=1, source_target_pairs={{12,13},{13,12},{14,15},{15,14},{28,29},{29,28},{30,31},{31,30}} | collective-permute-start | bytes 3145736 | tf_op jit(solution)/shard_map/ppermute | solution.py:636
  35.1 8.4 %collective-permute-start.12 = (f32[2,2,128,128]{3,2,1,0:T(8,128)S(1)}, f32[2,2,128,128]{3,2,1,0:T(8,128)S(1)}, u32[]{:S(2)}, u32[]{:S(2)}) collective-permute-start(f32[2,2,128,128]{3,2,1,0:T(8,128)S(1)} %get-tuple-element.109), channel_id=1, source_target_pairs={{0,4},{4,8},{8,12},{1,5},{5,9},{9,13},{2,6},{6,10},{10,14},{3,7},{... | collective-permute-start | bytes 786440 | tf_op jit(solution)/shard_map/ppermute | solution.py:615
  44.4 8.3 %collective-permute-start.14 = (f32[2,2,128,128]{3,2,1,0:T(8,128)S(1)}, f32[2,2,128,128]{3,2,1,0:T(8,128)S(1)}, u32[]{:S(2)}, u32[]{:S(2)}) collective-permute-start(f32[2,2,128,128]{3,2,1,0:T(8,128)S(1)} %get-tuple-element.111.refs_1_), channel_id=1, source_target_pairs={{0,4},{4,8},{8,12},{1,5},{5,9},{9,13},{2,6},{6,10},{10,14},{3,7},{... | collective-permute-start | bytes 786440 | tf_op jit(solution)/shard_map/ppermute | solution.py:615
  51.4 8.6 %collective-permute-start.13 = (f32[2,2,128,128]{3,2,1,0:T(8,128)S(1)}, f32[2,2,128,128]{3,2,1,0:T(8,128)S(1)}, u32[]{:S(2)}, u32[]{:S(2)}) collective-permute-start(f32[2,2,128,128]{3,2,1,0:T(8,128)S(1)} %get-tuple-element.113), channel_id=1, source_target_pairs={{12,8},{13,9},{14,10},{15,11},{28,24},{29,25},{30,26},{31,27}} | collective-permute-start | bytes 786440 | tf_op jit(solution)/shard_map/ppermute | solution.py:615
  53.6 10.8 %collective-permute-start.16 = (f32[2,2,128,128]{3,2,1,0:T(8,128)S(1)}, f32[2,2,128,128]{3,2,1,0:T(8,128)S(1)}, u32[]{:S(2)}, u32[]{:S(2)}) collective-permute-start(f32[2,2,128,128]{3,2,1,0:T(8,128)S(1)} %get-tuple-element.115.refs_2_), channel_id=1, source_target_pairs={{0,4},{4,8},{8,12},{1,5},{5,9},{9,13},{2,6},{6,10},{10,14},{3,7},{... | collective-permute-start | bytes 786440 | tf_op jit(solution)/shard_map/ppermute | solution.py:615
  60.0 9.8 %collective-permute-start.15 = (f32[2,2,128,128]{3,2,1,0:T(8,128)S(1)}, f32[2,2,128,128]{3,2,1,0:T(8,128)S(1)}, u32[]{:S(2)}, u32[]{:S(2)}) collective-permute-start(f32[2,2,128,128]{3,2,1,0:T(8,128)S(1)} %get-tuple-element.117), channel_id=1, source_target_pairs={{8,4},{12,8},{9,5},{13,9},{10,6},{14,10},{11,7},{15,11},{24,20},{2... | collective-permute-start | bytes 786440 | tf_op jit(solution)/shard_map/ppermute | solution.py:615
  65.4 8.3 %collective-permute-start.18 = (f32[2,2,128,128]{3,2,1,0:T(8,128)S(1)}, f32[2,2,128,128]{3,2,1,0:T(8,128)S(1)}, u32[]{:S(2)}, u32[]{:S(2)}) collective-permute-start(f32[2,2,128,128]{3,2,1,0:T(8,128)S(1)} %get-tuple-element.119.refs_2_), channel_id=1, source_target_pairs={{0,4},{4,8},{8,12},{1,5},{5,9},{9,13},{2,6},{6,10},{10,14},{3,7},{... | collective-permute-start | bytes 786440 | tf_op jit(solution)/shard_map/ppermute | solution.py:615
  70.0 9.9 %collective-permute-start.17 = (f32[2,2,128,128]{3,2,1,0:T(8,128)S(1)}, f32[2,2,128,128]{3,2,1,0:T(8,128)S(1)}, u32[]{:S(2)}, u32[]{:S(2)}) collective-permute-start(f32[2,2,128,128]{3,2,1,0:T(8,128)S(1)} %get-tuple-element.121), channel_id=1, source_target_pairs={{4,0},{8,4},{12,8},{5,1},{9,5},{13,9},{6,2},{10,6},{14,10},{7,3},{... | collective-permute-start | bytes 786440 | tf_op jit(solution)/shard_map/ppermute | solution.py:615
  74.6 8.8 %collective-permute-start.20 = (f32[2,2,128,128]{3,2,1,0:T(8,128)S(1)}, f32[2,2,128,128]{3,2,1,0:T(8,128)S(1)}, u32[]{:S(2)}, u32[]{:S(2)}) collective-permute-start(f32[2,2,128,128]{3,2,1,0:T(8,128)S(1)} %get-tuple-element.123.refs_2_), channel_id=1, source_target_pairs={{0,4},{4,8},{8,12},{1,5},{5,9},{9,13},{2,6},{6,10},{10,14},{3,7},{... | collective-permute-start | bytes 786440 | tf_op jit(solution)/shard_map/ppermute | solution.py:615
  80.8 8.5 %collective-permute-start.19 = (f32[2,2,128,128]{3,2,1,0:T(8,128)S(1)}, f32[2,2,128,128]{3,2,1,0:T(8,128)S(1)}, u32[]{:S(2)}, u32[]{:S(2)}) collective-permute-start(f32[2,2,128,128]{3,2,1,0:T(8,128)S(1)} %get-tuple-element.125), channel_id=1, source_target_pairs={{4,0},{8,4},{12,8},{5,1},{9,5},{13,9},{6,2},{10,6},{14,10},{7,3},{... | collective-permute-start | bytes 786440 | tf_op jit(solution)/shard_map/ppermute | solution.py:615
  84.3 8.9 %collective-permute-start.22 = (f32[2,2,128,128]{3,2,1,0:T(8,128)S(1)}, f32[2,2,128,128]{3,2,1,0:T(8,128)S(1)}, u32[]{:S(2)}, u32[]{:S(2)}) collective-permute-start(f32[2,2,128,128]{3,2,1,0:T(8,128)S(1)} %get-tuple-element.127.refs_2_), channel_id=1, source_target_pairs={{0,4},{4,8},{8,12},{1,5},{5,9},{9,13},{2,6},{6,10},{10,14},{3,7},{... | collective-permute-start | bytes 786440 | tf_op jit(solution)/shard_map/ppermute | solution.py:615
  90.2 8.3 %collective-permute-start.21 = (f32[2,2,128,128]{3,2,1,0:T(8,128)S(1)}, f32[2,2,128,128]{3,2,1,0:T(8,128)S(1)}, u32[]{:S(2)}, u32[]{:S(2)}) collective-permute-start(f32[2,2,128,128]{3,2,1,0:T(8,128)S(1)} %get-tuple-element.129), channel_id=1, source_target_pairs={{4,0},{8,4},{12,8},{5,1},{9,5},{13,9},{6,2},{10,6},{14,10},{7,3},{... | collective-permute-start | bytes 786440 | tf_op jit(solution)/shard_map/ppermute | solution.py:615
  91.6 28.5 %collective-permute-start.29 = (f32[2048,128]{1,0:T(8,128)S(1)}, f32[2048,128]{1,0:T(8,128)S(1)}, u32[]{:S(2)}, u32[]{:S(2)}) collective-permute-start(f32[2048,128]{1,0:T(8,128)S(1)} %slice.17), channel_id=1, source_target_pairs={{0,2},{2,0},{1,3},{3,1},{4,6},{6,4},{5,7},{7,5},{8,10},{10,8},{9,1... | collective-permute-start | bytes 3145736 | tf_op jit(solution)/shard_map/ppermute | solution.py:510
  93.3 8.5 %collective-permute-start.24 = (f32[2,2,128,128]{3,2,1,0:T(8,128)S(1)}, f32[2,2,128,128]{3,2,1,0:T(8,128)S(1)}, u32[]{:S(2)}, u32[]{:S(2)}) collective-permute-start(f32[2,2,128,128]{3,2,1,0:T(8,128)S(1)} %get-tuple-element.131.refs_2_), channel_id=1, source_target_pairs={{4,8},{8,12},{5,9},{9,13},{6,10},{10,14},{7,11},{11,15},{20,24},{2... | collective-permute-start | bytes 786440 | tf_op jit(solution)/shard_map/ppermute | solution.py:615
  99.4 8.6 %collective-permute-start.23 = (f32[2,2,128,128]{3,2,1,0:T(8,128)S(1)}, f32[2,2,128,128]{3,2,1,0:T(8,128)S(1)}, u32[]{:S(2)}, u32[]{:S(2)}) collective-permute-start(f32[2,2,128,128]{3,2,1,0:T(8,128)S(1)} %get-tuple-element.133), channel_id=1, source_target_pairs={{4,0},{8,4},{12,8},{5,1},{9,5},{13,9},{6,2},{10,6},{14,10},{7,3},{... | collective-permute-start | bytes 786440 | tf_op jit(solution)/shard_map/ppermute | solution.py:615
  101.8 11.1 %collective-permute-start.27 = (f32[2,2,128,128]{3,2,1,0:T(8,128)S(1)}, f32[2,2,128,128]{3,2,1,0:T(8,128)S(1)}, u32[]{:S(2)}, u32[]{:S(2)}) collective-permute-start(f32[2,2,128,128]{3,2,1,0:T(8,128)S(1)} %get-tuple-element.135.refs_2_), channel_id=1, source_target_pairs={{8,12},{9,13},{10,14},{11,15},{24,28},{25,29},{26,30},{27,31}} | collective-permute-start | bytes 786440 | tf_op jit(solution)/shard_map/ppermute | solution.py:615
  108.9 9.0 %collective-permute-start.26 = (f32[2,2,128,128]{3,2,1,0:T(8,128)S(1)}, f32[2,2,128,128]{3,2,1,0:T(8,128)S(1)}, u32[]{:S(2)}, u32[]{:S(2)}) collective-permute-start(f32[2,2,128,128]{3,2,1,0:T(8,128)S(1)} %get-tuple-element.138), channel_id=1, source_target_pairs={{4,0},{8,4},{12,8},{5,1},{9,5},{13,9},{6,2},{10,6},{14,10},{7,3},{... | collective-permute-start | bytes 786440 | tf_op jit(solution)/shard_map/ppermute | solution.py:615
  110.2 33.4 %collective-permute-start.25 = (f32[2048,128]{1,0:T(8,128)S(1)}, f32[2048,128]{1,0:T(8,128)S(1)}, u32[]{:S(2)}, u32[]{:S(2)}) collective-permute-start(f32[2048,128]{1,0:T(8,128)S(1)} %slice.16), channel_id=1, source_target_pairs={{0,2},{2,0},{1,3},{3,1},{4,6},{6,4},{5,7},{7,5},{8,10},{10,8},{9,1... | collective-permute-start | bytes 3145736 | tf_op jit(solution)/shard_map/ppermute | solution.py:510
  118.7 10.2 %collective-permute-start.28 = (f32[2,2,128,128]{3,2,1,0:T(8,128)S(1)}, f32[2,2,128,128]{3,2,1,0:T(8,128)S(1)}, u32[]{:S(2)}, u32[]{:S(2)}) collective-permute-start(f32[2,2,128,128]{3,2,1,0:T(8,128)S(1)} %get-tuple-element.141), channel_id=1, source_target_pairs={{4,0},{8,4},{12,8},{5,1},{9,5},{13,9},{6,2},{10,6},{14,10},{7,3},{... | collective-permute-start | bytes 786440 | tf_op jit(solution)/shard_map/ppermute | solution.py:615
  129.8 11.6 %collective-permute-start.30 = (f32[2,2,128,128]{3,2,1,0:T(8,128)S(1)}, f32[2,2,128,128]{3,2,1,0:T(8,128)S(1)}, u32[]{:S(2)}, u32[]{:S(2)}) collective-permute-start(f32[2,2,128,128]{3,2,1,0:T(8,128)S(1)} %get-tuple-element.143), channel_id=1, source_target_pairs={{4,0},{8,4},{5,1},{9,5},{6,2},{10,6},{7,3},{11,7},{20,16},{24,20},... | collective-permute-start | bytes 786440 | tf_op jit(solution)/shard_map/ppermute | solution.py:615
  142.4 8.3 %collective-permute-start.31 = (f32[2,2,128,128]{3,2,1,0:T(8,128)S(1)}, f32[2,2,128,128]{3,2,1,0:T(8,128)S(1)}, u32[]{:S(2)}, u32[]{:S(2)}) collective-permute-start(f32[2,2,128,128]{3,2,1,0:T(8,128)S(1)} %get-tuple-element.146), channel_id=1, source_target_pairs={{4,0},{5,1},{6,2},{7,3},{20,16},{21,17},{22,18},{23,19}} | collective-permute-start | bytes 786440 | tf_op jit(solution)/shard_map/ppermute | solution.py:615
  150.6 32.8 %collective-permute-start.33 = (f32[2,2,1,6,192,128]{5,4,3,2,1,0:T(8,128)}, f32[2,2,1,6,192,128]{5,4,3,2,1,0:T(8,128)}, u32[]{:S(2)}, u32[]{:S(2)}) collective-permute-start(f32[2,2,1,6,192,128]{5,4,3,2,1,0:T(8,128)} %take_rows.6), channel_id=1, source_target_pairs={{0,1},{1,0},{2,3},{3,2},{4,5},{5,4},{6,7},{7,6},{8,9},{9,8},{10,11... | collective-permute-start | bytes 7077896 | tf_op jit(solution)/shard_map/ppermute | solution.py:510
  152.2 7.2 %copy-start = (f32[42368,128]{1,0:T(8,128)}, f32[42368,128]{1,0:T(8,128)S(1)}, u32[]{:S(2)}) copy-start(f32[42368,128]{1,0:T(8,128)S(1)} %get-tuple-element.149.refs_1_) | copy-start | bytes 65077252
  159.5 8.8 %collective-permute-start.32 = (f32[1024,128]{1,0:T(8,128)S(1)}, f32[1024,128]{1,0:T(8,128)S(1)}, u32[]{:S(2)}, u32[]{:S(2)}) collective-permute-start(f32[1024,128]{1,0:T(8,128)S(1)} %get-tuple-element.148), channel_id=1, source_target_pairs={{0,1},{1,0},{2,3},{3,2},{4,5},{5,4},{6,7},{7,6},{8,9},{9,8},{10,11... | collective-permute-start | bytes 1572872 | tf_op jit(solution)/shard_map/ppermute | solution.py:510
  160.0 7.2 %copy-start.1 = (f32[42368,128]{1,0:T(8,128)S(1)}, f32[42368,128]{1,0:T(8,128)}, u32[]{:S(2)}) copy-start(f32[42368,128]{1,0:T(8,128)} %copy-done) | copy-start | bytes 65077252
  168.9 7.2 %copy-start.2 = (f32[42368,128]{1,0:T(8,128)}, f32[42368,128]{1,0:T(8,128)S(1)}, u32[]{:S(2)}) copy-start(f32[42368,128]{1,0:T(8,128)S(1)} %deposit_patches.25.state) | copy-start | bytes 65077252
  176.1 7.2 %copy-start.3 = (f32[42368,128]{1,0:T(8,128)S(1)}, f32[42368,128]{1,0:T(8,128)}, u32[]{:S(2)}) copy-start(f32[42368,128]{1,0:T(8,128)} %copy-done.2) | copy-start | bytes 65077252

commit v3 on v2

--- a/solution.py
+++ b/solution.py
@@ -338,11 +338,11 @@
     )
 
 
-def run_backward(lay, tick, sections, tables, state, arrived, own, copied=False):
+def run_backward(lay, tick, sections, tables, state, arrived, own):
     def body(tables, *refs):
         arrived_ref = refs[0] if arrived is not None else None
         own_ref = refs[1 if arrived is not None else 0] if own is not None else None
-        state, leave = refs[-3:-1] if copied else refs[-2:]
+        state, leave = refs[-2:]
         section = lax.axis_index("depth")
         group = tick - (2 * (sections - 1) - section)
         final = (section == sections - 1).astype(jnp.int32)
@@ -367,9 +367,6 @@
                     real, imag = times_conj(chi[i], pair(state, functools.partial(lay.seen, group, i, layer)))
                     state[lay.grad(group, i, layer, 0), :] = real
                     state[lay.grad(group, i, layer, 1), :] = imag
-                    if copied:
-                        refs[-1][lay.patch(0, i, layer, 0), :] = real
-                        refs[-1][lay.patch(0, i, layer, 1), :] = imag
                     wave.append(times_conj(chi[i], pair(state, functools.partial(lay.patch, group, i, layer))))
             for i in range(lay.count):
                 leave[i, 0] = wave[i][0]
@@ -381,7 +378,7 @@
         body,
         state,
         [("vmem", tables), *waves],
-        [(lay.count, 2, lay.pixels, lay.pixels)] + [(lay.stack // lay.groups, lay.pixels)] * copied,
+        [(lay.count, 2, lay.pixels, lay.pixels)],
         name="backward_section",
         **section_cost(lay),
     )
@@ -428,7 +425,7 @@
                 add(
                     first * lay.count + i,
                     whose,
-                    (lax.axis_index("depth") == 0) | (whose != 2),
+                    True,
                     lambda layer, part: ref[lay.patch(0, i, layer, part), :],
                 )
                 return 0
@@ -445,65 +442,62 @@
     )[0]
 
 
-def take_rows(lay, state, owners, others):
+def split_rows(lay, state, owners, taken=(0, 8)):
     rows = lay.rows // (2 * owners)
-
-    def body(state, out):
-        core = lax.axis_index("lat")
-        core = 1 - core if others else core
-        for part in range(2):
-            for layer in range(lay.layers):
-                for owner in range(owners):
-                    for block in range(lay.blocks):
-                        start = lay.total(part, layer, block, lay.tall + (2 * owner + core) * rows)
-                        out[part, layer, owner, block] = state[pl.ds(pl.multiple_of(start, 8), rows), :]
-
+    pieces = 4 * owners * lay.layers * lay.blocks
+
+    def body(state, keep, send, rest, sems):
+        lat = lax.axis_index("lat")
+        copies = [pltpu.make_async_copy(state.at[pl.ds(taken[0], taken[1] - taken[0]), :], rest, sems.at[pieces])]
+        for owner in range(owners):
+            for kind, target in ((lat, keep), (1 - lat, send)):
+                for part in range(2):
+                    for layer in range(lay.layers):
+                        for block in range(lay.blocks):
+                            start = lay.total(part, layer, block, lay.tall + (2 * owner + kind) * rows)
+                            copies.append(
+                                pltpu.make_async_copy(
+                                    state.at[pl.ds(pl.multiple_of(start, 8), rows), :],
+                                    target.at[part, layer, owner, :, pl.ds(block * lay.pixels, lay.pixels)],
+                                    sems.at[len(copies) - 1],
+                                )
+                            )
+        for copy in copies:
+            copy.start()
+        for copy in copies:
+            copy.wait()
+
+    half = (2, lay.layers, owners, rows, lay.width)
     return pl.pallas_call(
         body,
         in_specs=[VMEM],
-        out_specs=VMEM,
-        out_shape=pltpu.VMEM((2, lay.layers, owners, lay.blocks, rows, lay.pixels), F32),
+        out_specs=[VMEM, VMEM, HBM],
+        out_shape=[
+            pltpu.VMEM(half, F32),
+            pltpu.VMEM(half, F32),
+            pltpu.HBM((taken[1] - taken[0], lay.pixels), F32),
+        ],
+        scratch_shapes=[pltpu.SemaphoreType.DMA((pieces + 1,))],
         compiler_params=pltpu.CompilerParams(vmem_limit_bytes=SCOPED),
-        cost_estimate=pl.CostEstimate(flops=1000, bytes_accessed=1000, transcendentals=0),
-        name="take_rows",
+        name="split_rows",
     )(in_vmem(state))
 
 
-def put_aside(state, begin, end):
-    def body(state, out, sem):
-        copy = pltpu.make_async_copy(state.at[pl.ds(begin, end - begin), :], out, sem)
-        copy.start()
-        copy.wait()
+def add_up(a, b):
+    each = pl.BlockSpec((1, 1, *a.shape[2:]), lambda i, j: (i, j, 0, 0, 0))
+
+    def body(a, b, out):
+        out[...] = a[...] + b[...]
 
     return pl.pallas_call(
         body,
-        in_specs=[VMEM],
-        out_specs=HBM,
-        out_shape=pltpu.HBM((end - begin, state.shape[1]), F32),
-        scratch_shapes=[pltpu.SemaphoreType.DMA(())],
-        compiler_params=pltpu.CompilerParams(vmem_limit_bytes=SCOPED),
-        cost_estimate=pl.CostEstimate(flops=1000, bytes_accessed=1000, transcendentals=0),
-        name="put_aside",
-    )(in_vmem(state))
-
-
-def add_up(kept, received):
-    _, layers, _, blocks, rows, pixels = kept.shape
-    each = pl.BlockSpec((1, 1, 1, blocks, rows, pixels), lambda i, j: (i, j, 0, 0, 0, 0))
-
-    def body(kept, received, out):
-        for block in range(blocks):
-            out[0, 0, :, pl.ds(block * pixels, pixels)] = kept[0, 0, 0, block] + received[0, 0, 0, block]
-
-    return pl.pallas_call(
-        body,
-        grid=(2, layers),
+        grid=a.shape[:2],
         in_specs=[each, each],
-        out_specs=pl.BlockSpec((1, 1, rows, blocks * pixels), lambda i, j: (i, j, 0, 0)),
-        out_shape=pltpu.HBM((2, layers, rows, blocks * pixels), F32),
+        out_specs=each,
+        out_shape=pltpu.HBM(a.shape, F32),
         compiler_params=pltpu.CompilerParams(vmem_limit_bytes=SCOPED),
         name="add_up",
-    )(kept, received)
+    )(a, b)
 
 
 def swap(shard, axis):
@@ -628,7 +622,6 @@
 
     cuts = {0: (count, upto(3)), 2: (upto(3), upto(5)), 3: (upto(5), probes)}
     last_tick = lay.groups + 2 * fill - 1
-    sent = None
     for tick in range(lay.groups + 2 * fill):
         own = None
         if paired and tick == fill - 1:
@@ -649,8 +642,7 @@
                 pools = [frames, mine, *crossed] if paired else [frames]
                 state, late = place_frames(lay, sections, info, everyone, pools, state)
         if tick >= fill:
-            copied = paired and tick == last_tick
-            state, rising, *rest = run_backward(lay, tick, sections, tables, state, up, own, copied)
+            state, rising = run_backward(lay, tick, sections, tables, state, up, own)
             up = pass_on(rising, tick, -1)
             received = crossing.pop(tick, [])
             for begin, end in parts:
@@ -658,35 +650,24 @@
                     due = min(tick + CROSSING, last_tick - 1)
                     crossing.setdefault(due, []).append((begin, 1, swap(grads_of(state, begin, end), "probe")))
             state = deposit(lay, tick, sections, info, received, state)
-            if paired and tick == last_tick - 1:
-                aside = put_aside(state, *lay.grads_of(early, lay.groups))
-                going = take_rows(lay, state, 1, True)
-                going, aside, up = lax.optimization_barrier((going, aside, up))
-                sent = swap(going, "lat")
-    if paired:
-        last = swap(rest[0], "lat")
-        state = deposit(lay, None, sections, info, [(lay.groups - 1, 2, last)], state)
     if not paired:
-        whole = take_rows(lay, state, owners, False) + swap(take_rows(lay, state, owners, True), "lat")
-        whole = jnp.moveaxis(whole, 3, 4).reshape((2, layers, owners, -1, width))
-        return lax.psum_scatter(whole, "probe", scatter_dimension=2, tiled=False)
-
-    def as_they_are(kept, received, grads, last):
-        return add_up(kept, received)
-
-    def with_partners(kept, received, grads, last):
-        each = grads.shape[0] // (lay.groups - early)
-        last = jnp.where(section == 0, last, grads[-each:])
-        grads = swap(jnp.concatenate([grads[:-each], last]), "probe")
+        keep, send, _ = split_rows(lay, state, owners)
+        return lax.psum_scatter(keep + swap(send, "lat"), "probe", scatter_dimension=2, tiled=False)
+
+    keep, send, late_grads = split_rows(lay, state, 1, lay.grads_of(early, lay.groups))
+
+    def as_they_are(keep, received, grads):
+        return add_up(keep, received)
+
+    def with_partners(keep, received, grads):
         sums = Layout(probes, count, layers, pixels, half, height, width, only_sums=True)
         state = clear_total(sums, None)
-        state = deposit(sums, None, sections, info, [(early, 1, grads)], state)
-        kept = kept + take_rows(sums, state, 1, False)
-        return add_up(kept, received + swap(take_rows(sums, state, 1, True), "lat"))
-
-    section = lax.axis_index("depth")
-    kept = take_rows(lay, state, 1, False)
-    return lax.cond(late[0, 0] > 0, with_partners, as_they_are, kept, sent, aside, rest[0])
+        state = deposit(sums, None, sections, info, [(early, 1, swap(grads, "probe"))], state)
+        more, send, _ = split_rows(sums, state, 1)
+        return add_up(keep + more, received + swap(send, "lat"))
+
+    result = lax.cond(late[0, 0] > 0, with_partners, as_they_are, keep, swap(send, "lat"), late_grads)
+    return result[:, :, 0]
 
 
 def solution(mesh):

time: 188 us -> 162 us (0.86)
  local copies, waits for them, and re-layouts: 29.6 us -> 0.8 us
  waiting for transfers between devices: 49.2 us -> 53.9 us
  Pallas kernels: 48.8 us -> 44.9 us
  starting transfers between devices: 59 us -> 61.4 us
    unnamed x16 -> x8, local copies, waits for them, and re-layouts: 29.5 us -> 0.66 us
    ppermute x9 -> x8, waiting for transfers between devices: 5.77 us -> 9.75 us  [swap(): return lax.ppermute(shard, axis, [(0, 1), (1, 0)])]
    pallas_call x4 -> x2, Pallas kernels: 7.05 us -> 3.81 us  [the longest x1 1.94 us: add_up(): pl.pallas_call(body, grid=a.shape[:2], in_specs=[each, each], out_specs=e...]
    pallas_call x40 -> x39, Pallas kernels: 37.8 us -> 37.1 us  [call(): pl.pallas_call(kernel, in_specs=specs, out_specs=[VMEM] * (1 + len(outs)...]
    ppermute x9 -> x8, starting transfers between devices: 7.74 us -> 8.35 us  [swap(): return lax.ppermute(shard, axis, [(0, 1), (1, 0)])]
  transfers between devices with their start and end apart: 32 -> 31, of which waited for: 19 -> 19; matrix products, arithmetic and copies ran while one was open for 0% -> 0% of each run, Pallas kernels for 23% -> 23%
where the time goes in v3:
time: 162 us
  starting transfers between devices  61.4 us (38%)
  waiting for transfers between devices  53.9 us (33%)
  Pallas kernels  44.9 us (28%)
    ppermute x20, starting transfers between devices, pass_on(): return lax.ppermute(wave, 'depth', pairs) if pairs else None  50.9 us
    ppermute x20, waiting for transfers between devices, pass_on(): return lax.ppermute(wave, 'depth', pairs) if pairs else None  44.2 us
    pallas_call x39, Pallas kernels, call(): pl.pallas_call(kernel, in_specs=specs, out_specs=[VMEM] * (1 + len(outs)...  37.1 us
    ppermute x8, waiting for transfers between devices, swap(): return lax.ppermute(shard, axis, [(0, 1), (1, 0)])  9.75 us
    ppermute x8, starting transfers between devices, swap(): return lax.ppermute(shard, axis, [(0, 1), (1, 0)])  8.35 us
  transfers between devices with their start and end apart: 31, of which 19 were waited for; matrix products, arithmetic and copies ran while one was open for 0% of the time, Pallas kernels for 23%

profile of v3, /device:TPU:0, one launch (start us, length us, event | category | flops | bytes accessed | tf_op | source)
XLA Modules:
  0.0 161.7 jit_solution(12744068883835387199)
XLA Ops:
  1.7 2.7 %collective-permute-start.2 = (s32[16]{0:T(128)}, s32[16]{0:T(128)S(1)}, u32[]{:S(2)}, u32[]{:S(2)}) collective-permute-start(s32[16]{0:T(128)} %bitcast.14), channel_id=1, source_target_pairs={{0,2},{2,0},{1,3},{3,1},{4,6},{6,4},{5,7},{7,5},{8,10},{10,8},{9,1... | collective-permute-start | bytes 200 | tf_op jit(solution)/shard_map/ppermute | solution.py:504
  4.4 1.6 %collective-permute-done.2.refs_1_ = s32[16]{0:T(128)S(1)} collective-permute-done((s32[16]{0:T(128)}, s32[16]{0:T(128)S(1)}, u32[]{:S(2)}, u32[]{:S(2)}) %collective-permute-start.2) | collective-permute-done | bytes 96 | tf_op jit(solution)/shard_map/ppermute | solution.py:504
  6.1 1.9 %collective-permute-done.4.refs_3_ = s32[16]{0:T(128)S(1)} collective-permute-done((s32[16]{0:T(128)S(1)}, s32[16]{0:T(128)S(1)}, u32[]{:S(2)}, u32[]{:S(2)}) %collective-permute-start.4) | collective-permute-done | bytes 96 | tf_op jit(solution)/shard_map/ppermute | solution.py:504
  9.3 1.7 %sort_probes.1.refs_0_ = s32[1,128]{1,0:T(1,128)S(1)} custom-call(s32[2,512]{1,0:T(2,128)} %bitcast.20, s32[16]{0:T(128)S(1)} %bitcast.15, s32[16]{0:T(128)S(1)} %collective-permute-done.2.refs_1_, s32[16]{0:T(128)S(1)} %collective-permute-done.3.refs_2_, s32[16]{0:T(128)S(1)} %collective-permute-done.4.refs_3_), custom_call_target="tpu_custom_call" | custom-call | tf_op jit(solution)/shard_map/sort_probes/pallas_call | solution.py:538
  11.0 2.9 %cut_patches.4.refs_2_ = f32[42368,128]{1,0:T(8,128)S(1)} custom-call(s32[1,128]{1,0:T(1,128)S(1)} %sort_probes.1.refs_0_, f32[2,2,384,768]{3,2,1,0:T(8,128)} %x, f32[2,2,384,768]{3,2,1,0:T(8,128)S(1)} %collective-permute-done.5.refs_2_), custom_call_target="tpu_custom_call" | custom-call | flops 1000 | bytes 1000 | tf_op jit(solution)/shard_map/cut_patches/pallas_call | solution.py:157
  14.9 2.6 %collective-permute-start.6 = (f32[2,2,128,128]{3,2,1,0:T(8,128)S(1)}, f32[2,2,128,128]{3,2,1,0:T(8,128)S(1)}, u32[]{:S(2)}, u32[]{:S(2)}) collective-permute-start(f32[2,2,128,128]{3,2,1,0:T(8,128)S(1)} %get-tuple-element.94), channel_id=1, source_target_pairs={{0,4},{1,5},{2,6},{3,7},{16,20},{17,21},{18,22},{19,23}} | collective-permute-start | bytes 786440 | tf_op jit(solution)/shard_map/ppermute | solution.py:609
  17.5 2.3 %bring.1.refs_1_ = f32[2,2,384,768]{3,2,1,0:T(8,128)S(1)} custom-call(f32[2,2,384,768]{3,2,1,0:T(8,128)} %x), custom_call_target="tpu_custom_call" | custom-call | flops 1000 | bytes 1000 | tf_op jit(solution)/shard_map/bring/pallas_call | solution.py:555
  19.9 1.7 %cut_patches.5.refs_0_ = f32[42368,128]{1,0:T(8,128)S(1)} custom-call(s32[1,128]{1,0:T(1,128)S(1)} %sort_probes.1.refs_0_, f32[2,2,384,768]{3,2,1,0:T(8,128)S(1)} %bring.1.refs_1_, f32[2,2,384,768]{3,2,1,0:T(8,128)S(1)} %collective-permute-done.5.refs_2_, f32[42368,128]{1,0:T(8,128)S(1)} %get-tuple-element.96.refs_3_), custom_call_target="tpu_custom_call", output_to_operand_aliasing={{}: (3, {})} | custom-call | flops 1000 | bytes 1000 | tf_op jit(solution)/shard_map/cut_patches/pallas_call | solution.py:157
  23.1 4.4 %collective-permute-start.7 = (f32[2,2,128,128]{3,2,1,0:T(8,128)S(1)}, f32[2,2,128,128]{3,2,1,0:T(8,128)S(1)}, u32[]{:S(2)}, u32[]{:S(2)}) collective-permute-start(f32[2,2,128,128]{3,2,1,0:T(8,128)S(1)} %get-tuple-element.97), channel_id=1, source_target_pairs={{0,4},{4,8},{1,5},{5,9},{2,6},{6,10},{3,7},{7,11},{16,20},{20,24},... | collective-permute-start | bytes 786440 | tf_op jit(solution)/shard_map/ppermute | solution.py:609
  27.5 2.6 %collective-permute-start.9 = (s32[1,128]{1,0:T(1,128)S(1)}, s32[1,128]{1,0:T(1,128)S(1)}, u32[]{:S(2)}, u32[]{:S(2)}) collective-permute-start(s32[1,128]{1,0:T(1,128)S(1)} %sort_probes.1.refs_0_), channel_id=1, source_target_pairs={{0,16},{16,0},{1,17},{17,1},{2,18},{18,2},{3,19},{19,3},{4,20},{20... | collective-permute-start | bytes 1544 | tf_op jit(solution)/shard_map/ppermute | solution.py:504
  33.4 4.1 %collective-permute-start.12 = (f32[2,2,128,128]{3,2,1,0:T(8,128)S(1)}, f32[2,2,128,128]{3,2,1,0:T(8,128)S(1)}, u32[]{:S(2)}, u32[]{:S(2)}) collective-permute-start(f32[2,2,128,128]{3,2,1,0:T(8,128)S(1)} %get-tuple-element.105), channel_id=1, source_target_pairs={{0,4},{4,8},{8,12},{1,5},{5,9},{9,13},{2,6},{6,10},{10,14},{3,7},{... | collective-permute-start | bytes 786440 | tf_op jit(solution)/shard_map/ppermute | solution.py:609
  37.5 1.7 %cut_patches.6.refs_6_ = f32[42368,128]{1,0:T(8,128)S(1)} custom-call(s32[1,128]{1,0:T(1,128)S(1)} %sort_probes.1.refs_0_, f32[2,2,384,768]{3,2,1,0:T(8,128)S(1)} %bring.1.refs_1_, f32[2,2,384,768]{3,2,1,0:T(8,128)S(1)} %collective-permute-done.5.refs_2_, f32[42368,128]{1,0:T(8,128)S(1)} %get-tuple-element.103.refs_3_), custom_call_target="tpu_custom_call", output_to_operand_aliasing={{}: (3, {})} | custom-call | flops 1000 | bytes 1000 | tf_op jit(solution)/shard_map/cut_patches/pallas_call | solution.py:157
  39.9 1.4 collective-permute-done.12.refs_1_
  42.3 4.4 %collective-permute-start.14 = (f32[2,2,128,128]{3,2,1,0:T(8,128)S(1)}, f32[2,2,128,128]{3,2,1,0:T(8,128)S(1)}, u32[]{:S(2)}, u32[]{:S(2)}) collective-permute-start(f32[2,2,128,128]{3,2,1,0:T(8,128)S(1)} %get-tuple-element.107.refs_1_), channel_id=1, source_target_pairs={{0,4},{4,8},{8,12},{1,5},{5,9},{9,13},{2,6},{6,10},{10,14},{3,7},{... | collective-permute-start | bytes 786440 | tf_op jit(solution)/shard_map/ppermute | solution.py:609
  46.7 2.5 %cut_patches.7.refs_2_ = f32[42368,128]{1,0:T(8,128)S(1)} custom-call(s32[1,128]{1,0:T(1,128)S(1)} %sort_probes.1.refs_0_, f32[2,2,384,768]{3,2,1,0:T(8,128)S(1)} %bring.1.refs_1_, f32[2,2,384,768]{3,2,1,0:T(8,128)S(1)} %collective-permute-done.5.refs_2_, f32[42368,128]{1,0:T(8,128)S(1)} %get-tuple-element.108.refs_3_), custom_call_target="tpu_custom_call", output_to_operand_aliasing={{}: (3, {})} | custom-call | flops 1000 | bytes 1000 | tf_op jit(solution)/shard_map/cut_patches/pallas_call | solution.py:157
  51.5 8.4 %collective-permute-start.16 = (f32[2,2,128,128]{3,2,1,0:T(8,128)S(1)}, f32[2,2,128,128]{3,2,1,0:T(8,128)S(1)}, u32[]{:S(2)}, u32[]{:S(2)}) collective-permute-start(f32[2,2,128,128]{3,2,1,0:T(8,128)S(1)} %get-tuple-element.111.refs_2_), channel_id=1, source_target_pairs={{0,4},{4,8},{8,12},{1,5},{5,9},{9,13},{2,6},{6,10},{10,14},{3,7},{... | collective-permute-start | bytes 786440 | tf_op jit(solution)/shard_map/ppermute | solution.py:609
  60.9 3.5 %collective-permute-done.16.refs_1_ = f32[2,2,128,128]{3,2,1,0:T(8,128)S(1)} collective-permute-done((f32[2,2,128,128]{3,2,1,0:T(8,128)S(1)}, f32[2,2,128,128]{3,2,1,0:T(8,128)S(1)}, u32[]{:S(2)}, u32[]{:S(2)}) %collective-permute-start.16) | collective-permute-done | bytes 262176 | tf_op jit(solution)/shard_map/ppermute | solution.py:609
  65.4 4.4 %collective-permute-start.18 = (f32[2,2,128,128]{3,2,1,0:T(8,128)S(1)}, f32[2,2,128,128]{3,2,1,0:T(8,128)S(1)}, u32[]{:S(2)}, u32[]{:S(2)}) collective-permute-start(f32[2,2,128,128]{3,2,1,0:T(8,128)S(1)} %get-tuple-element.115.refs_2_), channel_id=1, source_target_pairs={{0,4},{4,8},{8,12},{1,5},{5,9},{9,13},{2,6},{6,10},{10,14},{3,7},{... | collective-permute-start | bytes 786440 | tf_op jit(solution)/shard_map/ppermute | solution.py:609
  70.0 1.3 collective-permute-start.17
  71.6 2.0 %collective-permute-done.18.refs_1_ = f32[2,2,128,128]{3,2,1,0:T(8,128)S(1)} collective-permute-done((f32[2,2,128,128]{3,2,1,0:T(8,128)S(1)}, f32[2,2,128,128]{3,2,1,0:T(8,128)S(1)}, u32[]{:S(2)}, u32[]{:S(2)}) %collective-permute-start.18) | collective-permute-done | bytes 262176 | tf_op jit(solution)/shard_map/ppermute | solution.py:609
  74.6 5.0 %collective-permute-start.20 = (f32[2,2,128,128]{3,2,1,0:T(8,128)S(1)}, f32[2,2,128,128]{3,2,1,0:T(8,128)S(1)}, u32[]{:S(2)}, u32[]{:S(2)}) collective-permute-start(f32[2,2,128,128]{3,2,1,0:T(8,128)S(1)} %get-tuple-element.119.refs_2_), channel_id=1, source_target_pairs={{0,4},{4,8},{8,12},{1,5},{5,9},{9,13},{2,6},{6,10},{10,14},{3,7},{... | collective-permute-start | bytes 786440 | tf_op jit(solution)/shard_map/ppermute | solution.py:609
  80.8 1.3 collective-permute-start.19
  82.1 1.1 deposit_patches.16.refs_3_
  84.3 4.6 %collective-permute-start.22 = (f32[2,2,128,128]{3,2,1,0:T(8,128)S(1)}, f32[2,2,128,128]{3,2,1,0:T(8,128)S(1)}, u32[]{:S(2)}, u32[]{:S(2)}) collective-permute-start(f32[2,2,128,128]{3,2,1,0:T(8,128)S(1)} %get-tuple-element.123.refs_2_), channel_id=1, source_target_pairs={{0,4},{4,8},{8,12},{1,5},{5,9},{9,13},{2,6},{6,10},{10,14},{3,7},{... | collective-permute-start | bytes 786440 | tf_op jit(solution)/shard_map/ppermute | solution.py:609
  90.2 1.3 collective-permute-start.21
  92.2 1.1 deposit_patches.17.refs_2_
  93.9 4.5 %collective-permute-done.21.refs_1_ = f32[2,2,128,128]{3,2,1,0:T(8,128)S(1)} collective-permute-done((f32[2,2,128,128]{3,2,1,0:T(8,128)S(1)}, f32[2,2,128,128]{3,2,1,0:T(8,128)S(1)}, u32[]{:S(2)}, u32[]{:S(2)}) %collective-permute-start.21) | collective-permute-done | bytes 262176 | tf_op jit(solution)/shard_map/ppermute | solution.py:609
  99.4 1.3 collective-permute-start.23
  100.7 1.1 deposit_patches.18.refs_2_
  102.5 5.5 %collective-permute-done.23.refs_1_ = f32[2,2,128,128]{3,2,1,0:T(8,128)S(1)} collective-permute-done((f32[2,2,128,128]{3,2,1,0:T(8,128)S(1)}, f32[2,2,128,128]{3,2,1,0:T(8,128)S(1)}, u32[]{:S(2)}, u32[]{:S(2)}) %collective-permute-start.23) | collective-permute-done | bytes 262176 | tf_op jit(solution)/shard_map/ppermute | solution.py:609
  108.9 1.3 collective-permute-start.25
  110.2 1.6 collective-permute-start.31
  112.9 4.9 %collective-permute-done.25.refs_1_ = f32[2,2,128,128]{3,2,1,0:T(8,128)S(1)} collective-permute-done((f32[2,2,128,128]{3,2,1,0:T(8,128)S(1)}, f32[2,2,128,128]{3,2,1,0:T(8,128)S(1)}, u32[]{:S(2)}, u32[]{:S(2)}) %collective-permute-start.25) | collective-permute-done | bytes 262176 | tf_op jit(solution)/shard_map/ppermute | solution.py:609
  118.7 1.3 collective-permute-start.27
  120.0 2.3 %deposit_patches.20.refs_2_ = f32[42368,128]{1,0:T(8,128)S(1)} custom-call(s32[1,128]{1,0:T(1,128)S(1)} %sort_probes.1.refs_0_, f32[2048,128]{1,0:T(8,128)S(1)} %collective-permute-done.28.refs_1_, f32[42368,128]{1,0:T(8,128)S(1)} %get-tuple-element.138.refs_2_), custom_call_target="tpu_custom_call", output_to_operand_aliasing={{}: (2, {})} | custom-call | flops 1000 | bytes 1000 | tf_op jit(solution)/shard_map/deposit_patches/pallas_call | solution.py:157
  122.3 6.6 %collective-permute-done.27.refs_1_ = f32[2,2,128,128]{3,2,1,0:T(8,128)S(1)} collective-permute-done((f32[2,2,128,128]{3,2,1,0:T(8,128)S(1)}, f32[2,2,128,128]{3,2,1,0:T(8,128)S(1)}, u32[]{:S(2)}, u32[]{:S(2)}) %collective-permute-start.27) | collective-permute-done | bytes 262176 | tf_op jit(solution)/shard_map/ppermute | solution.py:609
  129.8 1.3 collective-permute-start.29
  131.1 1.1 deposit_patches.21.refs_2_
  132.2 9.2 %collective-permute-done.29.refs_1_ = f32[2,2,128,128]{3,2,1,0:T(8,128)S(1)} collective-permute-done((f32[2,2,128,128]{3,2,1,0:T(8,128)S(1)}, f32[2,2,128,128]{3,2,1,0:T(8,128)S(1)}, u32[]{:S(2)}, u32[]{:S(2)}) %collective-permute-start.29) | collective-permute-done | bytes 262176 | tf_op jit(solution)/shard_map/ppermute | solution.py:609
  142.4 1.3 collective-permute-start.30
  143.7 1.8 %deposit_patches.22.refs_2_ = f32[42368,128]{1,0:T(8,128)S(1)} custom-call(s32[1,128]{1,0:T(1,128)S(1)} %sort_probes.1.refs_0_, f32[2048,128]{1,0:T(8,128)S(1)} %collective-permute-done.31.refs_1_, f32[42368,128]{1,0:T(8,128)S(1)} %get-tuple-element.142.refs_2_), custom_call_target="tpu_custom_call", output_to_operand_aliasing={{}: (2, {})} | custom-call | flops 1000 | bytes 1000 | tf_op jit(solution)/shard_map/deposit_patches/pallas_call | solution.py:157
  145.5 5.1 %collective-permute-done.30.refs_1_ = f32[2,2,128,128]{3,2,1,0:T(8,128)S(1)} collective-permute-done((f32[2,2,128,128]{3,2,1,0:T(8,128)S(1)}, f32[2,2,128,128]{3,2,1,0:T(8,128)S(1)}, u32[]{:S(2)}, u32[]{:S(2)}) %collective-permute-start.30) | collective-permute-done | bytes 262176 | tf_op jit(solution)/shard_map/ppermute | solution.py:609
  150.6 1.6 backward_section.21
  152.2 1.1 deposit_patches.23.state
  153.3 1.9 %split_rows.3 = (f32[2,2,1,192,768]{4,3,2,1,0:T(8,128)S(1)}, f32[2,2,1,192,768]{4,3,2,1,0:T(8,128)S(1)}, f32[4096,128]{1,0:T(8,128)}) custom-call(f32[42368,128]{1,0:T(8,128)S(1)} %deposit_patches.23.state), custom_call_target="tpu_custom_call" | custom-call | tf_op jit(solution)/shard_map/split_rows/pallas_call | solution.py:471
  155.3 4.5 %collective-permute-done.32 = f32[2,2,1,192,768]{4,3,2,1,0:T(8,128)S(1)} collective-permute-done((f32[2,2,1,192,768]{4,3,2,1,0:T(8,128)S(1)}, f32[2,2,1,192,768]{4,3,2,1,0:T(8,128)S(1)}, u32[]{:S(2)}, u32[]{:S(2)}) %collective-permute-start.32) | collective-permute-done | bytes 2359328 | tf_op jit(solution)/shard_map/ppermute | solution.py:504
  159.8 1.9 %conditional.1 = (f32[2,2,192,768]{3,2,1,0:T(8,128)}) conditional(s32[]{:T(128)} %bitcast.8, (f32[2,2,1,192,768]{4,3,2,1,0:T(8,128)S(1)}, f32[2,2,1,192,768]{4,3,2,1,0:T(8,128)S(1)}) %tuple.21, (f32[4096,128]{1,0:T(8,128)}, s32[1,128]{1,0:T(1,128)S(1)}, f32[2,2,1,192,768]{4,3,2,1,0:T(8,128)S(1)}, f32[2,2,1,192,768]{4,3,2,1,0:T(8,128)S(1)}) %tuple.22), branch_computations={%region_0.0_spmd, %region_1.0_spmd} | conditional | flops 1181648 | bytes 31983656 | solution.py:669
  159.8 1.9 %add_up.2 = f32[2,2,1,192,768]{4,3,2,1,0:T(8,128)} custom-call(f32[2,2,1,192,768]{4,3,2,1,0:T(8,128)S(1)} %get-tuple-element.21.a, f32[2,2,1,192,768]{4,3,2,1,0:T(8,128)S(1)} %get-tuple-element.22.b), custom_call_target="tpu_custom_call" | custom-call | tf_op jit(solution)/shard_map/cond/branch_0_fun/add_up/pallas_call | solution.py:492
  (68 shorter events, 27.4 us)
Async XLA Ops:
  0.0 14.0 %copy-start = (bf16[2,2,2,256,256]{4,3,2,1,0:T(8,128)(2,1)S(1)}, bf16[2,2,2,256,256]{4,3,2,1,0:T(8,128)(2,1)}, u32[]{:S(2)}) copy-start(bf16[2,2,2,256,256]{4,3,2,1,0:T(8,128)(2,1)} %constant.5.clone.refs_0_) | copy-start | bytes 3145732
  0.0 14.0 %copy-start.1 = (f32[2,128,128]{2,1,0:T(8,128)S(1)}, f32[2,128,128]{2,1,0:T(8,128)}, u32[]{:S(2)}) copy-start(f32[2,128,128]{2,1,0:T(8,128)} %refs_2_.13) | copy-start | bytes 393220
  0.0 1.4 collective-permute-start.3
  1.4 9.6 %collective-permute-start.5 = (f32[2,2,384,768]{3,2,1,0:T(8,128)}, f32[2,2,384,768]{3,2,1,0:T(8,128)S(1)}, u32[]{:S(2)}, u32[]{:S(2)}) collective-permute-start(f32[2,2,384,768]{3,2,1,0:T(8,128)} %x), channel_id=1, source_target_pairs={{0,1},{1,0},{2,3},{3,2},{4,5},{5,4},{6,7},{7,6},{8,9},{9,8},{10,11... | collective-permute-start | bytes 14155784 | tf_op jit(solution)/shard_map/ppermute | solution.py:504
  1.7 4.3 %collective-permute-start.2 = (s32[16]{0:T(128)}, s32[16]{0:T(128)S(1)}, u32[]{:S(2)}, u32[]{:S(2)}) collective-permute-start(s32[16]{0:T(128)} %bitcast.14), channel_id=1, source_target_pairs={{0,2},{2,0},{1,3},{3,1},{4,6},{6,4},{5,7},{7,5},{8,10},{10,8},{9,1... | collective-permute-start | bytes 200 | tf_op jit(solution)/shard_map/ppermute | solution.py:504
  4.4 3.5 %collective-permute-start.4 = (s32[16]{0:T(128)S(1)}, s32[16]{0:T(128)S(1)}, u32[]{:S(2)}, u32[]{:S(2)}) collective-permute-start(s32[16]{0:T(128)S(1)} %collective-permute-done.3.refs_2_), channel_id=1, source_target_pairs={{0,2},{2,0},{1,3},{3,1},{4,6},{6,4},{5,7},{7,5},{8,10},{10,8},{9,1... | collective-permute-start | bytes 200 | tf_op jit(solution)/shard_map/ppermute | solution.py:504
  7.9 23.7 %collective-permute-start.8 = (f32[16,1,128,128]{3,2,1,0:T(8,128)}, f32[16,1,128,128]{3,2,1,0:T(8,128)S(1)}, u32[]{:S(2)}, u32[]{:S(2)}) collective-permute-start(f32[16,1,128,128]{3,2,1,0:T(8,128)} %param.12), channel_id=1, source_target_pairs={{12,14},{14,12},{13,15},{15,13},{28,30},{30,28},{29,31},{31,29}} | collective-permute-start | bytes 3145736 | tf_op jit(solution)/shard_map/ppermute | solution.py:590
  8.7 0.7 copy-start.2
  14.9 7.3 %collective-permute-start.6 = (f32[2,2,128,128]{3,2,1,0:T(8,128)S(1)}, f32[2,2,128,128]{3,2,1,0:T(8,128)S(1)}, u32[]{:S(2)}, u32[]{:S(2)}) collective-permute-start(f32[2,2,128,128]{3,2,1,0:T(8,128)S(1)} %get-tuple-element.94), channel_id=1, source_target_pairs={{0,4},{1,5},{2,6},{3,7},{16,20},{17,21},{18,22},{19,23}} | collective-permute-start | bytes 786440 | tf_op jit(solution)/shard_map/ppermute | solution.py:609
  22.1 8.1 %copy-start.3 = (f32[16,1,128,128]{3,2,1,0:T(8,128)S(1)}, f32[16,1,128,128]{3,2,1,0:T(8,128)}, u32[]{:S(2)}) copy-start(f32[16,1,128,128]{3,2,1,0:T(8,128)} %param.12) | copy-start | bytes 3145732
  23.1 8.6 %collective-permute-start.7 = (f32[2,2,128,128]{3,2,1,0:T(8,128)S(1)}, f32[2,2,128,128]{3,2,1,0:T(8,128)S(1)}, u32[]{:S(2)}, u32[]{:S(2)}) collective-permute-start(f32[2,2,128,128]{3,2,1,0:T(8,128)S(1)} %get-tuple-element.97), channel_id=1, source_target_pairs={{0,4},{4,8},{1,5},{5,9},{2,6},{6,10},{3,7},{7,11},{16,20},{20,24},... | collective-permute-start | bytes 786440 | tf_op jit(solution)/shard_map/ppermute | solution.py:609
  27.5 4.2 %collective-permute-start.9 = (s32[1,128]{1,0:T(1,128)S(1)}, s32[1,128]{1,0:T(1,128)S(1)}, u32[]{:S(2)}, u32[]{:S(2)}) collective-permute-start(s32[1,128]{1,0:T(1,128)S(1)} %sort_probes.1.refs_0_), channel_id=1, source_target_pairs={{0,16},{16,0},{1,17},{17,1},{2,18},{18,2},{3,19},{19,3},{4,20},{20... | collective-permute-start | bytes 1544 | tf_op jit(solution)/shard_map/ppermute | solution.py:504
  30.2 9.0 %collective-permute-start.10 = (f32[16,1,128,128]{3,2,1,0:T(8,128)S(1)}, f32[16,1,128,128]{3,2,1,0:T(8,128)S(1)}, u32[]{:S(2)}, u32[]{:S(2)}) collective-permute-start(f32[16,1,128,128]{3,2,1,0:T(8,128)S(1)} %copy-done.3), channel_id=1, source_target_pairs={{12,13},{13,12},{14,15},{15,14},{28,29},{29,28},{30,31},{31,30}} | collective-permute-start | bytes 3145736 | tf_op jit(solution)/shard_map/ppermute | solution.py:629
  31.7 7.5 %collective-permute-start.11 = (f32[16,1,128,128]{3,2,1,0:T(8,128)S(1)}, f32[16,1,128,128]{3,2,1,0:T(8,128)S(1)}, u32[]{:S(2)}, u32[]{:S(2)}) collective-permute-start(f32[16,1,128,128]{3,2,1,0:T(8,128)S(1)} %collective-permute-done.8), channel_id=1, source_target_pairs={{12,13},{13,12},{14,15},{15,14},{28,29},{29,28},{30,31},{31,30}} | collective-permute-start | bytes 3145736 | tf_op jit(solution)/shard_map/ppermute | solution.py:629
  33.4 8.0 %collective-permute-start.12 = (f32[2,2,128,128]{3,2,1,0:T(8,128)S(1)}, f32[2,2,128,128]{3,2,1,0:T(8,128)S(1)}, u32[]{:S(2)}, u32[]{:S(2)}) collective-permute-start(f32[2,2,128,128]{3,2,1,0:T(8,128)S(1)} %get-tuple-element.105), channel_id=1, source_target_pairs={{0,4},{4,8},{8,12},{1,5},{5,9},{9,13},{2,6},{6,10},{10,14},{3,7},{... | collective-permute-start | bytes 786440 | tf_op jit(solution)/shard_map/ppermute | solution.py:609
  42.3 8.3 %collective-permute-start.14 = (f32[2,2,128,128]{3,2,1,0:T(8,128)S(1)}, f32[2,2,128,128]{3,2,1,0:T(8,128)S(1)}, u32[]{:S(2)}, u32[]{:S(2)}) collective-permute-start(f32[2,2,128,128]{3,2,1,0:T(8,128)S(1)} %get-tuple-element.107.refs_1_), channel_id=1, source_target_pairs={{0,4},{4,8},{8,12},{1,5},{5,9},{9,13},{2,6},{6,10},{10,14},{3,7},{... | collective-permute-start | bytes 786440 | tf_op jit(solution)/shard_map/ppermute | solution.py:609
  49.2 10.7 %collective-permute-start.13 = (f32[2,2,128,128]{3,2,1,0:T(8,128)S(1)}, f32[2,2,128,128]{3,2,1,0:T(8,128)S(1)}, u32[]{:S(2)}, u32[]{:S(2)}) collective-permute-start(f32[2,2,128,128]{3,2,1,0:T(8,128)S(1)} %get-tuple-element.109), channel_id=1, source_target_pairs={{12,8},{13,9},{14,10},{15,11},{28,24},{29,25},{30,26},{31,27}} | collective-permute-start | bytes 786440 | tf_op jit(solution)/shard_map/ppermute | solution.py:609
  51.5 13.0 %collective-permute-start.16 = (f32[2,2,128,128]{3,2,1,0:T(8,128)S(1)}, f32[2,2,128,128]{3,2,1,0:T(8,128)S(1)}, u32[]{:S(2)}, u32[]{:S(2)}) collective-permute-start(f32[2,2,128,128]{3,2,1,0:T(8,128)S(1)} %get-tuple-element.111.refs_2_), channel_id=1, source_target_pairs={{0,4},{4,8},{8,12},{1,5},{5,9},{9,13},{2,6},{6,10},{10,14},{3,7},{... | collective-permute-start | bytes 786440 | tf_op jit(solution)/shard_map/ppermute | solution.py:609
  60.0 9.8 %collective-permute-start.15 = (f32[2,2,128,128]{3,2,1,0:T(8,128)S(1)}, f32[2,2,128,128]{3,2,1,0:T(8,128)S(1)}, u32[]{:S(2)}, u32[]{:S(2)}) collective-permute-start(f32[2,2,128,128]{3,2,1,0:T(8,128)S(1)} %get-tuple-element.113), channel_id=1, source_target_pairs={{8,4},{12,8},{9,5},{13,9},{10,6},{14,10},{11,7},{15,11},{24,20},{2... | collective-permute-start | bytes 786440 | tf_op jit(solution)/shard_map/ppermute | solution.py:609
  65.4 8.3 %collective-permute-start.18 = (f32[2,2,128,128]{3,2,1,0:T(8,128)S(1)}, f32[2,2,128,128]{3,2,1,0:T(8,128)S(1)}, u32[]{:S(2)}, u32[]{:S(2)}) collective-permute-start(f32[2,2,128,128]{3,2,1,0:T(8,128)S(1)} %get-tuple-element.115.refs_2_), channel_id=1, source_target_pairs={{0,4},{4,8},{8,12},{1,5},{5,9},{9,13},{2,6},{6,10},{10,14},{3,7},{... | collective-permute-start | bytes 786440 | tf_op jit(solution)/shard_map/ppermute | solution.py:609
  70.0 9.9 %collective-permute-start.17 = (f32[2,2,128,128]{3,2,1,0:T(8,128)S(1)}, f32[2,2,128,128]{3,2,1,0:T(8,128)S(1)}, u32[]{:S(2)}, u32[]{:S(2)}) collective-permute-start(f32[2,2,128,128]{3,2,1,0:T(8,128)S(1)} %get-tuple-element.117), channel_id=1, source_target_pairs={{4,0},{8,4},{12,8},{5,1},{9,5},{13,9},{6,2},{10,6},{14,10},{7,3},{... | collective-permute-start | bytes 786440 | tf_op jit(solution)/shard_map/ppermute | solution.py:609
  74.6 8.8 %collective-permute-start.20 = (f32[2,2,128,128]{3,2,1,0:T(8,128)S(1)}, f32[2,2,128,128]{3,2,1,0:T(8,128)S(1)}, u32[]{:S(2)}, u32[]{:S(2)}) collective-permute-start(f32[2,2,128,128]{3,2,1,0:T(8,128)S(1)} %get-tuple-element.119.refs_2_), channel_id=1, source_target_pairs={{0,4},{4,8},{8,12},{1,5},{5,9},{9,13},{2,6},{6,10},{10,14},{3,7},{... | collective-permute-start | bytes 786440 | tf_op jit(solution)/shard_map/ppermute | solution.py:609
  80.8 8.5 %collective-permute-start.19 = (f32[2,2,128,128]{3,2,1,0:T(8,128)S(1)}, f32[2,2,128,128]{3,2,1,0:T(8,128)S(1)}, u32[]{:S(2)}, u32[]{:S(2)}) collective-permute-start(f32[2,2,128,128]{3,2,1,0:T(8,128)S(1)} %get-tuple-element.121), channel_id=1, source_target_pairs={{4,0},{8,4},{12,8},{5,1},{9,5},{13,9},{6,2},{10,6},{14,10},{7,3},{... | collective-permute-start | bytes 786440 | tf_op jit(solution)/shard_map/ppermute | solution.py:609
  84.3 8.9 %collective-permute-start.22 = (f32[2,2,128,128]{3,2,1,0:T(8,128)S(1)}, f32[2,2,128,128]{3,2,1,0:T(8,128)S(1)}, u32[]{:S(2)}, u32[]{:S(2)}) collective-permute-start(f32[2,2,128,128]{3,2,1,0:T(8,128)S(1)} %get-tuple-element.123.refs_2_), channel_id=1, source_target_pairs={{0,4},{4,8},{8,12},{1,5},{5,9},{9,13},{2,6},{6,10},{10,14},{3,7},{... | collective-permute-start | bytes 786440 | tf_op jit(solution)/shard_map/ppermute | solution.py:609
  90.2 8.3 %collective-permute-start.21 = (f32[2,2,128,128]{3,2,1,0:T(8,128)S(1)}, f32[2,2,128,128]{3,2,1,0:T(8,128)S(1)}, u32[]{:S(2)}, u32[]{:S(2)}) collective-permute-start(f32[2,2,128,128]{3,2,1,0:T(8,128)S(1)} %get-tuple-element.125), channel_id=1, source_target_pairs={{4,0},{8,4},{12,8},{5,1},{9,5},{13,9},{6,2},{10,6},{14,10},{7,3},{... | collective-permute-start | bytes 786440 | tf_op jit(solution)/shard_map/ppermute | solution.py:609
  91.6 28.5 %collective-permute-start.28 = (f32[2048,128]{1,0:T(8,128)S(1)}, f32[2048,128]{1,0:T(8,128)S(1)}, u32[]{:S(2)}, u32[]{:S(2)}) collective-permute-start(f32[2048,128]{1,0:T(8,128)S(1)} %slice.10), channel_id=1, source_target_pairs={{0,2},{2,0},{1,3},{3,1},{4,6},{6,4},{5,7},{7,5},{8,10},{10,8},{9,1... | collective-permute-start | bytes 3145736 | tf_op jit(solution)/shard_map/ppermute | solution.py:504
  93.3 8.5 %collective-permute-start.24 = (f32[2,2,128,128]{3,2,1,0:T(8,128)S(1)}, f32[2,2,128,128]{3,2,1,0:T(8,128)S(1)}, u32[]{:S(2)}, u32[]{:S(2)}) collective-permute-start(f32[2,2,128,128]{3,2,1,0:T(8,128)S(1)} %get-tuple-element.127.refs_2_), channel_id=1, source_target_pairs={{4,8},{8,12},{5,9},{9,13},{6,10},{10,14},{7,11},{11,15},{20,24},{2... | collective-permute-start | bytes 786440 | tf_op jit(solution)/shard_map/ppermute | solution.py:609
  99.4 8.6 %collective-permute-start.23 = (f32[2,2,128,128]{3,2,1,0:T(8,128)S(1)}, f32[2,2,128,128]{3,2,1,0:T(8,128)S(1)}, u32[]{:S(2)}, u32[]{:S(2)}) collective-permute-start(f32[2,2,128,128]{3,2,1,0:T(8,128)S(1)} %get-tuple-element.129), channel_id=1, source_target_pairs={{4,0},{8,4},{12,8},{5,1},{9,5},{13,9},{6,2},{10,6},{14,10},{7,3},{... | collective-permute-start | bytes 786440 | tf_op jit(solution)/shard_map/ppermute | solution.py:609
  101.8 11.1 %collective-permute-start.26 = (f32[2,2,128,128]{3,2,1,0:T(8,128)S(1)}, f32[2,2,128,128]{3,2,1,0:T(8,128)S(1)}, u32[]{:S(2)}, u32[]{:S(2)}) collective-permute-start(f32[2,2,128,128]{3,2,1,0:T(8,128)S(1)} %get-tuple-element.131.refs_2_), channel_id=1, source_target_pairs={{8,12},{9,13},{10,14},{11,15},{24,28},{25,29},{26,30},{27,31}} | collective-permute-start | bytes 786440 | tf_op jit(solution)/shard_map/ppermute | solution.py:609
  108.9 9.0 %collective-permute-start.25 = (f32[2,2,128,128]{3,2,1,0:T(8,128)S(1)}, f32[2,2,128,128]{3,2,1,0:T(8,128)S(1)}, u32[]{:S(2)}, u32[]{:S(2)}) collective-permute-start(f32[2,2,128,128]{3,2,1,0:T(8,128)S(1)} %get-tuple-element.133), channel_id=1, source_target_pairs={{4,0},{8,4},{12,8},{5,1},{9,5},{13,9},{6,2},{10,6},{14,10},{7,3},{... | collective-permute-start | bytes 786440 | tf_op jit(solution)/shard_map/ppermute | solution.py:609
  110.2 33.4 %collective-permute-start.31 = (f32[2048,128]{1,0:T(8,128)S(1)}, f32[2048,128]{1,0:T(8,128)S(1)}, u32[]{:S(2)}, u32[]{:S(2)}) collective-permute-start(f32[2048,128]{1,0:T(8,128)S(1)} %slice.11), channel_id=1, source_target_pairs={{0,2},{2,0},{1,3},{3,1},{4,6},{6,4},{5,7},{7,5},{8,10},{10,8},{9,1... | collective-permute-start | bytes 3145736 | tf_op jit(solution)/shard_map/ppermute | solution.py:504
  118.7 10.2 %collective-permute-start.27 = (f32[2,2,128,128]{3,2,1,0:T(8,128)S(1)}, f32[2,2,128,128]{3,2,1,0:T(8,128)S(1)}, u32[]{:S(2)}, u32[]{:S(2)}) collective-permute-start(f32[2,2,128,128]{3,2,1,0:T(8,128)S(1)} %get-tuple-element.137), channel_id=1, source_target_pairs={{4,0},{8,4},{12,8},{5,1},{9,5},{13,9},{6,2},{10,6},{14,10},{7,3},{... | collective-permute-start | bytes 786440 | tf_op jit(solution)/shard_map/ppermute | solution.py:609
  129.8 11.6 %collective-permute-start.29 = (f32[2,2,128,128]{3,2,1,0:T(8,128)S(1)}, f32[2,2,128,128]{3,2,1,0:T(8,128)S(1)}, u32[]{:S(2)}, u32[]{:S(2)}) collective-permute-start(f32[2,2,128,128]{3,2,1,0:T(8,128)S(1)} %get-tuple-element.139), channel_id=1, source_target_pairs={{4,0},{8,4},{5,1},{9,5},{6,2},{10,6},{7,3},{11,7},{20,16},{24,20},... | collective-permute-start | bytes 786440 | tf_op jit(solution)/shard_map/ppermute | solution.py:609
  142.4 8.3 %collective-permute-start.30 = (f32[2,2,128,128]{3,2,1,0:T(8,128)S(1)}, f32[2,2,128,128]{3,2,1,0:T(8,128)S(1)}, u32[]{:S(2)}, u32[]{:S(2)}) collective-permute-start(f32[2,2,128,128]{3,2,1,0:T(8,128)S(1)} %get-tuple-element.141), channel_id=1, source_target_pairs={{4,0},{5,1},{6,2},{7,3},{20,16},{21,17},{22,18},{23,19}} | collective-permute-start | bytes 786440 | tf_op jit(solution)/shard_map/ppermute | solution.py:609
  155.2 4.6 %collective-permute-start.32 = (f32[2,2,1,192,768]{4,3,2,1,0:T(8,128)S(1)}, f32[2,2,1,192,768]{4,3,2,1,0:T(8,128)S(1)}, u32[]{:S(2)}, u32[]{:S(2)}) collective-permute-start(f32[2,2,1,192,768]{4,3,2,1,0:T(8,128)S(1)} %get-tuple-element.145), channel_id=1, source_target_pairs={{0,1},{1,0},{2,3},{3,2},{4,5},{5,4},{6,7},{7,6},{8,9},{9,8},{10,11... | collective-permute-start | bytes 7077896 | tf_op jit(solution)/shard_map/ppermute | solution.py:504

commit v4 on v3

--- a/solution.py
+++ b/solution.py
@@ -78,6 +78,11 @@
 
 def times_conj(a, b):
     return a[0] * b[0] + a[1] * b[1], a[1] * b[0] - a[0] * b[1]
+
+
+def chosen(info):
+    near, far = info
+    return jnp.where(lax.axis_index("depth") == lax.axis_size("depth") - 1, far[...], near[...])
 
 
 class Layout:
@@ -131,8 +136,9 @@
         return key >> (self.column_bits + self.name_bits)
 
     def window(self, info, probe, whose=0):
+        info = chosen(info)
         lane = lax.broadcasted_iota(jnp.int32, info.shape, 1)
-        key = jnp.sum(jnp.where(lane == probe + whose * self.probes, info[...], 0))
+        key = jnp.sum(jnp.where(lane == probe + whose * self.probes, info, 0))
         row = self.row(key)
         column = (key >> self.name_bits) & ((1 << self.column_bits) - 1)
         row0 = jnp.minimum(row // 8 * 8, self.height - self.tall)
@@ -230,7 +236,8 @@
     half = own.shape[2]
     tall, pixels = lay.tall, lay.pixels
 
-    def one(probe, info, own, other, state, window, sem):
+    def one(probe, near, far, own, other, state, window, sem):
+        info = near, far
         row0, down, block, shift = lay.window(info, probe)
         own_top = lax.axis_index("lat") == 0
         near_at = pl.ds(pl.multiple_of(block * pixels, pixels), pixels)
@@ -265,16 +272,16 @@
                 patch = pltpu.roll(patch, (tall - down) % tall, 0)[:pixels]
                 state[lay.patch(0, probe, layer, part), :] = patch
 
-    def body(info, *refs):
+    def body(*refs):
         section = lax.axis_index("depth")
         bounds = [x(section) if callable(x) else x for x in (begin, end)]
-        lax.fori_loop(*bounds, lambda probe, _: one(probe, info, *refs) or 0, 0)
+        lax.fori_loop(*bounds, lambda probe, _: one(probe, *refs) or 0, 0)
 
     return call(
         lay,
         body,
         state,
-        [("vmem", info), ("hbm" if from_hbm else "vmem", own), ("vmem", other)],
+        [*(("vmem", x) for x in info), ("hbm" if from_hbm else "vmem", own), ("vmem", other)],
         [],
         scratch=[pltpu.VMEM((2, lay.layers, 2 * tall, 2 * pixels), F32), pltpu.SemaphoreType.DMA(())],
         name="cut_patches",
@@ -387,7 +394,8 @@
 def deposit(lay, tick, sections, info, received, state):
     pixels, tall = lay.pixels, lay.tall
 
-    def body(info, *refs):
+    def body(near, far, *refs):
+        info = near, far
         state = refs[-1]
         lane = lax.broadcasted_iota(jnp.int32, (tall, pixels), 1)
         blank = jnp.zeros((8, pixels), F32)
@@ -436,7 +444,7 @@
         lay,
         body,
         state,
-        [("vmem", info)] + [("vmem", grads) for *_, grads in received],
+        [("vmem", x) for x in info] + [("vmem", grads) for *_, grads in received],
         [],
         name="deposit_patches",
     )[0]
@@ -583,19 +591,19 @@
         beside = swap(scan, "lat")
         half_rows, beside = lax.optimization_barrier((specimen, beside))
         other = swap(half_rows, "lat")
-        indices = [scan, swap(scan, "probe"), beside, swap(beside, "probe")]
-        measured, *indices[1:] = lax.optimization_barrier((frames, *indices[1:]))
         end = sections - 1
         ends = [(2 * end, 2 * end + 1), (2 * end + 1, 2 * end)]
-        mine = lax.ppermute(measured, ("depth", "probe"), ends)
+        mine = lax.ppermute(frames, ("depth", "probe"), ends)
+        above = [(i, i ^ 1) for i in range(2 * end)]
+        cross_above = lambda x: lax.ppermute(x, ("depth", "probe"), above)
+        indices = [scan, cross_above(scan), beside, cross_above(beside)]
         info = sort_probes(lay, early, positions, indices)
-        everyone = swap(info, "groups") if lax.axis_size("groups") == 2 else info
     else:
         other = swap(specimen, "lat")
         corners = positions[scan_index.reshape(-1)]
         info = lay.pack(corners[:, 0], corners[:, 1], jnp.arange(probes, dtype=jnp.int32))
-        info = everyone = jnp.pad(info, (0, 3 * probes))[None]
-    state = cut_patches(lay, info, specimen, other, None, 0, count, from_hbm=True)
+        info = ranking = everyone = far = jnp.pad(info, (0, 3 * probes))[None]
+    state = cut_patches(lay, (info, info), specimen, other, None, 0, count, from_hbm=True)
     def busy(tick, source, by):
         delay = source if by > 0 else 2 * (sections - 1) - source
         return 0 <= tick - delay < lay.groups
@@ -620,17 +628,24 @@
         early_sections = min(group, lay.groups) * count
         return lambda section: jnp.where(section < 2, early_sections, probes)
 
-    cuts = {0: (count, upto(3)), 2: (upto(3), upto(5)), 3: (upto(5), probes)}
+    begin = lambda section: jnp.where(section == fill, 0, count)
+    cuts = {0: (begin, upto(3)), 2: (upto(3), upto(5)), 3: (upto(5), probes)}
     last_tick = lay.groups + 2 * fill - 1
     for tick in range(lay.groups + 2 * fill):
         own = None
         if paired and tick == fill - 1:
-            down, mine, everyone = lax.optimization_barrier((down, mine, everyone))
+            down, mine, near, far = lax.optimization_barrier((down, mine, *info))
+            ranking = jnp.where(lax.axis_index("depth") == fill, far, near)
+            everyone = swap(ranking, "groups") if lax.axis_size("groups") == 2 else ranking
             crossed = [lax.ppermute(x, ("depth", "lat"), ends) for x in (frames, mine)]
         if tick < lay.groups + fill:
             start_wave = illumination if tick < lay.groups else None
             state, own = run_forward(lay, tick, sections, tables, state, down, start_wave)
             if tick == 0:
+                if paired:
+                    own, near = lax.optimization_barrier((own, info))
+                    far = lax.ppermute(near, "depth", [(fill - 1, fill)])
+                info = info, far
                 own, specimen = lax.optimization_barrier((own, specimen))
                 brought = bring(specimen)
             down = pass_on(own, tick, 1)
@@ -640,7 +655,7 @@
                 state = clear_total(lay, state)
             if tick == fill - 1:
                 pools = [frames, mine, *crossed] if paired else [frames]
-                state, late = place_frames(lay, sections, info, everyone, pools, state)
+                state, late = place_frames(lay, sections, ranking, everyone, pools, state)
         if tick >= fill:
             state, rising = run_backward(lay, tick, sections, tables, state, up, own)
             up = pass_on(rising, tick, -1)

time: 162 us -> 207 us (1.28)
  local copies, waits for them, and re-layouts: 0.8 us -> 51.6 us
  waiting for transfers between devices: 53.9 us -> 45.3 us
    unnamed x8 -> x30, local copies, waits for them, and re-layouts: 0.66 us -> 49 us
    ppermute x20, waiting for transfers between devices: 44.2 us -> 36.3 us  [pass_on(): return lax.ppermute(wave, 'depth', pairs) if pairs else None]
    ppermute x1 -> x4, starting transfers between devices: 0.72 us -> 7.9 us  [the longest x2 6.52 us: local(): cross_above = lambda x: lax.ppermute(x, ('depth', 'probe'), above)]
    ppermute x20, starting transfers between devices: 50.9 us -> 45.3 us  [pass_on(): return lax.ppermute(wave, 'depth', pairs) if pairs else None]
    ppermute x8 -> x6, waiting for transfers between devices: 9.75 us -> 5.45 us  [swap(): return lax.ppermute(shard, axis, [(0, 1), (1, 0)])]
    ppermute x1 -> x4, waiting for transfers between devices: 0.01 us -> 3.5 us  [the longest x2 3.5 us: local(): cross_above = lambda x: lax.ppermute(x, ('depth', 'probe'), above)]
    ppermute x8 -> x6, starting transfers between devices: 8.35 us -> 5.47 us  [swap(): return lax.ppermute(shard, axis, [(0, 1), (1, 0)])]
    slice x2, local copies, waits for them, and re-layouts: 0.14 us -> 2.59 us  [grads_of(): return lax.slice_in_dim(state, begin, end)]
  transfers between devices with their start and end apart: 31 -> 32, of which waited for: 19 -> 12; matrix products, arithmetic and copies ran while one was open for 0% -> 1% of each run, Pallas kernels for 23% -> 19%
where the time goes in v4:
time: 207 us; the launch traced here: 205 us
  starting transfers between devices  61.1 us (30%)
  local copies, waits for them, and re-layouts  51.6 us (25%)
  Pallas kernels  46.4 us (22%)
  waiting for transfers between devices  45.3 us (22%)
    unnamed x30, local copies, waits for them, and re-layouts  49 us
    ppermute x20, starting transfers between devices, pass_on(): return lax.ppermute(wave, 'depth', pairs) if pairs else None  45.3 us
    pallas_call x39, Pallas kernels, call(): pl.pallas_call(kernel, in_specs=specs, out_specs=[VMEM] * (1 + len(outs)...  38.6 us
    ppermute x20, waiting for transfers between devices, pass_on(): return lax.ppermute(wave, 'depth', pairs) if pairs else None  36.3 us
    ppermute x2, starting transfers between devices, local(): cross_above = lambda x: lax.ppermute(x, ('depth', 'probe'), above)  6.52 us
    ppermute x6, starting transfers between devices, swap(): return lax.ppermute(shard, axis, [(0, 1), (1, 0)])  5.47 us
    ppermute x6, waiting for transfers between devices, swap(): return lax.ppermute(shard, axis, [(0, 1), (1, 0)])  5.45 us
  transfers between devices with their start and end apart: 32, of which 12 were waited for; matrix products, arithmetic and copies ran while one was open for 1% of the time, Pallas kernels for 19%

profile of v4, /device:TPU:0, one launch (start us, length us, event | category | flops | bytes accessed | tf_op | source)
XLA Modules:
  0.0 205.3 jit_solution(8379469002301582367)
XLA Ops:
  2.4 4.6 %collective-permute-start.2 = (s32[16]{0:T(128)}, s32[16]{0:T(128)S(1)}, u32[]{:S(2)}, u32[]{:S(2)}) collective-permute-start(s32[16]{0:T(128)} %bitcast.15), channel_id=1, source_target_pairs={{0,2},{2,0},{4,6},{6,4},{8,10},{10,8},{1,3},{3,1},{5,7},{7,5},{9,1... | collective-permute-start | bytes 200 | tf_op jit(solution)/shard_map/ppermute | solution.py:598
  7.0 1.9 collective-permute-start.4
  9.0 3.5 %collective-permute-done.4.refs_3_ = s32[16]{0:T(128)S(1)} collective-permute-done((s32[16]{0:T(128)S(1)}, s32[16]{0:T(128)S(1)}, u32[]{:S(2)}, u32[]{:S(2)}) %collective-permute-start.4) | collective-permute-done | bytes 96 | tf_op jit(solution)/shard_map/ppermute | solution.py:598
  13.1 1.7 sort_probes.1.refs_0_.refs_1_
  14.8 3.4 %cut_patches.4.refs_2_ = f32[42368,128]{1,0:T(8,128)S(1)} custom-call(s32[1,128]{1,0:T(1,128)S(1)} %sort_probes.1.refs_0_.refs_1_, s32[1,128]{1,0:T(1,128)S(1)} %sort_probes.1.refs_0_.refs_1_, f32[2,2,384,768]{3,2,1,0:T(8,128)} %x, f32[2,2,384,768]{3,2,1,0:T(8,128)S(1)} %collective-permute-done.5.refs_3_), custom_call_target="tpu_custom_call" | custom-call | flops 1000 | bytes 1000 | tf_op jit(solution)/shard_map/cut_patches/pallas_call | solution.py:163
  19.2 2.6 %collective-permute-start.6 = (f32[2,2,128,128]{3,2,1,0:T(8,128)S(1)}, f32[2,2,128,128]{3,2,1,0:T(8,128)S(1)}, u32[]{:S(2)}, u32[]{:S(2)}) collective-permute-start(f32[2,2,128,128]{3,2,1,0:T(8,128)S(1)} %get-tuple-element.94), channel_id=1, source_target_pairs={{0,4},{1,5},{2,6},{3,7},{16,20},{17,21},{18,22},{19,23}} | collective-permute-start | bytes 786440 | tf_op jit(solution)/shard_map/ppermute | solution.py:617
  22.4 2.3 %bring.1.refs_2_ = f32[2,2,384,768]{3,2,1,0:T(8,128)S(1)} custom-call(f32[2,2,384,768]{3,2,1,0:T(8,128)} %x), custom_call_target="tpu_custom_call" | custom-call | flops 1000 | bytes 1000 | tf_op jit(solution)/shard_map/bring/pallas_call | solution.py:563
  24.8 1.7 cut_patches.5.refs_0_
  28.5 2.5 %collective-permute-start.8 = (f32[2,2,128,128]{3,2,1,0:T(8,128)S(1)}, f32[2,2,128,128]{3,2,1,0:T(8,128)S(1)}, u32[]{:S(2)}, u32[]{:S(2)}) collective-permute-start(f32[2,2,128,128]{3,2,1,0:T(8,128)S(1)} %get-tuple-element.98), channel_id=1, source_target_pairs={{0,4},{4,8},{1,5},{5,9},{2,6},{6,10},{3,7},{7,11},{16,20},{20,24},... | collective-permute-start | bytes 786440 | tf_op jit(solution)/shard_map/ppermute | solution.py:617
  31.7 3.1 %collective-permute-done.8.refs_1_ = f32[2,2,128,128]{3,2,1,0:T(8,128)S(1)} collective-permute-done((f32[2,2,128,128]{3,2,1,0:T(8,128)S(1)}, f32[2,2,128,128]{3,2,1,0:T(8,128)S(1)}, u32[]{:S(2)}, u32[]{:S(2)}) %collective-permute-start.8) | collective-permute-done | bytes 262176 | tf_op jit(solution)/shard_map/ppermute | solution.py:617
  34.8 1.7 collective-permute-start.12
  36.5 1.6 forward_section.13
  38.1 7.2 %copy-done = f32[42368,128]{1,0:T(8,128)} copy-done((f32[42368,128]{1,0:T(8,128)}, f32[42368,128]{1,0:T(8,128)S(1)}, u32[]{:S(2)}) %copy-start) | copy-done | bytes 21692440
  45.3 5.1 %collective-permute-start.13 = (f32[2,2,128,128]{3,2,1,0:T(8,128)}, f32[2,2,128,128]{3,2,1,0:T(8,128)S(1)}, u32[]{:S(2)}, u32[]{:S(2)}) collective-permute-start(f32[2,2,128,128]{3,2,1,0:T(8,128)} %get-tuple-element.106), channel_id=1, source_target_pairs={{0,4},{4,8},{8,12},{1,5},{5,9},{9,13},{2,6},{6,10},{10,14},{3,7},{... | collective-permute-start | bytes 786440 | tf_op jit(solution)/shard_map/ppermute | solution.py:617
  50.5 2.5 %collective-permute-start.10 = (s32[1,128]{1,0:T(1,128)S(1)}, s32[1,128]{1,0:T(1,128)S(1)}, u32[]{:S(2)}, u32[]{:S(2)}) collective-permute-start(s32[1,128]{1,0:T(1,128)S(1)} %broadcast_select_fusion.refs_0_), channel_id=1, source_target_pairs={{0,16},{16,0},{1,17},{17,1},{2,18},{18,2},{3,19},{19,3},{4,20},{20... | collective-permute-start | bytes 1544 | tf_op jit(solution)/shard_map/ppermute | solution.py:512
  53.0 7.2 %copy-done.1 = f32[42368,128]{1,0:T(8,128)S(1)} copy-done((f32[42368,128]{1,0:T(8,128)S(1)}, f32[42368,128]{1,0:T(8,128)}, u32[]{:S(2)}) %copy-start.1) | copy-done | bytes 21692440
  60.1 2.3 %copy-done.8 = f32[2,2,384,768]{3,2,1,0:T(8,128)S(1)} copy-done((f32[2,2,384,768]{3,2,1,0:T(8,128)S(1)}, f32[2,2,384,768]{3,2,1,0:T(8,128)}, u32[]{:S(2)}) %copy-start.8) | copy-done | bytes 4718616
  62.5 2.3 %copy-done.10 = f32[2,2,384,768]{3,2,1,0:T(8,128)S(1)} copy-done((f32[2,2,384,768]{3,2,1,0:T(8,128)S(1)}, f32[2,2,384,768]{3,2,1,0:T(8,128)}, u32[]{:S(2)}) %copy-start.10) | copy-done | bytes 4718616
  64.8 1.7 cut_patches.6.refs_6_
  66.5 1.4 place_frames.1
  68.9 4.5 %collective-permute-start.15 = (f32[2,2,128,128]{3,2,1,0:T(8,128)S(1)}, f32[2,2,128,128]{3,2,1,0:T(8,128)S(1)}, u32[]{:S(2)}, u32[]{:S(2)}) collective-permute-start(f32[2,2,128,128]{3,2,1,0:T(8,128)S(1)} %get-tuple-element.108.refs_1_), channel_id=1, source_target_pairs={{0,4},{4,8},{8,12},{1,5},{5,9},{9,13},{2,6},{6,10},{10,14},{3,7},{... | collective-permute-start | bytes 786440 | tf_op jit(solution)/shard_map/ppermute | solution.py:617
  73.5 2.5 %cut_patches.7.refs_2_ = f32[42368,128]{1,0:T(8,128)S(1)} custom-call(s32[1,128]{1,0:T(1,128)S(1)} %sort_probes.1.refs_0_.refs_1_, s32[1,128]{1,0:T(1,128)S(1)} %collective-permute-done.7.refs_1_, f32[2,2,384,768]{3,2,1,0:T(8,128)S(1)} %bitcast.11, f32[2,2,384,768]{3,2,1,0:T(8,128)S(1)} %copy-done.10, ...), custom_call_target="tpu_custom_call", output_to_operand_aliasing={{}: (4, {})} | custom-call | flops 1000 | bytes 1000 | tf_op jit(solution)/shard_map/cut_patches/pallas_call | solution.py:163
  78.2 4.4 %collective-permute-start.17 = (f32[2,2,128,128]{3,2,1,0:T(8,128)S(1)}, f32[2,2,128,128]{3,2,1,0:T(8,128)S(1)}, u32[]{:S(2)}, u32[]{:S(2)}) collective-permute-start(f32[2,2,128,128]{3,2,1,0:T(8,128)S(1)} %get-tuple-element.112.refs_2_), channel_id=1, source_target_pairs={{0,4},{4,8},{8,12},{1,5},{5,9},{9,13},{2,6},{6,10},{10,14},{3,7},{... | collective-permute-start | bytes 786440 | tf_op jit(solution)/shard_map/ppermute | solution.py:617
  83.7 2.8 %collective-permute-done.17.refs_1_ = f32[2,2,128,128]{3,2,1,0:T(8,128)S(1)} collective-permute-done((f32[2,2,128,128]{3,2,1,0:T(8,128)S(1)}, f32[2,2,128,128]{3,2,1,0:T(8,128)S(1)}, u32[]{:S(2)}, u32[]{:S(2)}) %collective-permute-start.17) | collective-permute-done | bytes 262176 | tf_op jit(solution)/shard_map/ppermute | solution.py:617
  87.4 4.4 %collective-permute-start.19 = (f32[2,2,128,128]{3,2,1,0:T(8,128)S(1)}, f32[2,2,128,128]{3,2,1,0:T(8,128)S(1)}, u32[]{:S(2)}, u32[]{:S(2)}) collective-permute-start(f32[2,2,128,128]{3,2,1,0:T(8,128)S(1)} %get-tuple-element.116.refs_2_), channel_id=1, source_target_pairs={{0,4},{4,8},{8,12},{1,5},{5,9},{9,13},{2,6},{6,10},{10,14},{3,7},{... | collective-permute-start | bytes 786440 | tf_op jit(solution)/shard_map/ppermute | solution.py:617
  92.0 1.3 collective-permute-start.18
  93.6 2.6 %collective-permute-done.19.refs_1_ = f32[2,2,128,128]{3,2,1,0:T(8,128)S(1)} collective-permute-done((f32[2,2,128,128]{3,2,1,0:T(8,128)S(1)}, f32[2,2,128,128]{3,2,1,0:T(8,128)S(1)}, u32[]{:S(2)}, u32[]{:S(2)}) %collective-permute-start.19) | collective-permute-done | bytes 262176 | tf_op jit(solution)/shard_map/ppermute | solution.py:617
  97.2 4.4 %collective-permute-start.21 = (f32[2,2,128,128]{3,2,1,0:T(8,128)S(1)}, f32[2,2,128,128]{3,2,1,0:T(8,128)S(1)}, u32[]{:S(2)}, u32[]{:S(2)}) collective-permute-start(f32[2,2,128,128]{3,2,1,0:T(8,128)S(1)} %get-tuple-element.120.refs_2_), channel_id=1, source_target_pairs={{0,4},{4,8},{8,12},{1,5},{5,9},{9,13},{2,6},{6,10},{10,14},{3,7},{... | collective-permute-start | bytes 786440 | tf_op jit(solution)/shard_map/ppermute | solution.py:617
  104.9 1.9 collective-permute-done.21.refs_1_
  107.8 4.4 %collective-permute-start.23 = (f32[2,2,128,128]{3,2,1,0:T(8,128)S(1)}, f32[2,2,128,128]{3,2,1,0:T(8,128)S(1)}, u32[]{:S(2)}, u32[]{:S(2)}) collective-permute-start(f32[2,2,128,128]{3,2,1,0:T(8,128)S(1)} %get-tuple-element.124.refs_2_), channel_id=1, source_target_pairs={{0,4},{4,8},{8,12},{1,5},{5,9},{9,13},{2,6},{6,10},{10,14},{3,7},{... | collective-permute-start | bytes 786440 | tf_op jit(solution)/shard_map/ppermute | solution.py:617
  113.1 7.2 %copy-done.2 = f32[42368,128]{1,0:T(8,128)} copy-done((f32[42368,128]{1,0:T(8,128)}, f32[42368,128]{1,0:T(8,128)S(1)}, u32[]{:S(2)}) %copy-start.2) | copy-done | bytes 21692440
  121.6 1.3 slice.10
  123.0 7.2 %copy-done.3 = f32[42368,128]{1,0:T(8,128)S(1)} copy-done((f32[42368,128]{1,0:T(8,128)S(1)}, f32[42368,128]{1,0:T(8,128)}, u32[]{:S(2)}) %copy-start.3) | copy-done | bytes 21692440
  136.0 7.9 %collective-permute-done.24.refs_1_ = f32[2,2,128,128]{3,2,1,0:T(8,128)S(1)} collective-permute-done((f32[2,2,128,128]{3,2,1,0:T(8,128)S(1)}, f32[2,2,128,128]{3,2,1,0:T(8,128)S(1)}, u32[]{:S(2)}, u32[]{:S(2)}) %collective-permute-start.24) | collective-permute-done | bytes 262176 | tf_op jit(solution)/shard_map/ppermute | solution.py:617
  144.9 7.2 %copy-done.4 = f32[42368,128]{1,0:T(8,128)} copy-done((f32[42368,128]{1,0:T(8,128)}, f32[42368,128]{1,0:T(8,128)S(1)}, u32[]{:S(2)}) %copy-start.4) | copy-done | bytes 21692440
  153.4 1.3 slice.11
  154.7 2.1 %collective-permute-start.32 = (f32[2048,128]{1,0:T(8,128)S(1)}, f32[2048,128]{1,0:T(8,128)S(1)}, u32[]{:S(2)}, u32[]{:S(2)}) collective-permute-start(f32[2048,128]{1,0:T(8,128)S(1)} %slice.11), channel_id=1, source_target_pairs={{0,2},{2,0},{1,3},{3,1},{4,6},{6,4},{5,7},{7,5},{8,10},{10,8},{9,1... | collective-permute-start | bytes 3145736 | tf_op jit(solution)/shard_map/ppermute | solution.py:512
  156.8 7.2 %copy-done.5 = f32[42368,128]{1,0:T(8,128)S(1)} copy-done((f32[42368,128]{1,0:T(8,128)S(1)}, f32[42368,128]{1,0:T(8,128)}, u32[]{:S(2)}) %copy-start.5) | copy-done | bytes 21692440
  167.3 2.1 %deposit_patches.20.refs_2_ = f32[42368,128]{1,0:T(8,128)S(1)} custom-call(s32[1,128]{1,0:T(1,128)S(1)} %sort_probes.1.refs_0_.refs_1_, s32[1,128]{1,0:T(1,128)S(1)} %collective-permute-done.7.refs_1_, f32[2048,128]{1,0:T(8,128)S(1)} %collective-permute-done.29.refs_2_, f32[42368,128]{1,0:T(8,128)S(1)} %get-tuple-element.139.refs_3_), custom_call_target="tpu_custom_call", output_to_operand_aliasing={{}: (3, {})} | custom-call | flops 1000 | bytes 1000 | tf_op jit(solution)/shard_map/deposit_patches/pallas_call | solution.py:163
  169.4 6.4 %collective-permute-done.28.refs_1_ = f32[2,2,128,128]{3,2,1,0:T(8,128)S(1)} collective-permute-done((f32[2,2,128,128]{3,2,1,0:T(8,128)S(1)}, f32[2,2,128,128]{3,2,1,0:T(8,128)S(1)}, u32[]{:S(2)}, u32[]{:S(2)}) %collective-permute-start.28) | collective-permute-done | bytes 262176 | tf_op jit(solution)/shard_map/ppermute | solution.py:617
  179.1 5.9 %collective-permute-done.30.refs_1_ = f32[2,2,128,128]{3,2,1,0:T(8,128)S(1)} collective-permute-done((f32[2,2,128,128]{3,2,1,0:T(8,128)S(1)}, f32[2,2,128,128]{3,2,1,0:T(8,128)S(1)}, u32[]{:S(2)}, u32[]{:S(2)}) %collective-permute-start.30) | collective-permute-done | bytes 262176 | tf_op jit(solution)/shard_map/ppermute | solution.py:617
  187.2 1.7 deposit_patches.22.refs_2_
  188.9 5.3 %collective-permute-done.31.refs_1_ = f32[2,2,128,128]{3,2,1,0:T(8,128)S(1)} collective-permute-done((f32[2,2,128,128]{3,2,1,0:T(8,128)S(1)}, f32[2,2,128,128]{3,2,1,0:T(8,128)S(1)}, u32[]{:S(2)}, u32[]{:S(2)}) %collective-permute-start.31) | collective-permute-done | bytes 262176 | tf_op jit(solution)/shard_map/ppermute | solution.py:617
  194.2 1.6 backward_section.21
  196.8 1.8 split_rows.3
  198.8 4.5 %collective-permute-done.33 = f32[2,2,1,192,768]{4,3,2,1,0:T(8,128)S(1)} collective-permute-done((f32[2,2,1,192,768]{4,3,2,1,0:T(8,128)S(1)}, f32[2,2,1,192,768]{4,3,2,1,0:T(8,128)S(1)}, u32[]{:S(2)}, u32[]{:S(2)}) %collective-permute-start.33) | collective-permute-done | bytes 2359328 | tf_op jit(solution)/shard_map/ppermute | solution.py:512
  203.3 2.0 conditional.1
  203.3 2.0 add_up.2
  (94 shorter events, 38.1 us)
Async XLA Ops:
  0.0 18.2 %copy-start.6 = (bf16[2,2,2,256,256]{4,3,2,1,0:T(8,128)(2,1)S(1)}, bf16[2,2,2,256,256]{4,3,2,1,0:T(8,128)(2,1)}, u32[]{:S(2)}) copy-start(bf16[2,2,2,256,256]{4,3,2,1,0:T(8,128)(2,1)} %constant.12.clone.refs_0_) | copy-start | bytes 3145732
  0.0 18.2 %copy-start.11 = (f32[2,128,128]{2,1,0:T(8,128)S(1)}, f32[2,128,128]{2,1,0:T(8,128)}, u32[]{:S(2)}) copy-start(f32[2,128,128]{2,1,0:T(8,128)} %refs_2_.15) | copy-start | bytes 393220
  0.0 1.4 collective-permute-start.3
  1.4 13.4 %collective-permute-start.5 = (f32[2,2,384,768]{3,2,1,0:T(8,128)}, f32[2,2,384,768]{3,2,1,0:T(8,128)S(1)}, u32[]{:S(2)}, u32[]{:S(2)}) collective-permute-start(f32[2,2,384,768]{3,2,1,0:T(8,128)} %x), channel_id=1, source_target_pairs={{0,1},{1,0},{2,3},{3,2},{4,5},{5,4},{6,7},{7,6},{8,9},{9,8},{10,11... | collective-permute-start | bytes 14155784 | tf_op jit(solution)/shard_map/ppermute | solution.py:512
  1.7 30.0 %collective-permute-start.9 = (f32[16,1,128,128]{3,2,1,0:T(8,128)}, f32[16,1,128,128]{3,2,1,0:T(8,128)S(1)}, u32[]{:S(2)}, u32[]{:S(2)}) collective-permute-start(f32[16,1,128,128]{3,2,1,0:T(8,128)} %param.12), channel_id=1, source_target_pairs={{12,14},{14,12},{13,15},{15,13},{28,30},{30,28},{29,31},{31,29}} | collective-permute-start | bytes 3145736 | tf_op jit(solution)/shard_map/ppermute | solution.py:596
  2.4 6.5 %collective-permute-start.2 = (s32[16]{0:T(128)}, s32[16]{0:T(128)S(1)}, u32[]{:S(2)}, u32[]{:S(2)}) collective-permute-start(s32[16]{0:T(128)} %bitcast.15), channel_id=1, source_target_pairs={{0,2},{2,0},{4,6},{6,4},{8,10},{10,8},{1,3},{3,1},{5,7},{7,5},{9,1... | collective-permute-start | bytes 200 | tf_op jit(solution)/shard_map/ppermute | solution.py:598
  7.0 5.4 %collective-permute-start.4 = (s32[16]{0:T(128)S(1)}, s32[16]{0:T(128)S(1)}, u32[]{:S(2)}, u32[]{:S(2)}) collective-permute-start(s32[16]{0:T(128)S(1)} %collective-permute-done.3.refs_2_), channel_id=1, source_target_pairs={{0,2},{2,0},{4,6},{6,4},{8,10},{10,8},{1,3},{3,1},{5,7},{7,5},{9,1... | collective-permute-start | bytes 200 | tf_op jit(solution)/shard_map/ppermute | solution.py:598
  12.5 0.7 copy-start.12
  14.8 10.0 %copy-start.9 = (f32[2,2,384,768]{3,2,1,0:T(8,128)}, f32[2,2,384,768]{3,2,1,0:T(8,128)S(1)}, u32[]{:S(2)}) copy-start(f32[2,2,384,768]{3,2,1,0:T(8,128)S(1)} %collective-permute-done.5.refs_3_) | copy-start | bytes 14155780
  19.2 8.4 %collective-permute-start.6 = (f32[2,2,128,128]{3,2,1,0:T(8,128)S(1)}, f32[2,2,128,128]{3,2,1,0:T(8,128)S(1)}, u32[]{:S(2)}, u32[]{:S(2)}) collective-permute-start(f32[2,2,128,128]{3,2,1,0:T(8,128)S(1)} %get-tuple-element.94), channel_id=1, source_target_pairs={{0,4},{1,5},{2,6},{3,7},{16,20},{17,21},{18,22},{19,23}} | collective-permute-start | bytes 786440 | tf_op jit(solution)/shard_map/ppermute | solution.py:617
  21.7 3.0 %collective-permute-start.7 = (s32[1,128]{1,0:T(1,128)S(1)}, s32[1,128]{1,0:T(1,128)S(1)}, u32[]{:S(2)}, u32[]{:S(2)}) collective-permute-start(s32[1,128]{1,0:T(1,128)S(1)} %sort_probes.1.refs_0_.refs_1_), channel_id=1, source_target_pairs={{8,12},{9,13},{10,14},{11,15},{24,28},{25,29},{26,30},{27,31}} | collective-permute-start | bytes 1544 | tf_op jit(solution)/shard_map/ppermute | solution.py:647
  24.8 2.2 %copy-start.7 = (f32[2,2,384,768]{3,2,1,0:T(8,128)}, f32[2,2,384,768]{3,2,1,0:T(8,128)S(1)}, u32[]{:S(2)}) copy-start(f32[2,2,384,768]{3,2,1,0:T(8,128)S(1)} %bring.1.refs_2_) | copy-start | bytes 14155780
  28.5 6.3 %collective-permute-start.8 = (f32[2,2,128,128]{3,2,1,0:T(8,128)S(1)}, f32[2,2,128,128]{3,2,1,0:T(8,128)S(1)}, u32[]{:S(2)}, u32[]{:S(2)}) collective-permute-start(f32[2,2,128,128]{3,2,1,0:T(8,128)S(1)} %get-tuple-element.98), channel_id=1, source_target_pairs={{0,4},{4,8},{1,5},{5,9},{2,6},{6,10},{3,7},{7,11},{16,20},{20,24},... | collective-permute-start | bytes 786440 | tf_op jit(solution)/shard_map/ppermute | solution.py:617
  30.9 35.6 %collective-permute-start.11 = (f32[16,1,128,128]{3,2,1,0:T(8,128)}, f32[16,1,128,128]{3,2,1,0:T(8,128)S(1)}, u32[]{:S(2)}, u32[]{:S(2)}) collective-permute-start(f32[16,1,128,128]{3,2,1,0:T(8,128)} %param.12), channel_id=1, source_target_pairs={{12,13},{13,12},{14,15},{15,14},{28,29},{29,28},{30,31},{31,30}} | collective-permute-start | bytes 3145736 | tf_op jit(solution)/shard_map/ppermute | solution.py:640
  34.8 31.7 %collective-permute-start.12 = (f32[16,1,128,128]{3,2,1,0:T(8,128)S(1)}, f32[16,1,128,128]{3,2,1,0:T(8,128)}, u32[]{:S(2)}, u32[]{:S(2)}) collective-permute-start(f32[16,1,128,128]{3,2,1,0:T(8,128)S(1)} %collective-permute-done.9), channel_id=1, source_target_pairs={{12,13},{13,12},{14,15},{15,14},{28,29},{29,28},{30,31},{31,30}} | collective-permute-start | bytes 3145736 | tf_op jit(solution)/shard_map/ppermute | solution.py:640
  38.1 7.2 %copy-start = (f32[42368,128]{1,0:T(8,128)}, f32[42368,128]{1,0:T(8,128)S(1)}, u32[]{:S(2)}) copy-start(f32[42368,128]{1,0:T(8,128)S(1)} %get-tuple-element.104.refs_4_) | copy-start | bytes 65077252
  45.3 22.6 %collective-permute-start.13 = (f32[2,2,128,128]{3,2,1,0:T(8,128)}, f32[2,2,128,128]{3,2,1,0:T(8,128)S(1)}, u32[]{:S(2)}, u32[]{:S(2)}) collective-permute-start(f32[2,2,128,128]{3,2,1,0:T(8,128)} %get-tuple-element.106), channel_id=1, source_target_pairs={{0,4},{4,8},{8,12},{1,5},{5,9},{9,13},{2,6},{6,10},{10,14},{3,7},{... | collective-permute-start | bytes 786440 | tf_op jit(solution)/shard_map/ppermute | solution.py:617
  50.5 16.0 %collective-permute-start.10 = (s32[1,128]{1,0:T(1,128)S(1)}, s32[1,128]{1,0:T(1,128)S(1)}, u32[]{:S(2)}, u32[]{:S(2)}) collective-permute-start(s32[1,128]{1,0:T(1,128)S(1)} %broadcast_select_fusion.refs_0_), channel_id=1, source_target_pairs={{0,16},{16,0},{1,17},{17,1},{2,18},{18,2},{3,19},{19,3},{4,20},{20... | collective-permute-start | bytes 1544 | tf_op jit(solution)/shard_map/ppermute | solution.py:512
  53.0 7.2 %copy-start.1 = (f32[42368,128]{1,0:T(8,128)S(1)}, f32[42368,128]{1,0:T(8,128)}, u32[]{:S(2)}) copy-start(f32[42368,128]{1,0:T(8,128)} %copy-done) | copy-start | bytes 65077252
  60.1 2.3 %copy-start.8 = (f32[2,2,384,768]{3,2,1,0:T(8,128)S(1)}, f32[2,2,384,768]{3,2,1,0:T(8,128)}, u32[]{:S(2)}) copy-start(f32[2,2,384,768]{3,2,1,0:T(8,128)} %copy-done.7) | copy-start | bytes 14155780
  62.5 2.3 %copy-start.10 = (f32[2,2,384,768]{3,2,1,0:T(8,128)S(1)}, f32[2,2,384,768]{3,2,1,0:T(8,128)}, u32[]{:S(2)}) copy-start(f32[2,2,384,768]{3,2,1,0:T(8,128)} %copy-done.9) | copy-start | bytes 14155780
  67.9 5.5 %slice-start = ((s8[4718592]{0:T(1024)(128)(4,1)}), s8[4194304]{0:T(1024)(128)(4,1)S(1)}, s32[]{:S(2)}) async-start(s8[4718592]{0:T(1024)(128)(4,1)} %bitcast.10), calls=%async_computation | async-start | bytes 8388608
  68.0 5.5 %slice-start.1 = ((s8[4718592]{0:T(1024)(128)(4,1)}), s8[524288]{0:T(1024)(128)(4,1)S(1)}, s32[]{:S(2)}) async-start(s8[4718592]{0:T(1024)(128)(4,1)} %bitcast.10), calls=%async_computation.1 | async-start | bytes 1048576
  68.9 8.4 %collective-permute-start.15 = (f32[2,2,128,128]{3,2,1,0:T(8,128)S(1)}, f32[2,2,128,128]{3,2,1,0:T(8,128)S(1)}, u32[]{:S(2)}, u32[]{:S(2)}) collective-permute-start(f32[2,2,128,128]{3,2,1,0:T(8,128)S(1)} %get-tuple-element.108.refs_1_), channel_id=1, source_target_pairs={{0,4},{4,8},{8,12},{1,5},{5,9},{9,13},{2,6},{6,10},{10,14},{3,7},{... | collective-permute-start | bytes 786440 | tf_op jit(solution)/shard_map/ppermute | solution.py:617
  76.0 6.6 %collective-permute-start.14 = (f32[2,2,128,128]{3,2,1,0:T(8,128)S(1)}, f32[2,2,128,128]{3,2,1,0:T(8,128)S(1)}, u32[]{:S(2)}, u32[]{:S(2)}) collective-permute-start(f32[2,2,128,128]{3,2,1,0:T(8,128)S(1)} %get-tuple-element.110), channel_id=1, source_target_pairs={{12,8},{13,9},{14,10},{15,11},{28,24},{29,25},{30,26},{31,27}} | collective-permute-start | bytes 786440 | tf_op jit(solution)/shard_map/ppermute | solution.py:617
  78.2 8.3 %collective-permute-start.17 = (f32[2,2,128,128]{3,2,1,0:T(8,128)S(1)}, f32[2,2,128,128]{3,2,1,0:T(8,128)S(1)}, u32[]{:S(2)}, u32[]{:S(2)}) collective-permute-start(f32[2,2,128,128]{3,2,1,0:T(8,128)S(1)} %get-tuple-element.112.refs_2_), channel_id=1, source_target_pairs={{0,4},{4,8},{8,12},{1,5},{5,9},{9,13},{2,6},{6,10},{10,14},{3,7},{... | collective-permute-start | bytes 786440 | tf_op jit(solution)/shard_map/ppermute | solution.py:617
  82.7 9.2 %collective-permute-start.16 = (f32[2,2,128,128]{3,2,1,0:T(8,128)S(1)}, f32[2,2,128,128]{3,2,1,0:T(8,128)S(1)}, u32[]{:S(2)}, u32[]{:S(2)}) collective-permute-start(f32[2,2,128,128]{3,2,1,0:T(8,128)S(1)} %get-tuple-element.114), channel_id=1, source_target_pairs={{8,4},{12,8},{9,5},{13,9},{10,6},{14,10},{11,7},{15,11},{24,20},{2... | collective-permute-start | bytes 786440 | tf_op jit(solution)/shard_map/ppermute | solution.py:617
  87.4 8.8 %collective-permute-start.19 = (f32[2,2,128,128]{3,2,1,0:T(8,128)S(1)}, f32[2,2,128,128]{3,2,1,0:T(8,128)S(1)}, u32[]{:S(2)}, u32[]{:S(2)}) collective-permute-start(f32[2,2,128,128]{3,2,1,0:T(8,128)S(1)} %get-tuple-element.116.refs_2_), channel_id=1, source_target_pairs={{0,4},{4,8},{8,12},{1,5},{5,9},{9,13},{2,6},{6,10},{10,14},{3,7},{... | collective-permute-start | bytes 786440 | tf_op jit(solution)/shard_map/ppermute | solution.py:617
  92.0 9.6 %collective-permute-start.18 = (f32[2,2,128,128]{3,2,1,0:T(8,128)S(1)}, f32[2,2,128,128]{3,2,1,0:T(8,128)S(1)}, u32[]{:S(2)}, u32[]{:S(2)}) collective-permute-start(f32[2,2,128,128]{3,2,1,0:T(8,128)S(1)} %get-tuple-element.118), channel_id=1, source_target_pairs={{4,0},{8,4},{12,8},{5,1},{9,5},{13,9},{6,2},{10,6},{14,10},{7,3},{... | collective-permute-start | bytes 786440 | tf_op jit(solution)/shard_map/ppermute | solution.py:617
  97.2 9.7 %collective-permute-start.21 = (f32[2,2,128,128]{3,2,1,0:T(8,128)S(1)}, f32[2,2,128,128]{3,2,1,0:T(8,128)S(1)}, u32[]{:S(2)}, u32[]{:S(2)}) collective-permute-start(f32[2,2,128,128]{3,2,1,0:T(8,128)S(1)} %get-tuple-element.120.refs_2_), channel_id=1, source_target_pairs={{0,4},{4,8},{8,12},{1,5},{5,9},{9,13},{2,6},{6,10},{10,14},{3,7},{... | collective-permute-start | bytes 786440 | tf_op jit(solution)/shard_map/ppermute | solution.py:617
  102.5 9.7 %collective-permute-start.20 = (f32[2,2,128,128]{3,2,1,0:T(8,128)S(1)}, f32[2,2,128,128]{3,2,1,0:T(8,128)S(1)}, u32[]{:S(2)}, u32[]{:S(2)}) collective-permute-start(f32[2,2,128,128]{3,2,1,0:T(8,128)S(1)} %get-tuple-element.122), channel_id=1, source_target_pairs={{4,0},{8,4},{12,8},{5,1},{9,5},{13,9},{6,2},{10,6},{14,10},{7,3},{... | collective-permute-start | bytes 786440 | tf_op jit(solution)/shard_map/ppermute | solution.py:617
  107.8 23.5 %collective-permute-start.23 = (f32[2,2,128,128]{3,2,1,0:T(8,128)S(1)}, f32[2,2,128,128]{3,2,1,0:T(8,128)S(1)}, u32[]{:S(2)}, u32[]{:S(2)}) collective-permute-start(f32[2,2,128,128]{3,2,1,0:T(8,128)S(1)} %get-tuple-element.124.refs_2_), channel_id=1, source_target_pairs={{0,4},{4,8},{8,12},{1,5},{5,9},{9,13},{2,6},{6,10},{10,14},{3,7},{... | collective-permute-start | bytes 786440 | tf_op jit(solution)/shard_map/ppermute | solution.py:617
  113.1 7.2 %copy-start.2 = (f32[42368,128]{1,0:T(8,128)}, f32[42368,128]{1,0:T(8,128)S(1)}, u32[]{:S(2)}) copy-start(f32[42368,128]{1,0:T(8,128)S(1)} %get-tuple-element.127.refs_2_) | copy-start | bytes 65077252
  120.3 11.6 %collective-permute-start.22 = (f32[2,2,128,128]{3,2,1,0:T(8,128)S(1)}, f32[2,2,128,128]{3,2,1,0:T(8,128)S(1)}, u32[]{:S(2)}, u32[]{:S(2)}) collective-permute-start(f32[2,2,128,128]{3,2,1,0:T(8,128)S(1)} %get-tuple-element.126), channel_id=1, source_target_pairs={{4,0},{8,4},{12,8},{5,1},{9,5},{13,9},{6,2},{10,6},{14,10},{7,3},{... | collective-permute-start | bytes 786440 | tf_op jit(solution)/shard_map/ppermute | solution.py:617
  122.9 44.3 %collective-permute-start.29 = (f32[2048,128]{1,0:T(8,128)S(1)}, f32[2048,128]{1,0:T(8,128)S(1)}, u32[]{:S(2)}, u32[]{:S(2)}) collective-permute-start(f32[2048,128]{1,0:T(8,128)S(1)} %slice.10), channel_id=1, source_target_pairs={{0,2},{2,0},{1,3},{3,1},{4,6},{6,4},{5,7},{7,5},{8,10},{10,8},{9,1... | collective-permute-start | bytes 3145736 | tf_op jit(solution)/shard_map/ppermute | solution.py:512
  123.0 7.2 %copy-start.3 = (f32[42368,128]{1,0:T(8,128)S(1)}, f32[42368,128]{1,0:T(8,128)}, u32[]{:S(2)}) copy-start(f32[42368,128]{1,0:T(8,128)} %copy-done.2) | copy-start | bytes 65077252
  131.3 4.0 %collective-permute-start.25 = (f32[2,2,128,128]{3,2,1,0:T(8,128)S(1)}, f32[2,2,128,128]{3,2,1,0:T(8,128)S(1)}, u32[]{:S(2)}, u32[]{:S(2)}) collective-permute-start(f32[2,2,128,128]{3,2,1,0:T(8,128)S(1)} %get-tuple-element.128.refs_2_), channel_id=1, source_target_pairs={{4,8},{8,12},{5,9},{9,13},{6,10},{10,14},{7,11},{11,15},{20,24},{2... | collective-permute-start | bytes 786440 | tf_op jit(solution)/shard_map/ppermute | solution.py:617
  132.9 11.0 %collective-permute-start.24 = (f32[2,2,128,128]{3,2,1,0:T(8,128)S(1)}, f32[2,2,128,128]{3,2,1,0:T(8,128)S(1)}, u32[]{:S(2)}, u32[]{:S(2)}) collective-permute-start(f32[2,2,128,128]{3,2,1,0:T(8,128)S(1)} %get-tuple-element.130), channel_id=1, source_target_pairs={{4,0},{8,4},{12,8},{5,1},{9,5},{13,9},{6,2},{10,6},{14,10},{7,3},{... | collective-permute-start | bytes 786440 | tf_op jit(solution)/shard_map/ppermute | solution.py:617
  135.3 29.7 %collective-permute-start.27 = (f32[2,2,128,128]{3,2,1,0:T(8,128)S(1)}, f32[2,2,128,128]{3,2,1,0:T(8,128)S(1)}, u32[]{:S(2)}, u32[]{:S(2)}) collective-permute-start(f32[2,2,128,128]{3,2,1,0:T(8,128)S(1)} %get-tuple-element.132.refs_2_), channel_id=1, source_target_pairs={{8,12},{9,13},{10,14},{11,15},{24,28},{25,29},{26,30},{27,31}} | collective-permute-start | bytes 786440 | tf_op jit(solution)/shard_map/ppermute | solution.py:617
  144.8 7.2 %copy-start.4 = (f32[42368,128]{1,0:T(8,128)}, f32[42368,128]{1,0:T(8,128)S(1)}, u32[]{:S(2)}) copy-start(f32[42368,128]{1,0:T(8,128)S(1)} %get-tuple-element.135.refs_2_) | copy-start | bytes 65077252
  152.1 12.9 %collective-permute-start.26 = (f32[2,2,128,128]{3,2,1,0:T(8,128)S(1)}, f32[2,2,128,128]{3,2,1,0:T(8,128)S(1)}, u32[]{:S(2)}, u32[]{:S(2)}) collective-permute-start(f32[2,2,128,128]{3,2,1,0:T(8,128)S(1)} %get-tuple-element.134), channel_id=1, source_target_pairs={{4,0},{8,4},{12,8},{5,1},{9,5},{13,9},{6,2},{10,6},{14,10},{7,3},{... | collective-permute-start | bytes 786440 | tf_op jit(solution)/shard_map/ppermute | solution.py:617
  154.7 32.5 %collective-permute-start.32 = (f32[2048,128]{1,0:T(8,128)S(1)}, f32[2048,128]{1,0:T(8,128)S(1)}, u32[]{:S(2)}, u32[]{:S(2)}) collective-permute-start(f32[2048,128]{1,0:T(8,128)S(1)} %slice.11), channel_id=1, source_target_pairs={{0,2},{2,0},{1,3},{3,1},{4,6},{6,4},{5,7},{7,5},{8,10},{10,8},{9,1... | collective-permute-start | bytes 3145736 | tf_op jit(solution)/shard_map/ppermute | solution.py:512
  156.8 7.2 %copy-start.5 = (f32[42368,128]{1,0:T(8,128)S(1)}, f32[42368,128]{1,0:T(8,128)}, u32[]{:S(2)}) copy-start(f32[42368,128]{1,0:T(8,128)} %copy-done.4) | copy-start | bytes 65077252
  166.0 9.9 %collective-permute-start.28 = (f32[2,2,128,128]{3,2,1,0:T(8,128)S(1)}, f32[2,2,128,128]{3,2,1,0:T(8,128)S(1)}, u32[]{:S(2)}, u32[]{:S(2)}) collective-permute-start(f32[2,2,128,128]{3,2,1,0:T(8,128)S(1)} %get-tuple-element.138), channel_id=1, source_target_pairs={{4,0},{8,4},{12,8},{5,1},{9,5},{13,9},{6,2},{10,6},{14,10},{7,3},{... | collective-permute-start | bytes 786440 | tf_op jit(solution)/shard_map/ppermute | solution.py:617
  176.7 8.3 %collective-permute-start.30 = (f32[2,2,128,128]{3,2,1,0:T(8,128)S(1)}, f32[2,2,128,128]{3,2,1,0:T(8,128)S(1)}, u32[]{:S(2)}, u32[]{:S(2)}) collective-permute-start(f32[2,2,128,128]{3,2,1,0:T(8,128)S(1)} %get-tuple-element.140), channel_id=1, source_target_pairs={{4,0},{8,4},{5,1},{9,5},{6,2},{10,6},{7,3},{11,7},{20,16},{24,20},... | collective-permute-start | bytes 786440 | tf_op jit(solution)/shard_map/ppermute | solution.py:617
  185.9 8.3 %collective-permute-start.31 = (f32[2,2,128,128]{3,2,1,0:T(8,128)S(1)}, f32[2,2,128,128]{3,2,1,0:T(8,128)S(1)}, u32[]{:S(2)}, u32[]{:S(2)}) collective-permute-start(f32[2,2,128,128]{3,2,1,0:T(8,128)S(1)} %get-tuple-element.142), channel_id=1, source_target_pairs={{4,0},{5,1},{6,2},{7,3},{20,16},{21,17},{22,18},{23,19}} | collective-permute-start | bytes 786440 | tf_op jit(solution)/shard_map/ppermute | solution.py:617
  198.7 4.6 %collective-permute-start.33 = (f32[2,2,1,192,768]{4,3,2,1,0:T(8,128)S(1)}, f32[2,2,1,192,768]{4,3,2,1,0:T(8,128)S(1)}, u32[]{:S(2)}, u32[]{:S(2)}) collective-permute-start(f32[2,2,1,192,768]{4,3,2,1,0:T(8,128)S(1)} %get-tuple-element.146), channel_id=1, source_target_pairs={{0,1},{1,0},{2,3},{3,2},{4,5},{5,4},{6,7},{7,6},{8,9},{9,8},{10,11... | collective-permute-start | bytes 7077896 | tf_op jit(solution)/shard_map/ppermute | solution.py:512

commit v5 on v4

--- a/solution.py
+++ b/solution.py
@@ -11,7 +11,7 @@
 from jax.sharding import PartitionSpec as P
 
 FRESNEL = 8.0
-SCOPED = 8 << 20
+SCOPED = 5 << 20
 CROSSING = 3
 F32 = jnp.float32
 BF16 = jnp.bfloat16
@@ -219,7 +219,7 @@
                         first += size
 
     pools = [pool.reshape((-1, lay.pixels)) for pool in pools]
-    pools = [("hbm", pools[0]), *(("vmem", pool) for pool in pools[1:])]
+    pools = [("hbm", pool) for pool in pools]
     return call(
         lay,
         body,

time: 207 us -> 207 us (level); the launches traced: 205 us -> 207 us
    unnamed x30 -> x32, local copies, waits for them, and re-layouts: 49 us -> 49 us
  transfers between devices with their start and end apart: 32 -> 32, of which waited for: 12 -> 12; matrix products, arithmetic and copies ran while one was open for 1% -> 1% of each run, Pallas kernels for 19% -> 18%
where the time goes in v5:
time: 207 us
  starting transfers between devices  62.3 us (30%)
  local copies, waits for them, and re-layouts  51.6 us (25%)
  waiting for transfers between devices  47.2 us (23%)
  Pallas kernels  45.4 us (22%)
    unnamed x32, local copies, waits for them, and re-layouts  49 us
    ppermute x20, starting transfers between devices, pass_on(): return lax.ppermute(wave, 'depth', pairs) if pairs else None  45.1 us
    ppermute x20, waiting for transfers between devices, pass_on(): return lax.ppermute(wave, 'depth', pairs) if pairs else None  38.3 us
    pallas_call x39, Pallas kernels, call(): pl.pallas_call(kernel, in_specs=specs, out_specs=[VMEM] * (1 + len(outs)...  37.6 us
    ppermute x2, starting transfers between devices, local(): cross_above = lambda x: lax.ppermute(x, ('depth', 'probe'), above)  6.51 us
    ppermute x6, waiting for transfers between devices, swap(): return lax.ppermute(shard, axis, [(0, 1), (1, 0)])  5.45 us
    ppermute x6, starting transfers between devices, swap(): return lax.ppermute(shard, axis, [(0, 1), (1, 0)])  5.02 us
  transfers between devices with their start and end apart: 32, of which 12 were waited for; matrix products, arithmetic and copies ran while one was open for 1% of the time, Pallas kernels for 18%

profile of v5, /device:TPU:0, one launch (start us, length us, event | category | flops | bytes accessed | tf_op | source)
XLA Modules:
  0.0 207.4 jit_solution(7174239807897358504)
XLA Ops:
  1.7 1.7 collective-permute-start.9
  3.4 4.6 %collective-permute-start.2 = (s32[16]{0:T(128)}, s32[16]{0:T(128)S(1)}, u32[]{:S(2)}, u32[]{:S(2)}) collective-permute-start(s32[16]{0:T(128)} %bitcast.13), channel_id=1, source_target_pairs={{0,2},{2,0},{4,6},{6,4},{8,10},{10,8},{1,3},{3,1},{5,7},{7,5},{9,1... | collective-permute-start | bytes 200 | tf_op jit(solution)/shard_map/ppermute | solution.py:598
  8.0 1.9 collective-permute-start.4
  9.9 3.5 %collective-permute-done.4.refs_3_ = s32[16]{0:T(128)S(1)} collective-permute-done((s32[16]{0:T(128)S(1)}, s32[16]{0:T(128)S(1)}, u32[]{:S(2)}, u32[]{:S(2)}) %collective-permute-start.4) | collective-permute-done | bytes 96 | tf_op jit(solution)/shard_map/ppermute | solution.py:598
  14.1 1.7 sort_probes.1.refs_0_.refs_1_
  15.8 3.4 %cut_patches.4.refs_2_ = f32[42368,128]{1,0:T(8,128)S(1)} custom-call(s32[1,128]{1,0:T(1,128)S(1)} %sort_probes.1.refs_0_.refs_1_, s32[1,128]{1,0:T(1,128)S(1)} %sort_probes.1.refs_0_.refs_1_, f32[2,2,384,768]{3,2,1,0:T(8,128)} %x, f32[2,2,384,768]{3,2,1,0:T(8,128)S(1)} %collective-permute-done.5.refs_3_), custom_call_target="tpu_custom_call" | custom-call | flops 1000 | bytes 1000 | tf_op jit(solution)/shard_map/cut_patches/pallas_call | solution.py:163
  20.1 2.6 %collective-permute-start.6 = (f32[2,2,128,128]{3,2,1,0:T(8,128)S(1)}, f32[2,2,128,128]{3,2,1,0:T(8,128)S(1)}, u32[]{:S(2)}, u32[]{:S(2)}) collective-permute-start(f32[2,2,128,128]{3,2,1,0:T(8,128)S(1)} %get-tuple-element.94), channel_id=1, source_target_pairs={{0,4},{1,5},{2,6},{3,7},{16,20},{17,21},{18,22},{19,23}} | collective-permute-start | bytes 786440 | tf_op jit(solution)/shard_map/ppermute | solution.py:617
  23.4 2.3 %bring.1.refs_2_ = f32[2,2,384,768]{3,2,1,0:T(8,128)S(1)} custom-call(f32[2,2,384,768]{3,2,1,0:T(8,128)} %x), custom_call_target="tpu_custom_call" | custom-call | flops 1000 | bytes 1000 | tf_op jit(solution)/shard_map/bring/pallas_call | solution.py:563
  25.8 1.7 cut_patches.5.refs_0_
  29.4 3.2 %collective-permute-start.8 = (f32[2,2,128,128]{3,2,1,0:T(8,128)S(1)}, f32[2,2,128,128]{3,2,1,0:T(8,128)S(1)}, u32[]{:S(2)}, u32[]{:S(2)}) collective-permute-start(f32[2,2,128,128]{3,2,1,0:T(8,128)S(1)} %get-tuple-element.98), channel_id=1, source_target_pairs={{0,4},{4,8},{1,5},{5,9},{2,6},{6,10},{3,7},{7,11},{16,20},{20,24},... | collective-permute-start | bytes 786440 | tf_op jit(solution)/shard_map/ppermute | solution.py:617
  32.6 1.6 collective-permute-start.11
  34.3 2.2 %collective-permute-done.8.refs_1_ = f32[2,2,128,128]{3,2,1,0:T(8,128)S(1)} collective-permute-done((f32[2,2,128,128]{3,2,1,0:T(8,128)S(1)}, f32[2,2,128,128]{3,2,1,0:T(8,128)S(1)}, u32[]{:S(2)}, u32[]{:S(2)}) %collective-permute-start.8) | collective-permute-done | bytes 262176 | tf_op jit(solution)/shard_map/ppermute | solution.py:617
  36.5 1.7 collective-permute-start.12
  39.1 7.2 %copy-done = f32[42368,128]{1,0:T(8,128)} copy-done((f32[42368,128]{1,0:T(8,128)}, f32[42368,128]{1,0:T(8,128)S(1)}, u32[]{:S(2)}) %copy-start) | copy-done | bytes 21692440
  46.3 5.3 %collective-permute-start.13 = (f32[2,2,128,128]{3,2,1,0:T(8,128)S(1)}, f32[2,2,128,128]{3,2,1,0:T(8,128)S(1)}, u32[]{:S(2)}, u32[]{:S(2)}) collective-permute-start(f32[2,2,128,128]{3,2,1,0:T(8,128)S(1)} %get-tuple-element.106), channel_id=1, source_target_pairs={{0,4},{4,8},{8,12},{1,5},{5,9},{9,13},{2,6},{6,10},{10,14},{3,7},{... | collective-permute-start | bytes 786440 | tf_op jit(solution)/shard_map/ppermute | solution.py:617
  51.6 2.0 collective-permute-start.10
  53.6 7.2 %copy-done.1 = f32[42368,128]{1,0:T(8,128)S(1)} copy-done((f32[42368,128]{1,0:T(8,128)S(1)}, f32[42368,128]{1,0:T(8,128)}, u32[]{:S(2)}) %copy-start.1) | copy-done | bytes 21692440
  60.7 2.3 %copy-done.8 = f32[2,2,384,768]{3,2,1,0:T(8,128)S(1)} copy-done((f32[2,2,384,768]{3,2,1,0:T(8,128)S(1)}, f32[2,2,384,768]{3,2,1,0:T(8,128)}, u32[]{:S(2)}) %copy-start.8) | copy-done | bytes 4718616
  63.1 2.3 %copy-done.10 = f32[2,2,384,768]{3,2,1,0:T(8,128)S(1)} copy-done((f32[2,2,384,768]{3,2,1,0:T(8,128)S(1)}, f32[2,2,384,768]{3,2,1,0:T(8,128)}, u32[]{:S(2)}) %copy-start.10) | copy-done | bytes 4718616
  65.4 1.7 cut_patches.6.refs_6_
  68.8 3.5 %collective-permute-start.15 = (f32[2,2,128,128]{3,2,1,0:T(8,128)S(1)}, f32[2,2,128,128]{3,2,1,0:T(8,128)S(1)}, u32[]{:S(2)}, u32[]{:S(2)}) collective-permute-start(f32[2,2,128,128]{3,2,1,0:T(8,128)S(1)} %get-tuple-element.108.refs_1_), channel_id=1, source_target_pairs={{0,4},{4,8},{8,12},{1,5},{5,9},{9,13},{2,6},{6,10},{10,14},{3,7},{... | collective-permute-start | bytes 786440 | tf_op jit(solution)/shard_map/ppermute | solution.py:617
  72.3 2.5 %cut_patches.7.refs_2_ = f32[42368,128]{1,0:T(8,128)S(1)} custom-call(s32[1,128]{1,0:T(1,128)S(1)} %sort_probes.1.refs_0_.refs_1_, s32[1,128]{1,0:T(1,128)S(1)} %collective-permute-done.7.refs_1_, f32[2,2,384,768]{3,2,1,0:T(8,128)S(1)} %bitcast.11, f32[2,2,384,768]{3,2,1,0:T(8,128)S(1)} %copy-done.10, ...), custom_call_target="tpu_custom_call", output_to_operand_aliasing={{}: (4, {})} | custom-call | flops 1000 | bytes 1000 | tf_op jit(solution)/shard_map/cut_patches/pallas_call | solution.py:163
  75.9 1.7 collective-permute-done.15.refs_1_
  78.5 4.4 %collective-permute-start.17 = (f32[2,2,128,128]{3,2,1,0:T(8,128)S(1)}, f32[2,2,128,128]{3,2,1,0:T(8,128)S(1)}, u32[]{:S(2)}, u32[]{:S(2)}) collective-permute-start(f32[2,2,128,128]{3,2,1,0:T(8,128)S(1)} %get-tuple-element.112.refs_2_), channel_id=1, source_target_pairs={{0,4},{4,8},{8,12},{1,5},{5,9},{9,13},{2,6},{6,10},{10,14},{3,7},{... | collective-permute-start | bytes 786440 | tf_op jit(solution)/shard_map/ppermute | solution.py:617
  84.0 3.4 %collective-permute-done.17.refs_1_ = f32[2,2,128,128]{3,2,1,0:T(8,128)S(1)} collective-permute-done((f32[2,2,128,128]{3,2,1,0:T(8,128)S(1)}, f32[2,2,128,128]{3,2,1,0:T(8,128)S(1)}, u32[]{:S(2)}, u32[]{:S(2)}) %collective-permute-start.17) | collective-permute-done | bytes 262176 | tf_op jit(solution)/shard_map/ppermute | solution.py:617
  88.3 4.4 %collective-permute-start.19 = (f32[2,2,128,128]{3,2,1,0:T(8,128)S(1)}, f32[2,2,128,128]{3,2,1,0:T(8,128)S(1)}, u32[]{:S(2)}, u32[]{:S(2)}) collective-permute-start(f32[2,2,128,128]{3,2,1,0:T(8,128)S(1)} %get-tuple-element.116.refs_2_), channel_id=1, source_target_pairs={{0,4},{4,8},{8,12},{1,5},{5,9},{9,13},{2,6},{6,10},{10,14},{3,7},{... | collective-permute-start | bytes 786440 | tf_op jit(solution)/shard_map/ppermute | solution.py:617
  94.5 2.0 collective-permute-done.19.refs_1_
  97.4 4.4 %collective-permute-start.21 = (f32[2,2,128,128]{3,2,1,0:T(8,128)S(1)}, f32[2,2,128,128]{3,2,1,0:T(8,128)S(1)}, u32[]{:S(2)}, u32[]{:S(2)}) collective-permute-start(f32[2,2,128,128]{3,2,1,0:T(8,128)S(1)} %get-tuple-element.120.refs_2_), channel_id=1, source_target_pairs={{0,4},{4,8},{8,12},{1,5},{5,9},{9,13},{2,6},{6,10},{10,14},{3,7},{... | collective-permute-start | bytes 786440 | tf_op jit(solution)/shard_map/ppermute | solution.py:617
  106.6 4.4 %collective-permute-start.23 = (f32[2,2,128,128]{3,2,1,0:T(8,128)S(1)}, f32[2,2,128,128]{3,2,1,0:T(8,128)S(1)}, u32[]{:S(2)}, u32[]{:S(2)}) collective-permute-start(f32[2,2,128,128]{3,2,1,0:T(8,128)S(1)} %get-tuple-element.124.refs_2_), channel_id=1, source_target_pairs={{0,4},{4,8},{8,12},{1,5},{5,9},{9,13},{2,6},{6,10},{10,14},{3,7},{... | collective-permute-start | bytes 786440 | tf_op jit(solution)/shard_map/ppermute | solution.py:617
  112.0 7.2 %copy-done.2 = f32[42368,128]{1,0:T(8,128)} copy-done((f32[42368,128]{1,0:T(8,128)}, f32[42368,128]{1,0:T(8,128)S(1)}, u32[]{:S(2)}) %copy-start.2) | copy-done | bytes 21692440
  120.5 1.3 slice.10
  122.2 7.2 %copy-done.3 = f32[42368,128]{1,0:T(8,128)S(1)} copy-done((f32[42368,128]{1,0:T(8,128)S(1)}, f32[42368,128]{1,0:T(8,128)}, u32[]{:S(2)}) %copy-start.3) | copy-done | bytes 21692440
  135.2 8.5 %collective-permute-done.24.refs_1_ = f32[2,2,128,128]{3,2,1,0:T(8,128)S(1)} collective-permute-done((f32[2,2,128,128]{3,2,1,0:T(8,128)S(1)}, f32[2,2,128,128]{3,2,1,0:T(8,128)S(1)}, u32[]{:S(2)}, u32[]{:S(2)}) %collective-permute-start.24) | collective-permute-done | bytes 262176 | tf_op jit(solution)/shard_map/ppermute | solution.py:617
  144.6 7.2 %copy-done.4 = f32[42368,128]{1,0:T(8,128)} copy-done((f32[42368,128]{1,0:T(8,128)}, f32[42368,128]{1,0:T(8,128)S(1)}, u32[]{:S(2)}) %copy-start.4) | copy-done | bytes 21692440
  153.1 1.3 slice.11
  154.4 1.8 collective-permute-start.32
  156.2 7.2 %copy-done.5 = f32[42368,128]{1,0:T(8,128)S(1)} copy-done((f32[42368,128]{1,0:T(8,128)S(1)}, f32[42368,128]{1,0:T(8,128)}, u32[]{:S(2)}) %copy-start.5) | copy-done | bytes 21692440
  166.7 2.3 %deposit_patches.20.refs_2_ = f32[42368,128]{1,0:T(8,128)S(1)} custom-call(s32[1,128]{1,0:T(1,128)S(1)} %sort_probes.1.refs_0_.refs_1_, s32[1,128]{1,0:T(1,128)S(1)} %collective-permute-done.7.refs_1_, f32[2048,128]{1,0:T(8,128)S(1)} %collective-permute-done.29.refs_2_, f32[42368,128]{1,0:T(8,128)S(1)} %get-tuple-element.139.refs_3_), custom_call_target="tpu_custom_call", output_to_operand_aliasing={{}: (3, {})} | custom-call | flops 1000 | bytes 1000 | tf_op jit(solution)/shard_map/deposit_patches/pallas_call | solution.py:163
  169.0 6.2 %collective-permute-done.28.refs_1_ = f32[2,2,128,128]{3,2,1,0:T(8,128)S(1)} collective-permute-done((f32[2,2,128,128]{3,2,1,0:T(8,128)S(1)}, f32[2,2,128,128]{3,2,1,0:T(8,128)S(1)}, u32[]{:S(2)}, u32[]{:S(2)}) %collective-permute-start.28) | collective-permute-done | bytes 262176 | tf_op jit(solution)/shard_map/ppermute | solution.py:617
  177.4 1.3 deposit_patches.21.refs_2_
  178.7 8.4 %collective-permute-done.30.refs_1_ = f32[2,2,128,128]{3,2,1,0:T(8,128)S(1)} collective-permute-done((f32[2,2,128,128]{3,2,1,0:T(8,128)S(1)}, f32[2,2,128,128]{3,2,1,0:T(8,128)S(1)}, u32[]{:S(2)}, u32[]{:S(2)}) %collective-permute-start.30) | collective-permute-done | bytes 262176 | tf_op jit(solution)/shard_map/ppermute | solution.py:617
  189.3 1.7 deposit_patches.22.refs_2_
  191.0 5.3 %collective-permute-done.31.refs_1_ = f32[2,2,128,128]{3,2,1,0:T(8,128)S(1)} collective-permute-done((f32[2,2,128,128]{3,2,1,0:T(8,128)S(1)}, f32[2,2,128,128]{3,2,1,0:T(8,128)S(1)}, u32[]{:S(2)}, u32[]{:S(2)}) %collective-permute-start.31) | collective-permute-done | bytes 262176 | tf_op jit(solution)/shard_map/ppermute | solution.py:617
  196.3 1.6 backward_section.21
  198.9 1.8 split_rows.3
  200.9 4.5 %collective-permute-done.33 = f32[2,2,1,192,768]{4,3,2,1,0:T(8,128)S(1)} collective-permute-done((f32[2,2,1,192,768]{4,3,2,1,0:T(8,128)S(1)}, f32[2,2,1,192,768]{4,3,2,1,0:T(8,128)S(1)}, u32[]{:S(2)}, u32[]{:S(2)}) %collective-permute-start.33) | collective-permute-done | bytes 2359328 | tf_op jit(solution)/shard_map/ppermute | solution.py:512
  205.4 2.0 conditional.1
  205.4 2.0 add_up.2
  (96 shorter events, 39.1 us)
Async XLA Ops:
  0.0 19.2 %copy-start.6 = (bf16[2,2,2,256,256]{4,3,2,1,0:T(8,128)(2,1)S(1)}, bf16[2,2,2,256,256]{4,3,2,1,0:T(8,128)(2,1)}, u32[]{:S(2)}) copy-start(bf16[2,2,2,256,256]{4,3,2,1,0:T(8,128)(2,1)} %constant.12.clone.refs_0_) | copy-start | bytes 3145732
  0.0 19.2 %copy-start.11 = (f32[2,128,128]{2,1,0:T(8,128)S(1)}, f32[2,128,128]{2,1,0:T(8,128)}, u32[]{:S(2)}) copy-start(f32[2,128,128]{2,1,0:T(8,128)} %refs_2_.15) | copy-start | bytes 393220
  0.0 1.4 collective-permute-start.3
  1.4 14.3 %collective-permute-start.5 = (f32[2,2,384,768]{3,2,1,0:T(8,128)}, f32[2,2,384,768]{3,2,1,0:T(8,128)S(1)}, u32[]{:S(2)}, u32[]{:S(2)}) collective-permute-start(f32[2,2,384,768]{3,2,1,0:T(8,128)} %x), channel_id=1, source_target_pairs={{0,1},{1,0},{2,3},{3,2},{4,5},{5,4},{6,7},{7,6},{8,9},{9,8},{10,11... | collective-permute-start | bytes 14155784 | tf_op jit(solution)/shard_map/ppermute | solution.py:512
  1.7 32.6 %collective-permute-start.9 = (f32[16,1,128,128]{3,2,1,0:T(8,128)}, f32[16,1,128,128]{3,2,1,0:T(8,128)}, u32[]{:S(2)}, u32[]{:S(2)}) collective-permute-start(f32[16,1,128,128]{3,2,1,0:T(8,128)} %param.12), channel_id=1, source_target_pairs={{12,14},{14,12},{13,15},{15,13},{28,30},{30,28},{29,31},{31,29}} | collective-permute-start | bytes 3145736 | tf_op jit(solution)/shard_map/ppermute | solution.py:596
  3.4 6.5 %collective-permute-start.2 = (s32[16]{0:T(128)}, s32[16]{0:T(128)S(1)}, u32[]{:S(2)}, u32[]{:S(2)}) collective-permute-start(s32[16]{0:T(128)} %bitcast.13), channel_id=1, source_target_pairs={{0,2},{2,0},{4,6},{6,4},{8,10},{10,8},{1,3},{3,1},{5,7},{7,5},{9,1... | collective-permute-start | bytes 200 | tf_op jit(solution)/shard_map/ppermute | solution.py:598
  8.0 5.4 %collective-permute-start.4 = (s32[16]{0:T(128)S(1)}, s32[16]{0:T(128)S(1)}, u32[]{:S(2)}, u32[]{:S(2)}) collective-permute-start(s32[16]{0:T(128)S(1)} %collective-permute-done.3.refs_2_), channel_id=1, source_target_pairs={{0,2},{2,0},{4,6},{6,4},{8,10},{10,8},{1,3},{3,1},{5,7},{7,5},{9,1... | collective-permute-start | bytes 200 | tf_op jit(solution)/shard_map/ppermute | solution.py:598
  13.4 0.7 copy-start.12
  15.7 10.0 %copy-start.9 = (f32[2,2,384,768]{3,2,1,0:T(8,128)}, f32[2,2,384,768]{3,2,1,0:T(8,128)S(1)}, u32[]{:S(2)}) copy-start(f32[2,2,384,768]{3,2,1,0:T(8,128)S(1)} %collective-permute-done.5.refs_3_) | copy-start | bytes 14155780
  20.1 8.4 %collective-permute-start.6 = (f32[2,2,128,128]{3,2,1,0:T(8,128)S(1)}, f32[2,2,128,128]{3,2,1,0:T(8,128)S(1)}, u32[]{:S(2)}, u32[]{:S(2)}) collective-permute-start(f32[2,2,128,128]{3,2,1,0:T(8,128)S(1)} %get-tuple-element.94), channel_id=1, source_target_pairs={{0,4},{1,5},{2,6},{3,7},{16,20},{17,21},{18,22},{19,23}} | collective-permute-start | bytes 786440 | tf_op jit(solution)/shard_map/ppermute | solution.py:617
  22.7 3.0 %collective-permute-start.7 = (s32[1,128]{1,0:T(1,128)S(1)}, s32[1,128]{1,0:T(1,128)S(1)}, u32[]{:S(2)}, u32[]{:S(2)}) collective-permute-start(s32[1,128]{1,0:T(1,128)S(1)} %sort_probes.1.refs_0_.refs_1_), channel_id=1, source_target_pairs={{8,12},{9,13},{10,14},{11,15},{24,28},{25,29},{26,30},{27,31}} | collective-permute-start | bytes 1544 | tf_op jit(solution)/shard_map/ppermute | solution.py:647
  25.7 2.2 %copy-start.7 = (f32[2,2,384,768]{3,2,1,0:T(8,128)}, f32[2,2,384,768]{3,2,1,0:T(8,128)S(1)}, u32[]{:S(2)}) copy-start(f32[2,2,384,768]{3,2,1,0:T(8,128)S(1)} %bring.1.refs_2_) | copy-start | bytes 14155780
  28.5 4.1 %copy-start.13 = (f32[16,1,128,128]{3,2,1,0:T(8,128)S(1)}, f32[16,1,128,128]{3,2,1,0:T(8,128)}, u32[]{:S(2)}) copy-start(f32[16,1,128,128]{3,2,1,0:T(8,128)} %param.12) | copy-start | bytes 3145732
  29.4 7.0 %collective-permute-start.8 = (f32[2,2,128,128]{3,2,1,0:T(8,128)S(1)}, f32[2,2,128,128]{3,2,1,0:T(8,128)S(1)}, u32[]{:S(2)}, u32[]{:S(2)}) collective-permute-start(f32[2,2,128,128]{3,2,1,0:T(8,128)S(1)} %get-tuple-element.98), channel_id=1, source_target_pairs={{0,4},{4,8},{1,5},{5,9},{2,6},{6,10},{3,7},{7,11},{16,20},{20,24},... | collective-permute-start | bytes 786440 | tf_op jit(solution)/shard_map/ppermute | solution.py:617
  32.6 34.5 %collective-permute-start.11 = (f32[16,1,128,128]{3,2,1,0:T(8,128)S(1)}, f32[16,1,128,128]{3,2,1,0:T(8,128)}, u32[]{:S(2)}, u32[]{:S(2)}) collective-permute-start(f32[16,1,128,128]{3,2,1,0:T(8,128)S(1)} %copy-done.13), channel_id=1, source_target_pairs={{12,13},{13,12},{14,15},{15,14},{28,29},{29,28},{30,31},{31,30}} | collective-permute-start | bytes 3145736 | tf_op jit(solution)/shard_map/ppermute | solution.py:640
  36.5 30.6 %collective-permute-start.12 = (f32[16,1,128,128]{3,2,1,0:T(8,128)}, f32[16,1,128,128]{3,2,1,0:T(8,128)}, u32[]{:S(2)}, u32[]{:S(2)}) collective-permute-start(f32[16,1,128,128]{3,2,1,0:T(8,128)} %collective-permute-done.9), channel_id=1, source_target_pairs={{12,13},{13,12},{14,15},{15,14},{28,29},{29,28},{30,31},{31,30}} | collective-permute-start | bytes 3145736 | tf_op jit(solution)/shard_map/ppermute | solution.py:640
  39.1 7.2 %copy-start = (f32[42368,128]{1,0:T(8,128)}, f32[42368,128]{1,0:T(8,128)S(1)}, u32[]{:S(2)}) copy-start(f32[42368,128]{1,0:T(8,128)S(1)} %get-tuple-element.104.refs_4_) | copy-start | bytes 65077252
  46.3 21.5 %collective-permute-start.13 = (f32[2,2,128,128]{3,2,1,0:T(8,128)S(1)}, f32[2,2,128,128]{3,2,1,0:T(8,128)S(1)}, u32[]{:S(2)}, u32[]{:S(2)}) collective-permute-start(f32[2,2,128,128]{3,2,1,0:T(8,128)S(1)} %get-tuple-element.106), channel_id=1, source_target_pairs={{0,4},{4,8},{8,12},{1,5},{5,9},{9,13},{2,6},{6,10},{10,14},{3,7},{... | collective-permute-start | bytes 786440 | tf_op jit(solution)/shard_map/ppermute | solution.py:617
  51.6 15.5 %collective-permute-start.10 = (s32[1,128]{1,0:T(1,128)S(1)}, s32[1,128]{1,0:T(1,128)S(1)}, u32[]{:S(2)}, u32[]{:S(2)}) collective-permute-start(s32[1,128]{1,0:T(1,128)S(1)} %broadcast_select_fusion.refs_0_), channel_id=1, source_target_pairs={{0,16},{16,0},{1,17},{17,1},{2,18},{18,2},{3,19},{19,3},{4,20},{20... | collective-permute-start | bytes 1544 | tf_op jit(solution)/shard_map/ppermute | solution.py:512
  53.6 7.2 %copy-start.1 = (f32[42368,128]{1,0:T(8,128)S(1)}, f32[42368,128]{1,0:T(8,128)}, u32[]{:S(2)}) copy-start(f32[42368,128]{1,0:T(8,128)} %copy-done) | copy-start | bytes 65077252
  60.7 2.3 %copy-start.8 = (f32[2,2,384,768]{3,2,1,0:T(8,128)S(1)}, f32[2,2,384,768]{3,2,1,0:T(8,128)}, u32[]{:S(2)}) copy-start(f32[2,2,384,768]{3,2,1,0:T(8,128)} %copy-done.7) | copy-start | bytes 14155780
  63.1 2.3 %copy-start.10 = (f32[2,2,384,768]{3,2,1,0:T(8,128)S(1)}, f32[2,2,384,768]{3,2,1,0:T(8,128)}, u32[]{:S(2)}) copy-start(f32[2,2,384,768]{3,2,1,0:T(8,128)} %copy-done.9) | copy-start | bytes 14155780
  67.9 4.5 %slice-start = ((s8[4718592]{0:T(1024)(128)(4,1)}), s8[4194304]{0:T(1024)(128)(4,1)S(1)}, s32[]{:S(2)}) async-start(s8[4718592]{0:T(1024)(128)(4,1)} %bitcast.10), calls=%async_computation | async-start | bytes 8388608
  67.9 4.4 %slice-start.1 = ((s8[4718592]{0:T(1024)(128)(4,1)}), s8[524288]{0:T(1024)(128)(4,1)S(1)}, s32[]{:S(2)}) async-start(s8[4718592]{0:T(1024)(128)(4,1)} %bitcast.10), calls=%async_computation.1 | async-start | bytes 1048576
  68.8 8.8 %collective-permute-start.15 = (f32[2,2,128,128]{3,2,1,0:T(8,128)S(1)}, f32[2,2,128,128]{3,2,1,0:T(8,128)S(1)}, u32[]{:S(2)}, u32[]{:S(2)}) collective-permute-start(f32[2,2,128,128]{3,2,1,0:T(8,128)S(1)} %get-tuple-element.108.refs_1_), channel_id=1, source_target_pairs={{0,4},{4,8},{8,12},{1,5},{5,9},{9,13},{2,6},{6,10},{10,14},{3,7},{... | collective-permute-start | bytes 786440 | tf_op jit(solution)/shard_map/ppermute | solution.py:617
  74.9 8.0 %collective-permute-start.14 = (f32[2,2,128,128]{3,2,1,0:T(8,128)S(1)}, f32[2,2,128,128]{3,2,1,0:T(8,128)S(1)}, u32[]{:S(2)}, u32[]{:S(2)}) collective-permute-start(f32[2,2,128,128]{3,2,1,0:T(8,128)S(1)} %get-tuple-element.110), channel_id=1, source_target_pairs={{12,8},{13,9},{14,10},{15,11},{28,24},{29,25},{30,26},{31,27}} | collective-permute-start | bytes 786440 | tf_op jit(solution)/shard_map/ppermute | solution.py:617
  78.5 8.8 %collective-permute-start.17 = (f32[2,2,128,128]{3,2,1,0:T(8,128)S(1)}, f32[2,2,128,128]{3,2,1,0:T(8,128)S(1)}, u32[]{:S(2)}, u32[]{:S(2)}) collective-permute-start(f32[2,2,128,128]{3,2,1,0:T(8,128)S(1)} %get-tuple-element.112.refs_2_), channel_id=1, source_target_pairs={{0,4},{4,8},{8,12},{1,5},{5,9},{9,13},{2,6},{6,10},{10,14},{3,7},{... | collective-permute-start | bytes 786440 | tf_op jit(solution)/shard_map/ppermute | solution.py:617
  83.0 9.7 %collective-permute-start.16 = (f32[2,2,128,128]{3,2,1,0:T(8,128)S(1)}, f32[2,2,128,128]{3,2,1,0:T(8,128)S(1)}, u32[]{:S(2)}, u32[]{:S(2)}) collective-permute-start(f32[2,2,128,128]{3,2,1,0:T(8,128)S(1)} %get-tuple-element.114), channel_id=1, source_target_pairs={{8,4},{12,8},{9,5},{13,9},{10,6},{14,10},{11,7},{15,11},{24,20},{2... | collective-permute-start | bytes 786440 | tf_op jit(solution)/shard_map/ppermute | solution.py:617
  88.3 8.3 %collective-permute-start.19 = (f32[2,2,128,128]{3,2,1,0:T(8,128)S(1)}, f32[2,2,128,128]{3,2,1,0:T(8,128)S(1)}, u32[]{:S(2)}, u32[]{:S(2)}) collective-permute-start(f32[2,2,128,128]{3,2,1,0:T(8,128)S(1)} %get-tuple-element.116.refs_2_), channel_id=1, source_target_pairs={{0,4},{4,8},{8,12},{1,5},{5,9},{9,13},{2,6},{6,10},{10,14},{3,7},{... | collective-permute-start | bytes 786440 | tf_op jit(solution)/shard_map/ppermute | solution.py:617
  92.7 9.2 %collective-permute-start.18 = (f32[2,2,128,128]{3,2,1,0:T(8,128)S(1)}, f32[2,2,128,128]{3,2,1,0:T(8,128)S(1)}, u32[]{:S(2)}, u32[]{:S(2)}) collective-permute-start(f32[2,2,128,128]{3,2,1,0:T(8,128)S(1)} %get-tuple-element.118), channel_id=1, source_target_pairs={{4,0},{8,4},{12,8},{5,1},{9,5},{13,9},{6,2},{10,6},{14,10},{7,3},{... | collective-permute-start | bytes 786440 | tf_op jit(solution)/shard_map/ppermute | solution.py:617
  97.4 8.3 %collective-permute-start.21 = (f32[2,2,128,128]{3,2,1,0:T(8,128)S(1)}, f32[2,2,128,128]{3,2,1,0:T(8,128)S(1)}, u32[]{:S(2)}, u32[]{:S(2)}) collective-permute-start(f32[2,2,128,128]{3,2,1,0:T(8,128)S(1)} %get-tuple-element.120.refs_2_), channel_id=1, source_target_pairs={{0,4},{4,8},{8,12},{1,5},{5,9},{9,13},{2,6},{6,10},{10,14},{3,7},{... | collective-permute-start | bytes 786440 | tf_op jit(solution)/shard_map/ppermute | solution.py:617
  102.8 8.3 %collective-permute-start.20 = (f32[2,2,128,128]{3,2,1,0:T(8,128)S(1)}, f32[2,2,128,128]{3,2,1,0:T(8,128)S(1)}, u32[]{:S(2)}, u32[]{:S(2)}) collective-permute-start(f32[2,2,128,128]{3,2,1,0:T(8,128)S(1)} %get-tuple-element.122), channel_id=1, source_target_pairs={{4,0},{8,4},{12,8},{5,1},{9,5},{13,9},{6,2},{10,6},{14,10},{7,3},{... | collective-permute-start | bytes 786440 | tf_op jit(solution)/shard_map/ppermute | solution.py:617
  106.6 23.8 %collective-permute-start.23 = (f32[2,2,128,128]{3,2,1,0:T(8,128)S(1)}, f32[2,2,128,128]{3,2,1,0:T(8,128)S(1)}, u32[]{:S(2)}, u32[]{:S(2)}) collective-permute-start(f32[2,2,128,128]{3,2,1,0:T(8,128)S(1)} %get-tuple-element.124.refs_2_), channel_id=1, source_target_pairs={{0,4},{4,8},{8,12},{1,5},{5,9},{9,13},{2,6},{6,10},{10,14},{3,7},{... | collective-permute-start | bytes 786440 | tf_op jit(solution)/shard_map/ppermute | solution.py:617
  112.0 7.2 %copy-start.2 = (f32[42368,128]{1,0:T(8,128)}, f32[42368,128]{1,0:T(8,128)S(1)}, u32[]{:S(2)}) copy-start(f32[42368,128]{1,0:T(8,128)S(1)} %get-tuple-element.127.refs_2_) | copy-start | bytes 65077252
  119.2 12.0 %collective-permute-start.22 = (f32[2,2,128,128]{3,2,1,0:T(8,128)S(1)}, f32[2,2,128,128]{3,2,1,0:T(8,128)S(1)}, u32[]{:S(2)}, u32[]{:S(2)}) collective-permute-start(f32[2,2,128,128]{3,2,1,0:T(8,128)S(1)} %get-tuple-element.126), channel_id=1, source_target_pairs={{4,0},{8,4},{12,8},{5,1},{9,5},{13,9},{6,2},{10,6},{14,10},{7,3},{... | collective-permute-start | bytes 786440 | tf_op jit(solution)/shard_map/ppermute | solution.py:617
  121.8 44.9 %collective-permute-start.29 = (f32[2048,128]{1,0:T(8,128)S(1)}, f32[2048,128]{1,0:T(8,128)S(1)}, u32[]{:S(2)}, u32[]{:S(2)}) collective-permute-start(f32[2048,128]{1,0:T(8,128)S(1)} %slice.10), channel_id=1, source_target_pairs={{0,2},{2,0},{1,3},{3,1},{4,6},{6,4},{5,7},{7,5},{8,10},{10,8},{9,1... | collective-permute-start | bytes 3145736 | tf_op jit(solution)/shard_map/ppermute | solution.py:512
  122.2 7.2 %copy-start.3 = (f32[42368,128]{1,0:T(8,128)S(1)}, f32[42368,128]{1,0:T(8,128)}, u32[]{:S(2)}) copy-start(f32[42368,128]{1,0:T(8,128)} %copy-done.2) | copy-start | bytes 65077252
  130.5 4.0 %collective-permute-start.25 = (f32[2,2,128,128]{3,2,1,0:T(8,128)S(1)}, f32[2,2,128,128]{3,2,1,0:T(8,128)S(1)}, u32[]{:S(2)}, u32[]{:S(2)}) collective-permute-start(f32[2,2,128,128]{3,2,1,0:T(8,128)S(1)} %get-tuple-element.128.refs_2_), channel_id=1, source_target_pairs={{4,8},{8,12},{5,9},{9,13},{6,10},{10,14},{7,11},{11,15},{20,24},{2... | collective-permute-start | bytes 786440 | tf_op jit(solution)/shard_map/ppermute | solution.py:617
  132.1 11.6 %collective-permute-start.24 = (f32[2,2,128,128]{3,2,1,0:T(8,128)S(1)}, f32[2,2,128,128]{3,2,1,0:T(8,128)S(1)}, u32[]{:S(2)}, u32[]{:S(2)}) collective-permute-start(f32[2,2,128,128]{3,2,1,0:T(8,128)S(1)} %get-tuple-element.130), channel_id=1, source_target_pairs={{4,0},{8,4},{12,8},{5,1},{9,5},{13,9},{6,2},{10,6},{14,10},{7,3},{... | collective-permute-start | bytes 786440 | tf_op jit(solution)/shard_map/ppermute | solution.py:617
  134.5 29.9 %collective-permute-start.27 = (f32[2,2,128,128]{3,2,1,0:T(8,128)S(1)}, f32[2,2,128,128]{3,2,1,0:T(8,128)S(1)}, u32[]{:S(2)}, u32[]{:S(2)}) collective-permute-start(f32[2,2,128,128]{3,2,1,0:T(8,128)S(1)} %get-tuple-element.132.refs_2_), channel_id=1, source_target_pairs={{8,12},{9,13},{10,14},{11,15},{24,28},{25,29},{26,30},{27,31}} | collective-permute-start | bytes 786440 | tf_op jit(solution)/shard_map/ppermute | solution.py:617
  144.6 7.2 %copy-start.4 = (f32[42368,128]{1,0:T(8,128)}, f32[42368,128]{1,0:T(8,128)S(1)}, u32[]{:S(2)}) copy-start(f32[42368,128]{1,0:T(8,128)S(1)} %get-tuple-element.135.refs_2_) | copy-start | bytes 65077252
  151.8 12.7 %collective-permute-start.26 = (f32[2,2,128,128]{3,2,1,0:T(8,128)S(1)}, f32[2,2,128,128]{3,2,1,0:T(8,128)S(1)}, u32[]{:S(2)}, u32[]{:S(2)}) collective-permute-start(f32[2,2,128,128]{3,2,1,0:T(8,128)S(1)} %get-tuple-element.134), channel_id=1, source_target_pairs={{4,0},{8,4},{12,8},{5,1},{9,5},{13,9},{6,2},{10,6},{14,10},{7,3},{... | collective-permute-start | bytes 786440 | tf_op jit(solution)/shard_map/ppermute | solution.py:617
  154.4 34.9 %collective-permute-start.32 = (f32[2048,128]{1,0:T(8,128)S(1)}, f32[2048,128]{1,0:T(8,128)S(1)}, u32[]{:S(2)}, u32[]{:S(2)}) collective-permute-start(f32[2048,128]{1,0:T(8,128)S(1)} %slice.11), channel_id=1, source_target_pairs={{0,2},{2,0},{1,3},{3,1},{4,6},{6,4},{5,7},{7,5},{8,10},{10,8},{9,1... | collective-permute-start | bytes 3145736 | tf_op jit(solution)/shard_map/ppermute | solution.py:512
  156.2 7.2 %copy-start.5 = (f32[42368,128]{1,0:T(8,128)S(1)}, f32[42368,128]{1,0:T(8,128)}, u32[]{:S(2)}) copy-start(f32[42368,128]{1,0:T(8,128)} %copy-done.4) | copy-start | bytes 65077252
  165.4 9.8 %collective-permute-start.28 = (f32[2,2,128,128]{3,2,1,0:T(8,128)S(1)}, f32[2,2,128,128]{3,2,1,0:T(8,128)S(1)}, u32[]{:S(2)}, u32[]{:S(2)}) collective-permute-start(f32[2,2,128,128]{3,2,1,0:T(8,128)S(1)} %get-tuple-element.138), channel_id=1, source_target_pairs={{4,0},{8,4},{12,8},{5,1},{9,5},{13,9},{6,2},{10,6},{14,10},{7,3},{... | collective-permute-start | bytes 786440 | tf_op jit(solution)/shard_map/ppermute | solution.py:617
  176.1 11.0 %collective-permute-start.30 = (f32[2,2,128,128]{3,2,1,0:T(8,128)S(1)}, f32[2,2,128,128]{3,2,1,0:T(8,128)S(1)}, u32[]{:S(2)}, u32[]{:S(2)}) collective-permute-start(f32[2,2,128,128]{3,2,1,0:T(8,128)S(1)} %get-tuple-element.140), channel_id=1, source_target_pairs={{4,0},{8,4},{5,1},{9,5},{6,2},{10,6},{7,3},{11,7},{20,16},{24,20},... | collective-permute-start | bytes 786440 | tf_op jit(solution)/shard_map/ppermute | solution.py:617
  188.0 8.3 %collective-permute-start.31 = (f32[2,2,128,128]{3,2,1,0:T(8,128)S(1)}, f32[2,2,128,128]{3,2,1,0:T(8,128)S(1)}, u32[]{:S(2)}, u32[]{:S(2)}) collective-permute-start(f32[2,2,128,128]{3,2,1,0:T(8,128)S(1)} %get-tuple-element.142), channel_id=1, source_target_pairs={{4,0},{5,1},{6,2},{7,3},{20,16},{21,17},{22,18},{23,19}} | collective-permute-start | bytes 786440 | tf_op jit(solution)/shard_map/ppermute | solution.py:617
  200.8 4.6 %collective-permute-start.33 = (f32[2,2,1,192,768]{4,3,2,1,0:T(8,128)S(1)}, f32[2,2,1,192,768]{4,3,2,1,0:T(8,128)S(1)}, u32[]{:S(2)}, u32[]{:S(2)}) collective-permute-start(f32[2,2,1,192,768]{4,3,2,1,0:T(8,128)S(1)} %get-tuple-element.146), channel_id=1, source_target_pairs={{0,1},{1,0},{2,3},{3,2},{4,5},{5,4},{6,7},{7,6},{8,9},{9,8},{10,11... | collective-permute-start | bytes 7077896 | tf_op jit(solution)/shard_map/ppermute | solution.py:512

commit v6 on v3

--- a/solution.py
+++ b/solution.py
@@ -620,7 +620,7 @@
         early_sections = min(group, lay.groups) * count
         return lambda section: jnp.where(section < 2, early_sections, probes)
 
-    cuts = {0: (count, upto(3)), 2: (upto(3), upto(5)), 3: (upto(5), probes)}
+    cuts = {0: (count, upto(3)), 2: (upto(3), upto(5)), 4: (upto(5), probes)}
     last_tick = lay.groups + 2 * fill - 1
     for tick in range(lay.groups + 2 * fill):
         own = None

time: 162 us -> 164 us (1.012)
  waiting for transfers between devices: 53.9 us -> 57.3 us
  starting transfers between devices: 61.4 us -> 59.2 us
    ppermute x20, waiting for transfers between devices: 44.2 us -> 47 us  [pass_on(): return lax.ppermute(wave, 'depth', pairs) if pairs else None]
  transfers between devices with their start and end apart: 31 -> 31, of which waited for: 19 -> 20; matrix products, arithmetic and copies ran while one was open for 0% -> 0% of each run, Pallas kernels for 23% -> 23%
where the time goes in v6:
time: 164 us; the launch traced here: 163 us
  starting transfers between devices  59.2 us (36%)
  waiting for transfers between devices  57.3 us (35%)
  Pallas kernels  44.9 us (27%)
    ppermute x20, starting transfers between devices, pass_on(): return lax.ppermute(wave, 'depth', pairs) if pairs else None  49.8 us
    ppermute x20, waiting for transfers between devices, pass_on(): return lax.ppermute(wave, 'depth', pairs) if pairs else None  47 us
    pallas_call x39, Pallas kernels, call(): pl.pallas_call(kernel, in_specs=specs, out_specs=[VMEM] * (1 + len(outs)...  37.1 us
    ppermute x8, waiting for transfers between devices, swap(): return lax.ppermute(shard, axis, [(0, 1), (1, 0)])  10.2 us
    ppermute x8, starting transfers between devices, swap(): return lax.ppermute(shard, axis, [(0, 1), (1, 0)])  7.25 us
  transfers between devices with their start and end apart: 31, of which 20 were waited for; matrix products, arithmetic and copies ran while one was open for 0% of the time, Pallas kernels for 23%

profile of v6, /device:TPU:0, one launch (start us, length us, event | category | flops | bytes accessed | tf_op | source)
XLA Modules:
  0.0 162.8 jit_solution(4836389581624459511)
XLA Ops:
  1.7 2.7 %collective-permute-start.2 = (s32[16]{0:T(128)}, s32[16]{0:T(128)S(1)}, u32[]{:S(2)}, u32[]{:S(2)}) collective-permute-start(s32[16]{0:T(128)} %bitcast.14), channel_id=1, source_target_pairs={{0,2},{2,0},{1,3},{3,1},{4,6},{6,4},{5,7},{7,5},{8,10},{10,8},{9,1... | collective-permute-start | bytes 200 | tf_op jit(solution)/shard_map/ppermute | solution.py:504
  4.4 1.6 collective-permute-done.2.refs_1_
  6.1 1.9 %collective-permute-done.4.refs_3_ = s32[16]{0:T(128)S(1)} collective-permute-done((s32[16]{0:T(128)S(1)}, s32[16]{0:T(128)S(1)}, u32[]{:S(2)}, u32[]{:S(2)}) %collective-permute-start.4) | collective-permute-done | bytes 96 | tf_op jit(solution)/shard_map/ppermute | solution.py:504
  9.3 1.7 %sort_probes.1.refs_0_ = s32[1,128]{1,0:T(1,128)S(1)} custom-call(s32[2,512]{1,0:T(2,128)} %bitcast.20, s32[16]{0:T(128)S(1)} %bitcast.15, s32[16]{0:T(128)S(1)} %collective-permute-done.2.refs_1_, s32[16]{0:T(128)S(1)} %collective-permute-done.3.refs_2_, s32[16]{0:T(128)S(1)} %collective-permute-done.4.refs_3_), custom_call_target="tpu_custom_call" | custom-call | tf_op jit(solution)/shard_map/sort_probes/pallas_call | solution.py:538
  11.0 2.9 %cut_patches.4.refs_2_ = f32[42368,128]{1,0:T(8,128)S(1)} custom-call(s32[1,128]{1,0:T(1,128)S(1)} %sort_probes.1.refs_0_, f32[2,2,384,768]{3,2,1,0:T(8,128)} %x, f32[2,2,384,768]{3,2,1,0:T(8,128)S(1)} %collective-permute-done.5.refs_2_), custom_call_target="tpu_custom_call" | custom-call | flops 1000 | bytes 1000 | tf_op jit(solution)/shard_map/cut_patches/pallas_call | solution.py:157
  14.9 2.6 %collective-permute-start.6 = (f32[2,2,128,128]{3,2,1,0:T(8,128)S(1)}, f32[2,2,128,128]{3,2,1,0:T(8,128)S(1)}, u32[]{:S(2)}, u32[]{:S(2)}) collective-permute-start(f32[2,2,128,128]{3,2,1,0:T(8,128)S(1)} %get-tuple-element.94), channel_id=1, source_target_pairs={{0,4},{1,5},{2,6},{3,7},{16,20},{17,21},{18,22},{19,23}} | collective-permute-start | bytes 786440 | tf_op jit(solution)/shard_map/ppermute | solution.py:609
  17.5 2.3 %bring.1.refs_1_ = f32[2,2,384,768]{3,2,1,0:T(8,128)S(1)} custom-call(f32[2,2,384,768]{3,2,1,0:T(8,128)} %x), custom_call_target="tpu_custom_call" | custom-call | flops 1000 | bytes 1000 | tf_op jit(solution)/shard_map/bring/pallas_call | solution.py:555
  19.9 1.7 %cut_patches.5.refs_0_ = f32[42368,128]{1,0:T(8,128)S(1)} custom-call(s32[1,128]{1,0:T(1,128)S(1)} %sort_probes.1.refs_0_, f32[2,2,384,768]{3,2,1,0:T(8,128)S(1)} %bring.1.refs_1_, f32[2,2,384,768]{3,2,1,0:T(8,128)S(1)} %collective-permute-done.5.refs_2_, f32[42368,128]{1,0:T(8,128)S(1)} %get-tuple-element.96.refs_3_), custom_call_target="tpu_custom_call", output_to_operand_aliasing={{}: (3, {})} | custom-call | flops 1000 | bytes 1000 | tf_op jit(solution)/shard_map/cut_patches/pallas_call | solution.py:157
  22.1 1.1 collective-permute-done.6.refs_1_
  24.2 4.4 %collective-permute-start.7 = (f32[2,2,128,128]{3,2,1,0:T(8,128)S(1)}, f32[2,2,128,128]{3,2,1,0:T(8,128)S(1)}, u32[]{:S(2)}, u32[]{:S(2)}) collective-permute-start(f32[2,2,128,128]{3,2,1,0:T(8,128)S(1)} %get-tuple-element.97), channel_id=1, source_target_pairs={{0,4},{4,8},{1,5},{5,9},{2,6},{6,10},{3,7},{7,11},{16,20},{20,24},... | collective-permute-start | bytes 786440 | tf_op jit(solution)/shard_map/ppermute | solution.py:609
  28.6 1.6 collective-permute-start.9
  30.9 1.3 collective-permute-done.9.refs_1_
  32.2 1.3 collective-permute-done.7.refs_1_
  35.1 4.4 %collective-permute-start.12 = (f32[2,2,128,128]{3,2,1,0:T(8,128)S(1)}, f32[2,2,128,128]{3,2,1,0:T(8,128)S(1)}, u32[]{:S(2)}, u32[]{:S(2)}) collective-permute-start(f32[2,2,128,128]{3,2,1,0:T(8,128)S(1)} %get-tuple-element.105), channel_id=1, source_target_pairs={{0,4},{4,8},{8,12},{1,5},{5,9},{9,13},{2,6},{6,10},{10,14},{3,7},{... | collective-permute-start | bytes 786440 | tf_op jit(solution)/shard_map/ppermute | solution.py:609
  39.5 1.7 %cut_patches.6.refs_6_ = f32[42368,128]{1,0:T(8,128)S(1)} custom-call(s32[1,128]{1,0:T(1,128)S(1)} %sort_probes.1.refs_0_, f32[2,2,384,768]{3,2,1,0:T(8,128)S(1)} %bring.1.refs_1_, f32[2,2,384,768]{3,2,1,0:T(8,128)S(1)} %collective-permute-done.5.refs_2_, f32[42368,128]{1,0:T(8,128)S(1)} %get-tuple-element.103.refs_3_), custom_call_target="tpu_custom_call", output_to_operand_aliasing={{}: (3, {})} | custom-call | flops 1000 | bytes 1000 | tf_op jit(solution)/shard_map/cut_patches/pallas_call | solution.py:157
  42.0 1.5 collective-permute-done.12.refs_1_
  44.4 4.4 %collective-permute-start.14 = (f32[2,2,128,128]{3,2,1,0:T(8,128)S(1)}, f32[2,2,128,128]{3,2,1,0:T(8,128)S(1)}, u32[]{:S(2)}, u32[]{:S(2)}) collective-permute-start(f32[2,2,128,128]{3,2,1,0:T(8,128)S(1)} %get-tuple-element.107.refs_1_), channel_id=1, source_target_pairs={{0,4},{4,8},{8,12},{1,5},{5,9},{9,13},{2,6},{6,10},{10,14},{3,7},{... | collective-permute-start | bytes 786440 | tf_op jit(solution)/shard_map/ppermute | solution.py:609
  49.8 2.9 %collective-permute-done.14.refs_1_ = f32[2,2,128,128]{3,2,1,0:T(8,128)S(1)} collective-permute-done((f32[2,2,128,128]{3,2,1,0:T(8,128)S(1)}, f32[2,2,128,128]{3,2,1,0:T(8,128)S(1)}, u32[]{:S(2)}, u32[]{:S(2)}) %collective-permute-start.14) | collective-permute-done | bytes 262176 | tf_op jit(solution)/shard_map/ppermute | solution.py:609
  53.6 6.3 %collective-permute-start.16 = (f32[2,2,128,128]{3,2,1,0:T(8,128)S(1)}, f32[2,2,128,128]{3,2,1,0:T(8,128)S(1)}, u32[]{:S(2)}, u32[]{:S(2)}) collective-permute-start(f32[2,2,128,128]{3,2,1,0:T(8,128)S(1)} %get-tuple-element.111.refs_2_), channel_id=1, source_target_pairs={{0,4},{4,8},{8,12},{1,5},{5,9},{9,13},{2,6},{6,10},{10,14},{3,7},{... | collective-permute-start | bytes 786440 | tf_op jit(solution)/shard_map/ppermute | solution.py:609
  59.9 2.5 %cut_patches.7.refs_3_ = f32[42368,128]{1,0:T(8,128)S(1)} custom-call(s32[1,128]{1,0:T(1,128)S(1)} %sort_probes.1.refs_0_, f32[2,2,384,768]{3,2,1,0:T(8,128)S(1)} %bring.1.refs_1_, f32[2,2,384,768]{3,2,1,0:T(8,128)S(1)} %collective-permute-done.5.refs_2_, f32[42368,128]{1,0:T(8,128)S(1)} %get-tuple-element.112.refs_3_), custom_call_target="tpu_custom_call", output_to_operand_aliasing={{}: (3, {})} | custom-call | flops 1000 | bytes 1000 | tf_op jit(solution)/shard_map/cut_patches/pallas_call | solution.py:157
  65.4 4.4 %collective-permute-start.18 = (f32[2,2,128,128]{3,2,1,0:T(8,128)S(1)}, f32[2,2,128,128]{3,2,1,0:T(8,128)S(1)}, u32[]{:S(2)}, u32[]{:S(2)}) collective-permute-start(f32[2,2,128,128]{3,2,1,0:T(8,128)S(1)} %get-tuple-element.115.refs_2_), channel_id=1, source_target_pairs={{0,4},{4,8},{8,12},{1,5},{5,9},{9,13},{2,6},{6,10},{10,14},{3,7},{... | collective-permute-start | bytes 786440 | tf_op jit(solution)/shard_map/ppermute | solution.py:609
  70.0 1.3 collective-permute-start.17
  71.6 2.1 %collective-permute-done.18.refs_1_ = f32[2,2,128,128]{3,2,1,0:T(8,128)S(1)} collective-permute-done((f32[2,2,128,128]{3,2,1,0:T(8,128)S(1)}, f32[2,2,128,128]{3,2,1,0:T(8,128)S(1)}, u32[]{:S(2)}, u32[]{:S(2)}) %collective-permute-start.18) | collective-permute-done | bytes 262176 | tf_op jit(solution)/shard_map/ppermute | solution.py:609
  74.6 5.8 %collective-permute-start.20 = (f32[2,2,128,128]{3,2,1,0:T(8,128)S(1)}, f32[2,2,128,128]{3,2,1,0:T(8,128)S(1)}, u32[]{:S(2)}, u32[]{:S(2)}) collective-permute-start(f32[2,2,128,128]{3,2,1,0:T(8,128)S(1)} %get-tuple-element.119.refs_2_), channel_id=1, source_target_pairs={{0,4},{4,8},{8,12},{1,5},{5,9},{9,13},{2,6},{6,10},{10,14},{3,7},{... | collective-permute-start | bytes 786440 | tf_op jit(solution)/shard_map/ppermute | solution.py:609
  81.7 1.3 collective-permute-start.19
  85.2 4.4 %collective-permute-start.22 = (f32[2,2,128,128]{3,2,1,0:T(8,128)S(1)}, f32[2,2,128,128]{3,2,1,0:T(8,128)S(1)}, u32[]{:S(2)}, u32[]{:S(2)}) collective-permute-start(f32[2,2,128,128]{3,2,1,0:T(8,128)S(1)} %get-tuple-element.123.refs_2_), channel_id=1, source_target_pairs={{0,4},{4,8},{8,12},{1,5},{5,9},{9,13},{2,6},{6,10},{10,14},{3,7},{... | collective-permute-start | bytes 786440 | tf_op jit(solution)/shard_map/ppermute | solution.py:609
  90.9 1.3 collective-permute-start.21
  94.6 4.5 %collective-permute-done.21.refs_1_ = f32[2,2,128,128]{3,2,1,0:T(8,128)S(1)} collective-permute-done((f32[2,2,128,128]{3,2,1,0:T(8,128)S(1)}, f32[2,2,128,128]{3,2,1,0:T(8,128)S(1)}, u32[]{:S(2)}, u32[]{:S(2)}) %collective-permute-start.21) | collective-permute-done | bytes 262176 | tf_op jit(solution)/shard_map/ppermute | solution.py:609
  100.0 1.3 collective-permute-start.23
  101.3 1.1 deposit_patches.18.refs_2_
  103.1 5.6 %collective-permute-done.23.refs_1_ = f32[2,2,128,128]{3,2,1,0:T(8,128)S(1)} collective-permute-done((f32[2,2,128,128]{3,2,1,0:T(8,128)S(1)}, f32[2,2,128,128]{3,2,1,0:T(8,128)S(1)}, u32[]{:S(2)}, u32[]{:S(2)}) %collective-permute-start.23) | collective-permute-done | bytes 262176 | tf_op jit(solution)/shard_map/ppermute | solution.py:609
  109.7 1.3 collective-permute-start.25
  111.1 1.5 collective-permute-start.31
  113.7 5.5 %collective-permute-done.25.refs_1_ = f32[2,2,128,128]{3,2,1,0:T(8,128)S(1)} collective-permute-done((f32[2,2,128,128]{3,2,1,0:T(8,128)S(1)}, f32[2,2,128,128]{3,2,1,0:T(8,128)S(1)}, u32[]{:S(2)}, u32[]{:S(2)}) %collective-permute-start.25) | collective-permute-done | bytes 262176 | tf_op jit(solution)/shard_map/ppermute | solution.py:609
  120.1 1.3 collective-permute-start.27
  121.4 2.3 %deposit_patches.20.refs_2_ = f32[42368,128]{1,0:T(8,128)S(1)} custom-call(s32[1,128]{1,0:T(1,128)S(1)} %sort_probes.1.refs_0_, f32[2048,128]{1,0:T(8,128)S(1)} %collective-permute-done.28.refs_1_, f32[42368,128]{1,0:T(8,128)S(1)} %get-tuple-element.138.refs_2_), custom_call_target="tpu_custom_call", output_to_operand_aliasing={{}: (2, {})} | custom-call | flops 1000 | bytes 1000 | tf_op jit(solution)/shard_map/deposit_patches/pallas_call | solution.py:157
  123.6 6.8 %collective-permute-done.27.refs_1_ = f32[2,2,128,128]{3,2,1,0:T(8,128)S(1)} collective-permute-done((f32[2,2,128,128]{3,2,1,0:T(8,128)S(1)}, f32[2,2,128,128]{3,2,1,0:T(8,128)S(1)}, u32[]{:S(2)}, u32[]{:S(2)}) %collective-permute-start.27) | collective-permute-done | bytes 262176 | tf_op jit(solution)/shard_map/ppermute | solution.py:609
  131.3 1.3 collective-permute-start.29
  132.6 1.1 deposit_patches.21.refs_2_
  133.7 8.9 %collective-permute-done.29.refs_1_ = f32[2,2,128,128]{3,2,1,0:T(8,128)S(1)} collective-permute-done((f32[2,2,128,128]{3,2,1,0:T(8,128)S(1)}, f32[2,2,128,128]{3,2,1,0:T(8,128)S(1)}, u32[]{:S(2)}, u32[]{:S(2)}) %collective-permute-start.29) | collective-permute-done | bytes 262176 | tf_op jit(solution)/shard_map/ppermute | solution.py:609
  143.5 1.3 collective-permute-start.30
  144.8 1.8 %deposit_patches.22.refs_2_ = f32[42368,128]{1,0:T(8,128)S(1)} custom-call(s32[1,128]{1,0:T(1,128)S(1)} %sort_probes.1.refs_0_, f32[2048,128]{1,0:T(8,128)S(1)} %collective-permute-done.31.refs_1_, f32[42368,128]{1,0:T(8,128)S(1)} %get-tuple-element.142.refs_2_), custom_call_target="tpu_custom_call", output_to_operand_aliasing={{}: (2, {})} | custom-call | flops 1000 | bytes 1000 | tf_op jit(solution)/shard_map/deposit_patches/pallas_call | solution.py:157
  146.6 5.1 %collective-permute-done.30.refs_1_ = f32[2,2,128,128]{3,2,1,0:T(8,128)S(1)} collective-permute-done((f32[2,2,128,128]{3,2,1,0:T(8,128)S(1)}, f32[2,2,128,128]{3,2,1,0:T(8,128)S(1)}, u32[]{:S(2)}, u32[]{:S(2)}) %collective-permute-start.30) | collective-permute-done | bytes 262176 | tf_op jit(solution)/shard_map/ppermute | solution.py:609
  151.7 1.6 backward_section.21
  154.4 1.9 %split_rows.3 = (f32[2,2,1,192,768]{4,3,2,1,0:T(8,128)S(1)}, f32[2,2,1,192,768]{4,3,2,1,0:T(8,128)S(1)}, f32[4096,128]{1,0:T(8,128)}) custom-call(f32[42368,128]{1,0:T(8,128)S(1)} %deposit_patches.23.state), custom_call_target="tpu_custom_call" | custom-call | tf_op jit(solution)/shard_map/split_rows/pallas_call | solution.py:471
  156.4 4.5 %collective-permute-done.32 = f32[2,2,1,192,768]{4,3,2,1,0:T(8,128)S(1)} collective-permute-done((f32[2,2,1,192,768]{4,3,2,1,0:T(8,128)S(1)}, f32[2,2,1,192,768]{4,3,2,1,0:T(8,128)S(1)}, u32[]{:S(2)}, u32[]{:S(2)}) %collective-permute-start.32) | collective-permute-done | bytes 2359328 | tf_op jit(solution)/shard_map/ppermute | solution.py:504
  160.9 1.9 %conditional.1 = (f32[2,2,192,768]{3,2,1,0:T(8,128)}) conditional(s32[]{:T(128)} %bitcast.8, (f32[2,2,1,192,768]{4,3,2,1,0:T(8,128)S(1)}, f32[2,2,1,192,768]{4,3,2,1,0:T(8,128)S(1)}) %tuple.21, (f32[4096,128]{1,0:T(8,128)}, s32[1,128]{1,0:T(1,128)S(1)}, f32[2,2,1,192,768]{4,3,2,1,0:T(8,128)S(1)}, f32[2,2,1,192,768]{4,3,2,1,0:T(8,128)S(1)}) %tuple.22), branch_computations={%region_0.0_spmd, %region_1.0_spmd} | conditional | flops 1181648 | bytes 31983656 | solution.py:669
  160.9 1.9 %add_up.2 = f32[2,2,1,192,768]{4,3,2,1,0:T(8,128)} custom-call(f32[2,2,1,192,768]{4,3,2,1,0:T(8,128)S(1)} %get-tuple-element.21.a, f32[2,2,1,192,768]{4,3,2,1,0:T(8,128)S(1)} %get-tuple-element.22.b), custom_call_target="tpu_custom_call" | custom-call | tf_op jit(solution)/shard_map/cond/branch_0_fun/add_up/pallas_call | solution.py:492
  (68 shorter events, 30.3 us)
Async XLA Ops:
  0.0 14.0 %copy-start = (bf16[2,2,2,256,256]{4,3,2,1,0:T(8,128)(2,1)S(1)}, bf16[2,2,2,256,256]{4,3,2,1,0:T(8,128)(2,1)}, u32[]{:S(2)}) copy-start(bf16[2,2,2,256,256]{4,3,2,1,0:T(8,128)(2,1)} %constant.5.clone.refs_0_) | copy-start | bytes 3145732
  0.0 14.0 %copy-start.1 = (f32[2,128,128]{2,1,0:T(8,128)S(1)}, f32[2,128,128]{2,1,0:T(8,128)}, u32[]{:S(2)}) copy-start(f32[2,128,128]{2,1,0:T(8,128)} %refs_2_.13) | copy-start | bytes 393220
  0.0 1.4 collective-permute-start.3
  1.4 9.6 %collective-permute-start.5 = (f32[2,2,384,768]{3,2,1,0:T(8,128)}, f32[2,2,384,768]{3,2,1,0:T(8,128)S(1)}, u32[]{:S(2)}, u32[]{:S(2)}) collective-permute-start(f32[2,2,384,768]{3,2,1,0:T(8,128)} %x), channel_id=1, source_target_pairs={{0,1},{1,0},{2,3},{3,2},{4,5},{5,4},{6,7},{7,6},{8,9},{9,8},{10,11... | collective-permute-start | bytes 14155784 | tf_op jit(solution)/shard_map/ppermute | solution.py:504
  1.7 4.3 %collective-permute-start.2 = (s32[16]{0:T(128)}, s32[16]{0:T(128)S(1)}, u32[]{:S(2)}, u32[]{:S(2)}) collective-permute-start(s32[16]{0:T(128)} %bitcast.14), channel_id=1, source_target_pairs={{0,2},{2,0},{1,3},{3,1},{4,6},{6,4},{5,7},{7,5},{8,10},{10,8},{9,1... | collective-permute-start | bytes 200 | tf_op jit(solution)/shard_map/ppermute | solution.py:504
  4.4 3.5 %collective-permute-start.4 = (s32[16]{0:T(128)S(1)}, s32[16]{0:T(128)S(1)}, u32[]{:S(2)}, u32[]{:S(2)}) collective-permute-start(s32[16]{0:T(128)S(1)} %collective-permute-done.3.refs_2_), channel_id=1, source_target_pairs={{0,2},{2,0},{1,3},{3,1},{4,6},{6,4},{5,7},{7,5},{8,10},{10,8},{9,1... | collective-permute-start | bytes 200 | tf_op jit(solution)/shard_map/ppermute | solution.py:504
  7.9 24.2 %collective-permute-start.8 = (f32[16,1,128,128]{3,2,1,0:T(8,128)}, f32[16,1,128,128]{3,2,1,0:T(8,128)S(1)}, u32[]{:S(2)}, u32[]{:S(2)}) collective-permute-start(f32[16,1,128,128]{3,2,1,0:T(8,128)} %param.12), channel_id=1, source_target_pairs={{12,14},{14,12},{13,15},{15,13},{28,30},{30,28},{29,31},{31,29}} | collective-permute-start | bytes 3145736 | tf_op jit(solution)/shard_map/ppermute | solution.py:590
  8.7 0.7 copy-start.2
  14.9 8.3 %collective-permute-start.6 = (f32[2,2,128,128]{3,2,1,0:T(8,128)S(1)}, f32[2,2,128,128]{3,2,1,0:T(8,128)S(1)}, u32[]{:S(2)}, u32[]{:S(2)}) collective-permute-start(f32[2,2,128,128]{3,2,1,0:T(8,128)S(1)} %get-tuple-element.94), channel_id=1, source_target_pairs={{0,4},{1,5},{2,6},{3,7},{16,20},{17,21},{18,22},{19,23}} | collective-permute-start | bytes 786440 | tf_op jit(solution)/shard_map/ppermute | solution.py:609
  22.1 8.1 %copy-start.3 = (f32[16,1,128,128]{3,2,1,0:T(8,128)S(1)}, f32[16,1,128,128]{3,2,1,0:T(8,128)}, u32[]{:S(2)}) copy-start(f32[16,1,128,128]{3,2,1,0:T(8,128)} %param.12) | copy-start | bytes 3145732
  24.2 9.3 %collective-permute-start.7 = (f32[2,2,128,128]{3,2,1,0:T(8,128)S(1)}, f32[2,2,128,128]{3,2,1,0:T(8,128)S(1)}, u32[]{:S(2)}, u32[]{:S(2)}) collective-permute-start(f32[2,2,128,128]{3,2,1,0:T(8,128)S(1)} %get-tuple-element.97), channel_id=1, source_target_pairs={{0,4},{4,8},{1,5},{5,9},{2,6},{6,10},{3,7},{7,11},{16,20},{20,24},... | collective-permute-start | bytes 786440 | tf_op jit(solution)/shard_map/ppermute | solution.py:609
  28.6 3.6 %collective-permute-start.9 = (s32[1,128]{1,0:T(1,128)S(1)}, s32[1,128]{1,0:T(1,128)S(1)}, u32[]{:S(2)}, u32[]{:S(2)}) collective-permute-start(s32[1,128]{1,0:T(1,128)S(1)} %sort_probes.1.refs_0_), channel_id=1, source_target_pairs={{0,16},{16,0},{1,17},{17,1},{2,18},{18,2},{3,19},{19,3},{4,20},{20... | collective-permute-start | bytes 1544 | tf_op jit(solution)/shard_map/ppermute | solution.py:504
  30.2 11.1 %collective-permute-start.10 = (f32[16,1,128,128]{3,2,1,0:T(8,128)S(1)}, f32[16,1,128,128]{3,2,1,0:T(8,128)S(1)}, u32[]{:S(2)}, u32[]{:S(2)}) collective-permute-start(f32[16,1,128,128]{3,2,1,0:T(8,128)S(1)} %copy-done.3), channel_id=1, source_target_pairs={{12,13},{13,12},{14,15},{15,14},{28,29},{29,28},{30,31},{31,30}} | collective-permute-start | bytes 3145736 | tf_op jit(solution)/shard_map/ppermute | solution.py:629
  33.4 7.8 %collective-permute-start.11 = (f32[16,1,128,128]{3,2,1,0:T(8,128)S(1)}, f32[16,1,128,128]{3,2,1,0:T(8,128)S(1)}, u32[]{:S(2)}, u32[]{:S(2)}) collective-permute-start(f32[16,1,128,128]{3,2,1,0:T(8,128)S(1)} %collective-permute-done.8), channel_id=1, source_target_pairs={{12,13},{13,12},{14,15},{15,14},{28,29},{29,28},{30,31},{31,30}} | collective-permute-start | bytes 3145736 | tf_op jit(solution)/shard_map/ppermute | solution.py:629
  35.1 8.4 %collective-permute-start.12 = (f32[2,2,128,128]{3,2,1,0:T(8,128)S(1)}, f32[2,2,128,128]{3,2,1,0:T(8,128)S(1)}, u32[]{:S(2)}, u32[]{:S(2)}) collective-permute-start(f32[2,2,128,128]{3,2,1,0:T(8,128)S(1)} %get-tuple-element.105), channel_id=1, source_target_pairs={{0,4},{4,8},{8,12},{1,5},{5,9},{9,13},{2,6},{6,10},{10,14},{3,7},{... | collective-permute-start | bytes 786440 | tf_op jit(solution)/shard_map/ppermute | solution.py:609
  44.4 8.3 %collective-permute-start.14 = (f32[2,2,128,128]{3,2,1,0:T(8,128)S(1)}, f32[2,2,128,128]{3,2,1,0:T(8,128)S(1)}, u32[]{:S(2)}, u32[]{:S(2)}) collective-permute-start(f32[2,2,128,128]{3,2,1,0:T(8,128)S(1)} %get-tuple-element.107.refs_1_), channel_id=1, source_target_pairs={{0,4},{4,8},{8,12},{1,5},{5,9},{9,13},{2,6},{6,10},{10,14},{3,7},{... | collective-permute-start | bytes 786440 | tf_op jit(solution)/shard_map/ppermute | solution.py:609
  48.8 13.6 %collective-permute-start.13 = (f32[2,2,128,128]{3,2,1,0:T(8,128)S(1)}, f32[2,2,128,128]{3,2,1,0:T(8,128)S(1)}, u32[]{:S(2)}, u32[]{:S(2)}) collective-permute-start(f32[2,2,128,128]{3,2,1,0:T(8,128)S(1)} %get-tuple-element.109), channel_id=1, source_target_pairs={{12,8},{13,9},{14,10},{15,11},{28,24},{29,25},{30,26},{31,27}} | collective-permute-start | bytes 786440 | tf_op jit(solution)/shard_map/ppermute | solution.py:609
  53.6 10.8 %collective-permute-start.16 = (f32[2,2,128,128]{3,2,1,0:T(8,128)S(1)}, f32[2,2,128,128]{3,2,1,0:T(8,128)S(1)}, u32[]{:S(2)}, u32[]{:S(2)}) collective-permute-start(f32[2,2,128,128]{3,2,1,0:T(8,128)S(1)} %get-tuple-element.111.refs_2_), channel_id=1, source_target_pairs={{0,4},{4,8},{8,12},{1,5},{5,9},{9,13},{2,6},{6,10},{10,14},{3,7},{... | collective-permute-start | bytes 786440 | tf_op jit(solution)/shard_map/ppermute | solution.py:609
  62.5 7.3 %collective-permute-start.15 = (f32[2,2,128,128]{3,2,1,0:T(8,128)S(1)}, f32[2,2,128,128]{3,2,1,0:T(8,128)S(1)}, u32[]{:S(2)}, u32[]{:S(2)}) collective-permute-start(f32[2,2,128,128]{3,2,1,0:T(8,128)S(1)} %get-tuple-element.113), channel_id=1, source_target_pairs={{8,4},{12,8},{9,5},{13,9},{10,6},{14,10},{11,7},{15,11},{24,20},{2... | collective-permute-start | bytes 786440 | tf_op jit(solution)/shard_map/ppermute | solution.py:609
  65.4 8.3 %collective-permute-start.18 = (f32[2,2,128,128]{3,2,1,0:T(8,128)S(1)}, f32[2,2,128,128]{3,2,1,0:T(8,128)S(1)}, u32[]{:S(2)}, u32[]{:S(2)}) collective-permute-start(f32[2,2,128,128]{3,2,1,0:T(8,128)S(1)} %get-tuple-element.115.refs_2_), channel_id=1, source_target_pairs={{0,4},{4,8},{8,12},{1,5},{5,9},{9,13},{2,6},{6,10},{10,14},{3,7},{... | collective-permute-start | bytes 786440 | tf_op jit(solution)/shard_map/ppermute | solution.py:609
  70.0 10.8 %collective-permute-start.17 = (f32[2,2,128,128]{3,2,1,0:T(8,128)S(1)}, f32[2,2,128,128]{3,2,1,0:T(8,128)S(1)}, u32[]{:S(2)}, u32[]{:S(2)}) collective-permute-start(f32[2,2,128,128]{3,2,1,0:T(8,128)S(1)} %get-tuple-element.117), channel_id=1, source_target_pairs={{4,0},{8,4},{12,8},{5,1},{9,5},{13,9},{6,2},{10,6},{14,10},{7,3},{... | collective-permute-start | bytes 786440 | tf_op jit(solution)/shard_map/ppermute | solution.py:609
  74.6 9.7 %collective-permute-start.20 = (f32[2,2,128,128]{3,2,1,0:T(8,128)S(1)}, f32[2,2,128,128]{3,2,1,0:T(8,128)S(1)}, u32[]{:S(2)}, u32[]{:S(2)}) collective-permute-start(f32[2,2,128,128]{3,2,1,0:T(8,128)S(1)} %get-tuple-element.119.refs_2_), channel_id=1, source_target_pairs={{0,4},{4,8},{8,12},{1,5},{5,9},{9,13},{2,6},{6,10},{10,14},{3,7},{... | collective-permute-start | bytes 786440 | tf_op jit(solution)/shard_map/ppermute | solution.py:609
  81.7 8.3 %collective-permute-start.19 = (f32[2,2,128,128]{3,2,1,0:T(8,128)S(1)}, f32[2,2,128,128]{3,2,1,0:T(8,128)S(1)}, u32[]{:S(2)}, u32[]{:S(2)}) collective-permute-start(f32[2,2,128,128]{3,2,1,0:T(8,128)S(1)} %get-tuple-element.121), channel_id=1, source_target_pairs={{4,0},{8,4},{12,8},{5,1},{9,5},{13,9},{6,2},{10,6},{14,10},{7,3},{... | collective-permute-start | bytes 786440 | tf_op jit(solution)/shard_map/ppermute | solution.py:609
  85.2 8.7 %collective-permute-start.22 = (f32[2,2,128,128]{3,2,1,0:T(8,128)S(1)}, f32[2,2,128,128]{3,2,1,0:T(8,128)S(1)}, u32[]{:S(2)}, u32[]{:S(2)}) collective-permute-start(f32[2,2,128,128]{3,2,1,0:T(8,128)S(1)} %get-tuple-element.123.refs_2_), channel_id=1, source_target_pairs={{0,4},{4,8},{8,12},{1,5},{5,9},{9,13},{2,6},{6,10},{10,14},{3,7},{... | collective-permute-start | bytes 786440 | tf_op jit(solution)/shard_map/ppermute | solution.py:609
  90.9 8.3 %collective-permute-start.21 = (f32[2,2,128,128]{3,2,1,0:T(8,128)S(1)}, f32[2,2,128,128]{3,2,1,0:T(8,128)S(1)}, u32[]{:S(2)}, u32[]{:S(2)}) collective-permute-start(f32[2,2,128,128]{3,2,1,0:T(8,128)S(1)} %get-tuple-element.125), channel_id=1, source_target_pairs={{4,0},{8,4},{12,8},{5,1},{9,5},{13,9},{6,2},{10,6},{14,10},{7,3},{... | collective-permute-start | bytes 786440 | tf_op jit(solution)/shard_map/ppermute | solution.py:609
  92.2 29.1 %collective-permute-start.28 = (f32[2048,128]{1,0:T(8,128)S(1)}, f32[2048,128]{1,0:T(8,128)S(1)}, u32[]{:S(2)}, u32[]{:S(2)}) collective-permute-start(f32[2048,128]{1,0:T(8,128)S(1)} %slice.10), channel_id=1, source_target_pairs={{0,2},{2,0},{1,3},{3,1},{4,6},{6,4},{5,7},{7,5},{8,10},{10,8},{9,1... | collective-permute-start | bytes 3145736 | tf_op jit(solution)/shard_map/ppermute | solution.py:504
  93.9 8.5 %collective-permute-start.24 = (f32[2,2,128,128]{3,2,1,0:T(8,128)S(1)}, f32[2,2,128,128]{3,2,1,0:T(8,128)S(1)}, u32[]{:S(2)}, u32[]{:S(2)}) collective-permute-start(f32[2,2,128,128]{3,2,1,0:T(8,128)S(1)} %get-tuple-element.127.refs_2_), channel_id=1, source_target_pairs={{4,8},{8,12},{5,9},{9,13},{6,10},{10,14},{7,11},{11,15},{20,24},{2... | collective-permute-start | bytes 786440 | tf_op jit(solution)/shard_map/ppermute | solution.py:609
  100.0 8.7 %collective-permute-start.23 = (f32[2,2,128,128]{3,2,1,0:T(8,128)S(1)}, f32[2,2,128,128]{3,2,1,0:T(8,128)S(1)}, u32[]{:S(2)}, u32[]{:S(2)}) collective-permute-start(f32[2,2,128,128]{3,2,1,0:T(8,128)S(1)} %get-tuple-element.129), channel_id=1, source_target_pairs={{4,0},{8,4},{12,8},{5,1},{9,5},{13,9},{6,2},{10,6},{14,10},{7,3},{... | collective-permute-start | bytes 786440 | tf_op jit(solution)/shard_map/ppermute | solution.py:609
  102.5 11.2 %collective-permute-start.26 = (f32[2,2,128,128]{3,2,1,0:T(8,128)S(1)}, f32[2,2,128,128]{3,2,1,0:T(8,128)S(1)}, u32[]{:S(2)}, u32[]{:S(2)}) collective-permute-start(f32[2,2,128,128]{3,2,1,0:T(8,128)S(1)} %get-tuple-element.131.refs_2_), channel_id=1, source_target_pairs={{8,12},{9,13},{10,14},{11,15},{24,28},{25,29},{26,30},{27,31}} | collective-permute-start | bytes 786440 | tf_op jit(solution)/shard_map/ppermute | solution.py:609
  109.7 9.5 %collective-permute-start.25 = (f32[2,2,128,128]{3,2,1,0:T(8,128)S(1)}, f32[2,2,128,128]{3,2,1,0:T(8,128)S(1)}, u32[]{:S(2)}, u32[]{:S(2)}) collective-permute-start(f32[2,2,128,128]{3,2,1,0:T(8,128)S(1)} %get-tuple-element.133), channel_id=1, source_target_pairs={{4,0},{8,4},{12,8},{5,1},{9,5},{13,9},{6,2},{10,6},{14,10},{7,3},{... | collective-permute-start | bytes 786440 | tf_op jit(solution)/shard_map/ppermute | solution.py:609
  111.1 33.7 %collective-permute-start.31 = (f32[2048,128]{1,0:T(8,128)S(1)}, f32[2048,128]{1,0:T(8,128)S(1)}, u32[]{:S(2)}, u32[]{:S(2)}) collective-permute-start(f32[2048,128]{1,0:T(8,128)S(1)} %slice.11), channel_id=1, source_target_pairs={{0,2},{2,0},{1,3},{3,1},{4,6},{6,4},{5,7},{7,5},{8,10},{10,8},{9,1... | collective-permute-start | bytes 3145736 | tf_op jit(solution)/shard_map/ppermute | solution.py:504
  120.1 10.3 %collective-permute-start.27 = (f32[2,2,128,128]{3,2,1,0:T(8,128)S(1)}, f32[2,2,128,128]{3,2,1,0:T(8,128)S(1)}, u32[]{:S(2)}, u32[]{:S(2)}) collective-permute-start(f32[2,2,128,128]{3,2,1,0:T(8,128)S(1)} %get-tuple-element.137), channel_id=1, source_target_pairs={{4,0},{8,4},{12,8},{5,1},{9,5},{13,9},{6,2},{10,6},{14,10},{7,3},{... | collective-permute-start | bytes 786440 | tf_op jit(solution)/shard_map/ppermute | solution.py:609
  131.3 11.2 %collective-permute-start.29 = (f32[2,2,128,128]{3,2,1,0:T(8,128)S(1)}, f32[2,2,128,128]{3,2,1,0:T(8,128)S(1)}, u32[]{:S(2)}, u32[]{:S(2)}) collective-permute-start(f32[2,2,128,128]{3,2,1,0:T(8,128)S(1)} %get-tuple-element.139), channel_id=1, source_target_pairs={{4,0},{8,4},{5,1},{9,5},{6,2},{10,6},{7,3},{11,7},{20,16},{24,20},... | collective-permute-start | bytes 786440 | tf_op jit(solution)/shard_map/ppermute | solution.py:609
  143.5 8.3 %collective-permute-start.30 = (f32[2,2,128,128]{3,2,1,0:T(8,128)S(1)}, f32[2,2,128,128]{3,2,1,0:T(8,128)S(1)}, u32[]{:S(2)}, u32[]{:S(2)}) collective-permute-start(f32[2,2,128,128]{3,2,1,0:T(8,128)S(1)} %get-tuple-element.141), channel_id=1, source_target_pairs={{4,0},{5,1},{6,2},{7,3},{20,16},{21,17},{22,18},{23,19}} | collective-permute-start | bytes 786440 | tf_op jit(solution)/shard_map/ppermute | solution.py:609
  156.3 4.6 %collective-permute-start.32 = (f32[2,2,1,192,768]{4,3,2,1,0:T(8,128)S(1)}, f32[2,2,1,192,768]{4,3,2,1,0:T(8,128)S(1)}, u32[]{:S(2)}, u32[]{:S(2)}) collective-permute-start(f32[2,2,1,192,768]{4,3,2,1,0:T(8,128)S(1)} %get-tuple-element.145), channel_id=1, source_target_pairs={{0,1},{1,0},{2,3},{3,2},{4,5},{5,4},{6,7},{7,6},{8,9},{9,8},{10,11... | collective-permute-start | bytes 7077896 | tf_op jit(solution)/shard_map/ppermute | solution.py:504

commit v7 on v3

--- a/solution.py
+++ b/solution.py
@@ -338,11 +338,11 @@
     )
 
 
-def run_backward(lay, tick, sections, tables, state, arrived, own):
+def run_backward(lay, tick, sections, tables, state, arrived, own, passes_on=True):
     def body(tables, *refs):
         arrived_ref = refs[0] if arrived is not None else None
         own_ref = refs[1 if arrived is not None else 0] if own is not None else None
-        state, leave = refs[-2:]
+        state, leave = refs[-2:] if passes_on else (refs[-1], None)
         section = lax.axis_index("depth")
         group = tick - (2 * (sections - 1) - section)
         final = (section == sections - 1).astype(jnp.int32)
@@ -368,7 +368,7 @@
                     state[lay.grad(group, i, layer, 0), :] = real
                     state[lay.grad(group, i, layer, 1), :] = imag
                     wave.append(times_conj(chi[i], pair(state, functools.partial(lay.patch, group, i, layer))))
-            for i in range(lay.count):
+            for i in range(lay.count if passes_on else 0):
                 leave[i, 0] = wave[i][0]
                 leave[i, 1] = wave[i][1]
 
@@ -378,7 +378,7 @@
         body,
         state,
         [("vmem", tables), *waves],
-        [(lay.count, 2, lay.pixels, lay.pixels)],
+        [(lay.count, 2, lay.pixels, lay.pixels)] * passes_on,
         name="backward_section",
         **section_cost(lay),
     )
@@ -442,62 +442,70 @@
     )[0]
 
 
-def split_rows(lay, state, owners, taken=(0, 8)):
+def split_rows(lay, state, owners, others, taken=None):
     rows = lay.rows // (2 * owners)
-    pieces = 4 * owners * lay.layers * lay.blocks
-
-    def body(state, keep, send, rest, sems):
-        lat = lax.axis_index("lat")
-        copies = [pltpu.make_async_copy(state.at[pl.ds(taken[0], taken[1] - taken[0]), :], rest, sems.at[pieces])]
+    pieces = 2 * owners * lay.layers * lay.blocks
+    half = pltpu.VMEM((2, lay.layers, owners, rows, lay.width), F32)
+    aside = [pltpu.HBM((taken[1] - taken[0], lay.pixels), F32)] if taken else []
+
+    def body(state, target, *refs):
+        sems = refs[-1]
+        core = lax.axis_index("lat")
+        core = 1 - core if others else core
+        copies = []
         for owner in range(owners):
-            for kind, target in ((lat, keep), (1 - lat, send)):
-                for part in range(2):
-                    for layer in range(lay.layers):
-                        for block in range(lay.blocks):
-                            start = lay.total(part, layer, block, lay.tall + (2 * owner + kind) * rows)
-                            copies.append(
-                                pltpu.make_async_copy(
-                                    state.at[pl.ds(pl.multiple_of(start, 8), rows), :],
-                                    target.at[part, layer, owner, :, pl.ds(block * lay.pixels, lay.pixels)],
-                                    sems.at[len(copies) - 1],
-                                )
+            for part in range(2):
+                for layer in range(lay.layers):
+                    for block in range(lay.blocks):
+                        start = lay.total(part, layer, block, lay.tall + (2 * owner + core) * rows)
+                        copies.append(
+                            pltpu.make_async_copy(
+                                state.at[pl.ds(pl.multiple_of(start, 8), rows), :],
+                                target.at[part, layer, owner, :, pl.ds(block * lay.pixels, lay.pixels)],
+                                sems.at[len(copies)],
                             )
+                        )
+        if taken:
+            rest = state.at[pl.ds(taken[0], taken[1] - taken[0]), :]
+            copies.append(pltpu.make_async_copy(rest, refs[0], sems.at[pieces]))
         for copy in copies:
             copy.start()
         for copy in copies:
             copy.wait()
 
-    half = (2, lay.layers, owners, rows, lay.width)
     return pl.pallas_call(
         body,
         in_specs=[VMEM],
-        out_specs=[VMEM, VMEM, HBM],
-        out_shape=[
-            pltpu.VMEM(half, F32),
-            pltpu.VMEM(half, F32),
-            pltpu.HBM((taken[1] - taken[0], lay.pixels), F32),
-        ],
+        out_specs=[VMEM] + [HBM] * len(aside),
+        out_shape=[half, *aside],
         scratch_shapes=[pltpu.SemaphoreType.DMA((pieces + 1,))],
         compiler_params=pltpu.CompilerParams(vmem_limit_bytes=SCOPED),
+        cost_estimate=pl.CostEstimate(flops=1000, bytes_accessed=1000, transcendentals=0),
         name="split_rows",
     )(in_vmem(state))
 
 
 def add_up(a, b):
-    each = pl.BlockSpec((1, 1, *a.shape[2:]), lambda i, j: (i, j, 0, 0, 0))
-
-    def body(a, b, out):
-        out[...] = a[...] + b[...]
+    pieces = [(i, j) for i in range(a.shape[0]) for j in range(a.shape[1])]
+
+    def body(a, b, out, total, sems):
+        copies = []
+        for n, (i, j) in enumerate(pieces):
+            total[i, j] = a[i, j] + b[i, j]
+            copies.append(pltpu.make_async_copy(total.at[i, j], out.at[i, j], sems.at[n]))
+            copies[-1].start()
+        for copy in copies:
+            copy.wait()
 
     return pl.pallas_call(
         body,
-        grid=a.shape[:2],
-        in_specs=[each, each],
-        out_specs=each,
+        in_specs=[VMEM, VMEM],
+        out_specs=HBM,
         out_shape=pltpu.HBM(a.shape, F32),
+        scratch_shapes=[pltpu.VMEM(a.shape, F32), pltpu.SemaphoreType.DMA((len(pieces),))],
         compiler_params=pltpu.CompilerParams(vmem_limit_bytes=SCOPED),
         name="add_up",
-    )(a, b)
+    )(in_vmem(a), in_vmem(b))
 
 
 def swap(shard, axis):
@@ -642,8 +650,8 @@
                 pools = [frames, mine, *crossed] if paired else [frames]
                 state, late = place_frames(lay, sections, info, everyone, pools, state)
         if tick >= fill:
-            state, rising = run_backward(lay, tick, sections, tables, state, up, own)
-            up = pass_on(rising, tick, -1)
+            state, *rising = run_backward(lay, tick, sections, tables, state, up, own, tick < last_tick)
+            up = pass_on(rising[0], tick, -1) if rising else None
             received = crossing.pop(tick, [])
             for begin, end in parts:
                 if tick == end - 1 + 2 * fill:
@@ -651,10 +659,14 @@
                     crossing.setdefault(due, []).append((begin, 1, swap(grads_of(state, begin, end), "probe")))
             state = deposit(lay, tick, sections, info, received, state)
     if not paired:
-        keep, send, _ = split_rows(lay, state, owners)
+        send, = split_rows(lay, state, owners, True)
+        keep, = split_rows(lay, state, owners, False)
         return lax.psum_scatter(keep + swap(send, "lat"), "probe", scatter_dimension=2, tiled=False)
 
-    keep, send, late_grads = split_rows(lay, state, 1, lay.grads_of(early, lay.groups))
+    send, = split_rows(lay, state, 1, True)
+    send, state = lax.optimization_barrier((send, state))
+    received = swap(send, "lat")
+    keep, late_grads = split_rows(lay, state, 1, False, lay.grads_of(early, lay.groups))
 
     def as_they_are(keep, received, grads):
         return add_up(keep, received)
@@ -663,10 +675,11 @@
         sums = Layout(probes, count, layers, pixels, half, height, width, only_sums=True)
         state = clear_total(sums, None)
         state = deposit(sums, None, sections, info, [(early, 1, swap(grads, "probe"))], state)
-        more, send, _ = split_rows(sums, state, 1)
+        send, = split_rows(sums, state, 1, True)
+        more, = split_rows(sums, state, 1, False)
         return add_up(keep + more, received + swap(send, "lat"))
 
-    result = lax.cond(late[0, 0] > 0, with_partners, as_they_are, keep, swap(send, "lat"), late_grads)
+    result = lax.cond(late[0, 0] > 0, with_partners, as_they_are, keep, received, late_grads)
     return result[:, :, 0]
 
 

time: 162 us -> 160 us (0.988)
  starting transfers between devices: 61.4 us -> 58.6 us
    ppermute x20, waiting for transfers between devices: 44.2 us -> 46.8 us  [pass_on(): return lax.ppermute(wave, 'depth', pairs) if pairs else None]
    ppermute x20, starting transfers between devices: 50.9 us -> 49.1 us  [pass_on(): return lax.ppermute(wave, 'depth', pairs) if pairs else None]
    pallas_call x2 -> x3, Pallas kernels: 3.81 us -> 3.73 us  [the longest x2 2.24 us: split_rows(): pl.pallas_call(body, in_specs=[VMEM], out_specs=[VMEM] + [HBM] * len(asid...]
  transfers between devices with their start and end apart: 31 -> 31, of which waited for: 19 -> 20; matrix products, arithmetic and copies ran while one was open for 0% -> 0% of each run, Pallas kernels for 23% -> 24%
where the time goes in v7:
time: 160 us; the launch traced here: 159 us
  starting transfers between devices  58.6 us (37%)
  waiting for transfers between devices  55.3 us (35%)
  Pallas kernels  43.8 us (27%)
    ppermute x20, starting transfers between devices, pass_on(): return lax.ppermute(wave, 'depth', pairs) if pairs else None  49.1 us
    ppermute x20, waiting for transfers between devices, pass_on(): return lax.ppermute(wave, 'depth', pairs) if pairs else None  46.8 us
    pallas_call x39, Pallas kernels, call(): pl.pallas_call(kernel, in_specs=specs, out_specs=[VMEM] * (1 + len(outs)...  36.1 us
    ppermute x8, waiting for transfers between devices, swap(): return lax.ppermute(shard, axis, [(0, 1), (1, 0)])  8.46 us
    ppermute x8, starting transfers between devices, swap(): return lax.ppermute(shard, axis, [(0, 1), (1, 0)])  7.3 us
  transfers between devices with their start and end apart: 31, of which 20 were waited for; matrix products, arithmetic and copies ran while one was open for 0% of the time, Pallas kernels for 24%

profile of v7, /device:TPU:0, one launch (start us, length us, event | category | flops | bytes accessed | tf_op | source)
XLA Modules:
  0.0 159.4 jit_solution(12262820350273346331)
XLA Ops:
  1.7 2.7 %collective-permute-start.2 = (s32[16]{0:T(128)}, s32[16]{0:T(128)S(1)}, u32[]{:S(2)}, u32[]{:S(2)}) collective-permute-start(s32[16]{0:T(128)} %bitcast.14), channel_id=1, source_target_pairs={{0,2},{2,0},{1,3},{3,1},{4,6},{6,4},{5,7},{7,5},{8,10},{10,8},{9,1... | collective-permute-start | bytes 200 | tf_op jit(solution)/shard_map/ppermute | solution.py:512
  4.4 1.6 %collective-permute-done.2.refs_1_ = s32[16]{0:T(128)S(1)} collective-permute-done((s32[16]{0:T(128)}, s32[16]{0:T(128)S(1)}, u32[]{:S(2)}, u32[]{:S(2)}) %collective-permute-start.2) | collective-permute-done | bytes 96 | tf_op jit(solution)/shard_map/ppermute | solution.py:512
  6.1 1.9 %collective-permute-done.4.refs_3_ = s32[16]{0:T(128)S(1)} collective-permute-done((s32[16]{0:T(128)S(1)}, s32[16]{0:T(128)S(1)}, u32[]{:S(2)}, u32[]{:S(2)}) %collective-permute-start.4) | collective-permute-done | bytes 96 | tf_op jit(solution)/shard_map/ppermute | solution.py:512
  9.3 1.7 %sort_probes.1.refs_0_ = s32[1,128]{1,0:T(1,128)S(1)} custom-call(s32[2,512]{1,0:T(2,128)} %bitcast.20, s32[16]{0:T(128)S(1)} %bitcast.15, s32[16]{0:T(128)S(1)} %collective-permute-done.2.refs_1_, s32[16]{0:T(128)S(1)} %collective-permute-done.3.refs_2_, s32[16]{0:T(128)S(1)} %collective-permute-done.4.refs_3_), custom_call_target="tpu_custom_call" | custom-call | tf_op jit(solution)/shard_map/sort_probes/pallas_call | solution.py:546
  11.0 2.9 %cut_patches.4.refs_2_ = f32[42368,128]{1,0:T(8,128)S(1)} custom-call(s32[1,128]{1,0:T(1,128)S(1)} %sort_probes.1.refs_0_, f32[2,2,384,768]{3,2,1,0:T(8,128)} %x, f32[2,2,384,768]{3,2,1,0:T(8,128)S(1)} %collective-permute-done.5.refs_2_), custom_call_target="tpu_custom_call" | custom-call | flops 1000 | bytes 1000 | tf_op jit(solution)/shard_map/cut_patches/pallas_call | solution.py:157
  14.9 2.6 %collective-permute-start.6 = (f32[2,2,128,128]{3,2,1,0:T(8,128)S(1)}, f32[2,2,128,128]{3,2,1,0:T(8,128)S(1)}, u32[]{:S(2)}, u32[]{:S(2)}) collective-permute-start(f32[2,2,128,128]{3,2,1,0:T(8,128)S(1)} %get-tuple-element.92), channel_id=1, source_target_pairs={{0,4},{1,5},{2,6},{3,7},{16,20},{17,21},{18,22},{19,23}} | collective-permute-start | bytes 786440 | tf_op jit(solution)/shard_map/ppermute | solution.py:617
  17.5 2.3 %bring.1.refs_1_ = f32[2,2,384,768]{3,2,1,0:T(8,128)S(1)} custom-call(f32[2,2,384,768]{3,2,1,0:T(8,128)} %x), custom_call_target="tpu_custom_call" | custom-call | flops 1000 | bytes 1000 | tf_op jit(solution)/shard_map/bring/pallas_call | solution.py:563
  19.9 1.8 %cut_patches.5.refs_0_ = f32[42368,128]{1,0:T(8,128)S(1)} custom-call(s32[1,128]{1,0:T(1,128)S(1)} %sort_probes.1.refs_0_, f32[2,2,384,768]{3,2,1,0:T(8,128)S(1)} %bring.1.refs_1_, f32[2,2,384,768]{3,2,1,0:T(8,128)S(1)} %collective-permute-done.5.refs_2_, f32[42368,128]{1,0:T(8,128)S(1)} %get-tuple-element.94.refs_3_), custom_call_target="tpu_custom_call", output_to_operand_aliasing={{}: (3, {})} | custom-call | flops 1000 | bytes 1000 | tf_op jit(solution)/shard_map/cut_patches/pallas_call | solution.py:157
  24.2 4.4 %collective-permute-start.7 = (f32[2,2,128,128]{3,2,1,0:T(8,128)S(1)}, f32[2,2,128,128]{3,2,1,0:T(8,128)S(1)}, u32[]{:S(2)}, u32[]{:S(2)}) collective-permute-start(f32[2,2,128,128]{3,2,1,0:T(8,128)S(1)} %get-tuple-element.95), channel_id=1, source_target_pairs={{0,4},{4,8},{1,5},{5,9},{2,6},{6,10},{3,7},{7,11},{16,20},{20,24},... | collective-permute-start | bytes 786440 | tf_op jit(solution)/shard_map/ppermute | solution.py:617
  28.6 1.6 collective-permute-start.9
  30.9 1.3 collective-permute-done.9.refs_1_
  32.2 1.3 collective-permute-done.7.refs_1_
  35.1 4.4 %collective-permute-start.12 = (f32[2,2,128,128]{3,2,1,0:T(8,128)S(1)}, f32[2,2,128,128]{3,2,1,0:T(8,128)S(1)}, u32[]{:S(2)}, u32[]{:S(2)}) collective-permute-start(f32[2,2,128,128]{3,2,1,0:T(8,128)S(1)} %get-tuple-element.103), channel_id=1, source_target_pairs={{0,4},{4,8},{8,12},{1,5},{5,9},{9,13},{2,6},{6,10},{10,14},{3,7},{... | collective-permute-start | bytes 786440 | tf_op jit(solution)/shard_map/ppermute | solution.py:617
  39.5 1.7 %cut_patches.6.refs_6_ = f32[42368,128]{1,0:T(8,128)S(1)} custom-call(s32[1,128]{1,0:T(1,128)S(1)} %sort_probes.1.refs_0_, f32[2,2,384,768]{3,2,1,0:T(8,128)S(1)} %bring.1.refs_1_, f32[2,2,384,768]{3,2,1,0:T(8,128)S(1)} %collective-permute-done.5.refs_2_, f32[42368,128]{1,0:T(8,128)S(1)} %get-tuple-element.101.refs_3_), custom_call_target="tpu_custom_call", output_to_operand_aliasing={{}: (3, {})} | custom-call | flops 1000 | bytes 1000 | tf_op jit(solution)/shard_map/cut_patches/pallas_call | solution.py:157
  42.0 1.5 collective-permute-done.12.refs_1_
  44.4 4.4 %collective-permute-start.14 = (f32[2,2,128,128]{3,2,1,0:T(8,128)S(1)}, f32[2,2,128,128]{3,2,1,0:T(8,128)S(1)}, u32[]{:S(2)}, u32[]{:S(2)}) collective-permute-start(f32[2,2,128,128]{3,2,1,0:T(8,128)S(1)} %get-tuple-element.105.refs_1_), channel_id=1, source_target_pairs={{0,4},{4,8},{8,12},{1,5},{5,9},{9,13},{2,6},{6,10},{10,14},{3,7},{... | collective-permute-start | bytes 786440 | tf_op jit(solution)/shard_map/ppermute | solution.py:617
  48.8 2.5 %cut_patches.7.refs_2_ = f32[42368,128]{1,0:T(8,128)S(1)} custom-call(s32[1,128]{1,0:T(1,128)S(1)} %sort_probes.1.refs_0_, f32[2,2,384,768]{3,2,1,0:T(8,128)S(1)} %bring.1.refs_1_, f32[2,2,384,768]{3,2,1,0:T(8,128)S(1)} %collective-permute-done.5.refs_2_, f32[42368,128]{1,0:T(8,128)S(1)} %get-tuple-element.106.refs_3_), custom_call_target="tpu_custom_call", output_to_operand_aliasing={{}: (3, {})} | custom-call | flops 1000 | bytes 1000 | tf_op jit(solution)/shard_map/cut_patches/pallas_call | solution.py:157
  53.6 6.3 %collective-permute-start.16 = (f32[2,2,128,128]{3,2,1,0:T(8,128)S(1)}, f32[2,2,128,128]{3,2,1,0:T(8,128)S(1)}, u32[]{:S(2)}, u32[]{:S(2)}) collective-permute-start(f32[2,2,128,128]{3,2,1,0:T(8,128)S(1)} %get-tuple-element.109.refs_2_), channel_id=1, source_target_pairs={{0,4},{4,8},{8,12},{1,5},{5,9},{9,13},{2,6},{6,10},{10,14},{3,7},{... | collective-permute-start | bytes 786440 | tf_op jit(solution)/shard_map/ppermute | solution.py:617
  60.9 3.5 %collective-permute-done.16.refs_1_ = f32[2,2,128,128]{3,2,1,0:T(8,128)S(1)} collective-permute-done((f32[2,2,128,128]{3,2,1,0:T(8,128)S(1)}, f32[2,2,128,128]{3,2,1,0:T(8,128)S(1)}, u32[]{:S(2)}, u32[]{:S(2)}) %collective-permute-start.16) | collective-permute-done | bytes 262176 | tf_op jit(solution)/shard_map/ppermute | solution.py:617
  65.4 4.4 %collective-permute-start.18 = (f32[2,2,128,128]{3,2,1,0:T(8,128)S(1)}, f32[2,2,128,128]{3,2,1,0:T(8,128)S(1)}, u32[]{:S(2)}, u32[]{:S(2)}) collective-permute-start(f32[2,2,128,128]{3,2,1,0:T(8,128)S(1)} %get-tuple-element.113.refs_2_), channel_id=1, source_target_pairs={{0,4},{4,8},{8,12},{1,5},{5,9},{9,13},{2,6},{6,10},{10,14},{3,7},{... | collective-permute-start | bytes 786440 | tf_op jit(solution)/shard_map/ppermute | solution.py:617
  70.0 1.3 collective-permute-start.17
  71.6 2.0 %collective-permute-done.18.refs_1_ = f32[2,2,128,128]{3,2,1,0:T(8,128)S(1)} collective-permute-done((f32[2,2,128,128]{3,2,1,0:T(8,128)S(1)}, f32[2,2,128,128]{3,2,1,0:T(8,128)S(1)}, u32[]{:S(2)}, u32[]{:S(2)}) %collective-permute-start.18) | collective-permute-done | bytes 262176 | tf_op jit(solution)/shard_map/ppermute | solution.py:617
  74.6 5.0 %collective-permute-start.20 = (f32[2,2,128,128]{3,2,1,0:T(8,128)S(1)}, f32[2,2,128,128]{3,2,1,0:T(8,128)S(1)}, u32[]{:S(2)}, u32[]{:S(2)}) collective-permute-start(f32[2,2,128,128]{3,2,1,0:T(8,128)S(1)} %get-tuple-element.117.refs_2_), channel_id=1, source_target_pairs={{0,4},{4,8},{8,12},{1,5},{5,9},{9,13},{2,6},{6,10},{10,14},{3,7},{... | collective-permute-start | bytes 786440 | tf_op jit(solution)/shard_map/ppermute | solution.py:617
  80.8 1.3 collective-permute-start.19
  82.1 1.1 deposit_patches.16.refs_3_
  84.3 4.6 %collective-permute-start.22 = (f32[2,2,128,128]{3,2,1,0:T(8,128)S(1)}, f32[2,2,128,128]{3,2,1,0:T(8,128)S(1)}, u32[]{:S(2)}, u32[]{:S(2)}) collective-permute-start(f32[2,2,128,128]{3,2,1,0:T(8,128)S(1)} %get-tuple-element.121.refs_2_), channel_id=1, source_target_pairs={{0,4},{4,8},{8,12},{1,5},{5,9},{9,13},{2,6},{6,10},{10,14},{3,7},{... | collective-permute-start | bytes 786440 | tf_op jit(solution)/shard_map/ppermute | solution.py:617
  90.2 1.3 collective-permute-start.21
  93.9 4.5 %collective-permute-done.21.refs_1_ = f32[2,2,128,128]{3,2,1,0:T(8,128)S(1)} collective-permute-done((f32[2,2,128,128]{3,2,1,0:T(8,128)S(1)}, f32[2,2,128,128]{3,2,1,0:T(8,128)S(1)}, u32[]{:S(2)}, u32[]{:S(2)}) %collective-permute-start.21) | collective-permute-done | bytes 262176 | tf_op jit(solution)/shard_map/ppermute | solution.py:617
  99.4 1.3 collective-permute-start.23
  100.7 1.1 deposit_patches.18.refs_2_
  102.5 5.5 %collective-permute-done.23.refs_1_ = f32[2,2,128,128]{3,2,1,0:T(8,128)S(1)} collective-permute-done((f32[2,2,128,128]{3,2,1,0:T(8,128)S(1)}, f32[2,2,128,128]{3,2,1,0:T(8,128)S(1)}, u32[]{:S(2)}, u32[]{:S(2)}) %collective-permute-start.23) | collective-permute-done | bytes 262176 | tf_op jit(solution)/shard_map/ppermute | solution.py:617
  108.9 1.3 collective-permute-start.25
  110.2 1.6 collective-permute-start.31
  112.9 4.9 %collective-permute-done.25.refs_1_ = f32[2,2,128,128]{3,2,1,0:T(8,128)S(1)} collective-permute-done((f32[2,2,128,128]{3,2,1,0:T(8,128)S(1)}, f32[2,2,128,128]{3,2,1,0:T(8,128)S(1)}, u32[]{:S(2)}, u32[]{:S(2)}) %collective-permute-start.25) | collective-permute-done | bytes 262176 | tf_op jit(solution)/shard_map/ppermute | solution.py:617
  118.7 1.3 collective-permute-start.27
  120.0 2.0 %deposit_patches.20.refs_2_ = f32[42368,128]{1,0:T(8,128)S(1)} custom-call(s32[1,128]{1,0:T(1,128)S(1)} %sort_probes.1.refs_0_, f32[2048,128]{1,0:T(8,128)S(1)} %collective-permute-done.28.refs_1_, f32[42368,128]{1,0:T(8,128)S(1)} %get-tuple-element.136.refs_2_), custom_call_target="tpu_custom_call", output_to_operand_aliasing={{}: (2, {})} | custom-call | flops 1000 | bytes 1000 | tf_op jit(solution)/shard_map/deposit_patches/pallas_call | solution.py:157
  122.0 6.9 %collective-permute-done.27.refs_1_ = f32[2,2,128,128]{3,2,1,0:T(8,128)S(1)} collective-permute-done((f32[2,2,128,128]{3,2,1,0:T(8,128)S(1)}, f32[2,2,128,128]{3,2,1,0:T(8,128)S(1)}, u32[]{:S(2)}, u32[]{:S(2)}) %collective-permute-start.27) | collective-permute-done | bytes 262176 | tf_op jit(solution)/shard_map/ppermute | solution.py:617
  129.8 1.3 collective-permute-start.29
  131.1 1.1 deposit_patches.21.refs_2_
  132.2 9.2 %collective-permute-done.29.refs_1_ = f32[2,2,128,128]{3,2,1,0:T(8,128)S(1)} collective-permute-done((f32[2,2,128,128]{3,2,1,0:T(8,128)S(1)}, f32[2,2,128,128]{3,2,1,0:T(8,128)S(1)}, u32[]{:S(2)}, u32[]{:S(2)}) %collective-permute-start.29) | collective-permute-done | bytes 262176 | tf_op jit(solution)/shard_map/ppermute | solution.py:617
  142.4 1.3 collective-permute-start.30
  143.7 1.7 %deposit_patches.22.refs_2_ = f32[42368,128]{1,0:T(8,128)S(1)} custom-call(s32[1,128]{1,0:T(1,128)S(1)} %sort_probes.1.refs_0_, f32[2048,128]{1,0:T(8,128)S(1)} %collective-permute-done.31.refs_1_, f32[42368,128]{1,0:T(8,128)S(1)} %get-tuple-element.140.refs_2_), custom_call_target="tpu_custom_call", output_to_operand_aliasing={{}: (2, {})} | custom-call | flops 1000 | bytes 1000 | tf_op jit(solution)/shard_map/deposit_patches/pallas_call | solution.py:157
  145.4 5.3 %collective-permute-done.30.refs_1_ = f32[2,2,128,128]{3,2,1,0:T(8,128)S(1)} collective-permute-done((f32[2,2,128,128]{3,2,1,0:T(8,128)S(1)}, f32[2,2,128,128]{3,2,1,0:T(8,128)S(1)}, u32[]{:S(2)}, u32[]{:S(2)}) %collective-permute-start.30) | collective-permute-done | bytes 262176 | tf_op jit(solution)/shard_map/ppermute | solution.py:617
  151.5 1.1 deposit_patches.23.state
  153.2 1.8 %split_rows.7 = (f32[2,2,1,192,768]{4,3,2,1,0:T(8,128)S(1)}, f32[4096,128]{1,0:T(8,128)}) custom-call(f32[42368,128]{1,0:T(8,128)S(1)} %deposit_patches.23.state), custom_call_target="tpu_custom_call" | custom-call | flops 1000 | bytes 1000 | tf_op jit(solution)/shard_map/split_rows/pallas_call | solution.py:476
  155.0 2.7 %collective-permute-done.32 = f32[2,2,1,192,768]{4,3,2,1,0:T(8,128)S(1)} collective-permute-done((f32[2,2,1,192,768]{4,3,2,1,0:T(8,128)S(1)}, f32[2,2,1,192,768]{4,3,2,1,0:T(8,128)S(1)}, u32[]{:S(2)}, u32[]{:S(2)}) %collective-permute-start.32) | collective-permute-done | bytes 2359328 | tf_op jit(solution)/shard_map/ppermute | solution.py:512
  157.7 1.5 conditional.1
  157.7 1.5 add_up.2
  (69 shorter events, 29.9 us)
Async XLA Ops:
  0.0 14.0 %copy-start = (bf16[2,2,2,256,256]{4,3,2,1,0:T(8,128)(2,1)S(1)}, bf16[2,2,2,256,256]{4,3,2,1,0:T(8,128)(2,1)}, u32[]{:S(2)}) copy-start(bf16[2,2,2,256,256]{4,3,2,1,0:T(8,128)(2,1)} %constant.5.clone.refs_0_) | copy-start | bytes 3145732
  0.0 14.0 %copy-start.1 = (f32[2,128,128]{2,1,0:T(8,128)S(1)}, f32[2,128,128]{2,1,0:T(8,128)}, u32[]{:S(2)}) copy-start(f32[2,128,128]{2,1,0:T(8,128)} %refs_2_.13) | copy-start | bytes 393220
  0.0 1.4 collective-permute-start.3
  1.4 9.6 %collective-permute-start.5 = (f32[2,2,384,768]{3,2,1,0:T(8,128)}, f32[2,2,384,768]{3,2,1,0:T(8,128)S(1)}, u32[]{:S(2)}, u32[]{:S(2)}) collective-permute-start(f32[2,2,384,768]{3,2,1,0:T(8,128)} %x), channel_id=1, source_target_pairs={{0,1},{1,0},{2,3},{3,2},{4,5},{5,4},{6,7},{7,6},{8,9},{9,8},{10,11... | collective-permute-start | bytes 14155784 | tf_op jit(solution)/shard_map/ppermute | solution.py:512
  1.7 4.3 %collective-permute-start.2 = (s32[16]{0:T(128)}, s32[16]{0:T(128)S(1)}, u32[]{:S(2)}, u32[]{:S(2)}) collective-permute-start(s32[16]{0:T(128)} %bitcast.14), channel_id=1, source_target_pairs={{0,2},{2,0},{1,3},{3,1},{4,6},{6,4},{5,7},{7,5},{8,10},{10,8},{9,1... | collective-permute-start | bytes 200 | tf_op jit(solution)/shard_map/ppermute | solution.py:512
  4.4 3.5 %collective-permute-start.4 = (s32[16]{0:T(128)S(1)}, s32[16]{0:T(128)S(1)}, u32[]{:S(2)}, u32[]{:S(2)}) collective-permute-start(s32[16]{0:T(128)S(1)} %collective-permute-done.3.refs_2_), channel_id=1, source_target_pairs={{0,2},{2,0},{1,3},{3,1},{4,6},{6,4},{5,7},{7,5},{8,10},{10,8},{9,1... | collective-permute-start | bytes 200 | tf_op jit(solution)/shard_map/ppermute | solution.py:512
  7.9 24.2 %collective-permute-start.8 = (f32[16,1,128,128]{3,2,1,0:T(8,128)}, f32[16,1,128,128]{3,2,1,0:T(8,128)S(1)}, u32[]{:S(2)}, u32[]{:S(2)}) collective-permute-start(f32[16,1,128,128]{3,2,1,0:T(8,128)} %param.12), channel_id=1, source_target_pairs={{12,14},{14,12},{13,15},{15,13},{28,30},{30,28},{29,31},{31,29}} | collective-permute-start | bytes 3145736 | tf_op jit(solution)/shard_map/ppermute | solution.py:598
  8.7 0.7 copy-start.2
  14.9 8.3 %collective-permute-start.6 = (f32[2,2,128,128]{3,2,1,0:T(8,128)S(1)}, f32[2,2,128,128]{3,2,1,0:T(8,128)S(1)}, u32[]{:S(2)}, u32[]{:S(2)}) collective-permute-start(f32[2,2,128,128]{3,2,1,0:T(8,128)S(1)} %get-tuple-element.92), channel_id=1, source_target_pairs={{0,4},{1,5},{2,6},{3,7},{16,20},{17,21},{18,22},{19,23}} | collective-permute-start | bytes 786440 | tf_op jit(solution)/shard_map/ppermute | solution.py:617
  22.3 7.9 %copy-start.3 = (f32[16,1,128,128]{3,2,1,0:T(8,128)S(1)}, f32[16,1,128,128]{3,2,1,0:T(8,128)}, u32[]{:S(2)}) copy-start(f32[16,1,128,128]{3,2,1,0:T(8,128)} %param.12) | copy-start | bytes 3145732
  24.2 9.3 %collective-permute-start.7 = (f32[2,2,128,128]{3,2,1,0:T(8,128)S(1)}, f32[2,2,128,128]{3,2,1,0:T(8,128)S(1)}, u32[]{:S(2)}, u32[]{:S(2)}) collective-permute-start(f32[2,2,128,128]{3,2,1,0:T(8,128)S(1)} %get-tuple-element.95), channel_id=1, source_target_pairs={{0,4},{4,8},{1,5},{5,9},{2,6},{6,10},{3,7},{7,11},{16,20},{20,24},... | collective-permute-start | bytes 786440 | tf_op jit(solution)/shard_map/ppermute | solution.py:617
  28.6 3.6 %collective-permute-start.9 = (s32[1,128]{1,0:T(1,128)S(1)}, s32[1,128]{1,0:T(1,128)S(1)}, u32[]{:S(2)}, u32[]{:S(2)}) collective-permute-start(s32[1,128]{1,0:T(1,128)S(1)} %sort_probes.1.refs_0_), channel_id=1, source_target_pairs={{0,16},{16,0},{1,17},{17,1},{2,18},{18,2},{3,19},{19,3},{4,20},{20... | collective-permute-start | bytes 1544 | tf_op jit(solution)/shard_map/ppermute | solution.py:512
  30.2 11.1 %collective-permute-start.10 = (f32[16,1,128,128]{3,2,1,0:T(8,128)S(1)}, f32[16,1,128,128]{3,2,1,0:T(8,128)S(1)}, u32[]{:S(2)}, u32[]{:S(2)}) collective-permute-start(f32[16,1,128,128]{3,2,1,0:T(8,128)S(1)} %copy-done.3), channel_id=1, source_target_pairs={{12,13},{13,12},{14,15},{15,14},{28,29},{29,28},{30,31},{31,30}} | collective-permute-start | bytes 3145736 | tf_op jit(solution)/shard_map/ppermute | solution.py:637
  33.4 7.8 %collective-permute-start.11 = (f32[16,1,128,128]{3,2,1,0:T(8,128)S(1)}, f32[16,1,128,128]{3,2,1,0:T(8,128)S(1)}, u32[]{:S(2)}, u32[]{:S(2)}) collective-permute-start(f32[16,1,128,128]{3,2,1,0:T(8,128)S(1)} %collective-permute-done.8), channel_id=1, source_target_pairs={{12,13},{13,12},{14,15},{15,14},{28,29},{29,28},{30,31},{31,30}} | collective-permute-start | bytes 3145736 | tf_op jit(solution)/shard_map/ppermute | solution.py:637
  35.1 8.4 %collective-permute-start.12 = (f32[2,2,128,128]{3,2,1,0:T(8,128)S(1)}, f32[2,2,128,128]{3,2,1,0:T(8,128)S(1)}, u32[]{:S(2)}, u32[]{:S(2)}) collective-permute-start(f32[2,2,128,128]{3,2,1,0:T(8,128)S(1)} %get-tuple-element.103), channel_id=1, source_target_pairs={{0,4},{4,8},{8,12},{1,5},{5,9},{9,13},{2,6},{6,10},{10,14},{3,7},{... | collective-permute-start | bytes 786440 | tf_op jit(solution)/shard_map/ppermute | solution.py:617
  44.4 8.3 %collective-permute-start.14 = (f32[2,2,128,128]{3,2,1,0:T(8,128)S(1)}, f32[2,2,128,128]{3,2,1,0:T(8,128)S(1)}, u32[]{:S(2)}, u32[]{:S(2)}) collective-permute-start(f32[2,2,128,128]{3,2,1,0:T(8,128)S(1)} %get-tuple-element.105.refs_1_), channel_id=1, source_target_pairs={{0,4},{4,8},{8,12},{1,5},{5,9},{9,13},{2,6},{6,10},{10,14},{3,7},{... | collective-permute-start | bytes 786440 | tf_op jit(solution)/shard_map/ppermute | solution.py:617
  51.4 8.6 %collective-permute-start.13 = (f32[2,2,128,128]{3,2,1,0:T(8,128)S(1)}, f32[2,2,128,128]{3,2,1,0:T(8,128)S(1)}, u32[]{:S(2)}, u32[]{:S(2)}) collective-permute-start(f32[2,2,128,128]{3,2,1,0:T(8,128)S(1)} %get-tuple-element.107), channel_id=1, source_target_pairs={{12,8},{13,9},{14,10},{15,11},{28,24},{29,25},{30,26},{31,27}} | collective-permute-start | bytes 786440 | tf_op jit(solution)/shard_map/ppermute | solution.py:617
  53.6 10.8 %collective-permute-start.16 = (f32[2,2,128,128]{3,2,1,0:T(8,128)S(1)}, f32[2,2,128,128]{3,2,1,0:T(8,128)S(1)}, u32[]{:S(2)}, u32[]{:S(2)}) collective-permute-start(f32[2,2,128,128]{3,2,1,0:T(8,128)S(1)} %get-tuple-element.109.refs_2_), channel_id=1, source_target_pairs={{0,4},{4,8},{8,12},{1,5},{5,9},{9,13},{2,6},{6,10},{10,14},{3,7},{... | collective-permute-start | bytes 786440 | tf_op jit(solution)/shard_map/ppermute | solution.py:617
  60.0 9.8 %collective-permute-start.15 = (f32[2,2,128,128]{3,2,1,0:T(8,128)S(1)}, f32[2,2,128,128]{3,2,1,0:T(8,128)S(1)}, u32[]{:S(2)}, u32[]{:S(2)}) collective-permute-start(f32[2,2,128,128]{3,2,1,0:T(8,128)S(1)} %get-tuple-element.111), channel_id=1, source_target_pairs={{8,4},{12,8},{9,5},{13,9},{10,6},{14,10},{11,7},{15,11},{24,20},{2... | collective-permute-start | bytes 786440 | tf_op jit(solution)/shard_map/ppermute | solution.py:617
  65.4 8.3 %collective-permute-start.18 = (f32[2,2,128,128]{3,2,1,0:T(8,128)S(1)}, f32[2,2,128,128]{3,2,1,0:T(8,128)S(1)}, u32[]{:S(2)}, u32[]{:S(2)}) collective-permute-start(f32[2,2,128,128]{3,2,1,0:T(8,128)S(1)} %get-tuple-element.113.refs_2_), channel_id=1, source_target_pairs={{0,4},{4,8},{8,12},{1,5},{5,9},{9,13},{2,6},{6,10},{10,14},{3,7},{... | collective-permute-start | bytes 786440 | tf_op jit(solution)/shard_map/ppermute | solution.py:617
  70.0 9.9 %collective-permute-start.17 = (f32[2,2,128,128]{3,2,1,0:T(8,128)S(1)}, f32[2,2,128,128]{3,2,1,0:T(8,128)S(1)}, u32[]{:S(2)}, u32[]{:S(2)}) collective-permute-start(f32[2,2,128,128]{3,2,1,0:T(8,128)S(1)} %get-tuple-element.115), channel_id=1, source_target_pairs={{4,0},{8,4},{12,8},{5,1},{9,5},{13,9},{6,2},{10,6},{14,10},{7,3},{... | collective-permute-start | bytes 786440 | tf_op jit(solution)/shard_map/ppermute | solution.py:617
  74.6 8.8 %collective-permute-start.20 = (f32[2,2,128,128]{3,2,1,0:T(8,128)S(1)}, f32[2,2,128,128]{3,2,1,0:T(8,128)S(1)}, u32[]{:S(2)}, u32[]{:S(2)}) collective-permute-start(f32[2,2,128,128]{3,2,1,0:T(8,128)S(1)} %get-tuple-element.117.refs_2_), channel_id=1, source_target_pairs={{0,4},{4,8},{8,12},{1,5},{5,9},{9,13},{2,6},{6,10},{10,14},{3,7},{... | collective-permute-start | bytes 786440 | tf_op jit(solution)/shard_map/ppermute | solution.py:617
  80.8 8.5 %collective-permute-start.19 = (f32[2,2,128,128]{3,2,1,0:T(8,128)S(1)}, f32[2,2,128,128]{3,2,1,0:T(8,128)S(1)}, u32[]{:S(2)}, u32[]{:S(2)}) collective-permute-start(f32[2,2,128,128]{3,2,1,0:T(8,128)S(1)} %get-tuple-element.119), channel_id=1, source_target_pairs={{4,0},{8,4},{12,8},{5,1},{9,5},{13,9},{6,2},{10,6},{14,10},{7,3},{... | collective-permute-start | bytes 786440 | tf_op jit(solution)/shard_map/ppermute | solution.py:617
  84.3 8.9 %collective-permute-start.22 = (f32[2,2,128,128]{3,2,1,0:T(8,128)S(1)}, f32[2,2,128,128]{3,2,1,0:T(8,128)S(1)}, u32[]{:S(2)}, u32[]{:S(2)}) collective-permute-start(f32[2,2,128,128]{3,2,1,0:T(8,128)S(1)} %get-tuple-element.121.refs_2_), channel_id=1, source_target_pairs={{0,4},{4,8},{8,12},{1,5},{5,9},{9,13},{2,6},{6,10},{10,14},{3,7},{... | collective-permute-start | bytes 786440 | tf_op jit(solution)/shard_map/ppermute | solution.py:617
  90.2 8.3 %collective-permute-start.21 = (f32[2,2,128,128]{3,2,1,0:T(8,128)S(1)}, f32[2,2,128,128]{3,2,1,0:T(8,128)S(1)}, u32[]{:S(2)}, u32[]{:S(2)}) collective-permute-start(f32[2,2,128,128]{3,2,1,0:T(8,128)S(1)} %get-tuple-element.123), channel_id=1, source_target_pairs={{4,0},{8,4},{12,8},{5,1},{9,5},{13,9},{6,2},{10,6},{14,10},{7,3},{... | collective-permute-start | bytes 786440 | tf_op jit(solution)/shard_map/ppermute | solution.py:617
  91.6 28.5 %collective-permute-start.28 = (f32[2048,128]{1,0:T(8,128)S(1)}, f32[2048,128]{1,0:T(8,128)S(1)}, u32[]{:S(2)}, u32[]{:S(2)}) collective-permute-start(f32[2048,128]{1,0:T(8,128)S(1)} %slice.10), channel_id=1, source_target_pairs={{0,2},{2,0},{1,3},{3,1},{4,6},{6,4},{5,7},{7,5},{8,10},{10,8},{9,1... | collective-permute-start | bytes 3145736 | tf_op jit(solution)/shard_map/ppermute | solution.py:512
  93.3 8.5 %collective-permute-start.24 = (f32[2,2,128,128]{3,2,1,0:T(8,128)S(1)}, f32[2,2,128,128]{3,2,1,0:T(8,128)S(1)}, u32[]{:S(2)}, u32[]{:S(2)}) collective-permute-start(f32[2,2,128,128]{3,2,1,0:T(8,128)S(1)} %get-tuple-element.125.refs_2_), channel_id=1, source_target_pairs={{4,8},{8,12},{5,9},{9,13},{6,10},{10,14},{7,11},{11,15},{20,24},{2... | collective-permute-start | bytes 786440 | tf_op jit(solution)/shard_map/ppermute | solution.py:617
  99.4 8.6 %collective-permute-start.23 = (f32[2,2,128,128]{3,2,1,0:T(8,128)S(1)}, f32[2,2,128,128]{3,2,1,0:T(8,128)S(1)}, u32[]{:S(2)}, u32[]{:S(2)}) collective-permute-start(f32[2,2,128,128]{3,2,1,0:T(8,128)S(1)} %get-tuple-element.127), channel_id=1, source_target_pairs={{4,0},{8,4},{12,8},{5,1},{9,5},{13,9},{6,2},{10,6},{14,10},{7,3},{... | collective-permute-start | bytes 786440 | tf_op jit(solution)/shard_map/ppermute | solution.py:617
  101.8 11.1 %collective-permute-start.26 = (f32[2,2,128,128]{3,2,1,0:T(8,128)S(1)}, f32[2,2,128,128]{3,2,1,0:T(8,128)S(1)}, u32[]{:S(2)}, u32[]{:S(2)}) collective-permute-start(f32[2,2,128,128]{3,2,1,0:T(8,128)S(1)} %get-tuple-element.129.refs_2_), channel_id=1, source_target_pairs={{8,12},{9,13},{10,14},{11,15},{24,28},{25,29},{26,30},{27,31}} | collective-permute-start | bytes 786440 | tf_op jit(solution)/shard_map/ppermute | solution.py:617
  108.9 9.0 %collective-permute-start.25 = (f32[2,2,128,128]{3,2,1,0:T(8,128)S(1)}, f32[2,2,128,128]{3,2,1,0:T(8,128)S(1)}, u32[]{:S(2)}, u32[]{:S(2)}) collective-permute-start(f32[2,2,128,128]{3,2,1,0:T(8,128)S(1)} %get-tuple-element.131), channel_id=1, source_target_pairs={{4,0},{8,4},{12,8},{5,1},{9,5},{13,9},{6,2},{10,6},{14,10},{7,3},{... | collective-permute-start | bytes 786440 | tf_op jit(solution)/shard_map/ppermute | solution.py:617
  110.2 33.4 %collective-permute-start.31 = (f32[2048,128]{1,0:T(8,128)S(1)}, f32[2048,128]{1,0:T(8,128)S(1)}, u32[]{:S(2)}, u32[]{:S(2)}) collective-permute-start(f32[2048,128]{1,0:T(8,128)S(1)} %slice.11), channel_id=1, source_target_pairs={{0,2},{2,0},{1,3},{3,1},{4,6},{6,4},{5,7},{7,5},{8,10},{10,8},{9,1... | collective-permute-start | bytes 3145736 | tf_op jit(solution)/shard_map/ppermute | solution.py:512
  118.7 10.2 %collective-permute-start.27 = (f32[2,2,128,128]{3,2,1,0:T(8,128)S(1)}, f32[2,2,128,128]{3,2,1,0:T(8,128)S(1)}, u32[]{:S(2)}, u32[]{:S(2)}) collective-permute-start(f32[2,2,128,128]{3,2,1,0:T(8,128)S(1)} %get-tuple-element.135), channel_id=1, source_target_pairs={{4,0},{8,4},{12,8},{5,1},{9,5},{13,9},{6,2},{10,6},{14,10},{7,3},{... | collective-permute-start | bytes 786440 | tf_op jit(solution)/shard_map/ppermute | solution.py:617
  129.8 11.6 %collective-permute-start.29 = (f32[2,2,128,128]{3,2,1,0:T(8,128)S(1)}, f32[2,2,128,128]{3,2,1,0:T(8,128)S(1)}, u32[]{:S(2)}, u32[]{:S(2)}) collective-permute-start(f32[2,2,128,128]{3,2,1,0:T(8,128)S(1)} %get-tuple-element.137), channel_id=1, source_target_pairs={{4,0},{8,4},{5,1},{9,5},{6,2},{10,6},{7,3},{11,7},{20,16},{24,20},... | collective-permute-start | bytes 786440 | tf_op jit(solution)/shard_map/ppermute | solution.py:617
  142.4 8.3 %collective-permute-start.30 = (f32[2,2,128,128]{3,2,1,0:T(8,128)S(1)}, f32[2,2,128,128]{3,2,1,0:T(8,128)S(1)}, u32[]{:S(2)}, u32[]{:S(2)}) collective-permute-start(f32[2,2,128,128]{3,2,1,0:T(8,128)S(1)} %get-tuple-element.139), channel_id=1, source_target_pairs={{4,0},{5,1},{6,2},{7,3},{20,16},{21,17},{22,18},{23,19}} | collective-permute-start | bytes 786440 | tf_op jit(solution)/shard_map/ppermute | solution.py:617
  153.1 4.6 %collective-permute-start.32 = (f32[2,2,1,192,768]{4,3,2,1,0:T(8,128)S(1)}, f32[2,2,1,192,768]{4,3,2,1,0:T(8,128)S(1)}, u32[]{:S(2)}, u32[]{:S(2)}) collective-permute-start(f32[2,2,1,192,768]{4,3,2,1,0:T(8,128)S(1)} %split_rows.6), channel_id=1, source_target_pairs={{0,1},{1,0},{2,3},{3,2},{4,5},{5,4},{6,7},{7,6},{8,9},{9,8},{10,11... | collective-permute-start | bytes 7077896 | tf_op jit(solution)/shard_map/ppermute | solution.py:512

commit v8 on v7

--- a/solution.py
+++ b/solution.py
@@ -516,11 +516,17 @@
     n = lay.probes
     total = 4 * n
 
-    def body(listed, *refs):
-        *scans, info, positions, sem = refs
-        copy = pltpu.make_async_copy(listed, positions, sem)
-        copy.start()
-        copy.wait()
+    def body(listed, scan, *refs):
+        *scans, info, positions, mine, sems = refs
+        copies = [
+            pltpu.make_async_copy(listed, positions, sems.at[0]),
+            pltpu.make_async_copy(scan, mine, sems.at[1]),
+        ]
+        for copy in copies:
+            copy.start()
+        for copy in copies:
+            copy.wait()
+        scans = [mine.at[0], *scans]
         lat, side = lax.axis_index("lat"), lax.axis_index("probe")
         lane = lax.broadcasted_iota(jnp.int32, (1, 128), 1)
         at = lax.broadcasted_iota(jnp.int32, (total, 128), 0)
@@ -545,13 +551,17 @@
 
     return pl.pallas_call(
         body,
-        in_specs=[HBM] + [SMEM] * 4,
+        in_specs=[HBM] * 2 + [SMEM] * 3,
         out_specs=VMEM,
         out_shape=pltpu.VMEM((1, 128), jnp.int32),
-        scratch_shapes=[pltpu.SMEM(positions.T.shape, jnp.int32), pltpu.SemaphoreType.DMA(())],
+        scratch_shapes=[
+            pltpu.SMEM(positions.T.shape, jnp.int32),
+            pltpu.SMEM((1, n), jnp.int32),
+            pltpu.SemaphoreType.DMA((2,)),
+        ],
         compiler_params=pltpu.CompilerParams(vmem_limit_bytes=SCOPED),
         name="sort_probes",
-    )(in_hbm(positions.T), *indices)
+    )(in_hbm(positions.T), in_hbm(indices[0].reshape((1, n))), *indices[1:])
 
 
 def bring(x):

time: 160 us -> 160 us (level)
  transfers between devices with their start and end apart: 31 -> 31, of which waited for: 20 -> 20; matrix products, arithmetic and copies ran while one was open for 0% -> 0% of each run, Pallas kernels for 24% -> 25%
where the time goes in v8:
time: 160 us; the launch traced here: 159 us
  starting transfers between devices  58.6 us (37%)
  waiting for transfers between devices  55.8 us (35%)
  Pallas kernels  44 us (28%)
    ppermute x20, starting transfers between devices, pass_on(): return lax.ppermute(wave, 'depth', pairs) if pairs else None  49.2 us
    ppermute x20, waiting for transfers between devices, pass_on(): return lax.ppermute(wave, 'depth', pairs) if pairs else None  47.3 us
    pallas_call x39, Pallas kernels, call(): pl.pallas_call(kernel, in_specs=specs, out_specs=[VMEM] * (1 + len(outs)...  36.2 us
    ppermute x8, waiting for transfers between devices, swap(): return lax.ppermute(shard, axis, [(0, 1), (1, 0)])  8.46 us
    ppermute x8, starting transfers between devices, swap(): return lax.ppermute(shard, axis, [(0, 1), (1, 0)])  7.3 us
  transfers between devices with their start and end apart: 31, of which 20 were waited for; matrix products, arithmetic and copies ran while one was open for 0% of the time, Pallas kernels for 25%

profile of v8, /device:TPU:0, one launch (start us, length us, event | category | flops | bytes accessed | tf_op | source)
XLA Modules:
  0.0 159.4 jit_solution(13140914179048459139)
XLA Ops:
  1.7 2.7 %collective-permute-start.2 = (s32[16]{0:T(128)}, s32[16]{0:T(128)S(1)}, u32[]{:S(2)}, u32[]{:S(2)}) collective-permute-start(s32[16]{0:T(128)} %bitcast.20), channel_id=1, source_target_pairs={{0,2},{2,0},{1,3},{3,1},{4,6},{6,4},{5,7},{7,5},{8,10},{10,8},{9,1... | collective-permute-start | bytes 200 | tf_op jit(solution)/shard_map/ppermute | solution.py:512
  4.4 1.6 %collective-permute-done.2.refs_0_ = s32[16]{0:T(128)S(1)} collective-permute-done((s32[16]{0:T(128)}, s32[16]{0:T(128)S(1)}, u32[]{:S(2)}, u32[]{:S(2)}) %collective-permute-start.2) | collective-permute-done | bytes 96 | tf_op jit(solution)/shard_map/ppermute | solution.py:512
  6.1 1.9 %collective-permute-done.4.refs_2_ = s32[16]{0:T(128)S(1)} collective-permute-done((s32[16]{0:T(128)S(1)}, s32[16]{0:T(128)S(1)}, u32[]{:S(2)}, u32[]{:S(2)}) %collective-permute-start.4) | collective-permute-done | bytes 96 | tf_op jit(solution)/shard_map/ppermute | solution.py:512
  8.7 1.7 %sort_probes.1.refs_0_ = s32[1,128]{1,0:T(1,128)S(1)} custom-call(s32[2,512]{1,0:T(2,128)} %bitcast.18, s32[1,16]{1,0:T(1,128)} %bitcast.21, s32[16]{0:T(128)S(1)} %collective-permute-done.2.refs_0_, s32[16]{0:T(128)S(1)} %collective-permute-done.3.refs_1_, s32[16]{0:T(128)S(1)} %collective-permute-done.4.refs_2_), custom_call_target="tpu_custom_call" | custom-call | tf_op jit(solution)/shard_map/sort_probes/pallas_call | solution.py:552
  10.4 2.9 %cut_patches.4.refs_2_ = f32[42368,128]{1,0:T(8,128)S(1)} custom-call(s32[1,128]{1,0:T(1,128)S(1)} %sort_probes.1.refs_0_, f32[2,2,384,768]{3,2,1,0:T(8,128)} %x, f32[2,2,384,768]{3,2,1,0:T(8,128)S(1)} %collective-permute-done.5.refs_2_), custom_call_target="tpu_custom_call" | custom-call | flops 1000 | bytes 1000 | tf_op jit(solution)/shard_map/cut_patches/pallas_call | solution.py:157
  14.3 3.0 %collective-permute-start.6 = (f32[2,2,128,128]{3,2,1,0:T(8,128)S(1)}, f32[2,2,128,128]{3,2,1,0:T(8,128)S(1)}, u32[]{:S(2)}, u32[]{:S(2)}) collective-permute-start(f32[2,2,128,128]{3,2,1,0:T(8,128)S(1)} %get-tuple-element.92), channel_id=1, source_target_pairs={{0,4},{1,5},{2,6},{3,7},{16,20},{17,21},{18,22},{19,23}} | collective-permute-start | bytes 786440 | tf_op jit(solution)/shard_map/ppermute | solution.py:627
  17.3 2.3 %bring.1.refs_1_ = f32[2,2,384,768]{3,2,1,0:T(8,128)S(1)} custom-call(f32[2,2,384,768]{3,2,1,0:T(8,128)} %x), custom_call_target="tpu_custom_call" | custom-call | flops 1000 | bytes 1000 | tf_op jit(solution)/shard_map/bring/pallas_call | solution.py:573
  19.7 1.8 %cut_patches.5.refs_0_ = f32[42368,128]{1,0:T(8,128)S(1)} custom-call(s32[1,128]{1,0:T(1,128)S(1)} %sort_probes.1.refs_0_, f32[2,2,384,768]{3,2,1,0:T(8,128)S(1)} %bring.1.refs_1_, f32[2,2,384,768]{3,2,1,0:T(8,128)S(1)} %collective-permute-done.5.refs_2_, f32[42368,128]{1,0:T(8,128)S(1)} %get-tuple-element.94.refs_3_), custom_call_target="tpu_custom_call", output_to_operand_aliasing={{}: (3, {})} | custom-call | flops 1000 | bytes 1000 | tf_op jit(solution)/shard_map/cut_patches/pallas_call | solution.py:157
  22.0 1.2 collective-permute-done.6.refs_1_
  24.2 4.4 %collective-permute-start.7 = (f32[2,2,128,128]{3,2,1,0:T(8,128)S(1)}, f32[2,2,128,128]{3,2,1,0:T(8,128)S(1)}, u32[]{:S(2)}, u32[]{:S(2)}) collective-permute-start(f32[2,2,128,128]{3,2,1,0:T(8,128)S(1)} %get-tuple-element.95), channel_id=1, source_target_pairs={{0,4},{4,8},{1,5},{5,9},{2,6},{6,10},{3,7},{7,11},{16,20},{20,24},... | collective-permute-start | bytes 786440 | tf_op jit(solution)/shard_map/ppermute | solution.py:627
  28.6 1.6 collective-permute-start.9
  30.9 1.3 collective-permute-done.9.refs_1_
  32.2 1.5 collective-permute-done.7.refs_1_
  35.3 4.4 %collective-permute-start.12 = (f32[2,2,128,128]{3,2,1,0:T(8,128)S(1)}, f32[2,2,128,128]{3,2,1,0:T(8,128)S(1)}, u32[]{:S(2)}, u32[]{:S(2)}) collective-permute-start(f32[2,2,128,128]{3,2,1,0:T(8,128)S(1)} %get-tuple-element.103), channel_id=1, source_target_pairs={{0,4},{4,8},{8,12},{1,5},{5,9},{9,13},{2,6},{6,10},{10,14},{3,7},{... | collective-permute-start | bytes 786440 | tf_op jit(solution)/shard_map/ppermute | solution.py:627
  39.7 1.7 %cut_patches.6.refs_6_ = f32[42368,128]{1,0:T(8,128)S(1)} custom-call(s32[1,128]{1,0:T(1,128)S(1)} %sort_probes.1.refs_0_, f32[2,2,384,768]{3,2,1,0:T(8,128)S(1)} %bring.1.refs_1_, f32[2,2,384,768]{3,2,1,0:T(8,128)S(1)} %collective-permute-done.5.refs_2_, f32[42368,128]{1,0:T(8,128)S(1)} %get-tuple-element.101.refs_3_), custom_call_target="tpu_custom_call", output_to_operand_aliasing={{}: (3, {})} | custom-call | flops 1000 | bytes 1000 | tf_op jit(solution)/shard_map/cut_patches/pallas_call | solution.py:157
  42.2 1.7 %collective-permute-done.12.refs_1_ = f32[2,2,128,128]{3,2,1,0:T(8,128)S(1)} collective-permute-done((f32[2,2,128,128]{3,2,1,0:T(8,128)S(1)}, f32[2,2,128,128]{3,2,1,0:T(8,128)S(1)}, u32[]{:S(2)}, u32[]{:S(2)}) %collective-permute-start.12) | collective-permute-done | bytes 262176 | tf_op jit(solution)/shard_map/ppermute | solution.py:627
  44.8 4.4 %collective-permute-start.14 = (f32[2,2,128,128]{3,2,1,0:T(8,128)S(1)}, f32[2,2,128,128]{3,2,1,0:T(8,128)S(1)}, u32[]{:S(2)}, u32[]{:S(2)}) collective-permute-start(f32[2,2,128,128]{3,2,1,0:T(8,128)S(1)} %get-tuple-element.105.refs_1_), channel_id=1, source_target_pairs={{0,4},{4,8},{8,12},{1,5},{5,9},{9,13},{2,6},{6,10},{10,14},{3,7},{... | collective-permute-start | bytes 786440 | tf_op jit(solution)/shard_map/ppermute | solution.py:627
  49.2 2.5 %cut_patches.7.refs_2_ = f32[42368,128]{1,0:T(8,128)S(1)} custom-call(s32[1,128]{1,0:T(1,128)S(1)} %sort_probes.1.refs_0_, f32[2,2,384,768]{3,2,1,0:T(8,128)S(1)} %bring.1.refs_1_, f32[2,2,384,768]{3,2,1,0:T(8,128)S(1)} %collective-permute-done.5.refs_2_, f32[42368,128]{1,0:T(8,128)S(1)} %get-tuple-element.106.refs_3_), custom_call_target="tpu_custom_call", output_to_operand_aliasing={{}: (3, {})} | custom-call | flops 1000 | bytes 1000 | tf_op jit(solution)/shard_map/cut_patches/pallas_call | solution.py:157
  54.0 5.9 %collective-permute-start.16 = (f32[2,2,128,128]{3,2,1,0:T(8,128)S(1)}, f32[2,2,128,128]{3,2,1,0:T(8,128)S(1)}, u32[]{:S(2)}, u32[]{:S(2)}) collective-permute-start(f32[2,2,128,128]{3,2,1,0:T(8,128)S(1)} %get-tuple-element.109.refs_2_), channel_id=1, source_target_pairs={{0,4},{4,8},{8,12},{1,5},{5,9},{9,13},{2,6},{6,10},{10,14},{3,7},{... | collective-permute-start | bytes 786440 | tf_op jit(solution)/shard_map/ppermute | solution.py:627
  60.9 3.5 %collective-permute-done.16.refs_1_ = f32[2,2,128,128]{3,2,1,0:T(8,128)S(1)} collective-permute-done((f32[2,2,128,128]{3,2,1,0:T(8,128)S(1)}, f32[2,2,128,128]{3,2,1,0:T(8,128)S(1)}, u32[]{:S(2)}, u32[]{:S(2)}) %collective-permute-start.16) | collective-permute-done | bytes 262176 | tf_op jit(solution)/shard_map/ppermute | solution.py:627
  65.4 4.4 %collective-permute-start.18 = (f32[2,2,128,128]{3,2,1,0:T(8,128)S(1)}, f32[2,2,128,128]{3,2,1,0:T(8,128)S(1)}, u32[]{:S(2)}, u32[]{:S(2)}) collective-permute-start(f32[2,2,128,128]{3,2,1,0:T(8,128)S(1)} %get-tuple-element.113.refs_2_), channel_id=1, source_target_pairs={{0,4},{4,8},{8,12},{1,5},{5,9},{9,13},{2,6},{6,10},{10,14},{3,7},{... | collective-permute-start | bytes 786440 | tf_op jit(solution)/shard_map/ppermute | solution.py:627
  70.0 1.3 collective-permute-start.17
  71.6 2.0 %collective-permute-done.18.refs_1_ = f32[2,2,128,128]{3,2,1,0:T(8,128)S(1)} collective-permute-done((f32[2,2,128,128]{3,2,1,0:T(8,128)S(1)}, f32[2,2,128,128]{3,2,1,0:T(8,128)S(1)}, u32[]{:S(2)}, u32[]{:S(2)}) %collective-permute-start.18) | collective-permute-done | bytes 262176 | tf_op jit(solution)/shard_map/ppermute | solution.py:627
  74.6 5.0 %collective-permute-start.20 = (f32[2,2,128,128]{3,2,1,0:T(8,128)S(1)}, f32[2,2,128,128]{3,2,1,0:T(8,128)S(1)}, u32[]{:S(2)}, u32[]{:S(2)}) collective-permute-start(f32[2,2,128,128]{3,2,1,0:T(8,128)S(1)} %get-tuple-element.117.refs_2_), channel_id=1, source_target_pairs={{0,4},{4,8},{8,12},{1,5},{5,9},{9,13},{2,6},{6,10},{10,14},{3,7},{... | collective-permute-start | bytes 786440 | tf_op jit(solution)/shard_map/ppermute | solution.py:627
  80.8 1.3 collective-permute-start.19
  84.3 4.6 %collective-permute-start.22 = (f32[2,2,128,128]{3,2,1,0:T(8,128)S(1)}, f32[2,2,128,128]{3,2,1,0:T(8,128)S(1)}, u32[]{:S(2)}, u32[]{:S(2)}) collective-permute-start(f32[2,2,128,128]{3,2,1,0:T(8,128)S(1)} %get-tuple-element.121.refs_2_), channel_id=1, source_target_pairs={{0,4},{4,8},{8,12},{1,5},{5,9},{9,13},{2,6},{6,10},{10,14},{3,7},{... | collective-permute-start | bytes 786440 | tf_op jit(solution)/shard_map/ppermute | solution.py:627
  90.2 1.3 collective-permute-start.21
  93.9 4.5 %collective-permute-done.21.refs_1_ = f32[2,2,128,128]{3,2,1,0:T(8,128)S(1)} collective-permute-done((f32[2,2,128,128]{3,2,1,0:T(8,128)S(1)}, f32[2,2,128,128]{3,2,1,0:T(8,128)S(1)}, u32[]{:S(2)}, u32[]{:S(2)}) %collective-permute-start.21) | collective-permute-done | bytes 262176 | tf_op jit(solution)/shard_map/ppermute | solution.py:627
  99.4 1.3 collective-permute-start.23
  100.7 1.1 deposit_patches.18.refs_2_
  102.5 5.5 %collective-permute-done.23.refs_1_ = f32[2,2,128,128]{3,2,1,0:T(8,128)S(1)} collective-permute-done((f32[2,2,128,128]{3,2,1,0:T(8,128)S(1)}, f32[2,2,128,128]{3,2,1,0:T(8,128)S(1)}, u32[]{:S(2)}, u32[]{:S(2)}) %collective-permute-start.23) | collective-permute-done | bytes 262176 | tf_op jit(solution)/shard_map/ppermute | solution.py:627
  108.9 1.3 collective-permute-start.25
  110.2 1.6 collective-permute-start.31
  112.9 4.9 %collective-permute-done.25.refs_1_ = f32[2,2,128,128]{3,2,1,0:T(8,128)S(1)} collective-permute-done((f32[2,2,128,128]{3,2,1,0:T(8,128)S(1)}, f32[2,2,128,128]{3,2,1,0:T(8,128)S(1)}, u32[]{:S(2)}, u32[]{:S(2)}) %collective-permute-start.25) | collective-permute-done | bytes 262176 | tf_op jit(solution)/shard_map/ppermute | solution.py:627
  118.7 1.3 collective-permute-start.27
  120.0 2.1 %deposit_patches.20.refs_2_ = f32[42368,128]{1,0:T(8,128)S(1)} custom-call(s32[1,128]{1,0:T(1,128)S(1)} %sort_probes.1.refs_0_, f32[2048,128]{1,0:T(8,128)S(1)} %collective-permute-done.28.refs_1_, f32[42368,128]{1,0:T(8,128)S(1)} %get-tuple-element.136.refs_2_), custom_call_target="tpu_custom_call", output_to_operand_aliasing={{}: (2, {})} | custom-call | flops 1000 | bytes 1000 | tf_op jit(solution)/shard_map/deposit_patches/pallas_call | solution.py:157
  122.2 6.8 %collective-permute-done.27.refs_1_ = f32[2,2,128,128]{3,2,1,0:T(8,128)S(1)} collective-permute-done((f32[2,2,128,128]{3,2,1,0:T(8,128)S(1)}, f32[2,2,128,128]{3,2,1,0:T(8,128)S(1)}, u32[]{:S(2)}, u32[]{:S(2)}) %collective-permute-start.27) | collective-permute-done | bytes 262176 | tf_op jit(solution)/shard_map/ppermute | solution.py:627
  129.8 1.3 collective-permute-start.29
  131.1 1.1 deposit_patches.21.refs_2_
  132.2 9.2 %collective-permute-done.29.refs_1_ = f32[2,2,128,128]{3,2,1,0:T(8,128)S(1)} collective-permute-done((f32[2,2,128,128]{3,2,1,0:T(8,128)S(1)}, f32[2,2,128,128]{3,2,1,0:T(8,128)S(1)}, u32[]{:S(2)}, u32[]{:S(2)}) %collective-permute-start.29) | collective-permute-done | bytes 262176 | tf_op jit(solution)/shard_map/ppermute | solution.py:627
  142.4 1.3 collective-permute-start.30
  143.7 1.7 %deposit_patches.22.refs_2_ = f32[42368,128]{1,0:T(8,128)S(1)} custom-call(s32[1,128]{1,0:T(1,128)S(1)} %sort_probes.1.refs_0_, f32[2048,128]{1,0:T(8,128)S(1)} %collective-permute-done.31.refs_1_, f32[42368,128]{1,0:T(8,128)S(1)} %get-tuple-element.140.refs_2_), custom_call_target="tpu_custom_call", output_to_operand_aliasing={{}: (2, {})} | custom-call | flops 1000 | bytes 1000 | tf_op jit(solution)/shard_map/deposit_patches/pallas_call | solution.py:157
  145.4 5.3 %collective-permute-done.30.refs_1_ = f32[2,2,128,128]{3,2,1,0:T(8,128)S(1)} collective-permute-done((f32[2,2,128,128]{3,2,1,0:T(8,128)S(1)}, f32[2,2,128,128]{3,2,1,0:T(8,128)S(1)}, u32[]{:S(2)}, u32[]{:S(2)}) %collective-permute-start.30) | collective-permute-done | bytes 262176 | tf_op jit(solution)/shard_map/ppermute | solution.py:627
  151.5 1.1 deposit_patches.23.state
  153.2 1.8 %split_rows.7 = (f32[2,2,1,192,768]{4,3,2,1,0:T(8,128)S(1)}, f32[4096,128]{1,0:T(8,128)}) custom-call(f32[42368,128]{1,0:T(8,128)S(1)} %deposit_patches.23.state), custom_call_target="tpu_custom_call" | custom-call | flops 1000 | bytes 1000 | tf_op jit(solution)/shard_map/split_rows/pallas_call | solution.py:476
  155.0 2.7 %collective-permute-done.32 = f32[2,2,1,192,768]{4,3,2,1,0:T(8,128)S(1)} collective-permute-done((f32[2,2,1,192,768]{4,3,2,1,0:T(8,128)S(1)}, f32[2,2,1,192,768]{4,3,2,1,0:T(8,128)S(1)}, u32[]{:S(2)}, u32[]{:S(2)}) %collective-permute-start.32) | collective-permute-done | bytes 2359328 | tf_op jit(solution)/shard_map/ppermute | solution.py:512
  157.7 1.5 conditional.1
  157.7 1.5 add_up.2
  (67 shorter events, 29.3 us)
Async XLA Ops:
  0.0 13.3 %copy-start = (bf16[2,2,2,256,256]{4,3,2,1,0:T(8,128)(2,1)S(1)}, bf16[2,2,2,256,256]{4,3,2,1,0:T(8,128)(2,1)}, u32[]{:S(2)}) copy-start(bf16[2,2,2,256,256]{4,3,2,1,0:T(8,128)(2,1)} %constant.5.clone.refs_0_) | copy-start | bytes 3145732
  0.0 13.3 %copy-start.1 = (f32[2,128,128]{2,1,0:T(8,128)S(1)}, f32[2,128,128]{2,1,0:T(8,128)}, u32[]{:S(2)}) copy-start(f32[2,128,128]{2,1,0:T(8,128)} %refs_2_.13) | copy-start | bytes 393220
  0.0 1.4 collective-permute-start.3
  1.4 9.0 %collective-permute-start.5 = (f32[2,2,384,768]{3,2,1,0:T(8,128)}, f32[2,2,384,768]{3,2,1,0:T(8,128)S(1)}, u32[]{:S(2)}, u32[]{:S(2)}) collective-permute-start(f32[2,2,384,768]{3,2,1,0:T(8,128)} %x), channel_id=1, source_target_pairs={{0,1},{1,0},{2,3},{3,2},{4,5},{5,4},{6,7},{7,6},{8,9},{9,8},{10,11... | collective-permute-start | bytes 14155784 | tf_op jit(solution)/shard_map/ppermute | solution.py:512
  1.7 4.3 %collective-permute-start.2 = (s32[16]{0:T(128)}, s32[16]{0:T(128)S(1)}, u32[]{:S(2)}, u32[]{:S(2)}) collective-permute-start(s32[16]{0:T(128)} %bitcast.20), channel_id=1, source_target_pairs={{0,2},{2,0},{1,3},{3,1},{4,6},{6,4},{5,7},{7,5},{8,10},{10,8},{9,1... | collective-permute-start | bytes 200 | tf_op jit(solution)/shard_map/ppermute | solution.py:512
  4.4 3.5 %collective-permute-start.4 = (s32[16]{0:T(128)S(1)}, s32[16]{0:T(128)S(1)}, u32[]{:S(2)}, u32[]{:S(2)}) collective-permute-start(s32[16]{0:T(128)S(1)} %collective-permute-done.3.refs_1_), channel_id=1, source_target_pairs={{0,2},{2,0},{1,3},{3,1},{4,6},{6,4},{5,7},{7,5},{8,10},{10,8},{9,1... | collective-permute-start | bytes 200 | tf_op jit(solution)/shard_map/ppermute | solution.py:512
  7.9 24.2 %collective-permute-start.8 = (f32[16,1,128,128]{3,2,1,0:T(8,128)}, f32[16,1,128,128]{3,2,1,0:T(8,128)S(1)}, u32[]{:S(2)}, u32[]{:S(2)}) collective-permute-start(f32[16,1,128,128]{3,2,1,0:T(8,128)} %param.12), channel_id=1, source_target_pairs={{12,14},{14,12},{13,15},{15,13},{28,30},{30,28},{29,31},{31,29}} | collective-permute-start | bytes 3145736 | tf_op jit(solution)/shard_map/ppermute | solution.py:608
  14.3 8.9 %collective-permute-start.6 = (f32[2,2,128,128]{3,2,1,0:T(8,128)S(1)}, f32[2,2,128,128]{3,2,1,0:T(8,128)S(1)}, u32[]{:S(2)}, u32[]{:S(2)}) collective-permute-start(f32[2,2,128,128]{3,2,1,0:T(8,128)S(1)} %get-tuple-element.92), channel_id=1, source_target_pairs={{0,4},{1,5},{2,6},{3,7},{16,20},{17,21},{18,22},{19,23}} | collective-permute-start | bytes 786440 | tf_op jit(solution)/shard_map/ppermute | solution.py:627
  22.0 8.1 %copy-start.2 = (f32[16,1,128,128]{3,2,1,0:T(8,128)S(1)}, f32[16,1,128,128]{3,2,1,0:T(8,128)}, u32[]{:S(2)}) copy-start(f32[16,1,128,128]{3,2,1,0:T(8,128)} %param.12) | copy-start | bytes 3145732
  24.2 9.5 %collective-permute-start.7 = (f32[2,2,128,128]{3,2,1,0:T(8,128)S(1)}, f32[2,2,128,128]{3,2,1,0:T(8,128)S(1)}, u32[]{:S(2)}, u32[]{:S(2)}) collective-permute-start(f32[2,2,128,128]{3,2,1,0:T(8,128)S(1)} %get-tuple-element.95), channel_id=1, source_target_pairs={{0,4},{4,8},{1,5},{5,9},{2,6},{6,10},{3,7},{7,11},{16,20},{20,24},... | collective-permute-start | bytes 786440 | tf_op jit(solution)/shard_map/ppermute | solution.py:627
  28.6 3.6 %collective-permute-start.9 = (s32[1,128]{1,0:T(1,128)S(1)}, s32[1,128]{1,0:T(1,128)S(1)}, u32[]{:S(2)}, u32[]{:S(2)}) collective-permute-start(s32[1,128]{1,0:T(1,128)S(1)} %sort_probes.1.refs_0_), channel_id=1, source_target_pairs={{0,16},{16,0},{1,17},{17,1},{2,18},{18,2},{3,19},{19,3},{4,20},{20... | collective-permute-start | bytes 1544 | tf_op jit(solution)/shard_map/ppermute | solution.py:512
  30.2 11.3 %collective-permute-start.10 = (f32[16,1,128,128]{3,2,1,0:T(8,128)S(1)}, f32[16,1,128,128]{3,2,1,0:T(8,128)S(1)}, u32[]{:S(2)}, u32[]{:S(2)}) collective-permute-start(f32[16,1,128,128]{3,2,1,0:T(8,128)S(1)} %copy-done.2), channel_id=1, source_target_pairs={{12,13},{13,12},{14,15},{15,14},{28,29},{29,28},{30,31},{31,30}} | collective-permute-start | bytes 3145736 | tf_op jit(solution)/shard_map/ppermute | solution.py:647
  33.7 7.8 %collective-permute-start.11 = (f32[16,1,128,128]{3,2,1,0:T(8,128)S(1)}, f32[16,1,128,128]{3,2,1,0:T(8,128)S(1)}, u32[]{:S(2)}, u32[]{:S(2)}) collective-permute-start(f32[16,1,128,128]{3,2,1,0:T(8,128)S(1)} %collective-permute-done.8), channel_id=1, source_target_pairs={{12,13},{13,12},{14,15},{15,14},{28,29},{29,28},{30,31},{31,30}} | collective-permute-start | bytes 3145736 | tf_op jit(solution)/shard_map/ppermute | solution.py:647
  35.3 8.6 %collective-permute-start.12 = (f32[2,2,128,128]{3,2,1,0:T(8,128)S(1)}, f32[2,2,128,128]{3,2,1,0:T(8,128)S(1)}, u32[]{:S(2)}, u32[]{:S(2)}) collective-permute-start(f32[2,2,128,128]{3,2,1,0:T(8,128)S(1)} %get-tuple-element.103), channel_id=1, source_target_pairs={{0,4},{4,8},{8,12},{1,5},{5,9},{9,13},{2,6},{6,10},{10,14},{3,7},{... | collective-permute-start | bytes 786440 | tf_op jit(solution)/shard_map/ppermute | solution.py:627
  44.8 8.3 %collective-permute-start.14 = (f32[2,2,128,128]{3,2,1,0:T(8,128)S(1)}, f32[2,2,128,128]{3,2,1,0:T(8,128)S(1)}, u32[]{:S(2)}, u32[]{:S(2)}) collective-permute-start(f32[2,2,128,128]{3,2,1,0:T(8,128)S(1)} %get-tuple-element.105.refs_1_), channel_id=1, source_target_pairs={{0,4},{4,8},{8,12},{1,5},{5,9},{9,13},{2,6},{6,10},{10,14},{3,7},{... | collective-permute-start | bytes 786440 | tf_op jit(solution)/shard_map/ppermute | solution.py:627
  51.8 8.1 %collective-permute-start.13 = (f32[2,2,128,128]{3,2,1,0:T(8,128)S(1)}, f32[2,2,128,128]{3,2,1,0:T(8,128)S(1)}, u32[]{:S(2)}, u32[]{:S(2)}) collective-permute-start(f32[2,2,128,128]{3,2,1,0:T(8,128)S(1)} %get-tuple-element.107), channel_id=1, source_target_pairs={{12,8},{13,9},{14,10},{15,11},{28,24},{29,25},{30,26},{31,27}} | collective-permute-start | bytes 786440 | tf_op jit(solution)/shard_map/ppermute | solution.py:627
  54.0 10.4 %collective-permute-start.16 = (f32[2,2,128,128]{3,2,1,0:T(8,128)S(1)}, f32[2,2,128,128]{3,2,1,0:T(8,128)S(1)}, u32[]{:S(2)}, u32[]{:S(2)}) collective-permute-start(f32[2,2,128,128]{3,2,1,0:T(8,128)S(1)} %get-tuple-element.109.refs_2_), channel_id=1, source_target_pairs={{0,4},{4,8},{8,12},{1,5},{5,9},{9,13},{2,6},{6,10},{10,14},{3,7},{... | collective-permute-start | bytes 786440 | tf_op jit(solution)/shard_map/ppermute | solution.py:627
  60.0 9.8 %collective-permute-start.15 = (f32[2,2,128,128]{3,2,1,0:T(8,128)S(1)}, f32[2,2,128,128]{3,2,1,0:T(8,128)S(1)}, u32[]{:S(2)}, u32[]{:S(2)}) collective-permute-start(f32[2,2,128,128]{3,2,1,0:T(8,128)S(1)} %get-tuple-element.111), channel_id=1, source_target_pairs={{8,4},{12,8},{9,5},{13,9},{10,6},{14,10},{11,7},{15,11},{24,20},{2... | collective-permute-start | bytes 786440 | tf_op jit(solution)/shard_map/ppermute | solution.py:627
  65.4 8.3 %collective-permute-start.18 = (f32[2,2,128,128]{3,2,1,0:T(8,128)S(1)}, f32[2,2,128,128]{3,2,1,0:T(8,128)S(1)}, u32[]{:S(2)}, u32[]{:S(2)}) collective-permute-start(f32[2,2,128,128]{3,2,1,0:T(8,128)S(1)} %get-tuple-element.113.refs_2_), channel_id=1, source_target_pairs={{0,4},{4,8},{8,12},{1,5},{5,9},{9,13},{2,6},{6,10},{10,14},{3,7},{... | collective-permute-start | bytes 786440 | tf_op jit(solution)/shard_map/ppermute | solution.py:627
  70.0 9.9 %collective-permute-start.17 = (f32[2,2,128,128]{3,2,1,0:T(8,128)S(1)}, f32[2,2,128,128]{3,2,1,0:T(8,128)S(1)}, u32[]{:S(2)}, u32[]{:S(2)}) collective-permute-start(f32[2,2,128,128]{3,2,1,0:T(8,128)S(1)} %get-tuple-element.115), channel_id=1, source_target_pairs={{4,0},{8,4},{12,8},{5,1},{9,5},{13,9},{6,2},{10,6},{14,10},{7,3},{... | collective-permute-start | bytes 786440 | tf_op jit(solution)/shard_map/ppermute | solution.py:627
  74.6 8.8 %collective-permute-start.20 = (f32[2,2,128,128]{3,2,1,0:T(8,128)S(1)}, f32[2,2,128,128]{3,2,1,0:T(8,128)S(1)}, u32[]{:S(2)}, u32[]{:S(2)}) collective-permute-start(f32[2,2,128,128]{3,2,1,0:T(8,128)S(1)} %get-tuple-element.117.refs_2_), channel_id=1, source_target_pairs={{0,4},{4,8},{8,12},{1,5},{5,9},{9,13},{2,6},{6,10},{10,14},{3,7},{... | collective-permute-start | bytes 786440 | tf_op jit(solution)/shard_map/ppermute | solution.py:627
  80.8 8.5 %collective-permute-start.19 = (f32[2,2,128,128]{3,2,1,0:T(8,128)S(1)}, f32[2,2,128,128]{3,2,1,0:T(8,128)S(1)}, u32[]{:S(2)}, u32[]{:S(2)}) collective-permute-start(f32[2,2,128,128]{3,2,1,0:T(8,128)S(1)} %get-tuple-element.119), channel_id=1, source_target_pairs={{4,0},{8,4},{12,8},{5,1},{9,5},{13,9},{6,2},{10,6},{14,10},{7,3},{... | collective-permute-start | bytes 786440 | tf_op jit(solution)/shard_map/ppermute | solution.py:627
  84.3 8.9 %collective-permute-start.22 = (f32[2,2,128,128]{3,2,1,0:T(8,128)S(1)}, f32[2,2,128,128]{3,2,1,0:T(8,128)S(1)}, u32[]{:S(2)}, u32[]{:S(2)}) collective-permute-start(f32[2,2,128,128]{3,2,1,0:T(8,128)S(1)} %get-tuple-element.121.refs_2_), channel_id=1, source_target_pairs={{0,4},{4,8},{8,12},{1,5},{5,9},{9,13},{2,6},{6,10},{10,14},{3,7},{... | collective-permute-start | bytes 786440 | tf_op jit(solution)/shard_map/ppermute | solution.py:627
  90.2 8.3 %collective-permute-start.21 = (f32[2,2,128,128]{3,2,1,0:T(8,128)S(1)}, f32[2,2,128,128]{3,2,1,0:T(8,128)S(1)}, u32[]{:S(2)}, u32[]{:S(2)}) collective-permute-start(f32[2,2,128,128]{3,2,1,0:T(8,128)S(1)} %get-tuple-element.123), channel_id=1, source_target_pairs={{4,0},{8,4},{12,8},{5,1},{9,5},{13,9},{6,2},{10,6},{14,10},{7,3},{... | collective-permute-start | bytes 786440 | tf_op jit(solution)/shard_map/ppermute | solution.py:627
  91.6 28.5 %collective-permute-start.28 = (f32[2048,128]{1,0:T(8,128)S(1)}, f32[2048,128]{1,0:T(8,128)S(1)}, u32[]{:S(2)}, u32[]{:S(2)}) collective-permute-start(f32[2048,128]{1,0:T(8,128)S(1)} %slice.10), channel_id=1, source_target_pairs={{0,2},{2,0},{1,3},{3,1},{4,6},{6,4},{5,7},{7,5},{8,10},{10,8},{9,1... | collective-permute-start | bytes 3145736 | tf_op jit(solution)/shard_map/ppermute | solution.py:512
  93.3 8.5 %collective-permute-start.24 = (f32[2,2,128,128]{3,2,1,0:T(8,128)S(1)}, f32[2,2,128,128]{3,2,1,0:T(8,128)S(1)}, u32[]{:S(2)}, u32[]{:S(2)}) collective-permute-start(f32[2,2,128,128]{3,2,1,0:T(8,128)S(1)} %get-tuple-element.125.refs_2_), channel_id=1, source_target_pairs={{4,8},{8,12},{5,9},{9,13},{6,10},{10,14},{7,11},{11,15},{20,24},{2... | collective-permute-start | bytes 786440 | tf_op jit(solution)/shard_map/ppermute | solution.py:627
  99.4 8.6 %collective-permute-start.23 = (f32[2,2,128,128]{3,2,1,0:T(8,128)S(1)}, f32[2,2,128,128]{3,2,1,0:T(8,128)S(1)}, u32[]{:S(2)}, u32[]{:S(2)}) collective-permute-start(f32[2,2,128,128]{3,2,1,0:T(8,128)S(1)} %get-tuple-element.127), channel_id=1, source_target_pairs={{4,0},{8,4},{12,8},{5,1},{9,5},{13,9},{6,2},{10,6},{14,10},{7,3},{... | collective-permute-start | bytes 786440 | tf_op jit(solution)/shard_map/ppermute | solution.py:627
  101.8 11.1 %collective-permute-start.26 = (f32[2,2,128,128]{3,2,1,0:T(8,128)S(1)}, f32[2,2,128,128]{3,2,1,0:T(8,128)S(1)}, u32[]{:S(2)}, u32[]{:S(2)}) collective-permute-start(f32[2,2,128,128]{3,2,1,0:T(8,128)S(1)} %get-tuple-element.129.refs_2_), channel_id=1, source_target_pairs={{8,12},{9,13},{10,14},{11,15},{24,28},{25,29},{26,30},{27,31}} | collective-permute-start | bytes 786440 | tf_op jit(solution)/shard_map/ppermute | solution.py:627
  108.9 9.0 %collective-permute-start.25 = (f32[2,2,128,128]{3,2,1,0:T(8,128)S(1)}, f32[2,2,128,128]{3,2,1,0:T(8,128)S(1)}, u32[]{:S(2)}, u32[]{:S(2)}) collective-permute-start(f32[2,2,128,128]{3,2,1,0:T(8,128)S(1)} %get-tuple-element.131), channel_id=1, source_target_pairs={{4,0},{8,4},{12,8},{5,1},{9,5},{13,9},{6,2},{10,6},{14,10},{7,3},{... | collective-permute-start | bytes 786440 | tf_op jit(solution)/shard_map/ppermute | solution.py:627
  110.2 33.4 %collective-permute-start.31 = (f32[2048,128]{1,0:T(8,128)S(1)}, f32[2048,128]{1,0:T(8,128)S(1)}, u32[]{:S(2)}, u32[]{:S(2)}) collective-permute-start(f32[2048,128]{1,0:T(8,128)S(1)} %slice.11), channel_id=1, source_target_pairs={{0,2},{2,0},{1,3},{3,1},{4,6},{6,4},{5,7},{7,5},{8,10},{10,8},{9,1... | collective-permute-start | bytes 3145736 | tf_op jit(solution)/shard_map/ppermute | solution.py:512
  118.7 10.2 %collective-permute-start.27 = (f32[2,2,128,128]{3,2,1,0:T(8,128)S(1)}, f32[2,2,128,128]{3,2,1,0:T(8,128)S(1)}, u32[]{:S(2)}, u32[]{:S(2)}) collective-permute-start(f32[2,2,128,128]{3,2,1,0:T(8,128)S(1)} %get-tuple-element.135), channel_id=1, source_target_pairs={{4,0},{8,4},{12,8},{5,1},{9,5},{13,9},{6,2},{10,6},{14,10},{7,3},{... | collective-permute-start | bytes 786440 | tf_op jit(solution)/shard_map/ppermute | solution.py:627
  129.8 11.6 %collective-permute-start.29 = (f32[2,2,128,128]{3,2,1,0:T(8,128)S(1)}, f32[2,2,128,128]{3,2,1,0:T(8,128)S(1)}, u32[]{:S(2)}, u32[]{:S(2)}) collective-permute-start(f32[2,2,128,128]{3,2,1,0:T(8,128)S(1)} %get-tuple-element.137), channel_id=1, source_target_pairs={{4,0},{8,4},{5,1},{9,5},{6,2},{10,6},{7,3},{11,7},{20,16},{24,20},... | collective-permute-start | bytes 786440 | tf_op jit(solution)/shard_map/ppermute | solution.py:627
  142.4 8.3 %collective-permute-start.30 = (f32[2,2,128,128]{3,2,1,0:T(8,128)S(1)}, f32[2,2,128,128]{3,2,1,0:T(8,128)S(1)}, u32[]{:S(2)}, u32[]{:S(2)}) collective-permute-start(f32[2,2,128,128]{3,2,1,0:T(8,128)S(1)} %get-tuple-element.139), channel_id=1, source_target_pairs={{4,0},{5,1},{6,2},{7,3},{20,16},{21,17},{22,18},{23,19}} | collective-permute-start | bytes 786440 | tf_op jit(solution)/shard_map/ppermute | solution.py:627
  153.1 4.6 %collective-permute-start.32 = (f32[2,2,1,192,768]{4,3,2,1,0:T(8,128)S(1)}, f32[2,2,1,192,768]{4,3,2,1,0:T(8,128)S(1)}, u32[]{:S(2)}, u32[]{:S(2)}) collective-permute-start(f32[2,2,1,192,768]{4,3,2,1,0:T(8,128)S(1)} %split_rows.6), channel_id=1, source_target_pairs={{0,1},{1,0},{2,3},{3,2},{4,5},{5,4},{6,7},{7,6},{8,9},{9,8},{10,11... | collective-permute-start | bytes 7077896 | tf_op jit(solution)/shard_map/ppermute | solution.py:512

commit v9 on v8

--- a/solution.py
+++ b/solution.py
@@ -638,13 +638,16 @@
         early_sections = min(group, lay.groups) * count
         return lambda section: jnp.where(section < 2, early_sections, probes)
 
-    cuts = {0: (count, upto(3)), 2: (upto(3), upto(5)), 3: (upto(5), probes)}
+    cuts = {0: (count, upto(3)), 1: (upto(3), upto(5)), 3: (upto(5), probes)}
     last_tick = lay.groups + 2 * fill - 1
     for tick in range(lay.groups + 2 * fill):
         own = None
-        if paired and tick == fill - 1:
-            down, mine, everyone = lax.optimization_barrier((down, mine, everyone))
-            crossed = [lax.ppermute(x, ("depth", "lat"), ends) for x in (frames, mine)]
+        if tick == fill:
+            pools = [frames]
+            if paired:
+                down, mine, everyone = lax.optimization_barrier((down, mine, everyone))
+                pools += [mine, *(lax.ppermute(x, ("depth", "lat"), ends) for x in (frames, mine))]
+            state, late = place_frames(lay, sections, info, everyone, pools, state)
         if tick < lay.groups + fill:
             start_wave = illumination if tick < lay.groups else None
             state, own = run_forward(lay, tick, sections, tables, state, down, start_wave)
@@ -656,9 +659,6 @@
                 state = cut_patches(lay, info, brought, other, state, *cuts[tick])
             if tick == 0:
                 state = clear_total(lay, state)
-            if tick == fill - 1:
-                pools = [frames, mine, *crossed] if paired else [frames]
-                state, late = place_frames(lay, sections, info, everyone, pools, state)
         if tick >= fill:
             state, *rising = run_backward(lay, tick, sections, tables, state, up, own, tick < last_tick)
             up = pass_on(rising[0], tick, -1) if rising else None

time: 160 us -> 165 us (1.031)
  starting transfers between devices: 58.6 us -> 65.3 us
  waiting for transfers between devices: 55.8 us -> 53.8 us
    ppermute x8, starting transfers between devices: 7.3 us -> 11.3 us  [swap(): return lax.ppermute(shard, axis, [(0, 1), (1, 0)])]
    ppermute x20, starting transfers between devices: 49.2 us -> 51.9 us  [pass_on(): return lax.ppermute(wave, 'depth', pairs) if pairs else None]
  transfers between devices with their start and end apart: 31 -> 31, of which waited for: 20 -> 18; matrix products, arithmetic and copies ran while one was open for 0% -> 0% of each run, Pallas kernels for 25% -> 23%
where the time goes in v9:
time: 165 us; the launch traced here: 164 us
  starting transfers between devices  65.3 us (40%)
  waiting for transfers between devices  53.8 us (33%)
  Pallas kernels  43.9 us (27%)
    ppermute x20, starting transfers between devices, pass_on(): return lax.ppermute(wave, 'depth', pairs) if pairs else None  51.9 us
    ppermute x20, waiting for transfers between devices, pass_on(): return lax.ppermute(wave, 'depth', pairs) if pairs else None  45.9 us
    pallas_call x39, Pallas kernels, call(): pl.pallas_call(kernel, in_specs=specs, out_specs=[VMEM] * (1 + len(outs)...  36.1 us
    ppermute x8, starting transfers between devices, swap(): return lax.ppermute(shard, axis, [(0, 1), (1, 0)])  11.3 us
    ppermute x8, waiting for transfers between devices, swap(): return lax.ppermute(shard, axis, [(0, 1), (1, 0)])  7.95 us
  transfers between devices with their start and end apart: 31, of which 18 were waited for; matrix products, arithmetic and copies ran while one was open for 0% of the time, Pallas kernels for 23%

profile of v9, /device:TPU:0, one launch (start us, length us, event | category | flops | bytes accessed | tf_op | source)
XLA Modules:
  0.0 164.0 jit_solution(7275647124762985220)
XLA Ops:
  1.7 2.7 %collective-permute-start.2 = (s32[16]{0:T(128)}, s32[16]{0:T(128)S(1)}, u32[]{:S(2)}, u32[]{:S(2)}) collective-permute-start(s32[16]{0:T(128)} %bitcast.20), channel_id=1, source_target_pairs={{0,2},{2,0},{1,3},{3,1},{4,6},{6,4},{5,7},{7,5},{8,10},{10,8},{9,1... | collective-permute-start | bytes 200 | tf_op jit(solution)/shard_map/ppermute | solution.py:512
  4.4 1.6 collective-permute-done.2.refs_0_
  6.1 1.9 %collective-permute-done.4.refs_2_ = s32[16]{0:T(128)S(1)} collective-permute-done((s32[16]{0:T(128)S(1)}, s32[16]{0:T(128)S(1)}, u32[]{:S(2)}, u32[]{:S(2)}) %collective-permute-start.4) | collective-permute-done | bytes 96 | tf_op jit(solution)/shard_map/ppermute | solution.py:512
  8.7 1.7 %sort_probes.1.refs_0_ = s32[1,128]{1,0:T(1,128)S(1)} custom-call(s32[2,512]{1,0:T(2,128)} %bitcast.18, s32[1,16]{1,0:T(1,128)} %bitcast.21, s32[16]{0:T(128)S(1)} %collective-permute-done.2.refs_0_, s32[16]{0:T(128)S(1)} %collective-permute-done.3.refs_1_, s32[16]{0:T(128)S(1)} %collective-permute-done.4.refs_2_), custom_call_target="tpu_custom_call" | custom-call | tf_op jit(solution)/shard_map/sort_probes/pallas_call | solution.py:552
  10.4 2.9 %cut_patches.4.refs_2_ = f32[42368,128]{1,0:T(8,128)S(1)} custom-call(s32[1,128]{1,0:T(1,128)S(1)} %sort_probes.1.refs_0_, f32[2,2,384,768]{3,2,1,0:T(8,128)} %x, f32[2,2,384,768]{3,2,1,0:T(8,128)S(1)} %collective-permute-done.5.refs_2_), custom_call_target="tpu_custom_call" | custom-call | flops 1000 | bytes 1000 | tf_op jit(solution)/shard_map/cut_patches/pallas_call | solution.py:157
  14.3 3.0 %collective-permute-start.6 = (f32[2,2,128,128]{3,2,1,0:T(8,128)S(1)}, f32[2,2,128,128]{3,2,1,0:T(8,128)S(1)}, u32[]{:S(2)}, u32[]{:S(2)}) collective-permute-start(f32[2,2,128,128]{3,2,1,0:T(8,128)S(1)} %get-tuple-element.92), channel_id=1, source_target_pairs={{0,4},{1,5},{2,6},{3,7},{16,20},{17,21},{18,22},{19,23}} | collective-permute-start | bytes 786440 | tf_op jit(solution)/shard_map/ppermute | solution.py:627
  17.3 2.3 %bring.1.refs_1_ = f32[2,2,384,768]{3,2,1,0:T(8,128)S(1)} custom-call(f32[2,2,384,768]{3,2,1,0:T(8,128)} %x), custom_call_target="tpu_custom_call" | custom-call | flops 1000 | bytes 1000 | tf_op jit(solution)/shard_map/bring/pallas_call | solution.py:573
  19.7 1.7 %cut_patches.5.refs_0_ = f32[42368,128]{1,0:T(8,128)S(1)} custom-call(s32[1,128]{1,0:T(1,128)S(1)} %sort_probes.1.refs_0_, f32[2,2,384,768]{3,2,1,0:T(8,128)S(1)} %bring.1.refs_1_, f32[2,2,384,768]{3,2,1,0:T(8,128)S(1)} %collective-permute-done.5.refs_2_, f32[42368,128]{1,0:T(8,128)S(1)} %get-tuple-element.94.refs_3_), custom_call_target="tpu_custom_call", output_to_operand_aliasing={{}: (3, {})} | custom-call | flops 1000 | bytes 1000 | tf_op jit(solution)/shard_map/cut_patches/pallas_call | solution.py:157
  23.1 4.4 %collective-permute-start.7 = (f32[2,2,128,128]{3,2,1,0:T(8,128)S(1)}, f32[2,2,128,128]{3,2,1,0:T(8,128)S(1)}, u32[]{:S(2)}, u32[]{:S(2)}) collective-permute-start(f32[2,2,128,128]{3,2,1,0:T(8,128)S(1)} %get-tuple-element.95), channel_id=1, source_target_pairs={{0,4},{4,8},{1,5},{5,9},{2,6},{6,10},{3,7},{7,11},{16,20},{20,24},... | collective-permute-start | bytes 786440 | tf_op jit(solution)/shard_map/ppermute | solution.py:627
  27.5 1.7 %cut_patches.6.refs_3_ = f32[42368,128]{1,0:T(8,128)S(1)} custom-call(s32[1,128]{1,0:T(1,128)S(1)} %sort_probes.1.refs_0_, f32[2,2,384,768]{3,2,1,0:T(8,128)S(1)} %bring.1.refs_1_, f32[2,2,384,768]{3,2,1,0:T(8,128)S(1)} %collective-permute-done.5.refs_2_, f32[42368,128]{1,0:T(8,128)S(1)} %get-tuple-element.96.refs_3_), custom_call_target="tpu_custom_call", output_to_operand_aliasing={{}: (3, {})} | custom-call | flops 1000 | bytes 1000 | tf_op jit(solution)/shard_map/cut_patches/pallas_call | solution.py:157
  29.2 2.2 %collective-permute-done.7.refs_1_ = f32[2,2,128,128]{3,2,1,0:T(8,128)S(1)} collective-permute-done((f32[2,2,128,128]{3,2,1,0:T(8,128)S(1)}, f32[2,2,128,128]{3,2,1,0:T(8,128)S(1)}, u32[]{:S(2)}, u32[]{:S(2)}) %collective-permute-start.7) | collective-permute-done | bytes 262176 | tf_op jit(solution)/shard_map/ppermute | solution.py:627
  32.4 4.4 %collective-permute-start.8 = (f32[2,2,128,128]{3,2,1,0:T(8,128)S(1)}, f32[2,2,128,128]{3,2,1,0:T(8,128)S(1)}, u32[]{:S(2)}, u32[]{:S(2)}) collective-permute-start(f32[2,2,128,128]{3,2,1,0:T(8,128)S(1)} %get-tuple-element.97), channel_id=1, source_target_pairs={{0,4},{4,8},{8,12},{1,5},{5,9},{9,13},{2,6},{6,10},{10,14},{3,7},{... | collective-permute-start | bytes 786440 | tf_op jit(solution)/shard_map/ppermute | solution.py:627
  36.8 3.8 %collective-permute-start.10 = (s32[1,128]{1,0:T(1,128)S(1)}, s32[1,128]{1,0:T(1,128)S(1)}, u32[]{:S(2)}, u32[]{:S(2)}) collective-permute-start(s32[1,128]{1,0:T(1,128)S(1)} %sort_probes.1.refs_0_), channel_id=1, source_target_pairs={{0,16},{16,0},{1,17},{17,1},{2,18},{18,2},{3,19},{19,3},{4,20},{20... | collective-permute-start | bytes 1544 | tf_op jit(solution)/shard_map/ppermute | solution.py:512
  44.5 3.0 %collective-permute-start.14 = (f32[2,2,128,128]{3,2,1,0:T(8,128)S(1)}, f32[2,2,128,128]{3,2,1,0:T(8,128)S(1)}, u32[]{:S(2)}, u32[]{:S(2)}) collective-permute-start(f32[2,2,128,128]{3,2,1,0:T(8,128)S(1)} %get-tuple-element.105.refs_1_), channel_id=1, source_target_pairs={{0,4},{4,8},{8,12},{1,5},{5,9},{9,13},{2,6},{6,10},{10,14},{3,7},{... | collective-permute-start | bytes 786440 | tf_op jit(solution)/shard_map/ppermute | solution.py:627
  47.5 2.5 %cut_patches.7.refs_2_ = f32[42368,128]{1,0:T(8,128)S(1)} custom-call(s32[1,128]{1,0:T(1,128)S(1)} %sort_probes.1.refs_0_, f32[2,2,384,768]{3,2,1,0:T(8,128)S(1)} %bring.1.refs_1_, f32[2,2,384,768]{3,2,1,0:T(8,128)S(1)} %collective-permute-done.5.refs_2_, f32[42368,128]{1,0:T(8,128)S(1)} %get-tuple-element.106.refs_3_), custom_call_target="tpu_custom_call", output_to_operand_aliasing={{}: (3, {})} | custom-call | flops 1000 | bytes 1000 | tf_op jit(solution)/shard_map/cut_patches/pallas_call | solution.py:157
  52.3 4.4 %collective-permute-start.16 = (f32[2,2,128,128]{3,2,1,0:T(8,128)S(1)}, f32[2,2,128,128]{3,2,1,0:T(8,128)S(1)}, u32[]{:S(2)}, u32[]{:S(2)}) collective-permute-start(f32[2,2,128,128]{3,2,1,0:T(8,128)S(1)} %get-tuple-element.109.refs_2_), channel_id=1, source_target_pairs={{0,4},{4,8},{8,12},{1,5},{5,9},{9,13},{2,6},{6,10},{10,14},{3,7},{... | collective-permute-start | bytes 786440 | tf_op jit(solution)/shard_map/ppermute | solution.py:627
  57.7 2.8 %collective-permute-done.16.refs_1_ = f32[2,2,128,128]{3,2,1,0:T(8,128)S(1)} collective-permute-done((f32[2,2,128,128]{3,2,1,0:T(8,128)S(1)}, f32[2,2,128,128]{3,2,1,0:T(8,128)S(1)}, u32[]{:S(2)}, u32[]{:S(2)}) %collective-permute-start.16) | collective-permute-done | bytes 262176 | tf_op jit(solution)/shard_map/ppermute | solution.py:627
  61.5 10.1 %collective-permute-start.18 = (f32[2,2,128,128]{3,2,1,0:T(8,128)S(1)}, f32[2,2,128,128]{3,2,1,0:T(8,128)S(1)}, u32[]{:S(2)}, u32[]{:S(2)}) collective-permute-start(f32[2,2,128,128]{3,2,1,0:T(8,128)S(1)} %get-tuple-element.113.refs_2_), channel_id=1, source_target_pairs={{0,4},{4,8},{8,12},{1,5},{5,9},{9,13},{2,6},{6,10},{10,14},{3,7},{... | collective-permute-start | bytes 786440 | tf_op jit(solution)/shard_map/ppermute | solution.py:627
  71.8 1.3 collective-permute-start.17
  73.4 2.0 %collective-permute-done.18.refs_1_ = f32[2,2,128,128]{3,2,1,0:T(8,128)S(1)} collective-permute-done((f32[2,2,128,128]{3,2,1,0:T(8,128)S(1)}, f32[2,2,128,128]{3,2,1,0:T(8,128)S(1)}, u32[]{:S(2)}, u32[]{:S(2)}) %collective-permute-start.18) | collective-permute-done | bytes 262176 | tf_op jit(solution)/shard_map/ppermute | solution.py:627
  76.4 5.0 %collective-permute-start.20 = (f32[2,2,128,128]{3,2,1,0:T(8,128)S(1)}, f32[2,2,128,128]{3,2,1,0:T(8,128)S(1)}, u32[]{:S(2)}, u32[]{:S(2)}) collective-permute-start(f32[2,2,128,128]{3,2,1,0:T(8,128)S(1)} %get-tuple-element.117.refs_2_), channel_id=1, source_target_pairs={{0,4},{4,8},{8,12},{1,5},{5,9},{9,13},{2,6},{6,10},{10,14},{3,7},{... | collective-permute-start | bytes 786440 | tf_op jit(solution)/shard_map/ppermute | solution.py:627
  82.8 1.3 collective-permute-start.19
  84.1 1.1 deposit_patches.16.refs_3_
  86.1 4.6 %collective-permute-start.22 = (f32[2,2,128,128]{3,2,1,0:T(8,128)S(1)}, f32[2,2,128,128]{3,2,1,0:T(8,128)S(1)}, u32[]{:S(2)}, u32[]{:S(2)}) collective-permute-start(f32[2,2,128,128]{3,2,1,0:T(8,128)S(1)} %get-tuple-element.121.refs_2_), channel_id=1, source_target_pairs={{0,4},{4,8},{8,12},{1,5},{5,9},{9,13},{2,6},{6,10},{10,14},{3,7},{... | collective-permute-start | bytes 786440 | tf_op jit(solution)/shard_map/ppermute | solution.py:627
  92.0 1.3 collective-permute-start.21
  93.4 3.7 %collective-permute-start.28 = (f32[2048,128]{1,0:T(8,128)S(1)}, f32[2048,128]{1,0:T(8,128)S(1)}, u32[]{:S(2)}, u32[]{:S(2)}) collective-permute-start(f32[2048,128]{1,0:T(8,128)S(1)} %slice.10), channel_id=1, source_target_pairs={{0,2},{2,0},{1,3},{3,1},{4,6},{6,4},{5,7},{7,5},{8,10},{10,8},{9,1... | collective-permute-start | bytes 3145736 | tf_op jit(solution)/shard_map/ppermute | solution.py:512
  97.0 1.1 deposit_patches.17.refs_2_
  98.8 1.4 collective-permute-done.21.refs_1_
  101.2 1.3 collective-permute-start.23
  102.5 1.1 deposit_patches.18.refs_2_
  104.3 8.6 %collective-permute-done.23.refs_1_ = f32[2,2,128,128]{3,2,1,0:T(8,128)S(1)} collective-permute-done((f32[2,2,128,128]{3,2,1,0:T(8,128)S(1)}, f32[2,2,128,128]{3,2,1,0:T(8,128)S(1)}, u32[]{:S(2)}, u32[]{:S(2)}) %collective-permute-start.23) | collective-permute-done | bytes 262176 | tf_op jit(solution)/shard_map/ppermute | solution.py:627
  113.7 1.3 collective-permute-start.25
  115.4 1.1 deposit_patches.19.refs_2_
  116.5 6.0 %collective-permute-done.25.refs_1_ = f32[2,2,128,128]{3,2,1,0:T(8,128)S(1)} collective-permute-done((f32[2,2,128,128]{3,2,1,0:T(8,128)S(1)}, f32[2,2,128,128]{3,2,1,0:T(8,128)S(1)}, u32[]{:S(2)}, u32[]{:S(2)}) %collective-permute-start.25) | collective-permute-done | bytes 262176 | tf_op jit(solution)/shard_map/ppermute | solution.py:627
  123.4 1.3 collective-permute-start.27
  124.7 2.1 %deposit_patches.20.refs_2_ = f32[42368,128]{1,0:T(8,128)S(1)} custom-call(s32[1,128]{1,0:T(1,128)S(1)} %sort_probes.1.refs_0_, f32[2048,128]{1,0:T(8,128)S(1)} %collective-permute-done.28.refs_1_, f32[42368,128]{1,0:T(8,128)S(1)} %get-tuple-element.136.refs_2_), custom_call_target="tpu_custom_call", output_to_operand_aliasing={{}: (2, {})} | custom-call | flops 1000 | bytes 1000 | tf_op jit(solution)/shard_map/deposit_patches/pallas_call | solution.py:157
  126.9 6.6 %collective-permute-done.27.refs_1_ = f32[2,2,128,128]{3,2,1,0:T(8,128)S(1)} collective-permute-done((f32[2,2,128,128]{3,2,1,0:T(8,128)S(1)}, f32[2,2,128,128]{3,2,1,0:T(8,128)S(1)}, u32[]{:S(2)}, u32[]{:S(2)}) %collective-permute-start.27) | collective-permute-done | bytes 262176 | tf_op jit(solution)/shard_map/ppermute | solution.py:627
  134.4 1.3 collective-permute-start.29
  135.7 1.1 deposit_patches.21.refs_2_
  136.8 9.4 %collective-permute-done.29.refs_1_ = f32[2,2,128,128]{3,2,1,0:T(8,128)S(1)} collective-permute-done((f32[2,2,128,128]{3,2,1,0:T(8,128)S(1)}, f32[2,2,128,128]{3,2,1,0:T(8,128)S(1)}, u32[]{:S(2)}, u32[]{:S(2)}) %collective-permute-start.29) | collective-permute-done | bytes 262176 | tf_op jit(solution)/shard_map/ppermute | solution.py:627
  147.0 1.3 collective-permute-start.30
  148.3 1.7 %deposit_patches.22.refs_2_ = f32[42368,128]{1,0:T(8,128)S(1)} custom-call(s32[1,128]{1,0:T(1,128)S(1)} %sort_probes.1.refs_0_, f32[2048,128]{1,0:T(8,128)S(1)} %collective-permute-done.31.refs_1_, f32[42368,128]{1,0:T(8,128)S(1)} %get-tuple-element.140.refs_2_), custom_call_target="tpu_custom_call", output_to_operand_aliasing={{}: (2, {})} | custom-call | flops 1000 | bytes 1000 | tf_op jit(solution)/shard_map/deposit_patches/pallas_call | solution.py:157
  150.0 5.3 %collective-permute-done.30.refs_1_ = f32[2,2,128,128]{3,2,1,0:T(8,128)S(1)} collective-permute-done((f32[2,2,128,128]{3,2,1,0:T(8,128)S(1)}, f32[2,2,128,128]{3,2,1,0:T(8,128)S(1)}, u32[]{:S(2)}, u32[]{:S(2)}) %collective-permute-start.30) | collective-permute-done | bytes 262176 | tf_op jit(solution)/shard_map/ppermute | solution.py:627
  156.2 1.1 deposit_patches.23.state
  157.9 1.8 %split_rows.7 = (f32[2,2,1,192,768]{4,3,2,1,0:T(8,128)S(1)}, f32[4096,128]{1,0:T(8,128)}) custom-call(f32[42368,128]{1,0:T(8,128)S(1)} %deposit_patches.23.state), custom_call_target="tpu_custom_call" | custom-call | flops 1000 | bytes 1000 | tf_op jit(solution)/shard_map/split_rows/pallas_call | solution.py:476
  159.7 2.7 %collective-permute-done.32 = f32[2,2,1,192,768]{4,3,2,1,0:T(8,128)S(1)} collective-permute-done((f32[2,2,1,192,768]{4,3,2,1,0:T(8,128)S(1)}, f32[2,2,1,192,768]{4,3,2,1,0:T(8,128)S(1)}, u32[]{:S(2)}, u32[]{:S(2)}) %collective-permute-start.32) | collective-permute-done | bytes 2359328 | tf_op jit(solution)/shard_map/ppermute | solution.py:512
  162.4 1.5 conditional.1
  162.4 1.5 add_up.2
  (67 shorter events, 26.9 us)
Async XLA Ops:
  0.0 13.3 %copy-start = (bf16[2,2,2,256,256]{4,3,2,1,0:T(8,128)(2,1)S(1)}, bf16[2,2,2,256,256]{4,3,2,1,0:T(8,128)(2,1)}, u32[]{:S(2)}) copy-start(bf16[2,2,2,256,256]{4,3,2,1,0:T(8,128)(2,1)} %constant.5.clone.refs_0_) | copy-start | bytes 3145732
  0.0 13.3 %copy-start.1 = (f32[2,128,128]{2,1,0:T(8,128)S(1)}, f32[2,128,128]{2,1,0:T(8,128)}, u32[]{:S(2)}) copy-start(f32[2,128,128]{2,1,0:T(8,128)} %refs_2_.13) | copy-start | bytes 393220
  0.0 1.4 collective-permute-start.3
  1.4 9.0 %collective-permute-start.5 = (f32[2,2,384,768]{3,2,1,0:T(8,128)}, f32[2,2,384,768]{3,2,1,0:T(8,128)S(1)}, u32[]{:S(2)}, u32[]{:S(2)}) collective-permute-start(f32[2,2,384,768]{3,2,1,0:T(8,128)} %x), channel_id=1, source_target_pairs={{0,1},{1,0},{2,3},{3,2},{4,5},{5,4},{6,7},{7,6},{8,9},{9,8},{10,11... | collective-permute-start | bytes 14155784 | tf_op jit(solution)/shard_map/ppermute | solution.py:512
  1.7 4.3 %collective-permute-start.2 = (s32[16]{0:T(128)}, s32[16]{0:T(128)S(1)}, u32[]{:S(2)}, u32[]{:S(2)}) collective-permute-start(s32[16]{0:T(128)} %bitcast.20), channel_id=1, source_target_pairs={{0,2},{2,0},{1,3},{3,1},{4,6},{6,4},{5,7},{7,5},{8,10},{10,8},{9,1... | collective-permute-start | bytes 200 | tf_op jit(solution)/shard_map/ppermute | solution.py:512
  4.4 3.5 %collective-permute-start.4 = (s32[16]{0:T(128)S(1)}, s32[16]{0:T(128)S(1)}, u32[]{:S(2)}, u32[]{:S(2)}) collective-permute-start(s32[16]{0:T(128)S(1)} %collective-permute-done.3.refs_1_), channel_id=1, source_target_pairs={{0,2},{2,0},{1,3},{3,1},{4,6},{6,4},{5,7},{7,5},{8,10},{10,8},{9,1... | collective-permute-start | bytes 200 | tf_op jit(solution)/shard_map/ppermute | solution.py:512
  7.9 34.2 %collective-permute-start.9 = (f32[16,1,128,128]{3,2,1,0:T(8,128)}, f32[16,1,128,128]{3,2,1,0:T(8,128)S(1)}, u32[]{:S(2)}, u32[]{:S(2)}) collective-permute-start(f32[16,1,128,128]{3,2,1,0:T(8,128)} %param.12), channel_id=1, source_target_pairs={{12,14},{14,12},{13,15},{15,13},{28,30},{30,28},{29,31},{31,29}} | collective-permute-start | bytes 3145736 | tf_op jit(solution)/shard_map/ppermute | solution.py:608
  14.3 7.9 %collective-permute-start.6 = (f32[2,2,128,128]{3,2,1,0:T(8,128)S(1)}, f32[2,2,128,128]{3,2,1,0:T(8,128)S(1)}, u32[]{:S(2)}, u32[]{:S(2)}) collective-permute-start(f32[2,2,128,128]{3,2,1,0:T(8,128)S(1)} %get-tuple-element.92), channel_id=1, source_target_pairs={{0,4},{1,5},{2,6},{3,7},{16,20},{17,21},{18,22},{19,23}} | collective-permute-start | bytes 786440 | tf_op jit(solution)/shard_map/ppermute | solution.py:627
  23.1 8.3 %collective-permute-start.7 = (f32[2,2,128,128]{3,2,1,0:T(8,128)S(1)}, f32[2,2,128,128]{3,2,1,0:T(8,128)S(1)}, u32[]{:S(2)}, u32[]{:S(2)}) collective-permute-start(f32[2,2,128,128]{3,2,1,0:T(8,128)S(1)} %get-tuple-element.95), channel_id=1, source_target_pairs={{0,4},{4,8},{1,5},{5,9},{2,6},{6,10},{3,7},{7,11},{16,20},{20,24},... | collective-permute-start | bytes 786440 | tf_op jit(solution)/shard_map/ppermute | solution.py:627
  29.2 11.4 %copy-start.2 = (f32[16,1,128,128]{3,2,1,0:T(8,128)S(1)}, f32[16,1,128,128]{3,2,1,0:T(8,128)}, u32[]{:S(2)}) copy-start(f32[16,1,128,128]{3,2,1,0:T(8,128)} %param.12) | copy-start | bytes 3145732
  32.4 9.7 %collective-permute-start.8 = (f32[2,2,128,128]{3,2,1,0:T(8,128)S(1)}, f32[2,2,128,128]{3,2,1,0:T(8,128)S(1)}, u32[]{:S(2)}, u32[]{:S(2)}) collective-permute-start(f32[2,2,128,128]{3,2,1,0:T(8,128)S(1)} %get-tuple-element.97), channel_id=1, source_target_pairs={{0,4},{4,8},{8,12},{1,5},{5,9},{9,13},{2,6},{6,10},{10,14},{3,7},{... | collective-permute-start | bytes 786440 | tf_op jit(solution)/shard_map/ppermute | solution.py:627
  36.8 5.3 %collective-permute-start.10 = (s32[1,128]{1,0:T(1,128)S(1)}, s32[1,128]{1,0:T(1,128)S(1)}, u32[]{:S(2)}, u32[]{:S(2)}) collective-permute-start(s32[1,128]{1,0:T(1,128)S(1)} %sort_probes.1.refs_0_), channel_id=1, source_target_pairs={{0,16},{16,0},{1,17},{17,1},{2,18},{18,2},{3,19},{19,3},{4,20},{20... | collective-permute-start | bytes 1544 | tf_op jit(solution)/shard_map/ppermute | solution.py:512
  40.6 2.3 %collective-permute-start.11 = (f32[16,1,128,128]{3,2,1,0:T(8,128)S(1)}, f32[16,1,128,128]{3,2,1,0:T(8,128)S(1)}, u32[]{:S(2)}, u32[]{:S(2)}) collective-permute-start(f32[16,1,128,128]{3,2,1,0:T(8,128)S(1)} %copy-done.2), channel_id=1, source_target_pairs={{12,13},{13,12},{14,15},{15,14},{28,29},{29,28},{30,31},{31,30}} | collective-permute-start | bytes 3145736 | tf_op jit(solution)/shard_map/ppermute | solution.py:649
  42.1 0.7 collective-permute-start.12
  44.5 6.8 %collective-permute-start.14 = (f32[2,2,128,128]{3,2,1,0:T(8,128)S(1)}, f32[2,2,128,128]{3,2,1,0:T(8,128)S(1)}, u32[]{:S(2)}, u32[]{:S(2)}) collective-permute-start(f32[2,2,128,128]{3,2,1,0:T(8,128)S(1)} %get-tuple-element.105.refs_1_), channel_id=1, source_target_pairs={{0,4},{4,8},{8,12},{1,5},{5,9},{9,13},{2,6},{6,10},{10,14},{3,7},{... | collective-permute-start | bytes 786440 | tf_op jit(solution)/shard_map/ppermute | solution.py:627
  50.0 6.7 %collective-permute-start.13 = (f32[2,2,128,128]{3,2,1,0:T(8,128)S(1)}, f32[2,2,128,128]{3,2,1,0:T(8,128)S(1)}, u32[]{:S(2)}, u32[]{:S(2)}) collective-permute-start(f32[2,2,128,128]{3,2,1,0:T(8,128)S(1)} %get-tuple-element.107), channel_id=1, source_target_pairs={{12,8},{13,9},{14,10},{15,11},{28,24},{29,25},{30,26},{31,27}} | collective-permute-start | bytes 786440 | tf_op jit(solution)/shard_map/ppermute | solution.py:627
  52.3 8.3 %collective-permute-start.16 = (f32[2,2,128,128]{3,2,1,0:T(8,128)S(1)}, f32[2,2,128,128]{3,2,1,0:T(8,128)S(1)}, u32[]{:S(2)}, u32[]{:S(2)}) collective-permute-start(f32[2,2,128,128]{3,2,1,0:T(8,128)S(1)} %get-tuple-element.109.refs_2_), channel_id=1, source_target_pairs={{0,4},{4,8},{8,12},{1,5},{5,9},{9,13},{2,6},{6,10},{10,14},{3,7},{... | collective-permute-start | bytes 786440 | tf_op jit(solution)/shard_map/ppermute | solution.py:627
  56.7 14.9 %collective-permute-start.15 = (f32[2,2,128,128]{3,2,1,0:T(8,128)S(1)}, f32[2,2,128,128]{3,2,1,0:T(8,128)S(1)}, u32[]{:S(2)}, u32[]{:S(2)}) collective-permute-start(f32[2,2,128,128]{3,2,1,0:T(8,128)S(1)} %get-tuple-element.111), channel_id=1, source_target_pairs={{8,4},{12,8},{9,5},{13,9},{10,6},{14,10},{11,7},{15,11},{24,20},{2... | collective-permute-start | bytes 786440 | tf_op jit(solution)/shard_map/ppermute | solution.py:627
  61.5 14.0 %collective-permute-start.18 = (f32[2,2,128,128]{3,2,1,0:T(8,128)S(1)}, f32[2,2,128,128]{3,2,1,0:T(8,128)S(1)}, u32[]{:S(2)}, u32[]{:S(2)}) collective-permute-start(f32[2,2,128,128]{3,2,1,0:T(8,128)S(1)} %get-tuple-element.113.refs_2_), channel_id=1, source_target_pairs={{0,4},{4,8},{8,12},{1,5},{5,9},{9,13},{2,6},{6,10},{10,14},{3,7},{... | collective-permute-start | bytes 786440 | tf_op jit(solution)/shard_map/ppermute | solution.py:627
  71.8 10.1 %collective-permute-start.17 = (f32[2,2,128,128]{3,2,1,0:T(8,128)S(1)}, f32[2,2,128,128]{3,2,1,0:T(8,128)S(1)}, u32[]{:S(2)}, u32[]{:S(2)}) collective-permute-start(f32[2,2,128,128]{3,2,1,0:T(8,128)S(1)} %get-tuple-element.115), channel_id=1, source_target_pairs={{4,0},{8,4},{12,8},{5,1},{9,5},{13,9},{6,2},{10,6},{14,10},{7,3},{... | collective-permute-start | bytes 786440 | tf_op jit(solution)/shard_map/ppermute | solution.py:627
  76.4 8.8 %collective-permute-start.20 = (f32[2,2,128,128]{3,2,1,0:T(8,128)S(1)}, f32[2,2,128,128]{3,2,1,0:T(8,128)S(1)}, u32[]{:S(2)}, u32[]{:S(2)}) collective-permute-start(f32[2,2,128,128]{3,2,1,0:T(8,128)S(1)} %get-tuple-element.117.refs_2_), channel_id=1, source_target_pairs={{0,4},{4,8},{8,12},{1,5},{5,9},{9,13},{2,6},{6,10},{10,14},{3,7},{... | collective-permute-start | bytes 786440 | tf_op jit(solution)/shard_map/ppermute | solution.py:627
  82.8 8.3 %collective-permute-start.19 = (f32[2,2,128,128]{3,2,1,0:T(8,128)S(1)}, f32[2,2,128,128]{3,2,1,0:T(8,128)S(1)}, u32[]{:S(2)}, u32[]{:S(2)}) collective-permute-start(f32[2,2,128,128]{3,2,1,0:T(8,128)S(1)} %get-tuple-element.119), channel_id=1, source_target_pairs={{4,0},{8,4},{12,8},{5,1},{9,5},{13,9},{6,2},{10,6},{14,10},{7,3},{... | collective-permute-start | bytes 786440 | tf_op jit(solution)/shard_map/ppermute | solution.py:627
  86.1 12.0 %collective-permute-start.22 = (f32[2,2,128,128]{3,2,1,0:T(8,128)S(1)}, f32[2,2,128,128]{3,2,1,0:T(8,128)S(1)}, u32[]{:S(2)}, u32[]{:S(2)}) collective-permute-start(f32[2,2,128,128]{3,2,1,0:T(8,128)S(1)} %get-tuple-element.121.refs_2_), channel_id=1, source_target_pairs={{0,4},{4,8},{8,12},{1,5},{5,9},{9,13},{2,6},{6,10},{10,14},{3,7},{... | collective-permute-start | bytes 786440 | tf_op jit(solution)/shard_map/ppermute | solution.py:627
  92.0 8.3 %collective-permute-start.21 = (f32[2,2,128,128]{3,2,1,0:T(8,128)S(1)}, f32[2,2,128,128]{3,2,1,0:T(8,128)S(1)}, u32[]{:S(2)}, u32[]{:S(2)}) collective-permute-start(f32[2,2,128,128]{3,2,1,0:T(8,128)S(1)} %get-tuple-element.123), channel_id=1, source_target_pairs={{4,0},{8,4},{12,8},{5,1},{9,5},{13,9},{6,2},{10,6},{14,10},{7,3},{... | collective-permute-start | bytes 786440 | tf_op jit(solution)/shard_map/ppermute | solution.py:627
  93.4 31.4 %collective-permute-start.28 = (f32[2048,128]{1,0:T(8,128)S(1)}, f32[2048,128]{1,0:T(8,128)S(1)}, u32[]{:S(2)}, u32[]{:S(2)}) collective-permute-start(f32[2048,128]{1,0:T(8,128)S(1)} %slice.10), channel_id=1, source_target_pairs={{0,2},{2,0},{1,3},{3,1},{4,6},{6,4},{5,7},{7,5},{8,10},{10,8},{9,1... | collective-permute-start | bytes 3145736 | tf_op jit(solution)/shard_map/ppermute | solution.py:512
  98.2 5.4 %collective-permute-start.24 = (f32[2,2,128,128]{3,2,1,0:T(8,128)S(1)}, f32[2,2,128,128]{3,2,1,0:T(8,128)S(1)}, u32[]{:S(2)}, u32[]{:S(2)}) collective-permute-start(f32[2,2,128,128]{3,2,1,0:T(8,128)S(1)} %get-tuple-element.125.refs_2_), channel_id=1, source_target_pairs={{4,8},{8,12},{5,9},{9,13},{6,10},{10,14},{7,11},{11,15},{20,24},{2... | collective-permute-start | bytes 786440 | tf_op jit(solution)/shard_map/ppermute | solution.py:627
  101.2 11.7 %collective-permute-start.23 = (f32[2,2,128,128]{3,2,1,0:T(8,128)S(1)}, f32[2,2,128,128]{3,2,1,0:T(8,128)S(1)}, u32[]{:S(2)}, u32[]{:S(2)}) collective-permute-start(f32[2,2,128,128]{3,2,1,0:T(8,128)S(1)} %get-tuple-element.127), channel_id=1, source_target_pairs={{4,0},{8,4},{12,8},{5,1},{9,5},{13,9},{6,2},{10,6},{14,10},{7,3},{... | collective-permute-start | bytes 786440 | tf_op jit(solution)/shard_map/ppermute | solution.py:627
  103.6 12.9 %collective-permute-start.26 = (f32[2,2,128,128]{3,2,1,0:T(8,128)S(1)}, f32[2,2,128,128]{3,2,1,0:T(8,128)S(1)}, u32[]{:S(2)}, u32[]{:S(2)}) collective-permute-start(f32[2,2,128,128]{3,2,1,0:T(8,128)S(1)} %get-tuple-element.129.refs_2_), channel_id=1, source_target_pairs={{8,12},{9,13},{10,14},{11,15},{24,28},{25,29},{26,30},{27,31}} | collective-permute-start | bytes 786440 | tf_op jit(solution)/shard_map/ppermute | solution.py:627
  113.7 8.8 %collective-permute-start.25 = (f32[2,2,128,128]{3,2,1,0:T(8,128)S(1)}, f32[2,2,128,128]{3,2,1,0:T(8,128)S(1)}, u32[]{:S(2)}, u32[]{:S(2)}) collective-permute-start(f32[2,2,128,128]{3,2,1,0:T(8,128)S(1)} %get-tuple-element.131), channel_id=1, source_target_pairs={{4,0},{8,4},{12,8},{5,1},{9,5},{13,9},{6,2},{10,6},{14,10},{7,3},{... | collective-permute-start | bytes 786440 | tf_op jit(solution)/shard_map/ppermute | solution.py:627
  115.1 33.2 %collective-permute-start.31 = (f32[2048,128]{1,0:T(8,128)S(1)}, f32[2048,128]{1,0:T(8,128)S(1)}, u32[]{:S(2)}, u32[]{:S(2)}) collective-permute-start(f32[2048,128]{1,0:T(8,128)S(1)} %slice.11), channel_id=1, source_target_pairs={{0,2},{2,0},{1,3},{3,1},{4,6},{6,4},{5,7},{7,5},{8,10},{10,8},{9,1... | collective-permute-start | bytes 3145736 | tf_op jit(solution)/shard_map/ppermute | solution.py:512
  123.4 10.0 %collective-permute-start.27 = (f32[2,2,128,128]{3,2,1,0:T(8,128)S(1)}, f32[2,2,128,128]{3,2,1,0:T(8,128)S(1)}, u32[]{:S(2)}, u32[]{:S(2)}) collective-permute-start(f32[2,2,128,128]{3,2,1,0:T(8,128)S(1)} %get-tuple-element.135), channel_id=1, source_target_pairs={{4,0},{8,4},{12,8},{5,1},{9,5},{13,9},{6,2},{10,6},{14,10},{7,3},{... | collective-permute-start | bytes 786440 | tf_op jit(solution)/shard_map/ppermute | solution.py:627
  134.4 11.8 %collective-permute-start.29 = (f32[2,2,128,128]{3,2,1,0:T(8,128)S(1)}, f32[2,2,128,128]{3,2,1,0:T(8,128)S(1)}, u32[]{:S(2)}, u32[]{:S(2)}) collective-permute-start(f32[2,2,128,128]{3,2,1,0:T(8,128)S(1)} %get-tuple-element.137), channel_id=1, source_target_pairs={{4,0},{8,4},{5,1},{9,5},{6,2},{10,6},{7,3},{11,7},{20,16},{24,20},... | collective-permute-start | bytes 786440 | tf_op jit(solution)/shard_map/ppermute | solution.py:627
  147.0 8.3 %collective-permute-start.30 = (f32[2,2,128,128]{3,2,1,0:T(8,128)S(1)}, f32[2,2,128,128]{3,2,1,0:T(8,128)S(1)}, u32[]{:S(2)}, u32[]{:S(2)}) collective-permute-start(f32[2,2,128,128]{3,2,1,0:T(8,128)S(1)} %get-tuple-element.139), channel_id=1, source_target_pairs={{4,0},{5,1},{6,2},{7,3},{20,16},{21,17},{22,18},{23,19}} | collective-permute-start | bytes 786440 | tf_op jit(solution)/shard_map/ppermute | solution.py:627
  157.8 4.6 %collective-permute-start.32 = (f32[2,2,1,192,768]{4,3,2,1,0:T(8,128)S(1)}, f32[2,2,1,192,768]{4,3,2,1,0:T(8,128)S(1)}, u32[]{:S(2)}, u32[]{:S(2)}) collective-permute-start(f32[2,2,1,192,768]{4,3,2,1,0:T(8,128)S(1)} %split_rows.6), channel_id=1, source_target_pairs={{0,1},{1,0},{2,3},{3,2},{4,5},{5,4},{6,7},{7,6},{8,9},{9,8},{10,11... | collective-permute-start | bytes 7077896 | tf_op jit(solution)/shard_map/ppermute | solution.py:512

commit v10 on v8

--- a/solution.py
+++ b/solution.py
@@ -526,7 +526,13 @@
             copy.start()
         for copy in copies:
             copy.wait()
-        scans = [mine.at[0], *scans]
+        across_probe, beside = scans
+        scans = [
+            lambda i: mine[0, i],
+            lambda i: across_probe[i],
+            lambda i: beside[i],
+            lambda i: across_probe[n + i],
+        ]
         lat, side = lax.axis_index("lat"), lax.axis_index("probe")
         lane = lax.broadcasted_iota(jnp.int32, (1, 128), 1)
         at = lax.broadcasted_iota(jnp.int32, (total, 128), 0)
@@ -535,7 +541,7 @@
         for which, scan in enumerate(scans):
             owner = (side ^ (which % 2)) * 2 + (lat ^ (which // 2))
             for i in range(n):
-                place = scan[i]
+                place = scan(i)
                 key = lay.pack(positions[0, place], positions[1, place], owner * n + i)
                 across = jnp.where(lane == which * n + i, key, across)
                 down = jnp.where(at == which * n + i, key, down)
@@ -551,7 +557,7 @@
 
     return pl.pallas_call(
         body,
-        in_specs=[HBM] * 2 + [SMEM] * 3,
+        in_specs=[HBM] * 2 + [SMEM] * 2,
         out_specs=VMEM,
         out_shape=pltpu.VMEM((1, 128), jnp.int32),
         scratch_shapes=[
@@ -601,8 +607,8 @@
         beside = swap(scan, "lat")
         half_rows, beside = lax.optimization_barrier((specimen, beside))
         other = swap(half_rows, "lat")
-        indices = [scan, swap(scan, "probe"), beside, swap(beside, "probe")]
-        measured, *indices[1:] = lax.optimization_barrier((frames, *indices[1:]))
+        indices = [scan, swap(jnp.concatenate([scan, beside]), "probe"), beside]
+        measured, indices[1] = lax.optimization_barrier((frames, indices[1]))
         end = sections - 1
         ends = [(2 * end, 2 * end + 1), (2 * end + 1, 2 * end)]
         mine = lax.ppermute(measured, ("depth", "probe"), ends)

time: 160 us -> 161 us (level)
    ppermute x8 -> x7, waiting for transfers between devices: 8.46 us -> 6.95 us  [swap(): return lax.ppermute(shard, axis, [(0, 1), (1, 0)])]
    ppermute x8 -> x7, starting transfers between devices: 7.3 us -> 7.26 us  [swap(): return lax.ppermute(shard, axis, [(0, 1), (1, 0)])]
  transfers between devices with their start and end apart: 31 -> 30, of which waited for: 20 -> 20; matrix products, arithmetic and copies ran while one was open for 0% -> 1% of each run, Pallas kernels for 25% -> 24%
where the time goes in v10:
time: 161 us; the launch traced here: 160 us
  starting transfers between devices  58.9 us (37%)
  waiting for transfers between devices  55.3 us (34%)
  Pallas kernels  43.9 us (27%)
    ppermute x20, starting transfers between devices, pass_on(): return lax.ppermute(wave, 'depth', pairs) if pairs else None  49.5 us
    ppermute x20, waiting for transfers between devices, pass_on(): return lax.ppermute(wave, 'depth', pairs) if pairs else None  48.3 us
    pallas_call x39, Pallas kernels, call(): pl.pallas_call(kernel, in_specs=specs, out_specs=[VMEM] * (1 + len(outs)...  36.2 us
    ppermute x7, starting transfers between devices, swap(): return lax.ppermute(shard, axis, [(0, 1), (1, 0)])  7.26 us
    ppermute x7, waiting for transfers between devices, swap(): return lax.ppermute(shard, axis, [(0, 1), (1, 0)])  6.95 us
  transfers between devices with their start and end apart: 30, of which 20 were waited for; matrix products, arithmetic and copies ran while one was open for 1% of the time, Pallas kernels for 24%

profile of v10, /device:TPU:0, one launch (start us, length us, event | category | flops | bytes accessed | tf_op | source)
XLA Modules:
  0.0 159.9 jit_solution(9378175990732237158)
XLA Ops:
  2.4 2.7 %collective-permute-start.3 = (s32[32]{0:T(128)S(1)}, s32[32]{0:T(128)S(1)}, u32[]{:S(2)}, u32[]{:S(2)}) collective-permute-start(s32[32]{0:T(128)S(1)} %pad_add_fusion), channel_id=1, source_target_pairs={{0,2},{2,0},{1,3},{3,1},{4,6},{6,4},{5,7},{7,5},{8,10},{10,8},{9,1... | collective-permute-start | bytes 392 | tf_op jit(solution)/shard_map/ppermute | solution.py:512
  5.1 1.5 collective-permute-done.3.refs_0_
  7.4 1.7 %sort_probes.1.refs_0_ = s32[1,128]{1,0:T(1,128)S(1)} custom-call(s32[2,512]{1,0:T(2,128)} %bitcast.18, s32[1,16]{1,0:T(1,128)} %bitcast.21, s32[32]{0:T(128)S(1)} %collective-permute-done.3.refs_0_, s32[16]{0:T(128)S(1)} %collective-permute-done.2.refs_1_), custom_call_target="tpu_custom_call" | custom-call | tf_op jit(solution)/shard_map/sort_probes/pallas_call | solution.py:558
  9.5 2.9 %cut_patches.4.refs_2_ = f32[42368,128]{1,0:T(8,128)S(1)} custom-call(s32[1,128]{1,0:T(1,128)S(1)} %sort_probes.1.refs_0_, f32[2,2,384,768]{3,2,1,0:T(8,128)} %x, f32[2,2,384,768]{3,2,1,0:T(8,128)S(1)} %collective-permute-done.4.refs_2_), custom_call_target="tpu_custom_call" | custom-call | flops 1000 | bytes 1000 | tf_op jit(solution)/shard_map/cut_patches/pallas_call | solution.py:157
  13.4 3.9 %collective-permute-start.5 = (f32[2,2,128,128]{3,2,1,0:T(8,128)S(1)}, f32[2,2,128,128]{3,2,1,0:T(8,128)S(1)}, u32[]{:S(2)}, u32[]{:S(2)}) collective-permute-start(f32[2,2,128,128]{3,2,1,0:T(8,128)S(1)} %get-tuple-element.88), channel_id=1, source_target_pairs={{0,4},{1,5},{2,6},{3,7},{16,20},{17,21},{18,22},{19,23}} | collective-permute-start | bytes 786440 | tf_op jit(solution)/shard_map/ppermute | solution.py:633
  17.3 2.3 %bring.1.refs_1_ = f32[2,2,384,768]{3,2,1,0:T(8,128)S(1)} custom-call(f32[2,2,384,768]{3,2,1,0:T(8,128)} %x), custom_call_target="tpu_custom_call" | custom-call | flops 1000 | bytes 1000 | tf_op jit(solution)/shard_map/bring/pallas_call | solution.py:579
  19.7 1.8 %cut_patches.5.refs_0_ = f32[42368,128]{1,0:T(8,128)S(1)} custom-call(s32[1,128]{1,0:T(1,128)S(1)} %sort_probes.1.refs_0_, f32[2,2,384,768]{3,2,1,0:T(8,128)S(1)} %bring.1.refs_1_, f32[2,2,384,768]{3,2,1,0:T(8,128)S(1)} %collective-permute-done.4.refs_2_, f32[42368,128]{1,0:T(8,128)S(1)} %get-tuple-element.90.refs_3_), custom_call_target="tpu_custom_call", output_to_operand_aliasing={{}: (3, {})} | custom-call | flops 1000 | bytes 1000 | tf_op jit(solution)/shard_map/cut_patches/pallas_call | solution.py:157
  22.0 1.2 collective-permute-done.5.refs_1_
  24.2 4.4 %collective-permute-start.6 = (f32[2,2,128,128]{3,2,1,0:T(8,128)S(1)}, f32[2,2,128,128]{3,2,1,0:T(8,128)S(1)}, u32[]{:S(2)}, u32[]{:S(2)}) collective-permute-start(f32[2,2,128,128]{3,2,1,0:T(8,128)S(1)} %get-tuple-element.91), channel_id=1, source_target_pairs={{0,4},{4,8},{1,5},{5,9},{2,6},{6,10},{3,7},{7,11},{16,20},{20,24},... | collective-permute-start | bytes 786440 | tf_op jit(solution)/shard_map/ppermute | solution.py:633
  28.6 1.6 collective-permute-start.8
  30.9 1.3 collective-permute-done.8.refs_1_
  32.2 1.5 collective-permute-done.6.refs_1_
  35.3 4.4 %collective-permute-start.11 = (f32[2,2,128,128]{3,2,1,0:T(8,128)S(1)}, f32[2,2,128,128]{3,2,1,0:T(8,128)S(1)}, u32[]{:S(2)}, u32[]{:S(2)}) collective-permute-start(f32[2,2,128,128]{3,2,1,0:T(8,128)S(1)} %get-tuple-element.99), channel_id=1, source_target_pairs={{0,4},{4,8},{8,12},{1,5},{5,9},{9,13},{2,6},{6,10},{10,14},{3,7},{... | collective-permute-start | bytes 786440 | tf_op jit(solution)/shard_map/ppermute | solution.py:633
  39.7 1.7 %cut_patches.6.refs_6_ = f32[42368,128]{1,0:T(8,128)S(1)} custom-call(s32[1,128]{1,0:T(1,128)S(1)} %sort_probes.1.refs_0_, f32[2,2,384,768]{3,2,1,0:T(8,128)S(1)} %bring.1.refs_1_, f32[2,2,384,768]{3,2,1,0:T(8,128)S(1)} %collective-permute-done.4.refs_2_, f32[42368,128]{1,0:T(8,128)S(1)} %get-tuple-element.97.refs_3_), custom_call_target="tpu_custom_call", output_to_operand_aliasing={{}: (3, {})} | custom-call | flops 1000 | bytes 1000 | tf_op jit(solution)/shard_map/cut_patches/pallas_call | solution.py:157
  42.2 1.7 %collective-permute-done.11.refs_1_ = f32[2,2,128,128]{3,2,1,0:T(8,128)S(1)} collective-permute-done((f32[2,2,128,128]{3,2,1,0:T(8,128)S(1)}, f32[2,2,128,128]{3,2,1,0:T(8,128)S(1)}, u32[]{:S(2)}, u32[]{:S(2)}) %collective-permute-start.11) | collective-permute-done | bytes 262176 | tf_op jit(solution)/shard_map/ppermute | solution.py:633
  44.8 4.4 %collective-permute-start.13 = (f32[2,2,128,128]{3,2,1,0:T(8,128)S(1)}, f32[2,2,128,128]{3,2,1,0:T(8,128)S(1)}, u32[]{:S(2)}, u32[]{:S(2)}) collective-permute-start(f32[2,2,128,128]{3,2,1,0:T(8,128)S(1)} %get-tuple-element.101.refs_1_), channel_id=1, source_target_pairs={{0,4},{4,8},{8,12},{1,5},{5,9},{9,13},{2,6},{6,10},{10,14},{3,7},{... | collective-permute-start | bytes 786440 | tf_op jit(solution)/shard_map/ppermute | solution.py:633
  49.2 2.5 %cut_patches.7.refs_2_ = f32[42368,128]{1,0:T(8,128)S(1)} custom-call(s32[1,128]{1,0:T(1,128)S(1)} %sort_probes.1.refs_0_, f32[2,2,384,768]{3,2,1,0:T(8,128)S(1)} %bring.1.refs_1_, f32[2,2,384,768]{3,2,1,0:T(8,128)S(1)} %collective-permute-done.4.refs_2_, f32[42368,128]{1,0:T(8,128)S(1)} %get-tuple-element.102.refs_3_), custom_call_target="tpu_custom_call", output_to_operand_aliasing={{}: (3, {})} | custom-call | flops 1000 | bytes 1000 | tf_op jit(solution)/shard_map/cut_patches/pallas_call | solution.py:157
  54.0 5.4 %collective-permute-start.15 = (f32[2,2,128,128]{3,2,1,0:T(8,128)S(1)}, f32[2,2,128,128]{3,2,1,0:T(8,128)S(1)}, u32[]{:S(2)}, u32[]{:S(2)}) collective-permute-start(f32[2,2,128,128]{3,2,1,0:T(8,128)S(1)} %get-tuple-element.105.refs_2_), channel_id=1, source_target_pairs={{0,4},{4,8},{8,12},{1,5},{5,9},{9,13},{2,6},{6,10},{10,14},{3,7},{... | collective-permute-start | bytes 786440 | tf_op jit(solution)/shard_map/ppermute | solution.py:633
  60.5 3.5 %collective-permute-done.15.refs_1_ = f32[2,2,128,128]{3,2,1,0:T(8,128)S(1)} collective-permute-done((f32[2,2,128,128]{3,2,1,0:T(8,128)S(1)}, f32[2,2,128,128]{3,2,1,0:T(8,128)S(1)}, u32[]{:S(2)}, u32[]{:S(2)}) %collective-permute-start.15) | collective-permute-done | bytes 262176 | tf_op jit(solution)/shard_map/ppermute | solution.py:633
  64.9 4.4 %collective-permute-start.17 = (f32[2,2,128,128]{3,2,1,0:T(8,128)S(1)}, f32[2,2,128,128]{3,2,1,0:T(8,128)S(1)}, u32[]{:S(2)}, u32[]{:S(2)}) collective-permute-start(f32[2,2,128,128]{3,2,1,0:T(8,128)S(1)} %get-tuple-element.109.refs_2_), channel_id=1, source_target_pairs={{0,4},{4,8},{8,12},{1,5},{5,9},{9,13},{2,6},{6,10},{10,14},{3,7},{... | collective-permute-start | bytes 786440 | tf_op jit(solution)/shard_map/ppermute | solution.py:633
  69.5 1.3 collective-permute-start.16
  71.1 2.0 %collective-permute-done.17.refs_1_ = f32[2,2,128,128]{3,2,1,0:T(8,128)S(1)} collective-permute-done((f32[2,2,128,128]{3,2,1,0:T(8,128)S(1)}, f32[2,2,128,128]{3,2,1,0:T(8,128)S(1)}, u32[]{:S(2)}, u32[]{:S(2)}) %collective-permute-start.17) | collective-permute-done | bytes 262176 | tf_op jit(solution)/shard_map/ppermute | solution.py:633
  74.1 5.0 %collective-permute-start.19 = (f32[2,2,128,128]{3,2,1,0:T(8,128)S(1)}, f32[2,2,128,128]{3,2,1,0:T(8,128)S(1)}, u32[]{:S(2)}, u32[]{:S(2)}) collective-permute-start(f32[2,2,128,128]{3,2,1,0:T(8,128)S(1)} %get-tuple-element.113.refs_2_), channel_id=1, source_target_pairs={{0,4},{4,8},{8,12},{1,5},{5,9},{9,13},{2,6},{6,10},{10,14},{3,7},{... | collective-permute-start | bytes 786440 | tf_op jit(solution)/shard_map/ppermute | solution.py:633
  80.3 1.3 collective-permute-start.18
  81.6 1.1 deposit_patches.16.refs_3_
  83.8 4.6 %collective-permute-start.21 = (f32[2,2,128,128]{3,2,1,0:T(8,128)S(1)}, f32[2,2,128,128]{3,2,1,0:T(8,128)S(1)}, u32[]{:S(2)}, u32[]{:S(2)}) collective-permute-start(f32[2,2,128,128]{3,2,1,0:T(8,128)S(1)} %get-tuple-element.117.refs_2_), channel_id=1, source_target_pairs={{0,4},{4,8},{8,12},{1,5},{5,9},{9,13},{2,6},{6,10},{10,14},{3,7},{... | collective-permute-start | bytes 786440 | tf_op jit(solution)/shard_map/ppermute | solution.py:633
  89.7 1.3 collective-permute-start.20
  91.1 1.6 collective-permute-start.27
  94.4 3.5 %collective-permute-done.20.refs_1_ = f32[2,2,128,128]{3,2,1,0:T(8,128)S(1)} collective-permute-done((f32[2,2,128,128]{3,2,1,0:T(8,128)S(1)}, f32[2,2,128,128]{3,2,1,0:T(8,128)S(1)}, u32[]{:S(2)}, u32[]{:S(2)}) %collective-permute-start.20) | collective-permute-done | bytes 262176 | tf_op jit(solution)/shard_map/ppermute | solution.py:633
  98.9 1.3 collective-permute-start.22
  100.2 1.1 deposit_patches.18.refs_2_
  102.0 6.5 %collective-permute-done.22.refs_1_ = f32[2,2,128,128]{3,2,1,0:T(8,128)S(1)} collective-permute-done((f32[2,2,128,128]{3,2,1,0:T(8,128)S(1)}, f32[2,2,128,128]{3,2,1,0:T(8,128)S(1)}, u32[]{:S(2)}, u32[]{:S(2)}) %collective-permute-start.22) | collective-permute-done | bytes 262176 | tf_op jit(solution)/shard_map/ppermute | solution.py:633
  109.4 1.3 collective-permute-start.24
  112.4 5.9 %collective-permute-done.24.refs_1_ = f32[2,2,128,128]{3,2,1,0:T(8,128)S(1)} collective-permute-done((f32[2,2,128,128]{3,2,1,0:T(8,128)S(1)}, f32[2,2,128,128]{3,2,1,0:T(8,128)S(1)}, u32[]{:S(2)}, u32[]{:S(2)}) %collective-permute-start.24) | collective-permute-done | bytes 262176 | tf_op jit(solution)/shard_map/ppermute | solution.py:633
  119.2 1.3 collective-permute-start.26
  120.5 2.1 %deposit_patches.20.refs_2_ = f32[42368,128]{1,0:T(8,128)S(1)} custom-call(s32[1,128]{1,0:T(1,128)S(1)} %sort_probes.1.refs_0_, f32[2048,128]{1,0:T(8,128)S(1)} %collective-permute-done.27.refs_1_, f32[42368,128]{1,0:T(8,128)S(1)} %get-tuple-element.132.refs_2_), custom_call_target="tpu_custom_call", output_to_operand_aliasing={{}: (2, {})} | custom-call | flops 1000 | bytes 1000 | tf_op jit(solution)/shard_map/deposit_patches/pallas_call | solution.py:157
  122.6 6.8 %collective-permute-done.26.refs_1_ = f32[2,2,128,128]{3,2,1,0:T(8,128)S(1)} collective-permute-done((f32[2,2,128,128]{3,2,1,0:T(8,128)S(1)}, f32[2,2,128,128]{3,2,1,0:T(8,128)S(1)}, u32[]{:S(2)}, u32[]{:S(2)}) %collective-permute-start.26) | collective-permute-done | bytes 262176 | tf_op jit(solution)/shard_map/ppermute | solution.py:633
  130.3 1.3 collective-permute-start.28
  131.6 1.1 deposit_patches.21.refs_2_
  132.7 9.2 %collective-permute-done.28.refs_1_ = f32[2,2,128,128]{3,2,1,0:T(8,128)S(1)} collective-permute-done((f32[2,2,128,128]{3,2,1,0:T(8,128)S(1)}, f32[2,2,128,128]{3,2,1,0:T(8,128)S(1)}, u32[]{:S(2)}, u32[]{:S(2)}) %collective-permute-start.28) | collective-permute-done | bytes 262176 | tf_op jit(solution)/shard_map/ppermute | solution.py:633
  142.9 1.3 collective-permute-start.29
  144.2 1.7 %deposit_patches.22.refs_2_ = f32[42368,128]{1,0:T(8,128)S(1)} custom-call(s32[1,128]{1,0:T(1,128)S(1)} %sort_probes.1.refs_0_, f32[2048,128]{1,0:T(8,128)S(1)} %collective-permute-done.30.refs_1_, f32[42368,128]{1,0:T(8,128)S(1)} %get-tuple-element.136.refs_2_), custom_call_target="tpu_custom_call", output_to_operand_aliasing={{}: (2, {})} | custom-call | flops 1000 | bytes 1000 | tf_op jit(solution)/shard_map/deposit_patches/pallas_call | solution.py:157
  145.8 5.3 %collective-permute-done.29.refs_1_ = f32[2,2,128,128]{3,2,1,0:T(8,128)S(1)} collective-permute-done((f32[2,2,128,128]{3,2,1,0:T(8,128)S(1)}, f32[2,2,128,128]{3,2,1,0:T(8,128)S(1)}, u32[]{:S(2)}, u32[]{:S(2)}) %collective-permute-start.29) | collective-permute-done | bytes 262176 | tf_op jit(solution)/shard_map/ppermute | solution.py:633
  152.0 1.1 deposit_patches.23.state
  153.7 1.8 %split_rows.7 = (f32[2,2,1,192,768]{4,3,2,1,0:T(8,128)S(1)}, f32[4096,128]{1,0:T(8,128)}) custom-call(f32[42368,128]{1,0:T(8,128)S(1)} %deposit_patches.23.state), custom_call_target="tpu_custom_call" | custom-call | flops 1000 | bytes 1000 | tf_op jit(solution)/shard_map/split_rows/pallas_call | solution.py:476
  155.5 2.7 %collective-permute-done.31 = f32[2,2,1,192,768]{4,3,2,1,0:T(8,128)S(1)} collective-permute-done((f32[2,2,1,192,768]{4,3,2,1,0:T(8,128)S(1)}, f32[2,2,1,192,768]{4,3,2,1,0:T(8,128)S(1)}, u32[]{:S(2)}, u32[]{:S(2)}) %collective-permute-start.31) | collective-permute-done | bytes 2359328 | tf_op jit(solution)/shard_map/ppermute | solution.py:512
  158.2 1.5 conditional.1
  158.2 1.5 add_up.2
  (66 shorter events, 29.4 us)
Async XLA Ops:
  0.0 12.5 %copy-start = (bf16[2,2,2,256,256]{4,3,2,1,0:T(8,128)(2,1)S(1)}, bf16[2,2,2,256,256]{4,3,2,1,0:T(8,128)(2,1)}, u32[]{:S(2)}) copy-start(bf16[2,2,2,256,256]{4,3,2,1,0:T(8,128)(2,1)} %constant.5.clone.refs_0_) | copy-start | bytes 3145732
  0.0 12.5 %copy-start.1 = (f32[2,128,128]{2,1,0:T(8,128)S(1)}, f32[2,128,128]{2,1,0:T(8,128)}, u32[]{:S(2)}) copy-start(f32[2,128,128]{2,1,0:T(8,128)} %refs_2_.13) | copy-start | bytes 393220
  0.0 1.4 collective-permute-start.2
  1.4 8.1 %collective-permute-start.4 = (f32[2,2,384,768]{3,2,1,0:T(8,128)}, f32[2,2,384,768]{3,2,1,0:T(8,128)S(1)}, u32[]{:S(2)}, u32[]{:S(2)}) collective-permute-start(f32[2,2,384,768]{3,2,1,0:T(8,128)} %x), channel_id=1, source_target_pairs={{0,1},{1,0},{2,3},{3,2},{4,5},{5,4},{6,7},{7,6},{8,9},{9,8},{10,11... | collective-permute-start | bytes 14155784 | tf_op jit(solution)/shard_map/ppermute | solution.py:512
  2.4 4.2 %collective-permute-start.3 = (s32[32]{0:T(128)S(1)}, s32[32]{0:T(128)S(1)}, u32[]{:S(2)}, u32[]{:S(2)}) collective-permute-start(s32[32]{0:T(128)S(1)} %pad_add_fusion), channel_id=1, source_target_pairs={{0,2},{2,0},{1,3},{3,1},{4,6},{6,4},{5,7},{7,5},{8,10},{10,8},{9,1... | collective-permute-start | bytes 392 | tf_op jit(solution)/shard_map/ppermute | solution.py:512
  6.7 25.5 %collective-permute-start.7 = (f32[16,1,128,128]{3,2,1,0:T(8,128)}, f32[16,1,128,128]{3,2,1,0:T(8,128)S(1)}, u32[]{:S(2)}, u32[]{:S(2)}) collective-permute-start(f32[16,1,128,128]{3,2,1,0:T(8,128)} %param.12), channel_id=1, source_target_pairs={{12,14},{14,12},{13,15},{15,13},{28,30},{30,28},{29,31},{31,29}} | collective-permute-start | bytes 3145736 | tf_op jit(solution)/shard_map/ppermute | solution.py:614
  13.4 9.8 %collective-permute-start.5 = (f32[2,2,128,128]{3,2,1,0:T(8,128)S(1)}, f32[2,2,128,128]{3,2,1,0:T(8,128)S(1)}, u32[]{:S(2)}, u32[]{:S(2)}) collective-permute-start(f32[2,2,128,128]{3,2,1,0:T(8,128)S(1)} %get-tuple-element.88), channel_id=1, source_target_pairs={{0,4},{1,5},{2,6},{3,7},{16,20},{17,21},{18,22},{19,23}} | collective-permute-start | bytes 786440 | tf_op jit(solution)/shard_map/ppermute | solution.py:633
  22.0 8.1 %copy-start.2 = (f32[16,1,128,128]{3,2,1,0:T(8,128)S(1)}, f32[16,1,128,128]{3,2,1,0:T(8,128)}, u32[]{:S(2)}) copy-start(f32[16,1,128,128]{3,2,1,0:T(8,128)} %param.12) | copy-start | bytes 3145732
  24.2 9.5 %collective-permute-start.6 = (f32[2,2,128,128]{3,2,1,0:T(8,128)S(1)}, f32[2,2,128,128]{3,2,1,0:T(8,128)S(1)}, u32[]{:S(2)}, u32[]{:S(2)}) collective-permute-start(f32[2,2,128,128]{3,2,1,0:T(8,128)S(1)} %get-tuple-element.91), channel_id=1, source_target_pairs={{0,4},{4,8},{1,5},{5,9},{2,6},{6,10},{3,7},{7,11},{16,20},{20,24},... | collective-permute-start | bytes 786440 | tf_op jit(solution)/shard_map/ppermute | solution.py:633
  28.6 3.6 %collective-permute-start.8 = (s32[1,128]{1,0:T(1,128)S(1)}, s32[1,128]{1,0:T(1,128)S(1)}, u32[]{:S(2)}, u32[]{:S(2)}) collective-permute-start(s32[1,128]{1,0:T(1,128)S(1)} %sort_probes.1.refs_0_), channel_id=1, source_target_pairs={{0,16},{16,0},{1,17},{17,1},{2,18},{18,2},{3,19},{19,3},{4,20},{20... | collective-permute-start | bytes 1544 | tf_op jit(solution)/shard_map/ppermute | solution.py:512
  30.2 11.3 %collective-permute-start.9 = (f32[16,1,128,128]{3,2,1,0:T(8,128)S(1)}, f32[16,1,128,128]{3,2,1,0:T(8,128)S(1)}, u32[]{:S(2)}, u32[]{:S(2)}) collective-permute-start(f32[16,1,128,128]{3,2,1,0:T(8,128)S(1)} %copy-done.2), channel_id=1, source_target_pairs={{12,13},{13,12},{14,15},{15,14},{28,29},{29,28},{30,31},{31,30}} | collective-permute-start | bytes 3145736 | tf_op jit(solution)/shard_map/ppermute | solution.py:653
  33.7 7.8 %collective-permute-start.10 = (f32[16,1,128,128]{3,2,1,0:T(8,128)S(1)}, f32[16,1,128,128]{3,2,1,0:T(8,128)S(1)}, u32[]{:S(2)}, u32[]{:S(2)}) collective-permute-start(f32[16,1,128,128]{3,2,1,0:T(8,128)S(1)} %collective-permute-done.7), channel_id=1, source_target_pairs={{12,13},{13,12},{14,15},{15,14},{28,29},{29,28},{30,31},{31,30}} | collective-permute-start | bytes 3145736 | tf_op jit(solution)/shard_map/ppermute | solution.py:653
  35.3 8.6 %collective-permute-start.11 = (f32[2,2,128,128]{3,2,1,0:T(8,128)S(1)}, f32[2,2,128,128]{3,2,1,0:T(8,128)S(1)}, u32[]{:S(2)}, u32[]{:S(2)}) collective-permute-start(f32[2,2,128,128]{3,2,1,0:T(8,128)S(1)} %get-tuple-element.99), channel_id=1, source_target_pairs={{0,4},{4,8},{8,12},{1,5},{5,9},{9,13},{2,6},{6,10},{10,14},{3,7},{... | collective-permute-start | bytes 786440 | tf_op jit(solution)/shard_map/ppermute | solution.py:633
  44.8 8.3 %collective-permute-start.13 = (f32[2,2,128,128]{3,2,1,0:T(8,128)S(1)}, f32[2,2,128,128]{3,2,1,0:T(8,128)S(1)}, u32[]{:S(2)}, u32[]{:S(2)}) collective-permute-start(f32[2,2,128,128]{3,2,1,0:T(8,128)S(1)} %get-tuple-element.101.refs_1_), channel_id=1, source_target_pairs={{0,4},{4,8},{8,12},{1,5},{5,9},{9,13},{2,6},{6,10},{10,14},{3,7},{... | collective-permute-start | bytes 786440 | tf_op jit(solution)/shard_map/ppermute | solution.py:633
  51.8 7.7 %collective-permute-start.12 = (f32[2,2,128,128]{3,2,1,0:T(8,128)S(1)}, f32[2,2,128,128]{3,2,1,0:T(8,128)S(1)}, u32[]{:S(2)}, u32[]{:S(2)}) collective-permute-start(f32[2,2,128,128]{3,2,1,0:T(8,128)S(1)} %get-tuple-element.103), channel_id=1, source_target_pairs={{12,8},{13,9},{14,10},{15,11},{28,24},{29,25},{30,26},{31,27}} | collective-permute-start | bytes 786440 | tf_op jit(solution)/shard_map/ppermute | solution.py:633
  54.0 9.9 %collective-permute-start.15 = (f32[2,2,128,128]{3,2,1,0:T(8,128)S(1)}, f32[2,2,128,128]{3,2,1,0:T(8,128)S(1)}, u32[]{:S(2)}, u32[]{:S(2)}) collective-permute-start(f32[2,2,128,128]{3,2,1,0:T(8,128)S(1)} %get-tuple-element.105.refs_2_), channel_id=1, source_target_pairs={{0,4},{4,8},{8,12},{1,5},{5,9},{9,13},{2,6},{6,10},{10,14},{3,7},{... | collective-permute-start | bytes 786440 | tf_op jit(solution)/shard_map/ppermute | solution.py:633
  59.5 9.8 %collective-permute-start.14 = (f32[2,2,128,128]{3,2,1,0:T(8,128)S(1)}, f32[2,2,128,128]{3,2,1,0:T(8,128)S(1)}, u32[]{:S(2)}, u32[]{:S(2)}) collective-permute-start(f32[2,2,128,128]{3,2,1,0:T(8,128)S(1)} %get-tuple-element.107), channel_id=1, source_target_pairs={{8,4},{12,8},{9,5},{13,9},{10,6},{14,10},{11,7},{15,11},{24,20},{2... | collective-permute-start | bytes 786440 | tf_op jit(solution)/shard_map/ppermute | solution.py:633
  64.9 8.3 %collective-permute-start.17 = (f32[2,2,128,128]{3,2,1,0:T(8,128)S(1)}, f32[2,2,128,128]{3,2,1,0:T(8,128)S(1)}, u32[]{:S(2)}, u32[]{:S(2)}) collective-permute-start(f32[2,2,128,128]{3,2,1,0:T(8,128)S(1)} %get-tuple-element.109.refs_2_), channel_id=1, source_target_pairs={{0,4},{4,8},{8,12},{1,5},{5,9},{9,13},{2,6},{6,10},{10,14},{3,7},{... | collective-permute-start | bytes 786440 | tf_op jit(solution)/shard_map/ppermute | solution.py:633
  69.5 9.9 %collective-permute-start.16 = (f32[2,2,128,128]{3,2,1,0:T(8,128)S(1)}, f32[2,2,128,128]{3,2,1,0:T(8,128)S(1)}, u32[]{:S(2)}, u32[]{:S(2)}) collective-permute-start(f32[2,2,128,128]{3,2,1,0:T(8,128)S(1)} %get-tuple-element.111), channel_id=1, source_target_pairs={{4,0},{8,4},{12,8},{5,1},{9,5},{13,9},{6,2},{10,6},{14,10},{7,3},{... | collective-permute-start | bytes 786440 | tf_op jit(solution)/shard_map/ppermute | solution.py:633
  74.1 8.8 %collective-permute-start.19 = (f32[2,2,128,128]{3,2,1,0:T(8,128)S(1)}, f32[2,2,128,128]{3,2,1,0:T(8,128)S(1)}, u32[]{:S(2)}, u32[]{:S(2)}) collective-permute-start(f32[2,2,128,128]{3,2,1,0:T(8,128)S(1)} %get-tuple-element.113.refs_2_), channel_id=1, source_target_pairs={{0,4},{4,8},{8,12},{1,5},{5,9},{9,13},{2,6},{6,10},{10,14},{3,7},{... | collective-permute-start | bytes 786440 | tf_op jit(solution)/shard_map/ppermute | solution.py:633
  80.3 8.5 %collective-permute-start.18 = (f32[2,2,128,128]{3,2,1,0:T(8,128)S(1)}, f32[2,2,128,128]{3,2,1,0:T(8,128)S(1)}, u32[]{:S(2)}, u32[]{:S(2)}) collective-permute-start(f32[2,2,128,128]{3,2,1,0:T(8,128)S(1)} %get-tuple-element.115), channel_id=1, source_target_pairs={{4,0},{8,4},{12,8},{5,1},{9,5},{13,9},{6,2},{10,6},{14,10},{7,3},{... | collective-permute-start | bytes 786440 | tf_op jit(solution)/shard_map/ppermute | solution.py:633
  83.8 9.9 %collective-permute-start.21 = (f32[2,2,128,128]{3,2,1,0:T(8,128)S(1)}, f32[2,2,128,128]{3,2,1,0:T(8,128)S(1)}, u32[]{:S(2)}, u32[]{:S(2)}) collective-permute-start(f32[2,2,128,128]{3,2,1,0:T(8,128)S(1)} %get-tuple-element.117.refs_2_), channel_id=1, source_target_pairs={{0,4},{4,8},{8,12},{1,5},{5,9},{9,13},{2,6},{6,10},{10,14},{3,7},{... | collective-permute-start | bytes 786440 | tf_op jit(solution)/shard_map/ppermute | solution.py:633
  89.7 8.3 %collective-permute-start.20 = (f32[2,2,128,128]{3,2,1,0:T(8,128)S(1)}, f32[2,2,128,128]{3,2,1,0:T(8,128)S(1)}, u32[]{:S(2)}, u32[]{:S(2)}) collective-permute-start(f32[2,2,128,128]{3,2,1,0:T(8,128)S(1)} %get-tuple-element.119), channel_id=1, source_target_pairs={{4,0},{8,4},{12,8},{5,1},{9,5},{13,9},{6,2},{10,6},{14,10},{7,3},{... | collective-permute-start | bytes 786440 | tf_op jit(solution)/shard_map/ppermute | solution.py:633
  91.1 29.4 %collective-permute-start.27 = (f32[2048,128]{1,0:T(8,128)S(1)}, f32[2048,128]{1,0:T(8,128)S(1)}, u32[]{:S(2)}, u32[]{:S(2)}) collective-permute-start(f32[2048,128]{1,0:T(8,128)S(1)} %slice.10), channel_id=1, source_target_pairs={{0,2},{2,0},{1,3},{3,1},{4,6},{6,4},{5,7},{7,5},{8,10},{10,8},{9,1... | collective-permute-start | bytes 3145736 | tf_op jit(solution)/shard_map/ppermute | solution.py:512
  93.8 7.5 %collective-permute-start.23 = (f32[2,2,128,128]{3,2,1,0:T(8,128)S(1)}, f32[2,2,128,128]{3,2,1,0:T(8,128)S(1)}, u32[]{:S(2)}, u32[]{:S(2)}) collective-permute-start(f32[2,2,128,128]{3,2,1,0:T(8,128)S(1)} %get-tuple-element.121.refs_2_), channel_id=1, source_target_pairs={{4,8},{8,12},{5,9},{9,13},{6,10},{10,14},{7,11},{11,15},{20,24},{2... | collective-permute-start | bytes 786440 | tf_op jit(solution)/shard_map/ppermute | solution.py:633
  98.9 9.6 %collective-permute-start.22 = (f32[2,2,128,128]{3,2,1,0:T(8,128)S(1)}, f32[2,2,128,128]{3,2,1,0:T(8,128)S(1)}, u32[]{:S(2)}, u32[]{:S(2)}) collective-permute-start(f32[2,2,128,128]{3,2,1,0:T(8,128)S(1)} %get-tuple-element.123), channel_id=1, source_target_pairs={{4,0},{8,4},{12,8},{5,1},{9,5},{13,9},{6,2},{10,6},{14,10},{7,3},{... | collective-permute-start | bytes 786440 | tf_op jit(solution)/shard_map/ppermute | solution.py:633
  101.3 11.1 %collective-permute-start.25 = (f32[2,2,128,128]{3,2,1,0:T(8,128)S(1)}, f32[2,2,128,128]{3,2,1,0:T(8,128)S(1)}, u32[]{:S(2)}, u32[]{:S(2)}) collective-permute-start(f32[2,2,128,128]{3,2,1,0:T(8,128)S(1)} %get-tuple-element.125.refs_2_), channel_id=1, source_target_pairs={{8,12},{9,13},{10,14},{11,15},{24,28},{25,29},{26,30},{27,31}} | collective-permute-start | bytes 786440 | tf_op jit(solution)/shard_map/ppermute | solution.py:633
  109.4 9.0 %collective-permute-start.24 = (f32[2,2,128,128]{3,2,1,0:T(8,128)S(1)}, f32[2,2,128,128]{3,2,1,0:T(8,128)S(1)}, u32[]{:S(2)}, u32[]{:S(2)}) collective-permute-start(f32[2,2,128,128]{3,2,1,0:T(8,128)S(1)} %get-tuple-element.127), channel_id=1, source_target_pairs={{4,0},{8,4},{12,8},{5,1},{9,5},{13,9},{6,2},{10,6},{14,10},{7,3},{... | collective-permute-start | bytes 786440 | tf_op jit(solution)/shard_map/ppermute | solution.py:633
  110.7 33.4 %collective-permute-start.30 = (f32[2048,128]{1,0:T(8,128)S(1)}, f32[2048,128]{1,0:T(8,128)S(1)}, u32[]{:S(2)}, u32[]{:S(2)}) collective-permute-start(f32[2048,128]{1,0:T(8,128)S(1)} %slice.11), channel_id=1, source_target_pairs={{0,2},{2,0},{1,3},{3,1},{4,6},{6,4},{5,7},{7,5},{8,10},{10,8},{9,1... | collective-permute-start | bytes 3145736 | tf_op jit(solution)/shard_map/ppermute | solution.py:512
  119.2 10.2 %collective-permute-start.26 = (f32[2,2,128,128]{3,2,1,0:T(8,128)S(1)}, f32[2,2,128,128]{3,2,1,0:T(8,128)S(1)}, u32[]{:S(2)}, u32[]{:S(2)}) collective-permute-start(f32[2,2,128,128]{3,2,1,0:T(8,128)S(1)} %get-tuple-element.131), channel_id=1, source_target_pairs={{4,0},{8,4},{12,8},{5,1},{9,5},{13,9},{6,2},{10,6},{14,10},{7,3},{... | collective-permute-start | bytes 786440 | tf_op jit(solution)/shard_map/ppermute | solution.py:633
  130.3 11.6 %collective-permute-start.28 = (f32[2,2,128,128]{3,2,1,0:T(8,128)S(1)}, f32[2,2,128,128]{3,2,1,0:T(8,128)S(1)}, u32[]{:S(2)}, u32[]{:S(2)}) collective-permute-start(f32[2,2,128,128]{3,2,1,0:T(8,128)S(1)} %get-tuple-element.133), channel_id=1, source_target_pairs={{4,0},{8,4},{5,1},{9,5},{6,2},{10,6},{7,3},{11,7},{20,16},{24,20},... | collective-permute-start | bytes 786440 | tf_op jit(solution)/shard_map/ppermute | solution.py:633
  142.9 8.3 %collective-permute-start.29 = (f32[2,2,128,128]{3,2,1,0:T(8,128)S(1)}, f32[2,2,128,128]{3,2,1,0:T(8,128)S(1)}, u32[]{:S(2)}, u32[]{:S(2)}) collective-permute-start(f32[2,2,128,128]{3,2,1,0:T(8,128)S(1)} %get-tuple-element.135), channel_id=1, source_target_pairs={{4,0},{5,1},{6,2},{7,3},{20,16},{21,17},{22,18},{23,19}} | collective-permute-start | bytes 786440 | tf_op jit(solution)/shard_map/ppermute | solution.py:633
  153.6 4.6 %collective-permute-start.31 = (f32[2,2,1,192,768]{4,3,2,1,0:T(8,128)S(1)}, f32[2,2,1,192,768]{4,3,2,1,0:T(8,128)S(1)}, u32[]{:S(2)}, u32[]{:S(2)}) collective-permute-start(f32[2,2,1,192,768]{4,3,2,1,0:T(8,128)S(1)} %split_rows.6), channel_id=1, source_target_pairs={{0,1},{1,0},{2,3},{3,2},{4,5},{5,4},{6,7},{7,6},{8,9},{9,8},{10,11... | collective-permute-start | bytes 7077896 | tf_op jit(solution)/shard_map/ppermute | solution.py:512
